TPU v7x, 32 devices: a whole 2x2x4 slice. The times are simulated.
32 devices in a mesh: groups: 2 (over x), hid: 16 (over z, y, core).
Axes of the slice: x: 2, y: 2, z: 4, core: 2. Of those that a mesh axis runs over, the one named last changes fastest.
Arguments:
- tokens: bfloat16 [256, 8192], P(('groups', 'hid')), parts along dimension 0, may hold values from -6 to 6
- norm_gain: float32 [8192], replicated, may hold values from 0.1 to 1.9
- gate_weight: bfloat16 [8192, 16384], P(None, 'hid'), may hold values from -0.0625 to 0.0625
- up_weight: bfloat16 [8192, 16384], P(None, 'hid'), may hold values from -0.0625 to 0.0625
- down_weight: bfloat16 [16384, 8192], P('hid'), may hold values from -0.046875 to 0.046875
- clip_scale: float32 [16384], P('hid'), may hold values from 0.002 to 0.02
Outputs:
- mixed: bfloat16 [256, 8192], P(('groups', 'hid')), parts along dimension 0
There are 2 independent parts, one for each index of `groups`. A program takes and returns all parts, laid end to end along the dimension named above; an argument that names none is the same for every part. Nothing has to cross between parts.
All inputs are finite; a program needn't handle non-finite values.
Results may differ from a plain program's by a relative error of at most 0.006.
Values may be sent and summed in bfloat16 or wider, within the bound.
No kernel may reach another device: no remote copies, remote signals or barrier semaphores. Data moves between devices by JAX's collectives and lax.ppermute only.
A program may use at most 128 MiB of HBM per device.

v0:
```python
import jax
import jax.numpy as jnp
from jax import lax
from jax.sharding import PartitionSpec as P

FF = 16384
BLOCK = 256


def hadamard(count):
    rows = jnp.arange(count, dtype=jnp.int32)[:, None]
    cols = jnp.arange(count, dtype=jnp.int32)[None, :]
    both = rows & cols
    parity = jnp.zeros((count, count), jnp.int32)
    for place in range(max(count.bit_length(), 1)):
        parity = parity + (both >> place & 1)
    return jnp.where(parity % 2 == 0, 1.0, -1.0).astype(jnp.float32)


def normalize(rows_in, norm_gain):
    values = rows_in.astype(jnp.float32)
    inverse = lax.rsqrt(jnp.mean(values * values, axis=-1, keepdims=True) + 1e-05)
    return (values * inverse * norm_gain).astype(jnp.bfloat16)


def shards(tokens, norm_gain, gate_weight, up_weight, down_weight, clip_scale):
    whole = lax.all_gather(tokens, "hid", axis=0, tiled=True)
    normed = normalize(whole, norm_gain)
    gate = jnp.dot(normed, gate_weight, preferred_element_type=jnp.float32)
    up = jnp.dot(normed, up_weight, preferred_element_type=jnp.float32)
    hidden = jax.nn.silu(gate) * up
    row_count = hidden.shape[0]
    local_blocks = hidden.shape[1] // BLOCK
    shaped = hidden.reshape(row_count, local_blocks, BLOCK)
    shaped = jnp.einsum("tbc,cd->tbd", shaped, hadamard(BLOCK), precision=lax.Precision.HIGHEST)
    gathered = lax.all_to_all(shaped, "hid", split_axis=0, concat_axis=1, tiled=True)
    table = hadamard(gathered.shape[1])
    turned = jnp.einsum("tbc,be->tec", gathered, table, precision=lax.Precision.HIGHEST)
    shaped = lax.all_to_all(
        turned.astype(jnp.bfloat16), "hid", split_axis=1, concat_axis=0, tiled=True
    ).astype(turned.dtype)
    rotated = shaped.reshape(row_count, local_blocks * BLOCK) / jnp.sqrt(jnp.float32(FF))
    limit = 127.0 * clip_scale
    clipped = jnp.clip(rotated, -limit, limit).astype(jnp.bfloat16)
    summed = lax.psum_scatter(
        jnp.dot(clipped, down_weight, preferred_element_type=jnp.float32),
        "hid",
        scatter_dimension=0,
        tiled=True,
    )
    return (tokens.astype(jnp.float32) + summed).astype(jnp.bfloat16)


def solution(mesh):
    in_specs = (
        P(("groups", "hid"), None),
        P(),
        P(None, "hid"),
        P(None, "hid"),
        P("hid", None),
        P("hid"),
    )
    out_specs = P(("groups", "hid"), None)
    return jax.shard_map(shards, mesh=mesh, in_specs=in_specs, out_specs=out_specs, check_vma=False)
```

profile of v0, /device:TPU:0, one launch (start us, length us, event | category | flops | bytes accessed | tf_op | source)
XLA Modules:
  0.0 194.9 jit_solution(14691300666669389388)
XLA Ops:
  6.5 0.0 all-gather.2.cloned.1.call-start
  6.5 0.7 all-gather.2.cloned.1.call-update
  7.3 46.4 %all-gather.2.cloned.1.call-done = bf16[128,8192]{1,0:T(8,128)(2,1)} async-done(((bf16[8,8192]{1,0:T(8,128)(2,1)}), bf16[128,8192]{1,0:T(8,128)(2,1)}) %all-gather.2.cloned.1.call-update) | async-done | bytes 2097168 | tf_op jit(solution)/shard_map/all_gather | solution.py:27
  53.7 2.1 %fusion = f32[128]{0:T(128)S(1)} fusion(bf16[128,8192]{1,0:T(8,128)(2,1)} %all-gather.2.cloned.1.call-done), kind=kLoop, calls=%fused_computation.2 | loop fusion | flops 3145600 | bytes 2097664 | tf_op jit(solution)/shard_map/reduce_sum | solution.py:22
  55.7 0.0 copy-start
  55.7 0.0 copy-start.3
  55.8 0.0 copy-start.4
  55.8 8.9 %fusion.5 = f32[128,1024]{1,0:T(8,128)S(1)} fusion(bf16[8192,1024]{1,0:T(8,128)(2,1)} %param.8, bf16[128,8192]{1,0:T(8,128)(2,1)} %all-gather.2.cloned.1.call-done, f32[8192]{0:T(1024)} %param.7, f32[128]{0:T(128)S(1)} %add_rsqrt_fusion), kind=kOutput, calls=%fused_computation.8 | convolution fusion | flops 2151677952 | bytes 19431936 | tf_op jit(solution)/shard_map/dot_general | solution.py:29
  64.7 0.0 copy-done
  64.7 2.8 %copy-done.3 = bf16[8192,1024]{1,0:T(8,128)(2,1)S(1)} copy-done((bf16[8192,1024]{1,0:T(8,128)(2,1)S(1)}, bf16[8192,1024]{1,0:T(8,128)(2,1)}, u32[]{:S(2)}) %copy-start.3) | copy-done | bytes 16777240
  67.6 0.0 copy-done.4
  67.6 2.5 %convolution_multiply_fusion = f32[128,1024]{1,0:T(8,128)S(1)} fusion(bf16[8192,1024]{1,0:T(8,128)(2,1)S(1)} %copy-done.3, bf16[128,8192]{1,0:T(8,128)(2,1)S(1)} %copy-done, f32[8192]{0:T(1024)S(1)} %copy-done.4, f32[128]{0:T(128)S(1)} %add_rsqrt_fusion, f32[128,1024]{1,0:T(8,128)S(1)} %fusion.5), kind=kOutput, calls=%fused_computation.5 | convolution fusion | flops 2152333312 | bytes 19956224 | tf_op jit(solution)/shard_map/dot_general | solution.py:30
  70.1 0.0 copy-start.2
  70.1 0.9 fusion.7
  71.0 0.3 copy.13
  71.3 17.7 %all_to_all.27 = f32[128,4,256]{2,1,0:T(4,128)S(1)} all-to-all(f32[128,4,256]{2,1,0:T(4,128)S(1)} %copy.13), channel_id=1, replica_groups=mesh['groups'=2,'hid'=16] {'hid'}, dimensions={0} | all-to-all | bytes 1048576 | tf_op jit(solution)/shard_map/all_to_all | solution.py:36
  89.1 0.2 all_to_all.23
  89.3 0.6 fusion.3
  89.9 0.8 copy.15
  90.8 4.1 %all-to-all-start.1 = ((bf16[8,64,256]{2,0,1:T(8,128)(2,1)}), bf16[8,64,256]{2,0,1:T(8,128)(2,1)S(1)}, u32[]{:S(2)}, u32[]{:S(2)}) async-start(bf16[8,64,256]{2,0,1:T(8,128)(2,1)} %copy.15), calls=%async_computation.1 | async-start | bytes 524288 | tf_op jit(solution)/shard_map/all_to_all | solution.py:39
  94.9 0.0 reduce-scatter.2.cloned.1.call-start
  94.9 0.0 copy-done.2
  94.9 10.0 %all-to-all-done.1 = bf16[8,64,256]{2,0,1:T(8,128)(2,1)S(1)} async-done(((bf16[8,64,256]{2,0,1:T(8,128)(2,1)}), bf16[8,64,256]{2,0,1:T(8,128)(2,1)S(1)}, u32[]{:S(2)}, u32[]{:S(2)}) %all-to-all-start.1) | async-done | bytes 262176 | tf_op jit(solution)/shard_map/all_to_all | solution.py:39
  105.0 0.1 copy.25
  105.1 10.1 %fusion.12 = f32[128,8192]{1,0:T(8,128)} fusion(bf16[1024,8192]{1,0:T(8,128)(2,1)} %param.10, bf16[128,1024]{1,0:T(8,128)(2,1)S(1)} %bitcast.29, bf16[1024]{0:T(1024)(128)(2,1)S(1)} %get-tuple-element.6, bf16[1024]{0:T(1024)(128)(2,1)S(1)} %get-tuple-element.5), kind=kOutput, calls=%fused_computation.21 | convolution fusion | flops 2147745792 | bytes 21237760 | tf_op jit(solution)/shard_map/dot_general | solution.py:46
  115.2 0.0 copy-start.1
  115.2 0.0 reduce-scatter.2.cloned.1.call-update
  115.2 71.2 %reduce-scatter.2.cloned.1.call-done = f32[8,8192]{1,0:T(8,128)} async-done(((f32[128,8192]{1,0:T(8,128)}), f32[8,8192]{1,0:T(8,128)}) %reduce-scatter.2.cloned.1.call-update) | async-done | bytes 262160 | tf_op jit(solution)/shard_map/reduce_scatter | solution.py:45
  186.4 0.0 copy-done.1
  186.4 1.6 add_convert_fusion
  (5 shorter events, 0.1 us)
Async XLA Ops:
  6.5 47.1 %all-gather.2.cloned.1.call-start = ((), (), s32[]{:S(2)}) async-start(), calls=%async_computation.3 | async-start | bytes 2228224 | tf_op jit(solution)/shard_map/all_gather | solution.py:27
  55.7 9.0 %copy-start = (bf16[128,8192]{1,0:T(8,128)(2,1)S(1)}, bf16[128,8192]{1,0:T(8,128)(2,1)}, u32[]{:S(2)}) copy-start(bf16[128,8192]{1,0:T(8,128)(2,1)} %all-gather.2.cloned.1.call-done) | copy-start | bytes 6291460
  55.7 11.8 %copy-start.3 = (bf16[8192,1024]{1,0:T(8,128)(2,1)S(1)}, bf16[8192,1024]{1,0:T(8,128)(2,1)}, u32[]{:S(2)}) copy-start(bf16[8192,1024]{1,0:T(8,128)(2,1)} %param.9) | copy-start | bytes 50331652
  55.8 11.8 %copy-start.4 = (f32[8192]{0:T(1024)S(1)}, f32[8192]{0:T(1024)}, u32[]{:S(2)}) copy-start(f32[8192]{0:T(1024)} %param.7) | copy-start | bytes 98308
  70.1 24.9 %copy-start.2 = (f32[1024]{0:T(1024)S(1)}, f32[1024]{0:T(1024)}, u32[]{:S(2)}) copy-start(f32[1024]{0:T(1024)} %param.11) | copy-start | bytes 12292
  90.8 14.2 %all-to-all-start.1 = ((bf16[8,64,256]{2,0,1:T(8,128)(2,1)}), bf16[8,64,256]{2,0,1:T(8,128)(2,1)S(1)}, u32[]{:S(2)}, u32[]{:S(2)}) async-start(bf16[8,64,256]{2,0,1:T(8,128)(2,1)} %copy.15), calls=%async_computation.1 | async-start | bytes 524288 | tf_op jit(solution)/shard_map/all_to_all | solution.py:39
  94.9 91.5 %reduce-scatter.2.cloned.1.call-start = ((), (), s32[]{:S(2)}) async-start(), calls=%async_computation.4 | async-start | bytes 4456448 | tf_op jit(solution)/shard_map/reduce_scatter | solution.py:45
  115.2 71.2 %copy-start.1 = (bf16[8,8192]{1,0:T(8,128)(2,1)S(1)}, bf16[8,8192]{1,0:T(8,128)(2,1)}, u32[]{:S(2)}) copy-start(bf16[8,8192]{1,0:T(8,128)(2,1)} %param.6) | copy-start | bytes 393220
Sparse Core Ops, SparseCore 0:
  9.5 44.0 all-gather.1
  115.3 71.0 reduce-scatter.1
where the time goes:
time: 195 us
  waiting for transfers between devices  128 us (66%)
  matrix products  23 us (12%)
  blocking collectives  17.7 us (9%)
  between operations  13.5 us (7%)
  local copies, waits for them, and re-layouts  4.41 us (2%)
  starting transfers between devices  4.14 us (2%)
  other arithmetic  3.77 us (2%)
    reduce_scatter x1, waiting for transfers between devices, shards(): lax.psum_scatter(jnp.dot(clipped, down_weight, preferred_element_type=jnp...  71.2 us
    all_gather x1, waiting for transfers between devices, shards(): whole = lax.all_gather(tokens, 'hid', axis=0, tiled=True)  46.4 us
    all_to_all x1, blocking collectives, shards(): lax.all_to_all(shaped, 'hid', split_axis=0, concat_axis=1, tiled=True)  17.7 us
    dot_general x1, matrix products, shards(): jnp.dot(clipped, down_weight, preferred_element_type=jnp.float32)  10.1 us
    all_to_all x1, waiting for transfers between devices, shards(): lax.all_to_all(turned.astype(jnp.bfloat16), 'hid', split_axis=1, concat_a...  9.98 us
    dot_general x1, matrix products, shards(): gate = jnp.dot(normed, gate_weight, preferred_element_type=jnp.float32)  8.95 us
    all_to_all x1, starting transfers between devices, shards(): lax.all_to_all(turned.astype(jnp.bfloat16), 'hid', split_axis=1, concat_a...  4.1 us
  transfers between devices with their start and end apart: 3, of which 3 were waited for; matrix products, arithmetic and copies ran while one was open for 0% of the time, Pallas kernels for 0%

commit v1 on v0

v1 whole, which is shorter than its diff:
```python
import functools

import jax
import jax.numpy as jnp
from jax import lax
from jax.experimental import pallas as pl
from jax.experimental.pallas import tpu as pltpu
from jax.sharding import PartitionSpec as P

BLOCK = 256
MIB = 1 << 20


def hadamard(count):
    rows = lax.broadcasted_iota(jnp.int32, (count, count), 0)
    cols = lax.broadcasted_iota(jnp.int32, (count, count), 1)
    both = rows & cols
    parity = jnp.zeros((count, count), jnp.int32)
    for place in range(max(count.bit_length(), 1)):
        parity = parity + (both >> place & 1)
    return jnp.where(parity % 2 == 0, 1.0, -1.0).astype(jnp.bfloat16)


def normalize(rows_in, norm_gain):
    values = rows_in.astype(jnp.float32)
    inverse = lax.rsqrt(jnp.mean(values * values, axis=-1, keepdims=True) + 1e-05)
    return (values * inverse * norm_gain).astype(jnp.bfloat16)


def ring_of(chips):
    return list(range(0, chips, 2)) + list(range(chips - 1, 0, -2))


def up_kernel(count, blocks, place_ref, *refs):
    parts, (gate_ref, up_ref, out_a, out_b, rows_ref, hidden_ref) = refs[:count], refs[count:]
    own = parts[0].shape[0]
    for pair in range(count // 2):
        both = [parts[2 * pair + k][...].astype(jnp.float32) for k in range(2)]
        rows_ref[2 * own * pair : 2 * own * (pair + 1), :] = jnp.concatenate(both, axis=0).astype(jnp.bfloat16)
    rows = rows_ref.shape[0]
    depth = rows_ref.shape[1]
    step = min(1024, depth)
    turn = hadamard(BLOCK)
    outs = []
    for block in range(blocks):
        lanes = slice(block * BLOCK, (block + 1) * BLOCK)

        def add(at, sums):
            along = pl.ds(pl.multiple_of(at * step, step), step)
            values = rows_ref[:, along]
            gate = sums[0] + jnp.dot(values, gate_ref[along, lanes], preferred_element_type=jnp.float32)
            up = sums[1] + jnp.dot(values, up_ref[along, lanes], preferred_element_type=jnp.float32)
            return gate, up

        zero = jnp.zeros((rows, BLOCK), jnp.float32)
        gate, up = lax.fori_loop(0, depth // step, add, (zero, zero))
        hidden = gate / (1.0 + jnp.exp(-gate)) * up
        high = hidden.astype(jnp.bfloat16)
        low = (hidden - high.astype(jnp.float32)).astype(jnp.bfloat16)
        turned = jnp.dot(high, turn, preferred_element_type=jnp.float32) + jnp.dot(
            low, turn, preferred_element_type=jnp.float32
        )
        for part in range(count):
            spot = pl.multiple_of(place_ref[part] * own, own)
            hidden_ref[pl.ds(spot, own), lanes] = turned[part * own : (part + 1) * own]
    half = out_a.shape[1]
    out_a[...] = hidden_ref[:, :half].astype(jnp.bfloat16)
    out_b[...] = hidden_ref[:, half:].astype(jnp.bfloat16)


def up_project(place, parts, gate_weight, up_weight):
    count, own = len(parts), parts[0].shape[0]
    depth, width = gate_weight.shape
    rows = count * own
    half = jax.ShapeDtypeStruct((rows, width // 2), jnp.bfloat16)
    vmem = pl.BlockSpec(memory_space=pltpu.VMEM)
    return pl.pallas_call(
        functools.partial(up_kernel, count, width // BLOCK),
        out_shape=(half, half),
        in_specs=[pl.BlockSpec(memory_space=pltpu.SMEM)] + [vmem] * (count + 2),
        out_specs=(vmem, vmem),
        scratch_shapes=[pltpu.VMEM((rows, depth), jnp.bfloat16), pltpu.VMEM((rows, width), jnp.float32)],
        compiler_params=pltpu.CompilerParams(vmem_limit_bytes=20 * MIB),
        cost_estimate=pl.CostEstimate(
            flops=4 * rows * depth * width, bytes_accessed=4 * depth * width, transcendentals=rows * width
        ),
        name="up_project",
    )(place, *parts, gate_weight, up_weight)


def down_kernel(blocks, chips, scale, place_ref, first_ref, a_ref, b_ref, clip_ref, weight_ref, out_ref, rows_ref, mixed_ref):
    half = a_ref.shape[1]
    rows_ref[:, :half] = a_ref[...].astype(jnp.float32)
    rows_ref[:, half:] = b_ref[...].astype(jnp.float32)
    parts = [rows_ref[:, b * BLOCK : (b + 1) * BLOCK] for b in range(blocks)]
    span = 1
    while span < blocks:
        parts = [
            parts[b] + parts[b ^ span] if b & span == 0 else parts[b ^ span] - parts[b] for b in range(blocks)
        ]
        span *= 2
    for b in range(blocks):
        lanes = slice(b * BLOCK, (b + 1) * BLOCK)
        limit = 127.0 * clip_ref[:, lanes]
        rows_ref[:, lanes] = jnp.clip(parts[b] * scale, -limit, limit)
    rows = rows_ref.shape[0]
    each = rows // chips
    for chip in range(chips):
        spot = pl.multiple_of(place_ref[chip] * each, each)
        mixed_ref[chip * each : (chip + 1) * each, :] = rows_ref[pl.ds(spot, each), :].astype(jnp.bfloat16)
    wide = out_ref.shape[1]
    step = min(512, wide)

    def column(at, carry):
        lanes = pl.ds(pl.multiple_of(first_ref[0] * wide + at * step, step), step)
        product = jnp.dot(mixed_ref[...], weight_ref[:, lanes], preferred_element_type=jnp.float32)
        out_ref[:, pl.ds(pl.multiple_of(at * step, step), step)] = product.astype(jnp.bfloat16)
        return carry

    lax.fori_loop(0, wide // step, column, 0)


def down_project(place, first, a, b, clip_scale, weight, chips, total):
    rows = a.shape[0]
    width, depth = weight.shape
    vmem = pl.BlockSpec(memory_space=pltpu.VMEM)
    smem = pl.BlockSpec(memory_space=pltpu.SMEM)
    return pl.pallas_call(
        functools.partial(down_kernel, width // BLOCK, chips, total**-0.5),
        out_shape=jax.ShapeDtypeStruct((rows, depth // 2), jnp.bfloat16),
        in_specs=[smem, smem, vmem, vmem, vmem, vmem],
        out_specs=vmem,
        scratch_shapes=[pltpu.VMEM((rows, width), jnp.float32), pltpu.VMEM((rows, width), jnp.bfloat16)],
        compiler_params=pltpu.CompilerParams(vmem_limit_bytes=12 * MIB),
        cost_estimate=pl.CostEstimate(flops=rows * depth * width, bytes_accessed=depth * width, transcendentals=0),
        name="down_project",
    )(place, first, a, b, clip_scale, weight)


def shards(count, tokens, norm_gain, gate_weight, up_weight, down_weight, clip_scale):
    chips = count // 2
    order = ring_of(chips)
    me = lax.axis_index("hid")
    chip, core = me // 2, me % 2
    ring = jnp.array(order, jnp.int32)
    position = jnp.array([order.index(c) for c in range(chips)], jnp.int32)[chip]
    steps = chips // 2

    def hop(value, shift_even, shift_odd):
        pairs = []
        for at, c in enumerate(order):
            pairs.append((2 * c, 2 * order[(at + shift_even) % chips]))
            pairs.append((2 * c + 1, 2 * order[(at + shift_odd) % chips] + 1))
        return lax.ppermute(value, "hid", pairs)

    def right(value):
        return hop(value, 1, 1)

    def left(value):
        return hop(value, -1, -1)

    def cross(value, mask=1):
        return lax.ppermute(value, "hid", [(d, d ^ mask) for d in range(count)])

    normed = normalize(tokens, norm_gain)
    mine, shifts = [normed], [0]
    ahead = behind = normed
    for step in range(1, steps):
        ahead, behind = right(ahead), left(behind)
        mine += [ahead, behind]
        shifts += [-step, step]
    mine.append(hop(jnp.where(core == 0, ahead, behind), 1, -1))
    shifts.append(steps)
    parts = [block for own in mine for block in (own, cross(own))]
    chip_at = ring[(position + jnp.array(shifts, jnp.int32)) % chips]
    place = jnp.stack([2 * chip_at + core, 2 * chip_at + 1 - core], axis=1).reshape(-1).astype(jnp.int32)

    half_a, half_b = up_project(place, parts, gate_weight, up_weight)

    def butterfly(value, mask):
        sign = jnp.where(me & mask == 0, 1.0, -1.0).astype(jnp.float32)
        other = cross(value, mask)
        return (other.astype(jnp.float32) + sign * value.astype(jnp.float32)).astype(jnp.bfloat16)

    masks = [1 << bit for bit in range(count.bit_length() - 1)]
    orders = [masks[-1:] + masks[:-1], masks]
    for stage in range(len(masks)):
        half_a = butterfly(half_a, orders[0][stage])
        half_b = butterfly(half_b, orders[1][stage])

    turn = list(range(chips))
    places = ring[(position + jnp.array(turn, jnp.int32)) % chips]
    total = count * gate_weight.shape[1]
    limits = clip_scale.reshape(1, -1)
    theirs = down_project(places, (1 - core).reshape(1), half_a, half_b, limits, down_weight, chips, total)
    own = down_project(places, core.reshape(1), half_a, half_b, limits, down_weight, chips, total)
    arrived = cross(theirs)
    rows = own.shape[0] // chips

    def chunk(away):
        at = away % chips
        return own[at * rows : (at + 1) * rows].astype(jnp.float32) + arrived[at * rows : (at + 1) * rows].astype(
            jnp.float32
        )

    far = hop(chunk(steps).astype(jnp.bfloat16), 1, -1).astype(jnp.float32)
    zero = jnp.zeros_like(far)
    ahead = jnp.where(core == 0, far, zero)
    behind = jnp.where(core == 0, zero, far)
    for away in range(steps - 1, 0, -1):
        ahead = right((ahead + chunk(away)).astype(jnp.bfloat16)).astype(jnp.float32)
        behind = left((behind + chunk(-away)).astype(jnp.bfloat16)).astype(jnp.float32)
    summed = ahead + behind + chunk(0)
    part = rows // 2
    keep = lax.dynamic_slice_in_dim(summed, core * part, part, 0)
    give = lax.dynamic_slice_in_dim(summed, (1 - core) * part, part, 0)
    take = cross(give.astype(jnp.bfloat16)).astype(jnp.float32)
    low = jnp.where(core == 0, keep, take)
    high = jnp.where(core == 0, take, keep)
    return (tokens.astype(jnp.float32) + jnp.concatenate([low, high], axis=1)).astype(jnp.bfloat16)


def solution(mesh):
    in_specs = (
        P(("groups", "hid"), None),
        P(),
        P(None, "hid"),
        P(None, "hid"),
        P("hid", None),
        P("hid"),
    )
    out_specs = P(("groups", "hid"), None)
    body = functools.partial(shards, mesh.shape["hid"])
    return jax.shard_map(body, mesh=mesh, in_specs=in_specs, out_specs=out_specs, check_vma=False)
```

time: 195 us -> 123 us (0.63)
  waiting for transfers between devices: 128 us -> 49 us
  Pallas kernels: 0 us -> 24.4 us
  matrix products: 23 us -> 0 us
  starting transfers between devices: 4.14 us -> 23.5 us
  blocking collectives: 17.7 us -> 0 us
  local copies, waits for them, and re-layouts: 4.41 us -> 20.7 us
  between operations: 13.5 us -> 0.28 us
    reduce_scatter x1 -> x0, waiting for transfers between devices: 71.2 us -> none  [shards(): lax.psum_scatter(jnp.dot(clipped, down_weight, preferred_element_type=jnp...]
    ppermute x0 -> x32, waiting for transfers between devices: none -> 49 us  [the longest x14 25.2 us: hop(): return lax.ppermute(value, 'hid', pairs)]
    all_gather x1 -> x0, waiting for transfers between devices: 46.4 us -> none  [shards(): whole = lax.all_gather(tokens, 'hid', axis=0, tiled=True)]
    pallas_call x0 -> x3, Pallas kernels: none -> 24.4 us  [the longest x1 17.9 us: up_project(): pl.pallas_call(functools.partial(up_kernel, count, width // BLOCK), out_s...]
    ppermute x0 -> x32, starting transfers between devices: none -> 23.5 us  [the longest x14 15.2 us: hop(): return lax.ppermute(value, 'hid', pairs)]
    dot_general x5 -> x0, matrix products: 23 us -> none  [the longest x1 10.1 us: shards(): jnp.dot(clipped, down_weight, preferred_element_type=jnp.float32)]
    all_to_all x1 -> x0, blocking collectives: 17.7 us -> none  [shards(): lax.all_to_all(shaped, 'hid', split_axis=0, concat_axis=1, tiled=True)]
    unnamed x11 -> x12, local copies, waits for them, and re-layouts: 2.89 us -> 17.3 us
  transfers between devices with their start and end apart: 3 -> 32, of which waited for: 3 -> 23; matrix products, arithmetic and copies ran while one was open for 0% -> 4% of each run, Pallas kernels for 0% -> 3%
where the time goes in v1:
time: 123 us
  waiting for transfers between devices  49 us (40%)
  Pallas kernels  24.4 us (20%)
  starting transfers between devices  23.5 us (19%)
  local copies, waits for them, and re-layouts  20.7 us (17%)
  other arithmetic  4.91 us (4%)
    ppermute x14, waiting for transfers between devices, hop(): return lax.ppermute(value, 'hid', pairs)  25.2 us
    ppermute x18, waiting for transfers between devices, cross(): return lax.ppermute(value, 'hid', [(d, d ^ mask) for d in range(count)])  23.9 us
    pallas_call x1, Pallas kernels, up_project(): pl.pallas_call(functools.partial(up_kernel, count, width // BLOCK), out_s...  17.9 us
    unnamed x12, local copies, waits for them, and re-layouts  17.3 us
    ppermute x14, starting transfers between devices, hop(): return lax.ppermute(value, 'hid', pairs)  15.2 us
    ppermute x18, starting transfers between devices, cross(): return lax.ppermute(value, 'hid', [(d, d ^ mask) for d in range(count)])  8.35 us
    pallas_call x2, Pallas kernels, down_project(): pl.pallas_call(functools.partial(down_kernel, width // BLOCK, chips, tota...  6.59 us
  transfers between devices with their start and end apart: 32, of which 23 were waited for; matrix products, arithmetic and copies ran while one was open for 4% of the time, Pallas kernels for 3%

profile of v1, /device:TPU:0, one launch (start us, length us, event | category | flops | bytes accessed | tf_op | source)
XLA Modules:
  0.0 122.9 jit_solution(4142189928936623181)
XLA Ops:
  0.0 1.1 fusion.4
  1.1 1.0 fusion.6.refs_0_
  2.1 3.1 %collective-permute-start.1 = (bf16[8,8192]{1,0:T(8,128)(2,1)S(1)}, bf16[8,8192]{1,0:T(8,128)(2,1)S(1)}, u32[]{:S(2)}, u32[]{:S(2)}) collective-permute-start(bf16[8,8192]{1,0:T(8,128)(2,1)S(1)} %fusion.6.refs_0_), channel_id=1, source_target_pairs={{0,4},{1,5},{4,8},{5,9},{8,12},{9,13},{12,14},{13,15},{14,10},{15,... | collective-permute-start | bytes 393224 | tf_op jit(solution)/shard_map/ppermute | solution.py:154
  5.2 3.4 %collective-permute-done.1.refs_2_ = bf16[8,8192]{1,0:T(8,128)(2,1)S(1)} collective-permute-done((bf16[8,8192]{1,0:T(8,128)(2,1)S(1)}, bf16[8,8192]{1,0:T(8,128)(2,1)S(1)}, u32[]{:S(2)}, u32[]{:S(2)}) %collective-permute-start.1) | collective-permute-done | bytes 131104 | tf_op jit(solution)/shard_map/ppermute | solution.py:154
  8.6 1.8 %collective-permute-start.5 = (bf16[8,8192]{1,0:T(8,128)(2,1)S(1)}, bf16[8,8192]{1,0:T(8,128)(2,1)S(1)}, u32[]{:S(2)}, u32[]{:S(2)}) collective-permute-start(bf16[8,8192]{1,0:T(8,128)(2,1)S(1)} %collective-permute-done.1.refs_2_), channel_id=1, source_target_pairs={{0,4},{1,5},{4,8},{5,9},{8,12},{9,13},{12,14},{13,15},{14,10},{15,... | collective-permute-start | bytes 393224 | tf_op jit(solution)/shard_map/ppermute | solution.py:154
  10.4 0.2 collective-permute-start.7
  10.7 2.9 %collective-permute-done.5.refs_6_ = bf16[8,8192]{1,0:T(8,128)(2,1)S(1)} collective-permute-done((bf16[8,8192]{1,0:T(8,128)(2,1)S(1)}, bf16[8,8192]{1,0:T(8,128)(2,1)S(1)}, u32[]{:S(2)}, u32[]{:S(2)}) %collective-permute-start.5) | collective-permute-done | bytes 131104 | tf_op jit(solution)/shard_map/ppermute | solution.py:154
  13.6 1.8 %collective-permute-start.9 = (bf16[8,8192]{1,0:T(8,128)(2,1)S(1)}, bf16[8,8192]{1,0:T(8,128)(2,1)S(1)}, u32[]{:S(2)}, u32[]{:S(2)}) collective-permute-start(bf16[8,8192]{1,0:T(8,128)(2,1)S(1)} %collective-permute-done.5.refs_6_), channel_id=1, source_target_pairs={{0,4},{1,5},{4,8},{5,9},{8,12},{9,13},{12,14},{13,15},{14,10},{15,... | collective-permute-start | bytes 393224 | tf_op jit(solution)/shard_map/ppermute | solution.py:154
  15.4 0.2 collective-permute-start.11
  15.6 1.2 %dynamic_slice.9 = s32[1]{0:T(128)} dynamic-slice(s32[8]{0:T(128)} %constant.78.clone, s32[]{:T(128)S(6)} %select_n.89), dynamic_slice_sizes={1} | dynamic-slice | bytes 12 | tf_op jit(solution)/shard_map/dynamic_slice | solution.py:146
  16.9 0.5 collective-permute-start.2
  17.4 1.2 collective-permute-done.9.refs_10_
  18.6 1.8 %collective-permute-done.11.refs_12_ = bf16[8,8192]{1,0:T(8,128)(2,1)S(1)} collective-permute-done((bf16[8,8192]{1,0:T(8,128)(2,1)S(1)}, bf16[8,8192]{1,0:T(8,128)(2,1)S(1)}, u32[]{:S(2)}, u32[]{:S(2)}) %collective-permute-start.11) | collective-permute-done | bytes 131104 | tf_op jit(solution)/shard_map/ppermute | solution.py:154
  20.4 1.6 %collective-permute-start.13 = (bf16[8,8192]{1,0:T(8,128)(2,1)S(1)}, bf16[8,8192]{1,0:T(8,128)(2,1)S(1)}, u32[]{:S(2)}, u32[]{:S(2)}) collective-permute-start(bf16[8,8192]{1,0:T(8,128)(2,1)S(1)} %broadcast_select_fusion), channel_id=1, source_target_pairs={{0,4},{1,3},{4,8},{5,1},{8,12},{9,5},{12,14},{13,9},{14,10},{15,13... | collective-permute-start | bytes 393224 | tf_op jit(solution)/shard_map/ppermute | solution.py:154
  22.0 1.3 %compare_select_fusion = (s32[8]{0:T(128)S(1)}, s32[8]{0:T(128)S(1)}) fusion(s32[8]{0:T(128)} %constant.79.clone, s32[]{:T(128)} %bitcast), kind=kLoop, calls=%fused_computation.35 | loop fusion | flops 240 | bytes 100 | tf_op jit(solution)/shard_map/select_n | solution.py:175
  23.3 1.3 %gather_fusion.1 = s32[8]{0:T(128)S(1)} fusion(s32[8]{0:T(128)} %constant.77.clone, s32[1024]{0:T(1024)S(1)} %pad_clamp_fusion), kind=kCustom, calls=%fused_computation.1 | custom fusion | bytes 96 | tf_op jit(solution)/shard_map/gather | solution.py:175
  24.7 0.5 collective-permute-start.8
  25.2 0.1 collective-permute-start.10
  25.3 0.4 collective-permute-start.12
  25.7 0.1 collective-permute-start.14
  25.8 0.1 copy.12
  25.9 0.1 reshape.50.place_ref
  26.0 0.2 collective-permute-done.8.refs_9_
  26.2 0.3 collective-permute-done.10.refs_11_
  26.6 0.2 collective-permute-done.12.refs_13_
  26.8 0.3 collective-permute-done.14.refs_15_
  27.1 5.8 %copy-done.2 = bf16[8192,1024]{1,0:T(8,128)(2,1)S(1)} copy-done((bf16[8192,1024]{1,0:T(8,128)(2,1)S(1)}, bf16[8192,1024]{1,0:T(8,128)(2,1)}, u32[]{:S(2)}) %copy-start.2) | copy-done | bytes 16777240
  32.9 17.9 %up_project.1 = (bf16[128,512]{1,0:T(8,128)(2,1)S(1)}, bf16[128,512]{1,0:T(8,128)(2,1)S(1)}) custom-call(s32[16]{0:T(128)S(1)} %reshape.50.place_ref, bf16[8,8192]{1,0:T(8,128)(2,1)S(1)} %fusion.6.refs_0_, bf16[8,8192]{1,0:T(8,128)(2,1)S(1)} %collective-permute-done.refs_1_, bf16[8,8192]{1,0:T(8,128)(2,1)S(1)} %collective-permute-done.1.refs_2_, ...), custom_call_target="tpu_custom_call" | custom-call | flops 4294967296 | bytes 33554432 | tf_op jit(solution)/shard_map/up_project/pallas_call | solution.py:77
  50.7 2.6 %collective-permute-start.15 = (bf16[128,512]{1,0:T(8,128)(2,1)S(1)}, bf16[128,512]{1,0:T(8,128)(2,1)S(1)}, u32[]{:S(2)}, u32[]{:S(2)}) collective-permute-start(bf16[128,512]{1,0:T(8,128)(2,1)S(1)} %get-tuple-element.7), channel_id=1, source_target_pairs={{0,8},{1,9},{2,10},{3,11},{4,12},{5,13},{6,14},{7,15},{8,0},{9,1},... | collective-permute-start | bytes 393224 | tf_op jit(solution)/shard_map/ppermute | solution.py:163
  53.3 0.6 gather_fusion
  54.0 0.1 collective-permute-start.19
  54.1 6.0 %collective-permute-done.15 = bf16[128,512]{1,0:T(8,128)(2,1)S(1)} collective-permute-done((bf16[128,512]{1,0:T(8,128)(2,1)S(1)}, bf16[128,512]{1,0:T(8,128)(2,1)S(1)}, u32[]{:S(2)}, u32[]{:S(2)}) %collective-permute-start.15) | collective-permute-done | bytes 131104 | tf_op jit(solution)/shard_map/ppermute | solution.py:163
  60.3 0.5 collective-permute-start.20
  60.8 0.8 collective-permute-done.16
  61.6 0.9 collective-permute-start.17
  62.5 4.2 %collective-permute-done.20 = bf16[128,512]{1,0:T(8,128)(2,1)S(1)} collective-permute-done((bf16[128,512]{1,0:T(8,128)(2,1)S(1)}, bf16[128,512]{1,0:T(8,128)(2,1)S(1)}, u32[]{:S(2)}, u32[]{:S(2)}) %collective-permute-start.20) | collective-permute-done | bytes 131104 | tf_op jit(solution)/shard_map/ppermute | solution.py:163
  66.7 0.4 collective-permute-start.21
  67.1 1.9 %collective-permute-done.17 = bf16[128,512]{1,0:T(8,128)(2,1)S(1)} collective-permute-done((bf16[128,512]{1,0:T(8,128)(2,1)S(1)}, bf16[128,512]{1,0:T(8,128)(2,1)S(1)}, u32[]{:S(2)}, u32[]{:S(2)}) %collective-permute-start.17) | collective-permute-done | bytes 131104 | tf_op jit(solution)/shard_map/ppermute | solution.py:163
  69.1 0.4 collective-permute-start.18
  69.5 2.5 %collective-permute-done.21 = bf16[128,512]{1,0:T(8,128)(2,1)S(1)} collective-permute-done((bf16[128,512]{1,0:T(8,128)(2,1)S(1)}, bf16[128,512]{1,0:T(8,128)(2,1)S(1)}, u32[]{:S(2)}, u32[]{:S(2)}) %collective-permute-start.21) | collective-permute-done | bytes 131104 | tf_op jit(solution)/shard_map/ppermute | solution.py:163
  72.0 1.5 %collective-permute-start.22 = (bf16[128,512]{1,0:T(8,128)(2,1)S(1)}, bf16[128,512]{1,0:T(8,128)(2,1)S(1)}, u32[]{:S(2)}, u32[]{:S(2)}) collective-permute-start(bf16[128,512]{1,0:T(8,128)(2,1)S(1)} %add_convert_fusion.6), channel_id=1, source_target_pairs={{0,8},{1,9},{2,10},{3,11},{4,12},{5,13},{6,14},{7,15},{8,0},{9,1},... | collective-permute-start | bytes 393224 | tf_op jit(solution)/shard_map/ppermute | solution.py:163
  73.5 2.4 %collective-permute-done.18 = bf16[128,512]{1,0:T(8,128)(2,1)S(1)} collective-permute-done((bf16[128,512]{1,0:T(8,128)(2,1)S(1)}, bf16[128,512]{1,0:T(8,128)(2,1)S(1)}, u32[]{:S(2)}, u32[]{:S(2)}) %collective-permute-start.18) | collective-permute-done | bytes 131104 | tf_op jit(solution)/shard_map/ppermute | solution.py:163
  76.0 3.9 %collective-permute-done.22 = bf16[128,512]{1,0:T(8,128)(2,1)S(1)} collective-permute-done((bf16[128,512]{1,0:T(8,128)(2,1)S(1)}, bf16[128,512]{1,0:T(8,128)(2,1)S(1)}, u32[]{:S(2)}, u32[]{:S(2)}) %collective-permute-start.22) | collective-permute-done | bytes 131104 | tf_op jit(solution)/shard_map/ppermute | solution.py:163
  79.9 5.8 %copy-done = bf16[1024,8192]{1,0:T(8,128)(2,1)S(1)} copy-done((bf16[1024,8192]{1,0:T(8,128)(2,1)S(1)}, bf16[1024,8192]{1,0:T(8,128)(2,1)}, u32[]{:S(2)}) %copy-start) | copy-done | bytes 16777240
  85.7 3.3 %down_project.3 = bf16[128,4096]{1,0:T(8,128)(2,1)S(1)} custom-call(s32[8]{0:T(128)S(1)} %gather_fusion, s32[1]{0:T(128)} %bitcast.5.first_ref, bf16[128,512]{1,0:T(8,128)(2,1)S(1)} %add_convert_fusion.9.a_ref, bf16[128,512]{1,0:T(8,128)(2,1)S(1)} %add_convert_fusion.5.b_ref, f32[1,1024]{1,0:T(1,128)S(1)} %bitcast.8, bf16[1024,8192]{1,0:T(8,128)(2,1)S(1)} %copy-done), custom_call_target="tpu_custom_call" | custom-call | flops 1073741824 | bytes 8388608 | tf_op jit(solution)/shard_map/down_project/pallas_call | solution.py:128
  89.0 0.1 collective-permute-start.23
  89.1 5.8 %copy-done.1 = bf16[1024,8192]{1,0:T(8,128)(2,1)S(1)} copy-done((bf16[1024,8192]{1,0:T(8,128)(2,1)S(1)}, bf16[1024,8192]{1,0:T(8,128)(2,1)}, u32[]{:S(2)}) %copy-start.1) | copy-done | bytes 16777240
  94.8 3.3 %down_project.2 = bf16[128,4096]{1,0:T(8,128)(2,1)S(1)} custom-call(s32[8]{0:T(128)S(1)} %gather_fusion, s32[1]{0:T(128)} %bitcast.1.first_ref, bf16[128,512]{1,0:T(8,128)(2,1)S(1)} %add_convert_fusion.9.a_ref, bf16[128,512]{1,0:T(8,128)(2,1)S(1)} %add_convert_fusion.5.b_ref, f32[1,1024]{1,0:T(1,128)S(1)} %bitcast.9, bf16[1024,8192]{1,0:T(8,128)(2,1)S(1)} %copy-done.1), custom_call_target="tpu_custom_call" | custom-call | flops 1073741824 | bytes 8388608 | tf_op jit(solution)/shard_map/down_project/pallas_call | solution.py:128
  98.2 5.0 %collective-permute-done.24 = bf16[16,4096]{1,0:T(8,128)(2,1)S(1)} collective-permute-done((bf16[16,4096]{1,0:T(8,128)(2,1)S(1)}, bf16[16,4096]{1,0:T(8,128)(2,1)S(1)}, u32[]{:S(2)}, u32[]{:S(2)}) %collective-permute-start.24) | collective-permute-done | bytes 131104 | tf_op jit(solution)/shard_map/ppermute | solution.py:154
  103.2 0.1 fusion.1
  103.4 2.0 %collective-permute-start.28 = (bf16[16,4096]{1,0:T(8,128)(2,1)S(1)}, bf16[16,4096]{1,0:T(8,128)(2,1)S(1)}, u32[]{:S(2)}, u32[]{:S(2)}) collective-permute-start(bf16[16,4096]{1,0:T(8,128)(2,1)S(1)} %get-tuple-element.10), channel_id=1, source_target_pairs={{0,2},{1,3},{4,0},{5,1},{8,4},{9,5},{12,8},{13,9},{14,12},{15,13},... | collective-permute-start | bytes 393224 | tf_op jit(solution)/shard_map/ppermute | solution.py:154
  105.4 3.0 %collective-permute-done.25 = bf16[16,4096]{1,0:T(8,128)(2,1)S(1)} collective-permute-done((bf16[16,4096]{1,0:T(8,128)(2,1)S(1)}, bf16[16,4096]{1,0:T(8,128)(2,1)S(1)}, u32[]{:S(2)}, u32[]{:S(2)}) %collective-permute-start.25) | collective-permute-done | bytes 131104 | tf_op jit(solution)/shard_map/ppermute | solution.py:154
  108.5 0.1 add_convert_fusion.3
  108.6 1.5 %collective-permute-start.26 = (bf16[16,4096]{1,0:T(8,128)(2,1)S(1)}, bf16[16,4096]{1,0:T(8,128)(2,1)S(1)}, u32[]{:S(2)}, u32[]{:S(2)}) collective-permute-start(bf16[16,4096]{1,0:T(8,128)(2,1)S(1)} %get-tuple-element.13), channel_id=1, source_target_pairs={{0,4},{1,5},{4,8},{5,9},{8,12},{9,13},{12,14},{13,15},{14,10},{15,... | collective-permute-start | bytes 393224 | tf_op jit(solution)/shard_map/ppermute | solution.py:154
  110.1 0.6 collective-permute-start.29
  110.6 2.9 %collective-permute-done.26 = bf16[16,4096]{1,0:T(8,128)(2,1)S(1)} collective-permute-done((bf16[16,4096]{1,0:T(8,128)(2,1)S(1)}, bf16[16,4096]{1,0:T(8,128)(2,1)S(1)}, u32[]{:S(2)}, u32[]{:S(2)}) %collective-permute-start.26) | collective-permute-done | bytes 131104 | tf_op jit(solution)/shard_map/ppermute | solution.py:154
  113.6 1.5 %collective-permute-done.29 = bf16[16,4096]{1,0:T(8,128)(2,1)S(1)} collective-permute-done((bf16[16,4096]{1,0:T(8,128)(2,1)S(1)}, bf16[16,4096]{1,0:T(8,128)(2,1)S(1)}, u32[]{:S(2)}, u32[]{:S(2)}) %collective-permute-start.29) | collective-permute-done | bytes 131104 | tf_op jit(solution)/shard_map/ppermute | solution.py:154
  115.1 0.1 add_convert_fusion.2
  115.2 0.6 collective-permute-start.30
  115.8 1.6 %collective-permute-start.27 = (bf16[16,4096]{1,0:T(8,128)(2,1)S(1)}, bf16[16,4096]{1,0:T(8,128)(2,1)S(1)}, u32[]{:S(2)}, u32[]{:S(2)}) collective-permute-start(bf16[16,4096]{1,0:T(8,128)(2,1)S(1)} %get-tuple-element.11), channel_id=1, source_target_pairs={{0,4},{1,5},{4,8},{5,9},{8,12},{9,13},{12,14},{13,15},{14,10},{15,... | collective-permute-start | bytes 393224 | tf_op jit(solution)/shard_map/ppermute | solution.py:154
  117.4 2.9 %collective-permute-done.30 = bf16[16,4096]{1,0:T(8,128)(2,1)S(1)} collective-permute-done((bf16[16,4096]{1,0:T(8,128)(2,1)S(1)}, bf16[16,4096]{1,0:T(8,128)(2,1)S(1)}, u32[]{:S(2)}, u32[]{:S(2)}) %collective-permute-start.30) | collective-permute-done | bytes 131104 | tf_op jit(solution)/shard_map/ppermute | solution.py:154
  120.3 0.5 collective-permute-done.27
  120.9 1.2 %collective-permute-done.31 = bf16[8,4096]{1,0:T(8,128)(2,1)S(1)} collective-permute-done((bf16[8,4096]{1,0:T(8,128)(2,1)S(1)}, bf16[8,4096]{1,0:T(8,128)(2,1)S(1)}, u32[]{:S(2)}, u32[]{:S(2)}) %collective-permute-start.31) | collective-permute-done | bytes 65568 | tf_op jit(solution)/shard_map/ppermute | solution.py:163
  122.2 0.7 fusion.7
  (45 shorter events, 1.0 us)
Async XLA Ops:
  2.1 6.5 %collective-permute-start.1 = (bf16[8,8192]{1,0:T(8,128)(2,1)S(1)}, bf16[8,8192]{1,0:T(8,128)(2,1)S(1)}, u32[]{:S(2)}, u32[]{:S(2)}) collective-permute-start(bf16[8,8192]{1,0:T(8,128)(2,1)S(1)} %fusion.6.refs_0_), channel_id=1, source_target_pairs={{0,4},{1,5},{4,8},{5,9},{8,12},{9,13},{12,14},{13,15},{14,10},{15,... | collective-permute-start | bytes 393224 | tf_op jit(solution)/shard_map/ppermute | solution.py:154
  5.2 5.2 %collective-permute-start.3 = (bf16[8,8192]{1,0:T(8,128)(2,1)S(1)}, bf16[8,8192]{1,0:T(8,128)(2,1)S(1)}, u32[]{:S(2)}, u32[]{:S(2)}) collective-permute-start(bf16[8,8192]{1,0:T(8,128)(2,1)S(1)} %fusion.6.refs_0_), channel_id=1, source_target_pairs={{0,2},{1,3},{4,0},{5,1},{8,4},{9,5},{12,8},{13,9},{14,12},{15,13},... | collective-permute-start | bytes 393224 | tf_op jit(solution)/shard_map/ppermute | solution.py:154
  8.6 5.0 %collective-permute-start.5 = (bf16[8,8192]{1,0:T(8,128)(2,1)S(1)}, bf16[8,8192]{1,0:T(8,128)(2,1)S(1)}, u32[]{:S(2)}, u32[]{:S(2)}) collective-permute-start(bf16[8,8192]{1,0:T(8,128)(2,1)S(1)} %collective-permute-done.1.refs_2_), channel_id=1, source_target_pairs={{0,4},{1,5},{4,8},{5,9},{8,12},{9,13},{12,14},{13,15},{14,10},{15,... | collective-permute-start | bytes 393224 | tf_op jit(solution)/shard_map/ppermute | solution.py:154
  10.4 5.0 %collective-permute-start.7 = (bf16[8,8192]{1,0:T(8,128)(2,1)S(1)}, bf16[8,8192]{1,0:T(8,128)(2,1)S(1)}, u32[]{:S(2)}, u32[]{:S(2)}) collective-permute-start(bf16[8,8192]{1,0:T(8,128)(2,1)S(1)} %collective-permute-done.3.refs_4_), channel_id=1, source_target_pairs={{0,2},{1,3},{4,0},{5,1},{8,4},{9,5},{12,8},{13,9},{14,12},{15,13},... | collective-permute-start | bytes 393224 | tf_op jit(solution)/shard_map/ppermute | solution.py:154
  13.6 5.0 %collective-permute-start.9 = (bf16[8,8192]{1,0:T(8,128)(2,1)S(1)}, bf16[8,8192]{1,0:T(8,128)(2,1)S(1)}, u32[]{:S(2)}, u32[]{:S(2)}) collective-permute-start(bf16[8,8192]{1,0:T(8,128)(2,1)S(1)} %collective-permute-done.5.refs_6_), channel_id=1, source_target_pairs={{0,4},{1,5},{4,8},{5,9},{8,12},{9,13},{12,14},{13,15},{14,10},{15,... | collective-permute-start | bytes 393224 | tf_op jit(solution)/shard_map/ppermute | solution.py:154
  15.4 5.0 %collective-permute-start.11 = (bf16[8,8192]{1,0:T(8,128)(2,1)S(1)}, bf16[8,8192]{1,0:T(8,128)(2,1)S(1)}, u32[]{:S(2)}, u32[]{:S(2)}) collective-permute-start(bf16[8,8192]{1,0:T(8,128)(2,1)S(1)} %collective-permute-done.7.refs_8_), channel_id=1, source_target_pairs={{0,2},{1,3},{4,0},{5,1},{8,4},{9,5},{12,8},{13,9},{14,12},{15,13},... | collective-permute-start | bytes 393224 | tf_op jit(solution)/shard_map/ppermute | solution.py:154
  15.6 9.1 %collective-permute-start = (bf16[8,8192]{1,0:T(8,128)(2,1)S(1)}, bf16[8,8192]{1,0:T(8,128)(2,1)S(1)}, u32[]{:S(2)}, u32[]{:S(2)}) collective-permute-start(bf16[8,8192]{1,0:T(8,128)(2,1)S(1)} %fusion.6.refs_0_), channel_id=1, source_target_pairs={{0,1},{1,0},{2,3},{3,2},{4,5},{5,4},{6,7},{7,6},{8,9},{9,8},{10,11... | collective-permute-start | bytes 393224 | tf_op jit(solution)/shard_map/ppermute | solution.py:163
  16.9 8.4 %collective-permute-start.2 = (bf16[8,8192]{1,0:T(8,128)(2,1)S(1)}, bf16[8,8192]{1,0:T(8,128)(2,1)S(1)}, u32[]{:S(2)}, u32[]{:S(2)}) collective-permute-start(bf16[8,8192]{1,0:T(8,128)(2,1)S(1)} %collective-permute-done.1.refs_2_), channel_id=1, source_target_pairs={{0,1},{1,0},{2,3},{3,2},{4,5},{5,4},{6,7},{7,6},{8,9},{9,8},{10,11... | collective-permute-start | bytes 393224 | tf_op jit(solution)/shard_map/ppermute | solution.py:163
  17.4 7.9 %collective-permute-start.4 = (bf16[8,8192]{1,0:T(8,128)(2,1)S(1)}, bf16[8,8192]{1,0:T(8,128)(2,1)S(1)}, u32[]{:S(2)}, u32[]{:S(2)}) collective-permute-start(bf16[8,8192]{1,0:T(8,128)(2,1)S(1)} %collective-permute-done.3.refs_4_), channel_id=1, source_target_pairs={{0,1},{1,0},{2,3},{3,2},{4,5},{5,4},{6,7},{7,6},{8,9},{9,8},{10,11... | collective-permute-start | bytes 393224 | tf_op jit(solution)/shard_map/ppermute | solution.py:163
  20.4 5.4 %collective-permute-start.13 = (bf16[8,8192]{1,0:T(8,128)(2,1)S(1)}, bf16[8,8192]{1,0:T(8,128)(2,1)S(1)}, u32[]{:S(2)}, u32[]{:S(2)}) collective-permute-start(bf16[8,8192]{1,0:T(8,128)(2,1)S(1)} %broadcast_select_fusion), channel_id=1, source_target_pairs={{0,4},{1,3},{4,8},{5,1},{8,12},{9,5},{12,14},{13,9},{14,10},{15,13... | collective-permute-start | bytes 393224 | tf_op jit(solution)/shard_map/ppermute | solution.py:154
  24.6 1.4 %collective-permute-start.6 = (bf16[8,8192]{1,0:T(8,128)(2,1)S(1)}, bf16[8,8192]{1,0:T(8,128)(2,1)S(1)}, u32[]{:S(2)}, u32[]{:S(2)}) collective-permute-start(bf16[8,8192]{1,0:T(8,128)(2,1)S(1)} %collective-permute-done.5.refs_6_), channel_id=1, source_target_pairs={{0,1},{1,0},{2,3},{3,2},{4,5},{5,4},{6,7},{7,6},{8,9},{9,8},{10,11... | collective-permute-start | bytes 393224 | tf_op jit(solution)/shard_map/ppermute | solution.py:163
  24.7 1.5 %collective-permute-start.8 = (bf16[8,8192]{1,0:T(8,128)(2,1)S(1)}, bf16[8,8192]{1,0:T(8,128)(2,1)S(1)}, u32[]{:S(2)}, u32[]{:S(2)}) collective-permute-start(bf16[8,8192]{1,0:T(8,128)(2,1)S(1)} %collective-permute-done.7.refs_8_), channel_id=1, source_target_pairs={{0,1},{1,0},{2,3},{3,2},{4,5},{5,4},{6,7},{7,6},{8,9},{9,8},{10,11... | collective-permute-start | bytes 393224 | tf_op jit(solution)/shard_map/ppermute | solution.py:163
  25.2 1.3 %collective-permute-start.10 = (bf16[8,8192]{1,0:T(8,128)(2,1)S(1)}, bf16[8,8192]{1,0:T(8,128)(2,1)S(1)}, u32[]{:S(2)}, u32[]{:S(2)}) collective-permute-start(bf16[8,8192]{1,0:T(8,128)(2,1)S(1)} %collective-permute-done.9.refs_10_), channel_id=1, source_target_pairs={{0,1},{1,0},{2,3},{3,2},{4,5},{5,4},{6,7},{7,6},{8,9},{9,8},{10,11... | collective-permute-start | bytes 393224 | tf_op jit(solution)/shard_map/ppermute | solution.py:163
  25.3 1.4 %collective-permute-start.12 = (bf16[8,8192]{1,0:T(8,128)(2,1)S(1)}, bf16[8,8192]{1,0:T(8,128)(2,1)S(1)}, u32[]{:S(2)}, u32[]{:S(2)}) collective-permute-start(bf16[8,8192]{1,0:T(8,128)(2,1)S(1)} %collective-permute-done.11.refs_12_), channel_id=1, source_target_pairs={{0,1},{1,0},{2,3},{3,2},{4,5},{5,4},{6,7},{7,6},{8,9},{9,8},{10,11... | collective-permute-start | bytes 393224 | tf_op jit(solution)/shard_map/ppermute | solution.py:163
  25.7 1.3 %collective-permute-start.14 = (bf16[8,8192]{1,0:T(8,128)(2,1)S(1)}, bf16[8,8192]{1,0:T(8,128)(2,1)S(1)}, u32[]{:S(2)}, u32[]{:S(2)}) collective-permute-start(bf16[8,8192]{1,0:T(8,128)(2,1)S(1)} %collective-permute-done.13.refs_14_), channel_id=1, source_target_pairs={{0,1},{1,0},{2,3},{3,2},{4,5},{5,4},{6,7},{7,6},{8,9},{9,8},{10,11... | collective-permute-start | bytes 393224 | tf_op jit(solution)/shard_map/ppermute | solution.py:163
  25.9 27.4 %copy-start.4 = (s32[8]{0:T(128)S(1)}, s32[8]{0:T(128)}, u32[]{:S(2)}) copy-start(s32[8]{0:T(128)} %constant.77.clone) | copy-start | bytes 100
  25.9 53.9 %copy-start.3 = (f32[1024]{0:T(1024)S(1)}, f32[1024]{0:T(1024)}, u32[]{:S(2)}) copy-start(f32[1024]{0:T(1024)} %param.15) | copy-start | bytes 12292
  27.1 5.8 %copy-start.2 = (bf16[8192,1024]{1,0:T(8,128)(2,1)S(1)}, bf16[8192,1024]{1,0:T(8,128)(2,1)}, u32[]{:S(2)}) copy-start(bf16[8192,1024]{1,0:T(8,128)(2,1)} %refs_16_.1) | copy-start | bytes 50331652
  50.7 9.4 %collective-permute-start.15 = (bf16[128,512]{1,0:T(8,128)(2,1)S(1)}, bf16[128,512]{1,0:T(8,128)(2,1)S(1)}, u32[]{:S(2)}, u32[]{:S(2)}) collective-permute-start(bf16[128,512]{1,0:T(8,128)(2,1)S(1)} %get-tuple-element.7), channel_id=1, source_target_pairs={{0,8},{1,9},{2,10},{3,11},{4,12},{5,13},{6,14},{7,15},{8,0},{9,1},... | collective-permute-start | bytes 393224 | tf_op jit(solution)/shard_map/ppermute | solution.py:163
  54.0 6.2 %collective-permute-start.19 = (bf16[128,512]{1,0:T(8,128)(2,1)S(1)}, bf16[128,512]{1,0:T(8,128)(2,1)S(1)}, u32[]{:S(2)}, u32[]{:S(2)}) collective-permute-start(bf16[128,512]{1,0:T(8,128)(2,1)S(1)} %get-tuple-element.8), channel_id=1, source_target_pairs={{0,1},{1,0},{2,3},{3,2},{4,5},{5,4},{6,7},{7,6},{8,9},{9,8},{10,11... | collective-permute-start | bytes 393224 | tf_op jit(solution)/shard_map/ppermute | solution.py:163
  60.1 1.4 %collective-permute-start.16 = (bf16[128,512]{1,0:T(8,128)(2,1)S(1)}, bf16[128,512]{1,0:T(8,128)(2,1)S(1)}, u32[]{:S(2)}, u32[]{:S(2)}) collective-permute-start(bf16[128,512]{1,0:T(8,128)(2,1)S(1)} %add_convert_fusion.12), channel_id=1, source_target_pairs={{0,1},{1,0},{2,3},{3,2},{4,5},{5,4},{6,7},{7,6},{8,9},{9,8},{10,11... | collective-permute-start | bytes 393224 | tf_op jit(solution)/shard_map/ppermute | solution.py:163
  60.3 6.4 %collective-permute-start.20 = (bf16[128,512]{1,0:T(8,128)(2,1)S(1)}, bf16[128,512]{1,0:T(8,128)(2,1)S(1)}, u32[]{:S(2)}, u32[]{:S(2)}) collective-permute-start(bf16[128,512]{1,0:T(8,128)(2,1)S(1)} %add_convert_fusion.8), channel_id=1, source_target_pairs={{0,2},{1,3},{2,0},{3,1},{4,6},{5,7},{6,4},{7,5},{8,10},{9,11},{10,... | collective-permute-start | bytes 393224 | tf_op jit(solution)/shard_map/ppermute | solution.py:163
  61.6 7.4 %collective-permute-start.17 = (bf16[128,512]{1,0:T(8,128)(2,1)S(1)}, bf16[128,512]{1,0:T(8,128)(2,1)S(1)}, u32[]{:S(2)}, u32[]{:S(2)}) collective-permute-start(bf16[128,512]{1,0:T(8,128)(2,1)S(1)} %add_convert_fusion.11), channel_id=1, source_target_pairs={{0,2},{1,3},{2,0},{3,1},{4,6},{5,7},{6,4},{7,5},{8,10},{9,11},{10,... | collective-permute-start | bytes 393224 | tf_op jit(solution)/shard_map/ppermute | solution.py:163
  66.7 5.3 %collective-permute-start.21 = (bf16[128,512]{1,0:T(8,128)(2,1)S(1)}, bf16[128,512]{1,0:T(8,128)(2,1)S(1)}, u32[]{:S(2)}, u32[]{:S(2)}) collective-permute-start(bf16[128,512]{1,0:T(8,128)(2,1)S(1)} %add_convert_fusion.7), channel_id=1, source_target_pairs={{0,4},{1,5},{2,6},{3,7},{4,0},{5,1},{6,2},{7,3},{8,12},{9,13},{10,... | collective-permute-start | bytes 393224 | tf_op jit(solution)/shard_map/ppermute | solution.py:163
  69.1 6.8 %collective-permute-start.18 = (bf16[128,512]{1,0:T(8,128)(2,1)S(1)}, bf16[128,512]{1,0:T(8,128)(2,1)S(1)}, u32[]{:S(2)}, u32[]{:S(2)}) collective-permute-start(bf16[128,512]{1,0:T(8,128)(2,1)S(1)} %add_convert_fusion.10), channel_id=1, source_target_pairs={{0,4},{1,5},{2,6},{3,7},{4,0},{5,1},{6,2},{7,3},{8,12},{9,13},{10,... | collective-permute-start | bytes 393224 | tf_op jit(solution)/shard_map/ppermute | solution.py:163
  72.0 7.8 %collective-permute-start.22 = (bf16[128,512]{1,0:T(8,128)(2,1)S(1)}, bf16[128,512]{1,0:T(8,128)(2,1)S(1)}, u32[]{:S(2)}, u32[]{:S(2)}) collective-permute-start(bf16[128,512]{1,0:T(8,128)(2,1)S(1)} %add_convert_fusion.6), channel_id=1, source_target_pairs={{0,8},{1,9},{2,10},{3,11},{4,12},{5,13},{6,14},{7,15},{8,0},{9,1},... | collective-permute-start | bytes 393224 | tf_op jit(solution)/shard_map/ppermute | solution.py:163
  79.9 5.8 %copy-start = (bf16[1024,8192]{1,0:T(8,128)(2,1)S(1)}, bf16[1024,8192]{1,0:T(8,128)(2,1)}, u32[]{:S(2)}) copy-start(bf16[1024,8192]{1,0:T(8,128)(2,1)} %weight_ref.3) | copy-start | bytes 50331652
  85.7 36.5 %copy-start.5 = (bf16[8,8192]{1,0:T(8,128)(2,1)S(1)}, bf16[8,8192]{1,0:T(8,128)(2,1)}, u32[]{:S(2)}) copy-start(bf16[8,8192]{1,0:T(8,128)(2,1)} %param.10) | copy-start | bytes 393220
  89.0 9.1 %collective-permute-start.23 = (bf16[128,4096]{1,0:T(8,128)(2,1)S(1)}, bf16[128,4096]{1,0:T(8,128)(2,1)S(1)}, u32[]{:S(2)}, u32[]{:S(2)}) collective-permute-start(bf16[128,4096]{1,0:T(8,128)(2,1)S(1)} %down_project.3), channel_id=1, source_target_pairs={{0,1},{1,0},{2,3},{3,2},{4,5},{5,4},{6,7},{7,6},{8,9},{9,8},{10,11... | collective-permute-start | bytes 3145736 | tf_op jit(solution)/shard_map/ppermute | solution.py:163
  89.1 5.8 %copy-start.1 = (bf16[1024,8192]{1,0:T(8,128)(2,1)S(1)}, bf16[1024,8192]{1,0:T(8,128)(2,1)}, u32[]{:S(2)}) copy-start(bf16[1024,8192]{1,0:T(8,128)(2,1)} %weight_ref.3) | copy-start | bytes 50331652
  98.2 5.0 %collective-permute-start.24 = (bf16[16,4096]{1,0:T(8,128)(2,1)S(1)}, bf16[16,4096]{1,0:T(8,128)(2,1)S(1)}, u32[]{:S(2)}, u32[]{:S(2)}) collective-permute-start(bf16[16,4096]{1,0:T(8,128)(2,1)S(1)} %add_convert_fusion.4), channel_id=1, source_target_pairs={{0,4},{1,3},{4,8},{5,1},{8,12},{9,5},{12,14},{13,9},{14,10},{15,13... | collective-permute-start | bytes 393224 | tf_op jit(solution)/shard_map/ppermute | solution.py:154
  103.3 5.1 %collective-permute-start.25 = (bf16[16,4096]{1,0:T(8,128)(2,1)S(1)}, bf16[16,4096]{1,0:T(8,128)(2,1)S(1)}, u32[]{:S(2)}, u32[]{:S(2)}) collective-permute-start(bf16[16,4096]{1,0:T(8,128)(2,1)S(1)} %get-tuple-element.9), channel_id=1, source_target_pairs={{0,4},{1,5},{4,8},{5,9},{8,12},{9,13},{12,14},{13,15},{14,10},{15,... | collective-permute-start | bytes 393224 | tf_op jit(solution)/shard_map/ppermute | solution.py:154
  103.4 5.1 %collective-permute-start.28 = (bf16[16,4096]{1,0:T(8,128)(2,1)S(1)}, bf16[16,4096]{1,0:T(8,128)(2,1)S(1)}, u32[]{:S(2)}, u32[]{:S(2)}) collective-permute-start(bf16[16,4096]{1,0:T(8,128)(2,1)S(1)} %get-tuple-element.10), channel_id=1, source_target_pairs={{0,2},{1,3},{4,0},{5,1},{8,4},{9,5},{12,8},{13,9},{14,12},{15,13},... | collective-permute-start | bytes 393224 | tf_op jit(solution)/shard_map/ppermute | solution.py:154
  108.6 5.0 %collective-permute-start.26 = (bf16[16,4096]{1,0:T(8,128)(2,1)S(1)}, bf16[16,4096]{1,0:T(8,128)(2,1)S(1)}, u32[]{:S(2)}, u32[]{:S(2)}) collective-permute-start(bf16[16,4096]{1,0:T(8,128)(2,1)S(1)} %get-tuple-element.13), channel_id=1, source_target_pairs={{0,4},{1,5},{4,8},{5,9},{8,12},{9,13},{12,14},{13,15},{14,10},{15,... | collective-permute-start | bytes 393224 | tf_op jit(solution)/shard_map/ppermute | solution.py:154
  110.1 5.0 %collective-permute-start.29 = (bf16[16,4096]{1,0:T(8,128)(2,1)S(1)}, bf16[16,4096]{1,0:T(8,128)(2,1)S(1)}, u32[]{:S(2)}, u32[]{:S(2)}) collective-permute-start(bf16[16,4096]{1,0:T(8,128)(2,1)S(1)} %get-tuple-element.14), channel_id=1, source_target_pairs={{0,2},{1,3},{4,0},{5,1},{8,4},{9,5},{12,8},{13,9},{14,12},{15,13},... | collective-permute-start | bytes 393224 | tf_op jit(solution)/shard_map/ppermute | solution.py:154
  115.2 5.1 %collective-permute-start.30 = (bf16[16,4096]{1,0:T(8,128)(2,1)S(1)}, bf16[16,4096]{1,0:T(8,128)(2,1)S(1)}, u32[]{:S(2)}, u32[]{:S(2)}) collective-permute-start(bf16[16,4096]{1,0:T(8,128)(2,1)S(1)} %get-tuple-element.12), channel_id=1, source_target_pairs={{0,2},{1,3},{4,0},{5,1},{8,4},{9,5},{12,8},{13,9},{14,12},{15,13},... | collective-permute-start | bytes 393224 | tf_op jit(solution)/shard_map/ppermute | solution.py:154
  115.8 5.0 %collective-permute-start.27 = (bf16[16,4096]{1,0:T(8,128)(2,1)S(1)}, bf16[16,4096]{1,0:T(8,128)(2,1)S(1)}, u32[]{:S(2)}, u32[]{:S(2)}) collective-permute-start(bf16[16,4096]{1,0:T(8,128)(2,1)S(1)} %get-tuple-element.11), channel_id=1, source_target_pairs={{0,4},{1,5},{4,8},{5,9},{8,12},{9,13},{12,14},{13,15},{14,10},{15,... | collective-permute-start | bytes 393224 | tf_op jit(solution)/shard_map/ppermute | solution.py:154
  120.8 1.3 %collective-permute-start.31 = (bf16[8,4096]{1,0:T(8,128)(2,1)S(1)}, bf16[8,4096]{1,0:T(8,128)(2,1)S(1)}, u32[]{:S(2)}, u32[]{:S(2)}) collective-permute-start(bf16[8,4096]{1,0:T(8,128)(2,1)S(1)} %dynamic-slice_convert_fusion), channel_id=1, source_target_pairs={{0,1},{1,0},{2,3},{3,2},{4,5},{5,4},{6,7},{7,6},{8,9},{9,8},{10,11... | collective-permute-start | bytes 196616 | tf_op jit(solution)/shard_map/ppermute | solution.py:163

commit v2 on v1

v2 whole, which is shorter than its diff:
```python
import functools

import jax
import jax.numpy as jnp
from jax import lax
from jax.experimental import pallas as pl
from jax.experimental.pallas import tpu as pltpu
from jax.sharding import PartitionSpec as P

BLOCK = 256
MIB = 1 << 20


def hadamard(count):
    rows = lax.broadcasted_iota(jnp.int32, (count, count), 0)
    cols = lax.broadcasted_iota(jnp.int32, (count, count), 1)
    both = rows & cols
    parity = jnp.zeros((count, count), jnp.int32)
    for place in range(max(count.bit_length(), 1)):
        parity = parity + (both >> place & 1)
    return jnp.where(parity % 2 == 0, 1.0, -1.0).astype(jnp.bfloat16)


def normalize_kernel(rows_ref, gain_ref, out_ref):
    values = rows_ref[...].astype(jnp.float32)
    inverse = lax.rsqrt(jnp.mean(values * values, axis=-1, keepdims=True) + 1e-05)
    out_ref[...] = (values * inverse * gain_ref[...]).astype(jnp.bfloat16)


def normalize(rows_in, norm_gain):
    vmem = pl.BlockSpec(memory_space=pltpu.VMEM)
    return pl.pallas_call(
        normalize_kernel,
        out_shape=jax.ShapeDtypeStruct(rows_in.shape, jnp.bfloat16),
        in_specs=[vmem, vmem],
        out_specs=vmem,
        compiler_params=pltpu.CompilerParams(vmem_limit_bytes=4 * MIB),
        cost_estimate=pl.CostEstimate(flops=8 * rows_in.size, bytes_accessed=4 * rows_in.size, transcendentals=0),
        name="normalize",
    )(rows_in, norm_gain.reshape(1, -1))


def ring_of(chips):
    return list(range(0, chips, 2)) + list(range(chips - 1, 0, -2))


def ring_place(chip, shift, chips):
    spot = jnp.where(chip % 2 == 0, chip // 2, chips - 1 - (chip - 1) // 2)
    spot = (spot + shift) % chips
    return jnp.where(spot < (chips + 1) // 2, 2 * spot, 2 * (chips - spot) - 1)


def load_kernel(flip, splits, me_ref, weight_ref, after_ref, out_ref, sems):
    rows, cols = out_ref.shape
    wide = weight_ref.shape[1]
    start = splits[1] * cols
    if flip is not None:
        side = me_ref[0] % 2
        side = 1 - side if flip else side
        start = start + side * (wide // 2)
        start = pl.multiple_of(start, cols)
    each = rows // splits[0]
    copies = [
        pltpu.make_async_copy(
            weight_ref.at[pl.ds(part * each, each), pl.ds(start, cols)],
            out_ref.at[pl.ds(part * each, each), :],
            sems.at[part],
        )
        for part in range(splits[0])
    ]
    for copy in copies:
        copy.start()
    for copy in copies:
        copy.wait()


def load(me, weight, after, cols, at, flip=None):
    rows = weight.shape[0]
    hbm = pl.BlockSpec(memory_space=pltpu.HBM)
    return pl.pallas_call(
        functools.partial(load_kernel, flip, (8, at)),
        out_shape=jax.ShapeDtypeStruct((rows, cols), weight.dtype),
        in_specs=[pl.BlockSpec(memory_space=pltpu.SMEM), hbm, hbm],
        out_specs=pl.BlockSpec(memory_space=pltpu.VMEM),
        scratch_shapes=[pltpu.SemaphoreType.DMA((8,))],
        compiler_params=pltpu.CompilerParams(vmem_limit_bytes=1 * MIB),
        cost_estimate=pl.CostEstimate(flops=0, bytes_accessed=4 * rows * cols, transcendentals=0),
        name="load",
    )(me, pltpu.with_memory_space_constraint(weight, pltpu.HBM), after)


def up_kernel(count, shifts, me_ref, *refs):
    chip, core = me_ref[0] // 2, me_ref[0] % 2
    spots = []
    for shift in shifts:
        there = 2 * ring_place(chip, shift, count // 2)
        spots += [there + core, there + 1 - core]
    parts, (out_a, out_b, rows_ref, hidden_ref) = refs[:count], refs[-4:]
    gates, ups = refs[count:-4:2], refs[count + 1 : -4 : 2]
    own = parts[0].shape[0]
    for pair in range(count // 2):
        both = [parts[2 * pair + k][...].astype(jnp.float32) for k in range(2)]
        rows_ref[2 * own * pair : 2 * own * (pair + 1), :] = jnp.concatenate(both, axis=0).astype(jnp.bfloat16)
    turn = hadamard(BLOCK)
    values = rows_ref[...]
    for block in range(len(gates)):
        gate = jnp.dot(values, gates[block][...], preferred_element_type=jnp.float32)
        up = jnp.dot(values, ups[block][...], preferred_element_type=jnp.float32)
        hidden = gate / (1.0 + jnp.exp(-gate)) * up
        high = hidden.astype(jnp.bfloat16)
        low = (hidden - high.astype(jnp.float32)).astype(jnp.bfloat16)
        turned = jnp.dot(high, turn, preferred_element_type=jnp.float32) + jnp.dot(
            low, turn, preferred_element_type=jnp.float32
        )
        lanes = slice(block * BLOCK, (block + 1) * BLOCK)
        for part in range(count):
            spot = pl.multiple_of(spots[part] * own, own)
            hidden_ref[pl.ds(spot, own), lanes] = turned[part * own : (part + 1) * own]
    half = out_a.shape[1]
    out_a[...] = hidden_ref[:, :half].astype(jnp.bfloat16)
    out_b[...] = hidden_ref[:, half:].astype(jnp.bfloat16)


def up_project(me, shifts, parts, weights):
    count, own = len(parts), parts[0].shape[0]
    depth = weights[0].shape[0]
    width = BLOCK * len(weights) // 2
    rows = count * own
    half = jax.ShapeDtypeStruct((rows, width // 2), jnp.bfloat16)
    vmem = pl.BlockSpec(memory_space=pltpu.VMEM)
    return pl.pallas_call(
        functools.partial(up_kernel, count, shifts),
        out_shape=(half, half),
        in_specs=[pl.BlockSpec(memory_space=pltpu.SMEM)] + [vmem] * (count + len(weights)),
        out_specs=(vmem, vmem),
        scratch_shapes=[pltpu.VMEM((rows, depth), jnp.bfloat16), pltpu.VMEM((rows, width), jnp.float32)],
        compiler_params=pltpu.CompilerParams(vmem_limit_bytes=12 * MIB),
        cost_estimate=pl.CostEstimate(flops=4 * rows * depth * width, bytes_accessed=0, transcendentals=rows * width),
        name="up_project",
    )(me, *parts, *weights)


def down_kernel(blocks, chips, scale, me_ref, a_ref, b_ref, clip_ref, *refs):
    weights, (out_ref, rows_ref, mixed_ref) = refs[:-3], refs[-3:]
    half = a_ref.shape[1]
    rows_ref[:, :half] = a_ref[...].astype(jnp.float32)
    rows_ref[:, half:] = b_ref[...].astype(jnp.float32)
    parts = [rows_ref[:, b * BLOCK : (b + 1) * BLOCK] for b in range(blocks)]
    span = 1
    while span < blocks:
        parts = [
            parts[b] + parts[b ^ span] if b & span == 0 else parts[b ^ span] - parts[b] for b in range(blocks)
        ]
        span *= 2
    for b in range(blocks):
        lanes = slice(b * BLOCK, (b + 1) * BLOCK)
        limit = 127.0 * clip_ref[:, lanes]
        rows_ref[:, lanes] = jnp.clip(parts[b] * scale, -limit, limit)
    rows = rows_ref.shape[0]
    each = rows // chips
    for chip in range(chips):
        spot = pl.multiple_of(ring_place(me_ref[0] // 2, chip, chips) * each, each)
        mixed_ref[chip * each : (chip + 1) * each, :] = rows_ref[pl.ds(spot, each), :].astype(jnp.bfloat16)
    step = weights[0].shape[1]
    for at, weight_ref in enumerate(weights):
        product = jnp.dot(mixed_ref[...], weight_ref[...], preferred_element_type=jnp.float32)
        out_ref[:, at * step : (at + 1) * step] = product.astype(jnp.bfloat16)


def down_project(me, a, b, clip_scale, weights, chips, total):
    rows = a.shape[0]
    width = 2 * a.shape[1]
    depth = len(weights) * weights[0].shape[1]
    vmem = pl.BlockSpec(memory_space=pltpu.VMEM)
    smem = pl.BlockSpec(memory_space=pltpu.SMEM)
    return pl.pallas_call(
        functools.partial(down_kernel, width // BLOCK, chips, total**-0.5),
        out_shape=jax.ShapeDtypeStruct((rows, depth), jnp.bfloat16),
        in_specs=[smem, vmem, vmem, vmem] + [vmem] * len(weights),
        out_specs=vmem,
        scratch_shapes=[pltpu.VMEM((rows, width), jnp.float32), pltpu.VMEM((rows, width), jnp.bfloat16)],
        compiler_params=pltpu.CompilerParams(vmem_limit_bytes=8 * MIB),
        cost_estimate=pl.CostEstimate(flops=2 * rows * depth * width, bytes_accessed=0, transcendentals=0),
        name="down_project",
    )(me, a, b, clip_scale, *weights)


def shards(count, tokens, norm_gain, gate_weight, up_weight, down_weight, clip_scale):
    chips = count // 2
    order = ring_of(chips)
    me = lax.axis_index("hid")
    core = me & 1
    where = me.astype(jnp.int32).reshape(1)
    steps = chips // 2

    def hop(value, shift_even, shift_odd):
        pairs = []
        for at, c in enumerate(order):
            pairs.append((2 * c, 2 * order[(at + shift_even) % chips]))
            pairs.append((2 * c + 1, 2 * order[(at + shift_odd) % chips] + 1))
        return lax.ppermute(value, "hid", pairs)

    def right(value):
        return hop(value, 1, 1)

    def left(value):
        return hop(value, -1, -1)

    def cross(value, mask=1):
        return lax.ppermute(value, "hid", [(d, d ^ mask) for d in range(count)])

    normed = normalize(tokens, norm_gain)
    mine, shifts = [normed], [0]
    ahead = behind = normed
    for step in range(1, steps):
        ahead, behind = right(ahead), left(behind)
        mine += [ahead, behind]
        shifts += [-step, step]
    mine.append(hop(jnp.where(core == 0, ahead, behind), 1, -1))
    shifts.append(steps)
    parts = [block for own in mine for block in (own, cross(own))]
    blocks = gate_weight.shape[1] // BLOCK
    weights = []
    for block in range(blocks):
        for weight in (gate_weight, up_weight):
            weights.append(load(where, weight, normed, BLOCK, block))
    half_a, half_b = up_project(where, shifts, parts, weights)
    wide = down_weight.shape[1] // 4
    theirs_weight, own_weight = [
        [load(where, down_weight, half_a, wide, at, flip) for at in range(2)] for flip in (True, False)
    ]

    def butterfly(value, mask):
        sign = jnp.where(me & mask == 0, 1.0, -1.0).astype(jnp.float32)
        other = cross(value, mask)
        return (other.astype(jnp.float32) + sign * value.astype(jnp.float32)).astype(jnp.bfloat16)

    masks = [1 << bit for bit in range(count.bit_length() - 1)]
    orders = [masks[-1:] + masks[:-1], masks]
    for stage in range(len(masks)):
        half_a = butterfly(half_a, orders[0][stage])
        half_b = butterfly(half_b, orders[1][stage])

    total = count * gate_weight.shape[1]
    limits = clip_scale.reshape(1, -1)
    theirs = down_project(where, half_a, half_b, limits, theirs_weight, chips, total)
    own = down_project(where, half_a, half_b, limits, own_weight, chips, total)
    arrived = cross(theirs)
    rows = own.shape[0] // chips

    def chunk(away):
        at = away % chips
        return own[at * rows : (at + 1) * rows].astype(jnp.float32) + arrived[at * rows : (at + 1) * rows].astype(
            jnp.float32
        )

    far = hop(chunk(steps).astype(jnp.bfloat16), 1, -1).astype(jnp.float32)
    zero = jnp.zeros_like(far)
    ahead = jnp.where(core == 0, far, zero)
    behind = jnp.where(core == 0, zero, far)
    for away in range(steps - 1, 0, -1):
        ahead = right((ahead + chunk(away)).astype(jnp.bfloat16)).astype(jnp.float32)
        behind = left((behind + chunk(-away)).astype(jnp.bfloat16)).astype(jnp.float32)
    summed = ahead + behind + chunk(0)
    part = rows // 2
    keep = lax.dynamic_slice_in_dim(summed, core * part, part, 0)
    give = lax.dynamic_slice_in_dim(summed, (1 - core) * part, part, 0)
    take = cross(give.astype(jnp.bfloat16)).astype(jnp.float32)
    low = jnp.where(core == 0, keep, take)
    high = jnp.where(core == 0, take, keep)
    return (tokens.astype(jnp.float32) + jnp.concatenate([low, high], axis=1)).astype(jnp.bfloat16)


def solution(mesh):
    in_specs = (
        P(("groups", "hid"), None),
        P(),
        P(None, "hid"),
        P(None, "hid"),
        P("hid", None),
        P("hid"),
    )
    out_specs = P(("groups", "hid"), None)
    body = functools.partial(shards, mesh.shape["hid"])
    return jax.shard_map(body, mesh=mesh, in_specs=in_specs, out_specs=out_specs, check_vma=False)
```

time: 123 us -> 108 us (0.88)
  local copies, waits for them, and re-layouts: 20.7 us -> 1.69 us
  Pallas kernels: 24.4 us -> 36 us
  waiting for transfers between devices: 49 us -> 43.3 us
  other arithmetic: 4.91 us -> 1.46 us
  starting transfers between devices: 23.5 us -> 24.8 us
    unnamed x12 -> x8, local copies, waits for them, and re-layouts: 17.3 us -> 1.67 us
    pallas_call x1 -> x14, Pallas kernels: 17.9 us -> 33.1 us  [the longest x12 27.2 us: load(): pl.pallas_call(functools.partial(load_kernel, flip, (8, at)), out_shape=j...]
    ppermute x18, waiting for transfers between devices: 23.9 us -> 12.5 us  [cross(): return lax.ppermute(value, 'hid', [(d, d ^ mask) for d in range(count)])]
    ppermute x14, waiting for transfers between devices: 25.2 us -> 30.8 us  [hop(): return lax.ppermute(value, 'hid', pairs)]
    pallas_call x2, Pallas kernels: 6.59 us -> 2.88 us  [down_project(): pl.pallas_call(functools.partial(down_kernel, width // BLOCK, chips, tota...]
    ppermute x18, starting transfers between devices: 8.35 us -> 10.9 us  [cross(): return lax.ppermute(value, 'hid', [(d, d ^ mask) for d in range(count)])]
    gather x2 -> x0, local copies, waits for them, and re-layouts: 1.94 us -> none  [the longest x1 1.3 us: shards(): chip_at = ring[(position + jnp.array(shifts, jnp.int32)) % chips]]
    select_n x1 -> x0, other arithmetic: 1.31 us -> none  [shards(): chip_at = ring[(position + jnp.array(shifts, jnp.int32)) % chips]]
  transfers between devices with their start and end apart: 32 -> 32, of which waited for: 23 -> 18; matrix products, arithmetic and copies ran while one was open for 4% -> 0% of each run, Pallas kernels for 3% -> 27%
where the time goes in v2:
time: 108 us
  waiting for transfers between devices  43.3 us (40%)
  Pallas kernels  36 us (33%)
  starting transfers between devices  24.8 us (23%)
  local copies, waits for them, and re-layouts  1.69 us (2%)
  other arithmetic  1.46 us (1%)
    ppermute x14, waiting for transfers between devices, hop(): return lax.ppermute(value, 'hid', pairs)  30.8 us
    pallas_call x12, Pallas kernels, load(): pl.pallas_call(functools.partial(load_kernel, flip, (8, at)), out_shape=j...  27.2 us
    ppermute x14, starting transfers between devices, hop(): return lax.ppermute(value, 'hid', pairs)  13.9 us
    ppermute x18, waiting for transfers between devices, cross(): return lax.ppermute(value, 'hid', [(d, d ^ mask) for d in range(count)])  12.5 us
    ppermute x18, starting transfers between devices, cross(): return lax.ppermute(value, 'hid', [(d, d ^ mask) for d in range(count)])  10.9 us
    pallas_call x1, Pallas kernels, up_project(): pl.pallas_call(functools.partial(up_kernel, count, shifts), out_shape=(ha...  5.78 us
    pallas_call x2, Pallas kernels, down_project(): pl.pallas_call(functools.partial(down_kernel, width // BLOCK, chips, tota...  2.88 us
  transfers between devices with their start and end apart: 32, of which 18 were waited for; matrix products, arithmetic and copies ran while one was open for 0% of the time, Pallas kernels for 27%

profile of v2, /device:TPU:0, one launch (start us, length us, event | category | flops | bytes accessed | tf_op | source)
XLA Modules:
  0.0 107.7 jit_solution(8546635439193721132)
XLA Ops:
  0.0 0.9 copy-done
  0.9 0.8 copy-done.2
  1.7 0.2 normalize.1.after_ref.refs_0_
  1.9 3.0 %collective-permute-start.3 = (bf16[8,8192]{1,0:T(8,128)(2,1)S(1)}, bf16[8,8192]{1,0:T(8,128)(2,1)S(1)}, u32[]{:S(2)}, u32[]{:S(2)}) collective-permute-start(bf16[8,8192]{1,0:T(8,128)(2,1)S(1)} %normalize.1.after_ref.refs_0_), channel_id=1, source_target_pairs={{0,2},{1,3},{4,0},{5,1},{8,4},{9,5},{12,8},{13,9},{14,12},{15,13},... | collective-permute-start | bytes 393224 | tf_op jit(solution)/shard_map/ppermute | solution.py:201
  4.9 0.1 collective-permute-start.1
  5.0 3.4 %collective-permute-done.3.refs_4_ = bf16[8,8192]{1,0:T(8,128)(2,1)S(1)} collective-permute-done((bf16[8,8192]{1,0:T(8,128)(2,1)S(1)}, bf16[8,8192]{1,0:T(8,128)(2,1)S(1)}, u32[]{:S(2)}, u32[]{:S(2)}) %collective-permute-start.3) | collective-permute-done | bytes 131104 | tf_op jit(solution)/shard_map/ppermute | solution.py:201
  8.4 1.7 %collective-permute-start.7 = (bf16[8,8192]{1,0:T(8,128)(2,1)S(1)}, bf16[8,8192]{1,0:T(8,128)(2,1)S(1)}, u32[]{:S(2)}, u32[]{:S(2)}) collective-permute-start(bf16[8,8192]{1,0:T(8,128)(2,1)S(1)} %collective-permute-done.3.refs_4_), channel_id=1, source_target_pairs={{0,2},{1,3},{4,0},{5,1},{8,4},{9,5},{12,8},{13,9},{14,12},{15,13},... | collective-permute-start | bytes 393224 | tf_op jit(solution)/shard_map/ppermute | solution.py:201
  10.1 0.3 collective-permute-start.5
  10.5 2.9 %collective-permute-done.7.refs_8_ = bf16[8,8192]{1,0:T(8,128)(2,1)S(1)} collective-permute-done((bf16[8,8192]{1,0:T(8,128)(2,1)S(1)}, bf16[8,8192]{1,0:T(8,128)(2,1)S(1)}, u32[]{:S(2)}, u32[]{:S(2)}) %collective-permute-start.7) | collective-permute-done | bytes 131104 | tf_op jit(solution)/shard_map/ppermute | solution.py:201
  13.4 1.7 %collective-permute-start.11 = (bf16[8,8192]{1,0:T(8,128)(2,1)S(1)}, bf16[8,8192]{1,0:T(8,128)(2,1)S(1)}, u32[]{:S(2)}, u32[]{:S(2)}) collective-permute-start(bf16[8,8192]{1,0:T(8,128)(2,1)S(1)} %collective-permute-done.7.refs_8_), channel_id=1, source_target_pairs={{0,2},{1,3},{4,0},{5,1},{8,4},{9,5},{12,8},{13,9},{14,12},{15,13},... | collective-permute-start | bytes 393224 | tf_op jit(solution)/shard_map/ppermute | solution.py:201
  15.1 0.3 collective-permute-start.9
  15.4 0.5 collective-permute-start.2
  15.9 2.4 %collective-permute-done.11.refs_12_ = bf16[8,8192]{1,0:T(8,128)(2,1)S(1)} collective-permute-done((bf16[8,8192]{1,0:T(8,128)(2,1)S(1)}, bf16[8,8192]{1,0:T(8,128)(2,1)S(1)}, u32[]{:S(2)}, u32[]{:S(2)}) %collective-permute-start.11) | collective-permute-done | bytes 131104 | tf_op jit(solution)/shard_map/ppermute | solution.py:201
  18.4 1.7 %collective-permute-done.9.refs_10_ = bf16[8,8192]{1,0:T(8,128)(2,1)S(1)} collective-permute-done((bf16[8,8192]{1,0:T(8,128)(2,1)S(1)}, bf16[8,8192]{1,0:T(8,128)(2,1)S(1)}, u32[]{:S(2)}, u32[]{:S(2)}) %collective-permute-start.9) | collective-permute-done | bytes 131104 | tf_op jit(solution)/shard_map/ppermute | solution.py:201
  20.1 0.4 collective-permute-start.13
  20.5 0.5 collective-permute-start.8
  21.1 0.4 collective-permute-start.12
  21.5 3.6 %collective-permute-done.13.refs_14_ = bf16[8,8192]{1,0:T(8,128)(2,1)S(1)} collective-permute-done((bf16[8,8192]{1,0:T(8,128)(2,1)S(1)}, bf16[8,8192]{1,0:T(8,128)(2,1)S(1)}, u32[]{:S(2)}, u32[]{:S(2)}) %collective-permute-start.13) | collective-permute-done | bytes 131104 | tf_op jit(solution)/shard_map/ppermute | solution.py:201
  25.1 2.3 %load.12.refs_16_ = bf16[8192,256]{1,0:T(8,128)(2,1)S(1)} custom-call(s32[1]{0:T(128)} %bitcast.me_ref, bf16[8192,1024]{1,0:T(8,128)(2,1)} %weight_ref.18, bf16[8,8192]{1,0:T(8,128)(2,1)S(1)} %normalize.1.after_ref.refs_0_), custom_call_target="tpu_custom_call" | custom-call | bytes 8388608 | tf_op jit(solution)/shard_map/load/pallas_call | solution.py:80
  27.4 2.3 %load.14.refs_18_ = bf16[8192,256]{1,0:T(8,128)(2,1)S(1)} custom-call(s32[1]{0:T(128)} %bitcast.me_ref, bf16[8192,1024]{1,0:T(8,128)(2,1)} %weight_ref.18, bf16[8,8192]{1,0:T(8,128)(2,1)S(1)} %normalize.1.after_ref.refs_0_), custom_call_target="tpu_custom_call" | custom-call | bytes 8388608 | tf_op jit(solution)/shard_map/load/pallas_call | solution.py:80
  29.7 2.3 %load.13.refs_17_ = bf16[8192,256]{1,0:T(8,128)(2,1)S(1)} custom-call(s32[1]{0:T(128)} %bitcast.me_ref, bf16[8192,1024]{1,0:T(8,128)(2,1)} %weight_ref.19, bf16[8,8192]{1,0:T(8,128)(2,1)S(1)} %normalize.1.after_ref.refs_0_), custom_call_target="tpu_custom_call" | custom-call | bytes 8388608 | tf_op jit(solution)/shard_map/load/pallas_call | solution.py:80
  31.9 2.3 %load.15.refs_19_ = bf16[8192,256]{1,0:T(8,128)(2,1)S(1)} custom-call(s32[1]{0:T(128)} %bitcast.me_ref, bf16[8192,1024]{1,0:T(8,128)(2,1)} %weight_ref.19, bf16[8,8192]{1,0:T(8,128)(2,1)S(1)} %normalize.1.after_ref.refs_0_), custom_call_target="tpu_custom_call" | custom-call | bytes 8388608 | tf_op jit(solution)/shard_map/load/pallas_call | solution.py:80
  34.2 2.3 %load.16.refs_20_ = bf16[8192,256]{1,0:T(8,128)(2,1)S(1)} custom-call(s32[1]{0:T(128)} %bitcast.me_ref, bf16[8192,1024]{1,0:T(8,128)(2,1)} %weight_ref.18, bf16[8,8192]{1,0:T(8,128)(2,1)S(1)} %normalize.1.after_ref.refs_0_), custom_call_target="tpu_custom_call" | custom-call | bytes 8388608 | tf_op jit(solution)/shard_map/load/pallas_call | solution.py:80
  36.5 2.3 %load.17.refs_21_ = bf16[8192,256]{1,0:T(8,128)(2,1)S(1)} custom-call(s32[1]{0:T(128)} %bitcast.me_ref, bf16[8192,1024]{1,0:T(8,128)(2,1)} %weight_ref.19, bf16[8,8192]{1,0:T(8,128)(2,1)S(1)} %normalize.1.after_ref.refs_0_), custom_call_target="tpu_custom_call" | custom-call | bytes 8388608 | tf_op jit(solution)/shard_map/load/pallas_call | solution.py:80
  38.8 2.3 %load.18.refs_22_ = bf16[8192,256]{1,0:T(8,128)(2,1)S(1)} custom-call(s32[1]{0:T(128)} %bitcast.me_ref, bf16[8192,1024]{1,0:T(8,128)(2,1)} %weight_ref.18, bf16[8,8192]{1,0:T(8,128)(2,1)S(1)} %normalize.1.after_ref.refs_0_), custom_call_target="tpu_custom_call" | custom-call | bytes 8388608 | tf_op jit(solution)/shard_map/load/pallas_call | solution.py:80
  41.1 2.3 %load.19.refs_23_ = bf16[8192,256]{1,0:T(8,128)(2,1)S(1)} custom-call(s32[1]{0:T(128)} %bitcast.me_ref, bf16[8192,1024]{1,0:T(8,128)(2,1)} %weight_ref.19, bf16[8,8192]{1,0:T(8,128)(2,1)S(1)} %normalize.1.after_ref.refs_0_), custom_call_target="tpu_custom_call" | custom-call | bytes 8388608 | tf_op jit(solution)/shard_map/load/pallas_call | solution.py:80
  43.5 5.8 %up_project.1 = (bf16[128,512]{1,0:T(8,128)(2,1)S(1)}, bf16[128,512]{1,0:T(8,128)(2,1)S(1)}) custom-call(s32[1]{0:T(128)} %bitcast.me_ref, bf16[8,8192]{1,0:T(8,128)(2,1)S(1)} %normalize.1.after_ref.refs_0_, bf16[8,8192]{1,0:T(8,128)(2,1)S(1)} %collective-permute-done.refs_1_, bf16[8,8192]{1,0:T(8,128)(2,1)S(1)} %collective-permute-done.1.refs_2_, ...), custom_call_target="tpu_custom_call" | custom-call | flops 4294967296 | tf_op jit(solution)/shard_map/up_project/pallas_call | solution.py:131
  49.2 0.6 collective-permute-start.19
  49.8 1.5 %collective-permute-start.15 = (bf16[128,512]{1,0:T(8,128)(2,1)S(1)}, bf16[128,512]{1,0:T(8,128)(2,1)S(1)}, u32[]{:S(2)}, u32[]{:S(2)}) collective-permute-start(bf16[128,512]{1,0:T(8,128)(2,1)S(1)} %get-tuple-element.7.after_ref), channel_id=1, source_target_pairs={{0,8},{1,9},{2,10},{3,11},{4,12},{5,13},{6,14},{7,15},{8,0},{9,1},... | collective-permute-start | bytes 393224 | tf_op jit(solution)/shard_map/ppermute | solution.py:210
  51.3 2.2 %load.22.refs_0_ = bf16[1024,2048]{1,0:T(8,128)(2,1)S(1)} custom-call(s32[1]{0:T(128)} %bitcast.me_ref, bf16[1024,8192]{1,0:T(8,128)(2,1)} %weight_ref.23, bf16[128,512]{1,0:T(8,128)(2,1)S(1)} %get-tuple-element.7.after_ref), custom_call_target="tpu_custom_call" | custom-call | bytes 8388608 | tf_op jit(solution)/shard_map/load/pallas_call | solution.py:80
  53.6 2.2 %load.23.refs_1_ = bf16[1024,2048]{1,0:T(8,128)(2,1)S(1)} custom-call(s32[1]{0:T(128)} %bitcast.me_ref, bf16[1024,8192]{1,0:T(8,128)(2,1)} %weight_ref.23, bf16[128,512]{1,0:T(8,128)(2,1)S(1)} %get-tuple-element.7.after_ref), custom_call_target="tpu_custom_call" | custom-call | bytes 8388608 | tf_op jit(solution)/shard_map/load/pallas_call | solution.py:80
  55.9 2.7 %collective-permute-start.20 = (bf16[128,512]{1,0:T(8,128)(2,1)S(1)}, bf16[128,512]{1,0:T(8,128)(2,1)S(1)}, u32[]{:S(2)}, u32[]{:S(2)}) collective-permute-start(bf16[128,512]{1,0:T(8,128)(2,1)S(1)} %add_convert_fusion.8), channel_id=1, source_target_pairs={{0,2},{1,3},{2,0},{3,1},{4,6},{5,7},{6,4},{7,5},{8,10},{9,11},{10,... | collective-permute-start | bytes 393224 | tf_op jit(solution)/shard_map/ppermute | solution.py:210
  58.6 0.3 collective-permute-done.15
  59.0 0.1 collective-permute-start.16
  59.1 3.0 %collective-permute-done.20 = bf16[128,512]{1,0:T(8,128)(2,1)S(1)} collective-permute-done((bf16[128,512]{1,0:T(8,128)(2,1)S(1)}, bf16[128,512]{1,0:T(8,128)(2,1)S(1)}, u32[]{:S(2)}, u32[]{:S(2)}) %collective-permute-start.20) | collective-permute-done | bytes 131104 | tf_op jit(solution)/shard_map/ppermute | solution.py:210
  62.1 0.7 collective-permute-start.21
  62.9 1.6 %collective-permute-start.17 = (bf16[128,512]{1,0:T(8,128)(2,1)S(1)}, bf16[128,512]{1,0:T(8,128)(2,1)S(1)}, u32[]{:S(2)}, u32[]{:S(2)}) collective-permute-start(bf16[128,512]{1,0:T(8,128)(2,1)S(1)} %add_convert_fusion.11), channel_id=1, source_target_pairs={{0,2},{1,3},{2,0},{3,1},{4,6},{5,7},{6,4},{7,5},{8,10},{9,11},{10,... | collective-permute-start | bytes 393224 | tf_op jit(solution)/shard_map/ppermute | solution.py:210
  64.6 2.6 %collective-permute-done.21 = bf16[128,512]{1,0:T(8,128)(2,1)S(1)} collective-permute-done((bf16[128,512]{1,0:T(8,128)(2,1)S(1)}, bf16[128,512]{1,0:T(8,128)(2,1)S(1)}, u32[]{:S(2)}, u32[]{:S(2)}) %collective-permute-start.21) | collective-permute-done | bytes 131104 | tf_op jit(solution)/shard_map/ppermute | solution.py:210
  67.2 0.6 collective-permute-start.22
  67.8 0.2 collective-permute-done.17
  68.0 1.4 %collective-permute-start.18 = (bf16[128,512]{1,0:T(8,128)(2,1)S(1)}, bf16[128,512]{1,0:T(8,128)(2,1)S(1)}, u32[]{:S(2)}, u32[]{:S(2)}) collective-permute-start(bf16[128,512]{1,0:T(8,128)(2,1)S(1)} %add_convert_fusion.10), channel_id=1, source_target_pairs={{0,4},{1,5},{2,6},{3,7},{4,0},{5,1},{6,2},{7,3},{8,12},{9,13},{10,... | collective-permute-start | bytes 393224 | tf_op jit(solution)/shard_map/ppermute | solution.py:210
  69.4 5.1 %collective-permute-done.22 = bf16[128,512]{1,0:T(8,128)(2,1)S(1)} collective-permute-done((bf16[128,512]{1,0:T(8,128)(2,1)S(1)}, bf16[128,512]{1,0:T(8,128)(2,1)S(1)}, u32[]{:S(2)}, u32[]{:S(2)}) %collective-permute-start.22) | collective-permute-done | bytes 131104 | tf_op jit(solution)/shard_map/ppermute | solution.py:210
  74.7 1.4 %down_project.3 = bf16[128,4096]{1,0:T(8,128)(2,1)S(1)} custom-call(s32[1]{0:T(128)} %bitcast.me_ref, bf16[128,512]{1,0:T(8,128)(2,1)S(1)} %add_convert_fusion.9.a_ref, bf16[128,512]{1,0:T(8,128)(2,1)S(1)} %add_convert_fusion.5.b_ref, f32[1,1024]{1,0:T(1,128)S(1)} %bitcast.4, bf16[1024,2048]{1,0:T(8,128)(2,1)S(1)} %load.22.refs_0_, ...), custom_call_target="tpu_custom_call" | custom-call | flops 1073741824 | tf_op jit(solution)/shard_map/down_project/pallas_call | solution.py:176
  76.1 0.1 collective-permute-start.23
  76.2 2.2 %load.20.refs_0_ = bf16[1024,2048]{1,0:T(8,128)(2,1)S(1)} custom-call(s32[1]{0:T(128)} %bitcast.me_ref, bf16[1024,8192]{1,0:T(8,128)(2,1)} %weight_ref.23, bf16[128,512]{1,0:T(8,128)(2,1)S(1)} %get-tuple-element.7.after_ref), custom_call_target="tpu_custom_call" | custom-call | bytes 8388608 | tf_op jit(solution)/shard_map/load/pallas_call | solution.py:80
  78.4 2.2 %load.21.refs_1_ = bf16[1024,2048]{1,0:T(8,128)(2,1)S(1)} custom-call(s32[1]{0:T(128)} %bitcast.me_ref, bf16[1024,8192]{1,0:T(8,128)(2,1)} %weight_ref.23, bf16[128,512]{1,0:T(8,128)(2,1)S(1)} %get-tuple-element.7.after_ref), custom_call_target="tpu_custom_call" | custom-call | bytes 8388608 | tf_op jit(solution)/shard_map/load/pallas_call | solution.py:80
  80.7 1.4 %down_project.2 = bf16[128,4096]{1,0:T(8,128)(2,1)S(1)} custom-call(s32[1]{0:T(128)} %bitcast.me_ref, bf16[128,512]{1,0:T(8,128)(2,1)S(1)} %add_convert_fusion.9.a_ref, bf16[128,512]{1,0:T(8,128)(2,1)S(1)} %add_convert_fusion.5.b_ref, f32[1,1024]{1,0:T(1,128)S(1)} %bitcast.5, bf16[1024,2048]{1,0:T(8,128)(2,1)S(1)} %load.20.refs_0_, ...), custom_call_target="tpu_custom_call" | custom-call | flops 1073741824 | tf_op jit(solution)/shard_map/down_project/pallas_call | solution.py:176
  82.3 5.0 %collective-permute-done.24 = bf16[16,4096]{1,0:T(8,128)(2,1)S(1)} collective-permute-done((bf16[16,4096]{1,0:T(8,128)(2,1)S(1)}, bf16[16,4096]{1,0:T(8,128)(2,1)S(1)}, u32[]{:S(2)}, u32[]{:S(2)}) %collective-permute-start.24) | collective-permute-done | bytes 131104 | tf_op jit(solution)/shard_map/ppermute | solution.py:201
  87.2 0.1 fusion.1
  87.4 2.0 %collective-permute-start.28 = (bf16[16,4096]{1,0:T(8,128)(2,1)S(1)}, bf16[16,4096]{1,0:T(8,128)(2,1)S(1)}, u32[]{:S(2)}, u32[]{:S(2)}) collective-permute-start(bf16[16,4096]{1,0:T(8,128)(2,1)S(1)} %get-tuple-element.10), channel_id=1, source_target_pairs={{0,2},{1,3},{4,0},{5,1},{8,4},{9,5},{12,8},{13,9},{14,12},{15,13},... | collective-permute-start | bytes 393224 | tf_op jit(solution)/shard_map/ppermute | solution.py:201
  89.4 3.0 %collective-permute-done.25 = bf16[16,4096]{1,0:T(8,128)(2,1)S(1)} collective-permute-done((bf16[16,4096]{1,0:T(8,128)(2,1)S(1)}, bf16[16,4096]{1,0:T(8,128)(2,1)S(1)}, u32[]{:S(2)}, u32[]{:S(2)}) %collective-permute-start.25) | collective-permute-done | bytes 131104 | tf_op jit(solution)/shard_map/ppermute | solution.py:201
  92.5 0.1 add_convert_fusion.3
  92.6 1.2 %collective-permute-start.26 = (bf16[16,4096]{1,0:T(8,128)(2,1)S(1)}, bf16[16,4096]{1,0:T(8,128)(2,1)S(1)}, u32[]{:S(2)}, u32[]{:S(2)}) collective-permute-start(bf16[16,4096]{1,0:T(8,128)(2,1)S(1)} %get-tuple-element.13), channel_id=1, source_target_pairs={{0,4},{1,5},{4,8},{5,9},{8,12},{9,13},{12,14},{13,15},{14,10},{15,... | collective-permute-start | bytes 393224 | tf_op jit(solution)/shard_map/ppermute | solution.py:201
  93.7 0.9 collective-permute-start.29
  94.6 2.9 %collective-permute-done.26 = bf16[16,4096]{1,0:T(8,128)(2,1)S(1)} collective-permute-done((bf16[16,4096]{1,0:T(8,128)(2,1)S(1)}, bf16[16,4096]{1,0:T(8,128)(2,1)S(1)}, u32[]{:S(2)}, u32[]{:S(2)}) %collective-permute-start.26) | collective-permute-done | bytes 131104 | tf_op jit(solution)/shard_map/ppermute | solution.py:201
  97.6 1.1 %collective-permute-done.29 = bf16[16,4096]{1,0:T(8,128)(2,1)S(1)} collective-permute-done((bf16[16,4096]{1,0:T(8,128)(2,1)S(1)}, bf16[16,4096]{1,0:T(8,128)(2,1)S(1)}, u32[]{:S(2)}, u32[]{:S(2)}) %collective-permute-start.29) | collective-permute-done | bytes 131104 | tf_op jit(solution)/shard_map/ppermute | solution.py:201
  98.7 0.1 add_convert_fusion.2
  98.8 1.8 %collective-permute-start.27 = (bf16[16,4096]{1,0:T(8,128)(2,1)S(1)}, bf16[16,4096]{1,0:T(8,128)(2,1)S(1)}, u32[]{:S(2)}, u32[]{:S(2)}) collective-permute-start(bf16[16,4096]{1,0:T(8,128)(2,1)S(1)} %get-tuple-element.11), channel_id=1, source_target_pairs={{0,4},{1,5},{4,8},{5,9},{8,12},{9,13},{12,14},{13,15},{14,10},{15,... | collective-permute-start | bytes 393224 | tf_op jit(solution)/shard_map/ppermute | solution.py:201
  100.6 0.3 collective-permute-start.30
  100.9 2.9 %collective-permute-done.27 = bf16[16,4096]{1,0:T(8,128)(2,1)S(1)} collective-permute-done((bf16[16,4096]{1,0:T(8,128)(2,1)S(1)}, bf16[16,4096]{1,0:T(8,128)(2,1)S(1)}, u32[]{:S(2)}, u32[]{:S(2)}) %collective-permute-start.27) | collective-permute-done | bytes 131104 | tf_op jit(solution)/shard_map/ppermute | solution.py:201
  103.8 1.7 %collective-permute-done.30 = bf16[16,4096]{1,0:T(8,128)(2,1)S(1)} collective-permute-done((bf16[16,4096]{1,0:T(8,128)(2,1)S(1)}, bf16[16,4096]{1,0:T(8,128)(2,1)S(1)}, u32[]{:S(2)}, u32[]{:S(2)}) %collective-permute-start.30) | collective-permute-done | bytes 131104 | tf_op jit(solution)/shard_map/ppermute | solution.py:201
  105.6 0.1 collective-permute-start.31
  105.7 1.2 %collective-permute-done.31 = bf16[8,4096]{1,0:T(8,128)(2,1)S(1)} collective-permute-done((bf16[8,4096]{1,0:T(8,128)(2,1)S(1)}, bf16[8,4096]{1,0:T(8,128)(2,1)S(1)}, u32[]{:S(2)}, u32[]{:S(2)}) %collective-permute-start.31) | collective-permute-done | bytes 65568 | tf_op jit(solution)/shard_map/ppermute | solution.py:210
  107.0 0.7 fusion.4
  (41 shorter events, 0.8 us)
Async XLA Ops:
  0.0 0.9 copy-start
  0.9 0.8 copy-start.2
  1.9 6.6 %collective-permute-start.3 = (bf16[8,8192]{1,0:T(8,128)(2,1)S(1)}, bf16[8,8192]{1,0:T(8,128)(2,1)S(1)}, u32[]{:S(2)}, u32[]{:S(2)}) collective-permute-start(bf16[8,8192]{1,0:T(8,128)(2,1)S(1)} %normalize.1.after_ref.refs_0_), channel_id=1, source_target_pairs={{0,2},{1,3},{4,0},{5,1},{8,4},{9,5},{12,8},{13,9},{14,12},{15,13},... | collective-permute-start | bytes 393224 | tf_op jit(solution)/shard_map/ppermute | solution.py:201
  4.9 5.2 %collective-permute-start.1 = (bf16[8,8192]{1,0:T(8,128)(2,1)S(1)}, bf16[8,8192]{1,0:T(8,128)(2,1)S(1)}, u32[]{:S(2)}, u32[]{:S(2)}) collective-permute-start(bf16[8,8192]{1,0:T(8,128)(2,1)S(1)} %normalize.1.after_ref.refs_0_), channel_id=1, source_target_pairs={{0,4},{1,5},{4,8},{5,9},{8,12},{9,13},{12,14},{13,15},{14,10},{15,... | collective-permute-start | bytes 393224 | tf_op jit(solution)/shard_map/ppermute | solution.py:201
  8.4 5.0 %collective-permute-start.7 = (bf16[8,8192]{1,0:T(8,128)(2,1)S(1)}, bf16[8,8192]{1,0:T(8,128)(2,1)S(1)}, u32[]{:S(2)}, u32[]{:S(2)}) collective-permute-start(bf16[8,8192]{1,0:T(8,128)(2,1)S(1)} %collective-permute-done.3.refs_4_), channel_id=1, source_target_pairs={{0,2},{1,3},{4,0},{5,1},{8,4},{9,5},{12,8},{13,9},{14,12},{15,13},... | collective-permute-start | bytes 393224 | tf_op jit(solution)/shard_map/ppermute | solution.py:201
  10.1 5.0 %collective-permute-start.5 = (bf16[8,8192]{1,0:T(8,128)(2,1)S(1)}, bf16[8,8192]{1,0:T(8,128)(2,1)S(1)}, u32[]{:S(2)}, u32[]{:S(2)}) collective-permute-start(bf16[8,8192]{1,0:T(8,128)(2,1)S(1)} %collective-permute-done.1.refs_2_), channel_id=1, source_target_pairs={{0,4},{1,5},{4,8},{5,9},{8,12},{9,13},{12,14},{13,15},{14,10},{15,... | collective-permute-start | bytes 393224 | tf_op jit(solution)/shard_map/ppermute | solution.py:201
  13.4 5.0 %collective-permute-start.11 = (bf16[8,8192]{1,0:T(8,128)(2,1)S(1)}, bf16[8,8192]{1,0:T(8,128)(2,1)S(1)}, u32[]{:S(2)}, u32[]{:S(2)}) collective-permute-start(bf16[8,8192]{1,0:T(8,128)(2,1)S(1)} %collective-permute-done.7.refs_8_), channel_id=1, source_target_pairs={{0,2},{1,3},{4,0},{5,1},{8,4},{9,5},{12,8},{13,9},{14,12},{15,13},... | collective-permute-start | bytes 393224 | tf_op jit(solution)/shard_map/ppermute | solution.py:201
  15.1 5.0 %collective-permute-start.9 = (bf16[8,8192]{1,0:T(8,128)(2,1)S(1)}, bf16[8,8192]{1,0:T(8,128)(2,1)S(1)}, u32[]{:S(2)}, u32[]{:S(2)}) collective-permute-start(bf16[8,8192]{1,0:T(8,128)(2,1)S(1)} %collective-permute-done.5.refs_6_), channel_id=1, source_target_pairs={{0,4},{1,5},{4,8},{5,9},{8,12},{9,13},{12,14},{13,15},{14,10},{15,... | collective-permute-start | bytes 393224 | tf_op jit(solution)/shard_map/ppermute | solution.py:201
  15.4 5.0 %collective-permute-start = (bf16[8,8192]{1,0:T(8,128)(2,1)S(1)}, bf16[8,8192]{1,0:T(8,128)(2,1)S(1)}, u32[]{:S(2)}, u32[]{:S(2)}) collective-permute-start(bf16[8,8192]{1,0:T(8,128)(2,1)S(1)} %normalize.1.after_ref.refs_0_), channel_id=1, source_target_pairs={{0,1},{1,0},{2,3},{3,2},{4,5},{5,4},{6,7},{7,6},{8,9},{9,8},{10,11... | collective-permute-start | bytes 393224 | tf_op jit(solution)/shard_map/ppermute | solution.py:210
  15.4 5.6 %collective-permute-start.2 = (bf16[8,8192]{1,0:T(8,128)(2,1)S(1)}, bf16[8,8192]{1,0:T(8,128)(2,1)S(1)}, u32[]{:S(2)}, u32[]{:S(2)}) collective-permute-start(bf16[8,8192]{1,0:T(8,128)(2,1)S(1)} %collective-permute-done.1.refs_2_), channel_id=1, source_target_pairs={{0,1},{1,0},{2,3},{3,2},{4,5},{5,4},{6,7},{7,6},{8,9},{9,8},{10,11... | collective-permute-start | bytes 393224 | tf_op jit(solution)/shard_map/ppermute | solution.py:210
  15.9 5.1 %collective-permute-start.4 = (bf16[8,8192]{1,0:T(8,128)(2,1)S(1)}, bf16[8,8192]{1,0:T(8,128)(2,1)S(1)}, u32[]{:S(2)}, u32[]{:S(2)}) collective-permute-start(bf16[8,8192]{1,0:T(8,128)(2,1)S(1)} %collective-permute-done.3.refs_4_), channel_id=1, source_target_pairs={{0,1},{1,0},{2,3},{3,2},{4,5},{5,4},{6,7},{7,6},{8,9},{9,8},{10,11... | collective-permute-start | bytes 393224 | tf_op jit(solution)/shard_map/ppermute | solution.py:210
  20.1 5.0 %collective-permute-start.13 = (bf16[8,8192]{1,0:T(8,128)(2,1)S(1)}, bf16[8,8192]{1,0:T(8,128)(2,1)S(1)}, u32[]{:S(2)}, u32[]{:S(2)}) collective-permute-start(bf16[8,8192]{1,0:T(8,128)(2,1)S(1)} %broadcast_select_fusion), channel_id=1, source_target_pairs={{0,4},{1,3},{4,8},{5,1},{8,12},{9,5},{12,14},{13,9},{14,10},{15,13... | collective-permute-start | bytes 393224 | tf_op jit(solution)/shard_map/ppermute | solution.py:201
  20.5 22.9 %collective-permute-start.6 = (bf16[8,8192]{1,0:T(8,128)(2,1)S(1)}, bf16[8,8192]{1,0:T(8,128)(2,1)S(1)}, u32[]{:S(2)}, u32[]{:S(2)}) collective-permute-start(bf16[8,8192]{1,0:T(8,128)(2,1)S(1)} %collective-permute-done.5.refs_6_), channel_id=1, source_target_pairs={{0,1},{1,0},{2,3},{3,2},{4,5},{5,4},{6,7},{7,6},{8,9},{9,8},{10,11... | collective-permute-start | bytes 393224 | tf_op jit(solution)/shard_map/ppermute | solution.py:210
  20.5 23.0 %collective-permute-start.8 = (bf16[8,8192]{1,0:T(8,128)(2,1)S(1)}, bf16[8,8192]{1,0:T(8,128)(2,1)S(1)}, u32[]{:S(2)}, u32[]{:S(2)}) collective-permute-start(bf16[8,8192]{1,0:T(8,128)(2,1)S(1)} %collective-permute-done.7.refs_8_), channel_id=1, source_target_pairs={{0,1},{1,0},{2,3},{3,2},{4,5},{5,4},{6,7},{7,6},{8,9},{9,8},{10,11... | collective-permute-start | bytes 393224 | tf_op jit(solution)/shard_map/ppermute | solution.py:210
  21.0 22.4 %collective-permute-start.10 = (bf16[8,8192]{1,0:T(8,128)(2,1)S(1)}, bf16[8,8192]{1,0:T(8,128)(2,1)S(1)}, u32[]{:S(2)}, u32[]{:S(2)}) collective-permute-start(bf16[8,8192]{1,0:T(8,128)(2,1)S(1)} %collective-permute-done.9.refs_10_), channel_id=1, source_target_pairs={{0,1},{1,0},{2,3},{3,2},{4,5},{5,4},{6,7},{7,6},{8,9},{9,8},{10,11... | collective-permute-start | bytes 393224 | tf_op jit(solution)/shard_map/ppermute | solution.py:210
  21.1 22.4 %collective-permute-start.12 = (bf16[8,8192]{1,0:T(8,128)(2,1)S(1)}, bf16[8,8192]{1,0:T(8,128)(2,1)S(1)}, u32[]{:S(2)}, u32[]{:S(2)}) collective-permute-start(bf16[8,8192]{1,0:T(8,128)(2,1)S(1)} %collective-permute-done.11.refs_12_), channel_id=1, source_target_pairs={{0,1},{1,0},{2,3},{3,2},{4,5},{5,4},{6,7},{7,6},{8,9},{9,8},{10,11... | collective-permute-start | bytes 393224 | tf_op jit(solution)/shard_map/ppermute | solution.py:210
  25.1 18.4 %collective-permute-start.14 = (bf16[8,8192]{1,0:T(8,128)(2,1)S(1)}, bf16[8,8192]{1,0:T(8,128)(2,1)S(1)}, u32[]{:S(2)}, u32[]{:S(2)}) collective-permute-start(bf16[8,8192]{1,0:T(8,128)(2,1)S(1)} %collective-permute-done.13.refs_14_), channel_id=1, source_target_pairs={{0,1},{1,0},{2,3},{3,2},{4,5},{5,4},{6,7},{7,6},{8,9},{9,8},{10,11... | collective-permute-start | bytes 393224 | tf_op jit(solution)/shard_map/ppermute | solution.py:210
  49.2 6.6 %collective-permute-start.19 = (bf16[128,512]{1,0:T(8,128)(2,1)S(1)}, bf16[128,512]{1,0:T(8,128)(2,1)S(1)}, u32[]{:S(2)}, u32[]{:S(2)}) collective-permute-start(bf16[128,512]{1,0:T(8,128)(2,1)S(1)} %get-tuple-element.8), channel_id=1, source_target_pairs={{0,1},{1,0},{2,3},{3,2},{4,5},{5,4},{6,7},{7,6},{8,9},{9,8},{10,11... | collective-permute-start | bytes 393224 | tf_op jit(solution)/shard_map/ppermute | solution.py:210
  49.8 9.1 %collective-permute-start.15 = (bf16[128,512]{1,0:T(8,128)(2,1)S(1)}, bf16[128,512]{1,0:T(8,128)(2,1)S(1)}, u32[]{:S(2)}, u32[]{:S(2)}) collective-permute-start(bf16[128,512]{1,0:T(8,128)(2,1)S(1)} %get-tuple-element.7.after_ref), channel_id=1, source_target_pairs={{0,8},{1,9},{2,10},{3,11},{4,12},{5,13},{6,14},{7,15},{8,0},{9,1},... | collective-permute-start | bytes 393224 | tf_op jit(solution)/shard_map/ppermute | solution.py:210
  53.6 21.1 %copy-start.3 = (f32[1024]{0:T(1024)S(1)}, f32[1024]{0:T(1024)}, u32[]{:S(2)}) copy-start(f32[1024]{0:T(1024)} %param.11) | copy-start | bytes 12292
  55.9 6.2 %collective-permute-start.20 = (bf16[128,512]{1,0:T(8,128)(2,1)S(1)}, bf16[128,512]{1,0:T(8,128)(2,1)S(1)}, u32[]{:S(2)}, u32[]{:S(2)}) collective-permute-start(bf16[128,512]{1,0:T(8,128)(2,1)S(1)} %add_convert_fusion.8), channel_id=1, source_target_pairs={{0,2},{1,3},{2,0},{3,1},{4,6},{5,7},{6,4},{7,5},{8,10},{9,11},{10,... | collective-permute-start | bytes 393224 | tf_op jit(solution)/shard_map/ppermute | solution.py:210
  59.0 3.9 %collective-permute-start.16 = (bf16[128,512]{1,0:T(8,128)(2,1)S(1)}, bf16[128,512]{1,0:T(8,128)(2,1)S(1)}, u32[]{:S(2)}, u32[]{:S(2)}) collective-permute-start(bf16[128,512]{1,0:T(8,128)(2,1)S(1)} %add_convert_fusion.12), channel_id=1, source_target_pairs={{0,1},{1,0},{2,3},{3,2},{4,5},{5,4},{6,7},{7,6},{8,9},{9,8},{10,11... | collective-permute-start | bytes 393224 | tf_op jit(solution)/shard_map/ppermute | solution.py:210
  62.1 5.0 %collective-permute-start.21 = (bf16[128,512]{1,0:T(8,128)(2,1)S(1)}, bf16[128,512]{1,0:T(8,128)(2,1)S(1)}, u32[]{:S(2)}, u32[]{:S(2)}) collective-permute-start(bf16[128,512]{1,0:T(8,128)(2,1)S(1)} %add_convert_fusion.7), channel_id=1, source_target_pairs={{0,4},{1,5},{2,6},{3,7},{4,0},{5,1},{6,2},{7,3},{8,12},{9,13},{10,... | collective-permute-start | bytes 393224 | tf_op jit(solution)/shard_map/ppermute | solution.py:210
  62.9 5.0 %collective-permute-start.17 = (bf16[128,512]{1,0:T(8,128)(2,1)S(1)}, bf16[128,512]{1,0:T(8,128)(2,1)S(1)}, u32[]{:S(2)}, u32[]{:S(2)}) collective-permute-start(bf16[128,512]{1,0:T(8,128)(2,1)S(1)} %add_convert_fusion.11), channel_id=1, source_target_pairs={{0,2},{1,3},{2,0},{3,1},{4,6},{5,7},{6,4},{7,5},{8,10},{9,11},{10,... | collective-permute-start | bytes 393224 | tf_op jit(solution)/shard_map/ppermute | solution.py:210
  67.2 7.3 %collective-permute-start.22 = (bf16[128,512]{1,0:T(8,128)(2,1)S(1)}, bf16[128,512]{1,0:T(8,128)(2,1)S(1)}, u32[]{:S(2)}, u32[]{:S(2)}) collective-permute-start(bf16[128,512]{1,0:T(8,128)(2,1)S(1)} %add_convert_fusion.6), channel_id=1, source_target_pairs={{0,8},{1,9},{2,10},{3,11},{4,12},{5,13},{6,14},{7,15},{8,0},{9,1},... | collective-permute-start | bytes 393224 | tf_op jit(solution)/shard_map/ppermute | solution.py:210
  68.0 6.6 %collective-permute-start.18 = (bf16[128,512]{1,0:T(8,128)(2,1)S(1)}, bf16[128,512]{1,0:T(8,128)(2,1)S(1)}, u32[]{:S(2)}, u32[]{:S(2)}) collective-permute-start(bf16[128,512]{1,0:T(8,128)(2,1)S(1)} %add_convert_fusion.10), channel_id=1, source_target_pairs={{0,4},{1,5},{2,6},{3,7},{4,0},{5,1},{6,2},{7,3},{8,12},{9,13},{10,... | collective-permute-start | bytes 393224 | tf_op jit(solution)/shard_map/ppermute | solution.py:210
  76.1 6.0 %collective-permute-start.23 = (bf16[128,4096]{1,0:T(8,128)(2,1)S(1)}, bf16[128,4096]{1,0:T(8,128)(2,1)S(1)}, u32[]{:S(2)}, u32[]{:S(2)}) collective-permute-start(bf16[128,4096]{1,0:T(8,128)(2,1)S(1)} %down_project.3), channel_id=1, source_target_pairs={{0,1},{1,0},{2,3},{3,2},{4,5},{5,4},{6,7},{7,6},{8,9},{9,8},{10,11... | collective-permute-start | bytes 3145736 | tf_op jit(solution)/shard_map/ppermute | solution.py:210
  82.1 24.9 %copy-start.1 = (bf16[8,8192]{1,0:T(8,128)(2,1)S(1)}, bf16[8,8192]{1,0:T(8,128)(2,1)}, u32[]{:S(2)}) copy-start(bf16[8,8192]{1,0:T(8,128)(2,1)} %rows_ref.1) | copy-start | bytes 393220
  82.2 5.0 %collective-permute-start.24 = (bf16[16,4096]{1,0:T(8,128)(2,1)S(1)}, bf16[16,4096]{1,0:T(8,128)(2,1)S(1)}, u32[]{:S(2)}, u32[]{:S(2)}) collective-permute-start(bf16[16,4096]{1,0:T(8,128)(2,1)S(1)} %add_convert_fusion.4), channel_id=1, source_target_pairs={{0,4},{1,3},{4,8},{5,1},{8,12},{9,5},{12,14},{13,9},{14,10},{15,13... | collective-permute-start | bytes 393224 | tf_op jit(solution)/shard_map/ppermute | solution.py:201
  87.3 5.1 %collective-permute-start.25 = (bf16[16,4096]{1,0:T(8,128)(2,1)S(1)}, bf16[16,4096]{1,0:T(8,128)(2,1)S(1)}, u32[]{:S(2)}, u32[]{:S(2)}) collective-permute-start(bf16[16,4096]{1,0:T(8,128)(2,1)S(1)} %get-tuple-element.9), channel_id=1, source_target_pairs={{0,4},{1,5},{4,8},{5,9},{8,12},{9,13},{12,14},{13,15},{14,10},{15,... | collective-permute-start | bytes 393224 | tf_op jit(solution)/shard_map/ppermute | solution.py:201
  87.4 5.1 %collective-permute-start.28 = (bf16[16,4096]{1,0:T(8,128)(2,1)S(1)}, bf16[16,4096]{1,0:T(8,128)(2,1)S(1)}, u32[]{:S(2)}, u32[]{:S(2)}) collective-permute-start(bf16[16,4096]{1,0:T(8,128)(2,1)S(1)} %get-tuple-element.10), channel_id=1, source_target_pairs={{0,2},{1,3},{4,0},{5,1},{8,4},{9,5},{12,8},{13,9},{14,12},{15,13},... | collective-permute-start | bytes 393224 | tf_op jit(solution)/shard_map/ppermute | solution.py:201
  92.6 5.0 %collective-permute-start.26 = (bf16[16,4096]{1,0:T(8,128)(2,1)S(1)}, bf16[16,4096]{1,0:T(8,128)(2,1)S(1)}, u32[]{:S(2)}, u32[]{:S(2)}) collective-permute-start(bf16[16,4096]{1,0:T(8,128)(2,1)S(1)} %get-tuple-element.13), channel_id=1, source_target_pairs={{0,4},{1,5},{4,8},{5,9},{8,12},{9,13},{12,14},{13,15},{14,10},{15,... | collective-permute-start | bytes 393224 | tf_op jit(solution)/shard_map/ppermute | solution.py:201
  93.7 5.0 %collective-permute-start.29 = (bf16[16,4096]{1,0:T(8,128)(2,1)S(1)}, bf16[16,4096]{1,0:T(8,128)(2,1)S(1)}, u32[]{:S(2)}, u32[]{:S(2)}) collective-permute-start(bf16[16,4096]{1,0:T(8,128)(2,1)S(1)} %get-tuple-element.14), channel_id=1, source_target_pairs={{0,2},{1,3},{4,0},{5,1},{8,4},{9,5},{12,8},{13,9},{14,12},{15,13},... | collective-permute-start | bytes 393224 | tf_op jit(solution)/shard_map/ppermute | solution.py:201
  98.8 5.0 %collective-permute-start.27 = (bf16[16,4096]{1,0:T(8,128)(2,1)S(1)}, bf16[16,4096]{1,0:T(8,128)(2,1)S(1)}, u32[]{:S(2)}, u32[]{:S(2)}) collective-permute-start(bf16[16,4096]{1,0:T(8,128)(2,1)S(1)} %get-tuple-element.11), channel_id=1, source_target_pairs={{0,4},{1,5},{4,8},{5,9},{8,12},{9,13},{12,14},{13,15},{14,10},{15,... | collective-permute-start | bytes 393224 | tf_op jit(solution)/shard_map/ppermute | solution.py:201
  100.6 5.0 %collective-permute-start.30 = (bf16[16,4096]{1,0:T(8,128)(2,1)S(1)}, bf16[16,4096]{1,0:T(8,128)(2,1)S(1)}, u32[]{:S(2)}, u32[]{:S(2)}) collective-permute-start(bf16[16,4096]{1,0:T(8,128)(2,1)S(1)} %get-tuple-element.12), channel_id=1, source_target_pairs={{0,2},{1,3},{4,0},{5,1},{8,4},{9,5},{12,8},{13,9},{14,12},{15,13},... | collective-permute-start | bytes 393224 | tf_op jit(solution)/shard_map/ppermute | solution.py:201
  105.6 1.3 %collective-permute-start.31 = (bf16[8,4096]{1,0:T(8,128)(2,1)S(1)}, bf16[8,4096]{1,0:T(8,128)(2,1)S(1)}, u32[]{:S(2)}, u32[]{:S(2)}) collective-permute-start(bf16[8,4096]{1,0:T(8,128)(2,1)S(1)} %dynamic-slice_convert_fusion), channel_id=1, source_target_pairs={{0,1},{1,0},{2,3},{3,2},{4,5},{5,4},{6,7},{7,6},{8,9},{9,8},{10,11... | collective-permute-start | bytes 196616 | tf_op jit(solution)/shard_map/ppermute | solution.py:210

commit v3 on v2

v3 whole, which is shorter than its diff:
```python
import functools

import jax
import jax.numpy as jnp
from jax import lax
from jax.experimental import pallas as pl
from jax.experimental.pallas import tpu as pltpu
from jax.sharding import PartitionSpec as P

BLOCK = 256
MIB = 1 << 20


def hadamard(count):
    rows = lax.broadcasted_iota(jnp.int32, (count, count), 0)
    cols = lax.broadcasted_iota(jnp.int32, (count, count), 1)
    both = rows & cols
    parity = jnp.zeros((count, count), jnp.int32)
    for place in range(max(count.bit_length(), 1)):
        parity = parity + (both >> place & 1)
    return jnp.where(parity % 2 == 0, 1.0, -1.0).astype(jnp.bfloat16)


def normalize_kernel(rows_ref, gain_ref, out_ref):
    values = rows_ref[...].astype(jnp.float32)
    inverse = lax.rsqrt(jnp.mean(values * values, axis=-1, keepdims=True) + 1e-05)
    out_ref[...] = (values * inverse * gain_ref[...]).astype(jnp.bfloat16)


def normalize(rows_in, norm_gain):
    vmem = pl.BlockSpec(memory_space=pltpu.VMEM)
    return pl.pallas_call(
        normalize_kernel,
        out_shape=jax.ShapeDtypeStruct(rows_in.shape, jnp.bfloat16),
        in_specs=[vmem, vmem],
        out_specs=vmem,
        compiler_params=pltpu.CompilerParams(vmem_limit_bytes=4 * MIB),
        cost_estimate=pl.CostEstimate(flops=8 * rows_in.size, bytes_accessed=4 * rows_in.size, transcendentals=0),
        name="normalize",
    )(rows_in, norm_gain.reshape(1, -1))


def ring_of(chips):
    return list(range(0, chips, 2)) + list(range(chips - 1, 0, -2))


def ring_place(chip, shift, chips):
    spot = jnp.where(chip % 2 == 0, chip // 2, chips - 1 - (chip - 1) // 2)
    spot = (spot + shift) % chips
    return jnp.where(spot < (chips + 1) // 2, 2 * spot, 2 * (chips - spot) - 1)


def load_kernel(flip, at, weight_ref, after_ref, out_ref, sem):
    cols = out_ref.shape[1]
    wide = weight_ref.shape[1]
    start = at * cols
    if flip is not None:
        side = lax.axis_index("hid") % 2
        side = 1 - side if flip else side
        start = start + side * (wide // 2)
        start = pl.multiple_of(start, cols)
    copy = pltpu.make_async_copy(weight_ref.at[:, pl.ds(start, cols)], out_ref, sem)
    copy.start()
    copy.wait()


def load(weight, after, cols, at, flip=None):
    rows = weight.shape[0]
    hbm = pl.BlockSpec(memory_space=pltpu.HBM)
    return pl.pallas_call(
        functools.partial(load_kernel, flip, at),
        out_shape=jax.ShapeDtypeStruct((rows, cols), weight.dtype),
        in_specs=[hbm, hbm],
        out_specs=pl.BlockSpec(memory_space=pltpu.VMEM),
        scratch_shapes=[pltpu.SemaphoreType.DMA],
        compiler_params=pltpu.CompilerParams(vmem_limit_bytes=1 * MIB),
        cost_estimate=pl.CostEstimate(flops=0, bytes_accessed=2 * rows * cols, transcendentals=0),
        name="load",
    )(pltpu.with_memory_space_constraint(weight, pltpu.HBM), after)


def up_kernel(count, shifts, *refs):
    me = lax.axis_index("hid")
    chip, core = me // 2, me % 2
    spots = []
    for shift in shifts:
        there = 2 * ring_place(chip, shift, count // 2)
        spots += [there + core, there + 1 - core]
    parts, (out_a, out_b, rows_ref, hidden_ref) = refs[:count], refs[-4:]
    gates, ups = refs[count:-4:2], refs[count + 1 : -4 : 2]
    own = parts[0].shape[0]
    for pair in range(count // 2):
        both = [parts[2 * pair + k][...].astype(jnp.float32) for k in range(2)]
        rows_ref[2 * own * pair : 2 * own * (pair + 1), :] = jnp.concatenate(both, axis=0).astype(jnp.bfloat16)
    turn = hadamard(BLOCK)
    values = rows_ref[...]
    wide = gates[0].shape[1]
    for at in range(len(gates)):
        gate = jnp.dot(values, gates[at][...], preferred_element_type=jnp.float32)
        up = jnp.dot(values, ups[at][...], preferred_element_type=jnp.float32)
        hidden = gate / (1.0 + jnp.exp(-gate)) * up
        high = hidden.astype(jnp.bfloat16)
        low = (hidden - high.astype(jnp.float32)).astype(jnp.bfloat16)
        for block in range(wide // BLOCK):
            inner = slice(block * BLOCK, (block + 1) * BLOCK)
            outer = slice(at * wide + block * BLOCK, at * wide + (block + 1) * BLOCK)
            turned = jnp.dot(high[:, inner], turn, preferred_element_type=jnp.float32) + jnp.dot(
                low[:, inner], turn, preferred_element_type=jnp.float32
            )
            for part in range(count):
                spot = pl.multiple_of(spots[part] * own, own)
                hidden_ref[pl.ds(spot, own), outer] = turned[part * own : (part + 1) * own]
    half = out_a.shape[1]
    out_a[...] = hidden_ref[:, :half].astype(jnp.bfloat16)
    out_b[...] = hidden_ref[:, half:].astype(jnp.bfloat16)


def up_project(shifts, parts, weights):
    count, own = len(parts), parts[0].shape[0]
    depth = weights[0].shape[0]
    width = weights[0].shape[1] * len(weights) // 2
    rows = count * own
    half = jax.ShapeDtypeStruct((rows, width // 2), jnp.bfloat16)
    vmem = pl.BlockSpec(memory_space=pltpu.VMEM)
    return pl.pallas_call(
        functools.partial(up_kernel, count, shifts),
        out_shape=(half, half),
        in_specs=[vmem] * (count + len(weights)),
        out_specs=(vmem, vmem),
        scratch_shapes=[pltpu.VMEM((rows, depth), jnp.bfloat16), pltpu.VMEM((rows, width), jnp.float32)],
        compiler_params=pltpu.CompilerParams(vmem_limit_bytes=12 * MIB),
        cost_estimate=pl.CostEstimate(flops=4 * rows * depth * width, bytes_accessed=0, transcendentals=rows * width),
        name="up_project",
    )(*parts, *weights)


def down_kernel(blocks, chips, scale, a_ref, b_ref, clip_ref, *refs):
    weights, (out_ref, rows_ref, mixed_ref) = refs[:-3], refs[-3:]
    half = a_ref.shape[1]
    rows_ref[:, :half] = a_ref[...].astype(jnp.float32)
    rows_ref[:, half:] = b_ref[...].astype(jnp.float32)
    parts = [rows_ref[:, b * BLOCK : (b + 1) * BLOCK] for b in range(blocks)]
    span = 1
    while span < blocks:
        parts = [
            parts[b] + parts[b ^ span] if b & span == 0 else parts[b ^ span] - parts[b] for b in range(blocks)
        ]
        span *= 2
    for b in range(blocks):
        lanes = slice(b * BLOCK, (b + 1) * BLOCK)
        limit = 127.0 * clip_ref[:, lanes]
        rows_ref[:, lanes] = jnp.clip(parts[b] * scale, -limit, limit)
    rows = rows_ref.shape[0]
    each = rows // chips
    me = lax.axis_index("hid")
    for chip in range(chips):
        spot = pl.multiple_of(ring_place(me // 2, chip, chips) * each, each)
        mixed_ref[chip * each : (chip + 1) * each, :] = rows_ref[pl.ds(spot, each), :].astype(jnp.bfloat16)
    step = weights[0].shape[1]
    for at, weight_ref in enumerate(weights):
        product = jnp.dot(mixed_ref[...], weight_ref[...], preferred_element_type=jnp.float32)
        out_ref[:, at * step : (at + 1) * step] = product.astype(jnp.bfloat16)


def down_project(a, b, clip_scale, weights, chips, total):
    rows = a.shape[0]
    width = 2 * a.shape[1]
    depth = len(weights) * weights[0].shape[1]
    vmem = pl.BlockSpec(memory_space=pltpu.VMEM)
    return pl.pallas_call(
        functools.partial(down_kernel, width // BLOCK, chips, total**-0.5),
        out_shape=jax.ShapeDtypeStruct((rows, depth), jnp.bfloat16),
        in_specs=[vmem, vmem, vmem] + [vmem] * len(weights),
        out_specs=vmem,
        scratch_shapes=[pltpu.VMEM((rows, width), jnp.float32), pltpu.VMEM((rows, width), jnp.bfloat16)],
        compiler_params=pltpu.CompilerParams(vmem_limit_bytes=8 * MIB),
        cost_estimate=pl.CostEstimate(flops=2 * rows * depth * width, bytes_accessed=0, transcendentals=0),
        name="down_project",
    )(a, b, clip_scale, *weights)


def pick_kernel(even_ref, odd_ref, out_ref):
    core = lax.axis_index("hid") % 2

    @pl.when(core == 0)
    def _():
        out_ref[...] = even_ref[...]

    @pl.when(core != 0)
    def _():
        out_ref[...] = odd_ref[...]


def turn_kernel(mask, value_ref, other_ref, out_ref):
    sign = jnp.where(lax.axis_index("hid") & mask == 0, 1.0, -1.0).astype(jnp.float32)
    out_ref[...] = (other_ref[...].astype(jnp.float32) + sign * value_ref[...].astype(jnp.float32)).astype(jnp.bfloat16)


def both(body, first, second, name):
    vmem = pl.BlockSpec(memory_space=pltpu.VMEM)
    return pl.pallas_call(
        body,
        out_shape=jax.ShapeDtypeStruct(first.shape, first.dtype),
        in_specs=[vmem, vmem],
        out_specs=vmem,
        compiler_params=pltpu.CompilerParams(vmem_limit_bytes=2 * MIB),
        cost_estimate=pl.CostEstimate(flops=2 * first.size, bytes_accessed=0, transcendentals=0),
        name=name,
    )(first, second)


def chunk(away, chips, own_ref, arrived_ref):
    rows = own_ref.shape[0] // chips
    at = slice(away % chips * rows, (away % chips + 1) * rows)
    return own_ref[at, :].astype(jnp.float32) + arrived_ref[at, :].astype(jnp.float32)


def far_kernel(away, chips, own_ref, arrived_ref, out_ref):
    out_ref[...] = chunk(away, chips, own_ref, arrived_ref).astype(jnp.bfloat16)


def split_kernel(away, chips, far_ref, own_ref, arrived_ref, ahead_ref, behind_ref):
    ahead = chunk(away, chips, own_ref, arrived_ref)
    behind = chunk(-away, chips, own_ref, arrived_ref)
    core = lax.axis_index("hid") % 2
    far = far_ref[...].astype(jnp.float32)
    ahead_ref[...] = (ahead + jnp.where(core == 0, far, 0.0)).astype(jnp.bfloat16)
    behind_ref[...] = (behind + jnp.where(core == 0, 0.0, far)).astype(jnp.bfloat16)


def relay_kernel(away, chips, ahead_in, behind_in, own_ref, arrived_ref, ahead_ref, behind_ref):
    ahead = chunk(away, chips, own_ref, arrived_ref) + ahead_in[...].astype(jnp.float32)
    behind = chunk(-away, chips, own_ref, arrived_ref) + behind_in[...].astype(jnp.float32)
    ahead_ref[...] = ahead.astype(jnp.bfloat16)
    behind_ref[...] = behind.astype(jnp.bfloat16)


def last_kernel(chips, ahead_in, behind_in, own_ref, arrived_ref, keep_ref, give_ref, sum_ref):
    part = keep_ref.shape[0]
    core = lax.axis_index("hid") % 2
    sum_ref[...] = (
        chunk(0, chips, own_ref, arrived_ref) + ahead_in[...].astype(jnp.float32) + behind_in[...].astype(jnp.float32)
    )
    keep_ref[...] = sum_ref[pl.ds(pl.multiple_of(core * part, part), part), :]
    give_ref[...] = sum_ref[pl.ds(pl.multiple_of((1 - core) * part, part), part), :].astype(jnp.bfloat16)


def mix_kernel(tokens_ref, keep_ref, take_ref, out_ref):
    wide = keep_ref.shape[1]
    keep, take = keep_ref[...], take_ref[...].astype(jnp.float32)
    first = lax.axis_index("hid") % 2 == 0
    low, high = jnp.where(first, keep, take), jnp.where(first, take, keep)
    out_ref[:, :wide] = (tokens_ref[:, :wide].astype(jnp.float32) + low).astype(jnp.bfloat16)
    out_ref[:, wide:] = (tokens_ref[:, wide:].astype(jnp.float32) + high).astype(jnp.bfloat16)


def small(body, outs, operands, name, scratch=()):
    vmem = pl.BlockSpec(memory_space=pltpu.VMEM)
    return pl.pallas_call(
        body,
        out_shape=outs,
        in_specs=[vmem] * len(operands),
        out_specs=jax.tree.map(lambda _: vmem, outs),
        scratch_shapes=scratch,
        compiler_params=pltpu.CompilerParams(vmem_limit_bytes=4 * MIB),
        cost_estimate=pl.CostEstimate(flops=2 * operands[0].size, bytes_accessed=0, transcendentals=0),
        name=name,
    )(*operands)


def shards(count, tokens, norm_gain, gate_weight, up_weight, down_weight, clip_scale):
    chips = count // 2
    order = ring_of(chips)
    steps = chips // 2

    def hop(value, shift_even, shift_odd):
        pairs = []
        for at, c in enumerate(order):
            pairs.append((2 * c, 2 * order[(at + shift_even) % chips]))
            pairs.append((2 * c + 1, 2 * order[(at + shift_odd) % chips] + 1))
        return lax.ppermute(value, "hid", pairs)

    def right(value):
        return hop(value, 1, 1)

    def left(value):
        return hop(value, -1, -1)

    def cross(value, mask=1):
        return lax.ppermute(value, "hid", [(d, d ^ mask) for d in range(count)])

    normed = normalize(tokens, norm_gain)
    width = gate_weight.shape[1]
    wide = max(BLOCK, width // 2)
    wanted = [(weight, at) for at in range(width // wide) for weight in (gate_weight, up_weight)]
    weights = []

    def beside(after, *arrived):
        if len(weights) == len(wanted):
            return arrived
        weight, at = wanted[len(weights)]
        arrived = lax.optimization_barrier((load(weight, after, wide, at), *arrived))
        weights.append(arrived[0])
        return arrived[1:]

    mine, shifts = [normed], [0]
    ahead = behind = normed
    for step in range(1, steps):
        ahead, behind = beside(ahead, right(ahead), left(behind))
        mine += [ahead, behind]
        shifts += [-step, step]
    (far,) = beside(ahead, hop(both(pick_kernel, ahead, behind, "pick"), 1, -1))
    mine.append(far)
    shifts.append(steps)
    while len(weights) < len(wanted):
        (normed,) = beside(normed, normed)
    parts = [block for own in mine for block in (own, cross(own))]
    half_a, half_b = up_project(shifts, parts, weights)
    wide = down_weight.shape[1] // 2
    def butterfly(value, mask):
        return both(functools.partial(turn_kernel, mask), value, cross(value, mask), "turn")

    masks = [1 << bit for bit in range(count.bit_length() - 1)]
    orders = [masks[-1:] + masks[:-1], masks]
    down_weights = []
    for stage in range(len(masks)):
        before = half_a
        half_a = butterfly(half_a, orders[0][stage])
        half_b = butterfly(half_b, orders[1][stage])
        if stage < 2:
            columns = load(down_weight, before, wide, 0, stage == 0)
            columns, half_a, half_b = lax.optimization_barrier((columns, half_a, half_b))
            down_weights.append(columns)
    total = count * gate_weight.shape[1]
    limits = clip_scale.reshape(1, -1)
    theirs = down_project(half_a, half_b, limits, down_weights[:1], chips, total)
    own = down_project(half_a, half_b, limits, down_weights[1:], chips, total)
    arrived = cross(theirs)
    rows, wide = own.shape[0] // chips, own.shape[1]
    part = jax.ShapeDtypeStruct((rows, wide), jnp.bfloat16)

    far = hop(small(functools.partial(far_kernel, steps, chips), part, (own, arrived), "far"), 1, -1)
    for away in range(steps - 1, 0, -1):
        if away == steps - 1:
            body, operands = split_kernel, (far, own, arrived)
        else:
            body, operands = relay_kernel, (ahead, behind, own, arrived)
        ahead, behind = small(functools.partial(body, away, chips), (part, part), operands, "relay")
        ahead, behind = right(ahead), left(behind)
    half = jax.ShapeDtypeStruct((rows // 2, wide), jnp.bfloat16)
    kept = jax.ShapeDtypeStruct((rows // 2, wide), jnp.float32)
    keep, give = small(
        functools.partial(last_kernel, chips),
        (kept, half),
        (ahead, behind, own, arrived),
        "last",
        [pltpu.VMEM((rows, wide), jnp.float32)],
    )
    mixed = jax.ShapeDtypeStruct(tokens.shape, tokens.dtype)
    return small(mix_kernel, mixed, (tokens, keep, cross(give)), "mix")


def solution(mesh):
    in_specs = (
        P(("groups", "hid"), None),
        P(),
        P(None, "hid"),
        P(None, "hid"),
        P("hid", None),
        P("hid"),
    )
    out_specs = P(("groups", "hid"), None)
    body = functools.partial(shards, mesh.shape["hid"])
    return jax.shard_map(body, mesh=mesh, in_specs=in_specs, out_specs=out_specs, check_vma=False)
```

time: 108 us -> 95.2 us (0.88)
  Pallas kernels: 36 us -> 30.6 us
  waiting for transfers between devices: 43.3 us -> 39.4 us
  starting transfers between devices: 24.8 us -> 22.8 us
  other arithmetic: 1.46 us -> 0 us
    ppermute x14, waiting for transfers between devices: 30.8 us -> 19.9 us  [hop(): return lax.ppermute(value, 'hid', pairs)]
    ppermute x18, waiting for transfers between devices: 12.5 us -> 19.5 us  [cross(): return lax.ppermute(value, 'hid', [(d, d ^ mask) for d in range(count)])]
    pallas_call x12 -> x21, Pallas kernels: 27.2 us -> 22.5 us  [the longest x6 20.9 us: load(): pl.pallas_call(functools.partial(load_kernel, flip, at), out_shape=jax.Sh...]
    ppermute x18, starting transfers between devices: 10.9 us -> 8.82 us  [cross(): return lax.ppermute(value, 'hid', [(d, d ^ mask) for d in range(count)])]
    convert_element_type x13 -> x0, other arithmetic: 1.36 us -> none  [the longest x1 0.68 us: shards(): (tokens.astype(jnp.float32) + jnp.concatenate([low, high], axis=1)).astyp...]
  transfers between devices with their start and end apart: 32 -> 32, of which waited for: 18 -> 22; matrix products, arithmetic and copies ran while one was open for 0% -> 0% of each run, Pallas kernels for 27% -> 24%
where the time goes in v3:
time: 95.2 us; the launch traced here: 94.7 us
  waiting for transfers between devices  39.4 us (41%)
  Pallas kernels  30.6 us (32%)
  starting transfers between devices  22.8 us (24%)
  local copies, waits for them, and re-layouts  1.67 us (2%)
    pallas_call x6, Pallas kernels, load(): pl.pallas_call(functools.partial(load_kernel, flip, at), out_shape=jax.Sh...  20.9 us
    ppermute x14, waiting for transfers between devices, hop(): return lax.ppermute(value, 'hid', pairs)  19.9 us
    ppermute x18, waiting for transfers between devices, cross(): return lax.ppermute(value, 'hid', [(d, d ^ mask) for d in range(count)])  19.5 us
    ppermute x14, starting transfers between devices, hop(): return lax.ppermute(value, 'hid', pairs)  14 us
    ppermute x18, starting transfers between devices, cross(): return lax.ppermute(value, 'hid', [(d, d ^ mask) for d in range(count)])  8.82 us
    pallas_call x1, Pallas kernels, up_project(): pl.pallas_call(functools.partial(up_kernel, count, shifts), out_shape=(ha...  5.11 us
    pallas_call x2, Pallas kernels, down_project(): pl.pallas_call(functools.partial(down_kernel, width // BLOCK, chips, tota...  2.87 us
  transfers between devices with their start and end apart: 32, of which 22 were waited for; matrix products, arithmetic and copies ran while one was open for 0% of the time, Pallas kernels for 24%

profile of v3, /device:TPU:0, one launch (start us, length us, event | category | flops | bytes accessed | tf_op | source)
XLA Modules:
  0.0 94.7 jit_solution(1428904987740368618)
XLA Ops:
  0.0 0.9 copy-done
  0.9 0.8 copy-done.2
  1.7 0.2 normalize.1.after_ref.refs_0_
  1.9 3.0 %collective-permute-start.2 = (bf16[8,8192]{1,0:T(8,128)(2,1)S(1)}, bf16[8,8192]{1,0:T(8,128)(2,1)S(1)}, u32[]{:S(2)}, u32[]{:S(2)}) collective-permute-start(bf16[8,8192]{1,0:T(8,128)(2,1)S(1)} %normalize.1.after_ref.refs_0_), channel_id=1, source_target_pairs={{0,2},{1,3},{4,0},{5,1},{8,4},{9,5},{12,8},{13,9},{14,12},{15,13},... | collective-permute-start | bytes 393224 | tf_op jit(solution)/shard_map/ppermute | solution.py:281
  4.9 0.1 collective-permute-start.1
  5.0 3.6 %load.6.refs_16_ = bf16[8192,512]{1,0:T(8,128)(2,1)S(1)} custom-call(bf16[8192,1024]{1,0:T(8,128)(2,1)} %weight_ref.8, bf16[8,8192]{1,0:T(8,128)(2,1)S(1)} %normalize.1.after_ref.refs_0_), custom_call_target="tpu_custom_call" | custom-call | bytes 8388608 | tf_op jit(solution)/shard_map/load/pallas_call | solution.py:70
  8.6 1.3 %collective-permute-done.1.after_ref.refs_2_ = bf16[8,8192]{1,0:T(8,128)(2,1)S(1)} collective-permute-done((bf16[8,8192]{1,0:T(8,128)(2,1)S(1)}, bf16[8,8192]{1,0:T(8,128)(2,1)S(1)}, u32[]{:S(2)}, u32[]{:S(2)}) %collective-permute-start.1) | collective-permute-done | bytes 131104 | tf_op jit(solution)/shard_map/ppermute | solution.py:281
  9.8 1.6 %collective-permute-start.6 = (bf16[8,8192]{1,0:T(8,128)(2,1)S(1)}, bf16[8,8192]{1,0:T(8,128)(2,1)S(1)}, u32[]{:S(2)}, u32[]{:S(2)}) collective-permute-start(bf16[8,8192]{1,0:T(8,128)(2,1)S(1)} %collective-permute-done.2.refs_4_), channel_id=1, source_target_pairs={{0,2},{1,3},{4,0},{5,1},{8,4},{9,5},{12,8},{13,9},{14,12},{15,13},... | collective-permute-start | bytes 393224 | tf_op jit(solution)/shard_map/ppermute | solution.py:281
  11.4 0.4 collective-permute-start.5
  11.9 3.6 %load.7.refs_17_ = bf16[8192,512]{1,0:T(8,128)(2,1)S(1)} custom-call(bf16[8192,1024]{1,0:T(8,128)(2,1)} %weight_ref.9, bf16[8,8192]{1,0:T(8,128)(2,1)S(1)} %collective-permute-done.1.after_ref.refs_2_), custom_call_target="tpu_custom_call" | custom-call | bytes 8388608 | tf_op jit(solution)/shard_map/load/pallas_call | solution.py:70
  15.5 0.9 collective-permute-done.5.after_ref.refs_6_
  16.4 1.6 %collective-permute-start.10 = (bf16[8,8192]{1,0:T(8,128)(2,1)S(1)}, bf16[8,8192]{1,0:T(8,128)(2,1)S(1)}, u32[]{:S(2)}, u32[]{:S(2)}) collective-permute-start(bf16[8,8192]{1,0:T(8,128)(2,1)S(1)} %collective-permute-done.6.refs_8_), channel_id=1, source_target_pairs={{0,2},{1,3},{4,0},{5,1},{8,4},{9,5},{12,8},{13,9},{14,12},{15,13},... | collective-permute-start | bytes 393224 | tf_op jit(solution)/shard_map/ppermute | solution.py:281
  18.0 0.4 collective-permute-start.9
  18.4 3.5 %load.8.refs_18_ = bf16[8192,512]{1,0:T(8,128)(2,1)S(1)} custom-call(bf16[8192,1024]{1,0:T(8,128)(2,1)} %weight_ref.8, bf16[8,8192]{1,0:T(8,128)(2,1)S(1)} %collective-permute-done.5.after_ref.refs_6_), custom_call_target="tpu_custom_call" | custom-call | bytes 8388608 | tf_op jit(solution)/shard_map/load/pallas_call | solution.py:70
  21.9 1.0 %collective-permute-done.9.after_ref.even_ref.refs_10_ = bf16[8,8192]{1,0:T(8,128)(2,1)S(1)} collective-permute-done((bf16[8,8192]{1,0:T(8,128)(2,1)S(1)}, bf16[8,8192]{1,0:T(8,128)(2,1)S(1)}, u32[]{:S(2)}, u32[]{:S(2)}) %collective-permute-start.9) | collective-permute-done | bytes 131104 | tf_op jit(solution)/shard_map/ppermute | solution.py:281
  23.0 0.5 collective-permute-start.13
  23.5 0.5 collective-permute-start.4
  24.0 0.5 collective-permute-start.8
  24.5 3.5 %load.9.refs_19_ = bf16[8192,512]{1,0:T(8,128)(2,1)S(1)} custom-call(bf16[8192,1024]{1,0:T(8,128)(2,1)} %weight_ref.9, bf16[8,8192]{1,0:T(8,128)(2,1)S(1)} %collective-permute-done.9.after_ref.even_ref.refs_10_), custom_call_target="tpu_custom_call" | custom-call | bytes 8388608 | tf_op jit(solution)/shard_map/load/pallas_call | solution.py:70
  28.0 0.1 collective-permute-start.7
  28.1 0.5 collective-permute-start.12
  28.6 0.1 collective-permute-start.11
  28.7 0.4 collective-permute-start.14
  29.1 0.3 collective-permute-done.7.refs_7_
  29.4 0.2 collective-permute-done.12.refs_13_
  29.6 0.3 collective-permute-done.11.refs_11_
  29.9 0.2 collective-permute-done.14.refs_15_
  30.1 5.1 %up_project.1 = (bf16[128,512]{1,0:T(8,128)(2,1)S(1)}, bf16[128,512]{1,0:T(8,128)(2,1)S(1)}) custom-call(bf16[8,8192]{1,0:T(8,128)(2,1)S(1)} %normalize.1.after_ref.refs_0_, bf16[8,8192]{1,0:T(8,128)(2,1)S(1)} %collective-permute-done.refs_1_, bf16[8,8192]{1,0:T(8,128)(2,1)S(1)} %collective-permute-done.1.after_ref.refs_2_, ...), custom_call_target="tpu_custom_call" | custom-call | flops 4294967296 | tf_op jit(solution)/shard_map/up_project/pallas_call | solution.py:125
  35.2 0.4 collective-permute-start.16
  35.6 1.1 %collective-permute-start.15 = (bf16[128,512]{1,0:T(8,128)(2,1)S(1)}, bf16[128,512]{1,0:T(8,128)(2,1)S(1)}, u32[]{:S(2)}, u32[]{:S(2)}) collective-permute-start(bf16[128,512]{1,0:T(8,128)(2,1)S(1)} %get-tuple-element.43.after_ref.value_ref), channel_id=1, source_target_pairs={{0,8},{1,9},{2,10},{3,11},{4,12},{5,13},{6,14},{7,15},{8,0},{9,1},... | collective-permute-start | bytes 393224 | tf_op jit(solution)/shard_map/ppermute | solution.py:290
  36.7 3.4 %load.10.refs_0_ = bf16[1024,4096]{1,0:T(8,128)(2,1)S(1)} custom-call(bf16[1024,8192]{1,0:T(8,128)(2,1)} %weight_ref.11, bf16[128,512]{1,0:T(8,128)(2,1)S(1)} %get-tuple-element.43.after_ref.value_ref), custom_call_target="tpu_custom_call" | custom-call | bytes 8388608 | tf_op jit(solution)/shard_map/load/pallas_call | solution.py:70
  40.2 4.6 %collective-permute-done.15.other_ref = bf16[128,512]{1,0:T(8,128)(2,1)S(1)} collective-permute-done((bf16[128,512]{1,0:T(8,128)(2,1)S(1)}, bf16[128,512]{1,0:T(8,128)(2,1)S(1)}, u32[]{:S(2)}, u32[]{:S(2)}) %collective-permute-start.15) | collective-permute-done | bytes 131104 | tf_op jit(solution)/shard_map/ppermute | solution.py:290
  44.9 1.8 %collective-permute-start.18 = (bf16[128,512]{1,0:T(8,128)(2,1)S(1)}, bf16[128,512]{1,0:T(8,128)(2,1)S(1)}, u32[]{:S(2)}, u32[]{:S(2)}) collective-permute-start(bf16[128,512]{1,0:T(8,128)(2,1)S(1)} %turn.9.value_ref), channel_id=1, source_target_pairs={{0,2},{1,3},{2,0},{3,1},{4,6},{5,7},{6,4},{7,5},{8,10},{9,11},{10,... | collective-permute-start | bytes 393224 | tf_op jit(solution)/shard_map/ppermute | solution.py:290
  46.6 3.4 %load.11.refs_0_ = bf16[1024,4096]{1,0:T(8,128)(2,1)S(1)} custom-call(bf16[1024,8192]{1,0:T(8,128)(2,1)} %weight_ref.11, bf16[128,512]{1,0:T(8,128)(2,1)S(1)} %turn.8.after_ref.value_ref), custom_call_target="tpu_custom_call" | custom-call | bytes 8388608 | tf_op jit(solution)/shard_map/load/pallas_call | solution.py:70
  50.0 0.3 collective-permute-done.18.other_ref
  50.5 1.3 %collective-permute-start.19 = (bf16[128,512]{1,0:T(8,128)(2,1)S(1)}, bf16[128,512]{1,0:T(8,128)(2,1)S(1)}, u32[]{:S(2)}, u32[]{:S(2)}) collective-permute-start(bf16[128,512]{1,0:T(8,128)(2,1)S(1)} %turn.10.value_ref), channel_id=1, source_target_pairs={{0,2},{1,3},{2,0},{3,1},{4,6},{5,7},{6,4},{7,5},{8,10},{9,11},{10,... | collective-permute-start | bytes 393224 | tf_op jit(solution)/shard_map/ppermute | solution.py:290
  51.8 4.4 %collective-permute-done.19.other_ref = bf16[128,512]{1,0:T(8,128)(2,1)S(1)} collective-permute-done((bf16[128,512]{1,0:T(8,128)(2,1)S(1)}, bf16[128,512]{1,0:T(8,128)(2,1)S(1)}, u32[]{:S(2)}, u32[]{:S(2)}) %collective-permute-start.19) | collective-permute-done | bytes 131104 | tf_op jit(solution)/shard_map/ppermute | solution.py:290
  56.2 0.1 collective-permute-start.20
  56.3 0.5 collective-permute-done.21.other_ref
  56.8 2.0 %collective-permute-start.22 = (bf16[128,512]{1,0:T(8,128)(2,1)S(1)}, bf16[128,512]{1,0:T(8,128)(2,1)S(1)}, u32[]{:S(2)}, u32[]{:S(2)}) collective-permute-start(bf16[128,512]{1,0:T(8,128)(2,1)S(1)} %turn.14.value_ref), channel_id=1, source_target_pairs={{0,8},{1,9},{2,10},{3,11},{4,12},{5,13},{6,14},{7,15},{8,0},{9,1},... | collective-permute-start | bytes 393224 | tf_op jit(solution)/shard_map/ppermute | solution.py:290
  58.8 3.8 %collective-permute-done.20.other_ref = bf16[128,512]{1,0:T(8,128)(2,1)S(1)} collective-permute-done((bf16[128,512]{1,0:T(8,128)(2,1)S(1)}, bf16[128,512]{1,0:T(8,128)(2,1)S(1)}, u32[]{:S(2)}, u32[]{:S(2)}) %collective-permute-start.20) | collective-permute-done | bytes 131104 | tf_op jit(solution)/shard_map/ppermute | solution.py:290
  62.7 2.4 %collective-permute-done.22.other_ref = bf16[128,512]{1,0:T(8,128)(2,1)S(1)} collective-permute-done((bf16[128,512]{1,0:T(8,128)(2,1)S(1)}, bf16[128,512]{1,0:T(8,128)(2,1)S(1)}, u32[]{:S(2)}, u32[]{:S(2)}) %collective-permute-start.22) | collective-permute-done | bytes 131104 | tf_op jit(solution)/shard_map/ppermute | solution.py:290
  65.1 1.4 %down_project.3 = bf16[128,4096]{1,0:T(8,128)(2,1)S(1)} custom-call(bf16[128,512]{1,0:T(8,128)(2,1)S(1)} %turn.13.a_ref, bf16[128,512]{1,0:T(8,128)(2,1)S(1)} %turn.15.b_ref, f32[1,1024]{1,0:T(1,128)S(1)} %bitcast.3, bf16[1024,4096]{1,0:T(8,128)(2,1)S(1)} %load.10.refs_0_), custom_call_target="tpu_custom_call" | custom-call | flops 1073741824 | tf_op jit(solution)/shard_map/down_project/pallas_call | solution.py:170
  66.6 0.1 collective-permute-start.23
  66.6 1.4 %down_project.2.own_ref = bf16[128,4096]{1,0:T(8,128)(2,1)S(1)} custom-call(bf16[128,512]{1,0:T(8,128)(2,1)S(1)} %turn.13.a_ref, bf16[128,512]{1,0:T(8,128)(2,1)S(1)} %turn.15.b_ref, f32[1,1024]{1,0:T(1,128)S(1)} %bitcast.4, bf16[1024,4096]{1,0:T(8,128)(2,1)S(1)} %load.11.refs_0_), custom_call_target="tpu_custom_call" | custom-call | flops 1073741824 | tf_op jit(solution)/shard_map/down_project/pallas_call | solution.py:170
  68.1 1.2 %collective-permute-done.23.arrived_ref = bf16[128,4096]{1,0:T(8,128)(2,1)S(1)} collective-permute-done((bf16[128,4096]{1,0:T(8,128)(2,1)S(1)}, bf16[128,4096]{1,0:T(8,128)(2,1)S(1)}, u32[]{:S(2)}, u32[]{:S(2)}) %collective-permute-start.23) | collective-permute-done | bytes 1048608 | tf_op jit(solution)/shard_map/ppermute | solution.py:290
  69.4 5.0 %collective-permute-done.24.far_ref = bf16[16,4096]{1,0:T(8,128)(2,1)S(1)} collective-permute-done((bf16[16,4096]{1,0:T(8,128)(2,1)S(1)}, bf16[16,4096]{1,0:T(8,128)(2,1)S(1)}, u32[]{:S(2)}, u32[]{:S(2)}) %collective-permute-start.24) | collective-permute-done | bytes 131104 | tf_op jit(solution)/shard_map/ppermute | solution.py:281
  74.3 0.1 relay.3
  74.5 2.0 %collective-permute-start.26 = (bf16[16,4096]{1,0:T(8,128)(2,1)S(1)}, bf16[16,4096]{1,0:T(8,128)(2,1)S(1)}, u32[]{:S(2)}, u32[]{:S(2)}) collective-permute-start(bf16[16,4096]{1,0:T(8,128)(2,1)S(1)} %get-tuple-element.52), channel_id=1, source_target_pairs={{0,2},{1,3},{4,0},{5,1},{8,4},{9,5},{12,8},{13,9},{14,12},{15,13},... | collective-permute-start | bytes 393224 | tf_op jit(solution)/shard_map/ppermute | solution.py:281
  76.5 2.9 %collective-permute-done.25.ahead_in = bf16[16,4096]{1,0:T(8,128)(2,1)S(1)} collective-permute-done((bf16[16,4096]{1,0:T(8,128)(2,1)S(1)}, bf16[16,4096]{1,0:T(8,128)(2,1)S(1)}, u32[]{:S(2)}, u32[]{:S(2)}) %collective-permute-start.25) | collective-permute-done | bytes 131104 | tf_op jit(solution)/shard_map/ppermute | solution.py:281
  79.5 0.1 collective-permute-done.26.behind_in
  79.5 0.1 relay.4
  79.6 0.9 collective-permute-start.27
  80.5 1.2 %collective-permute-start.28 = (bf16[16,4096]{1,0:T(8,128)(2,1)S(1)}, bf16[16,4096]{1,0:T(8,128)(2,1)S(1)}, u32[]{:S(2)}, u32[]{:S(2)}) collective-permute-start(bf16[16,4096]{1,0:T(8,128)(2,1)S(1)} %get-tuple-element.54), channel_id=1, source_target_pairs={{0,2},{1,3},{4,0},{5,1},{8,4},{9,5},{12,8},{13,9},{14,12},{15,13},... | collective-permute-start | bytes 393224 | tf_op jit(solution)/shard_map/ppermute | solution.py:281
  81.7 2.9 %collective-permute-done.27.ahead_in = bf16[16,4096]{1,0:T(8,128)(2,1)S(1)} collective-permute-done((bf16[16,4096]{1,0:T(8,128)(2,1)S(1)}, bf16[16,4096]{1,0:T(8,128)(2,1)S(1)}, u32[]{:S(2)}, u32[]{:S(2)}) %collective-permute-start.27) | collective-permute-done | bytes 131104 | tf_op jit(solution)/shard_map/ppermute | solution.py:281
  84.7 0.8 collective-permute-done.28.behind_in
  85.5 0.1 relay.5
  85.6 2.1 %collective-permute-start.29 = (bf16[16,4096]{1,0:T(8,128)(2,1)S(1)}, bf16[16,4096]{1,0:T(8,128)(2,1)S(1)}, u32[]{:S(2)}, u32[]{:S(2)}) collective-permute-start(bf16[16,4096]{1,0:T(8,128)(2,1)S(1)} %get-tuple-element.55), channel_id=1, source_target_pairs={{0,4},{1,5},{4,8},{5,9},{8,12},{9,13},{12,14},{13,15},{14,10},{15,... | collective-permute-start | bytes 393224 | tf_op jit(solution)/shard_map/ppermute | solution.py:281
  87.6 2.9 %collective-permute-done.29.ahead_in = bf16[16,4096]{1,0:T(8,128)(2,1)S(1)} collective-permute-done((bf16[16,4096]{1,0:T(8,128)(2,1)S(1)}, bf16[16,4096]{1,0:T(8,128)(2,1)S(1)}, u32[]{:S(2)}, u32[]{:S(2)}) %collective-permute-start.29) | collective-permute-done | bytes 131104 | tf_op jit(solution)/shard_map/ppermute | solution.py:281
  90.6 2.0 %collective-permute-done.30.behind_in = bf16[16,4096]{1,0:T(8,128)(2,1)S(1)} collective-permute-done((bf16[16,4096]{1,0:T(8,128)(2,1)S(1)}, bf16[16,4096]{1,0:T(8,128)(2,1)S(1)}, u32[]{:S(2)}, u32[]{:S(2)}) %collective-permute-start.30) | collective-permute-done | bytes 131104 | tf_op jit(solution)/shard_map/ppermute | solution.py:281
  92.6 0.1 last.1
  92.7 0.1 collective-permute-start.31
  92.8 1.2 %collective-permute-done.31.take_ref = bf16[8,4096]{1,0:T(8,128)(2,1)S(1)} collective-permute-done((bf16[8,4096]{1,0:T(8,128)(2,1)S(1)}, bf16[8,4096]{1,0:T(8,128)(2,1)S(1)}, u32[]{:S(2)}, u32[]{:S(2)}) %collective-permute-start.31) | collective-permute-done | bytes 65568 | tf_op jit(solution)/shard_map/ppermute | solution.py:290
  94.0 0.7 mix.1
  (33 shorter events, 0.6 us)
Async XLA Ops:
  0.0 0.9 copy-start
  0.9 0.8 copy-start.2
  1.9 6.7 %collective-permute-start.2 = (bf16[8,8192]{1,0:T(8,128)(2,1)S(1)}, bf16[8,8192]{1,0:T(8,128)(2,1)S(1)}, u32[]{:S(2)}, u32[]{:S(2)}) collective-permute-start(bf16[8,8192]{1,0:T(8,128)(2,1)S(1)} %normalize.1.after_ref.refs_0_), channel_id=1, source_target_pairs={{0,2},{1,3},{4,0},{5,1},{8,4},{9,5},{12,8},{13,9},{14,12},{15,13},... | collective-permute-start | bytes 393224 | tf_op jit(solution)/shard_map/ppermute | solution.py:281
  4.9 5.0 %collective-permute-start.1 = (bf16[8,8192]{1,0:T(8,128)(2,1)S(1)}, bf16[8,8192]{1,0:T(8,128)(2,1)S(1)}, u32[]{:S(2)}, u32[]{:S(2)}) collective-permute-start(bf16[8,8192]{1,0:T(8,128)(2,1)S(1)} %normalize.1.after_ref.refs_0_), channel_id=1, source_target_pairs={{0,4},{1,5},{4,8},{5,9},{8,12},{9,13},{12,14},{13,15},{14,10},{15,... | collective-permute-start | bytes 393224 | tf_op jit(solution)/shard_map/ppermute | solution.py:281
  9.8 5.6 %collective-permute-start.6 = (bf16[8,8192]{1,0:T(8,128)(2,1)S(1)}, bf16[8,8192]{1,0:T(8,128)(2,1)S(1)}, u32[]{:S(2)}, u32[]{:S(2)}) collective-permute-start(bf16[8,8192]{1,0:T(8,128)(2,1)S(1)} %collective-permute-done.2.refs_4_), channel_id=1, source_target_pairs={{0,2},{1,3},{4,0},{5,1},{8,4},{9,5},{12,8},{13,9},{14,12},{15,13},... | collective-permute-start | bytes 393224 | tf_op jit(solution)/shard_map/ppermute | solution.py:281
  11.4 5.0 %collective-permute-start.5 = (bf16[8,8192]{1,0:T(8,128)(2,1)S(1)}, bf16[8,8192]{1,0:T(8,128)(2,1)S(1)}, u32[]{:S(2)}, u32[]{:S(2)}) collective-permute-start(bf16[8,8192]{1,0:T(8,128)(2,1)S(1)} %collective-permute-done.1.after_ref.refs_2_), channel_id=1, source_target_pairs={{0,4},{1,5},{4,8},{5,9},{8,12},{9,13},{12,14},{13,15},{14,10},{15,... | collective-permute-start | bytes 393224 | tf_op jit(solution)/shard_map/ppermute | solution.py:281
  16.4 5.5 %collective-permute-start.10 = (bf16[8,8192]{1,0:T(8,128)(2,1)S(1)}, bf16[8,8192]{1,0:T(8,128)(2,1)S(1)}, u32[]{:S(2)}, u32[]{:S(2)}) collective-permute-start(bf16[8,8192]{1,0:T(8,128)(2,1)S(1)} %collective-permute-done.6.refs_8_), channel_id=1, source_target_pairs={{0,2},{1,3},{4,0},{5,1},{8,4},{9,5},{12,8},{13,9},{14,12},{15,13},... | collective-permute-start | bytes 393224 | tf_op jit(solution)/shard_map/ppermute | solution.py:281
  18.0 5.0 %collective-permute-start.9 = (bf16[8,8192]{1,0:T(8,128)(2,1)S(1)}, bf16[8,8192]{1,0:T(8,128)(2,1)S(1)}, u32[]{:S(2)}, u32[]{:S(2)}) collective-permute-start(bf16[8,8192]{1,0:T(8,128)(2,1)S(1)} %collective-permute-done.5.after_ref.refs_6_), channel_id=1, source_target_pairs={{0,4},{1,5},{4,8},{5,9},{8,12},{9,13},{12,14},{13,15},{14,10},{15,... | collective-permute-start | bytes 393224 | tf_op jit(solution)/shard_map/ppermute | solution.py:281
  23.0 5.0 %collective-permute-start.13 = (bf16[8,8192]{1,0:T(8,128)(2,1)S(1)}, bf16[8,8192]{1,0:T(8,128)(2,1)S(1)}, u32[]{:S(2)}, u32[]{:S(2)}) collective-permute-start(bf16[8,8192]{1,0:T(8,128)(2,1)S(1)} %pick.1), channel_id=1, source_target_pairs={{0,4},{1,3},{4,8},{5,1},{8,12},{9,5},{12,14},{13,9},{14,10},{15,13... | collective-permute-start | bytes 393224 | tf_op jit(solution)/shard_map/ppermute | solution.py:281
  23.5 4.6 %collective-permute-start = (bf16[8,8192]{1,0:T(8,128)(2,1)S(1)}, bf16[8,8192]{1,0:T(8,128)(2,1)S(1)}, u32[]{:S(2)}, u32[]{:S(2)}) collective-permute-start(bf16[8,8192]{1,0:T(8,128)(2,1)S(1)} %normalize.1.after_ref.refs_0_), channel_id=1, source_target_pairs={{0,1},{1,0},{2,3},{3,2},{4,5},{5,4},{6,7},{7,6},{8,9},{9,8},{10,11... | collective-permute-start | bytes 393224 | tf_op jit(solution)/shard_map/ppermute | solution.py:290
  23.5 5.1 %collective-permute-start.4 = (bf16[8,8192]{1,0:T(8,128)(2,1)S(1)}, bf16[8,8192]{1,0:T(8,128)(2,1)S(1)}, u32[]{:S(2)}, u32[]{:S(2)}) collective-permute-start(bf16[8,8192]{1,0:T(8,128)(2,1)S(1)} %collective-permute-done.2.refs_4_), channel_id=1, source_target_pairs={{0,1},{1,0},{2,3},{3,2},{4,5},{5,4},{6,7},{7,6},{8,9},{9,8},{10,11... | collective-permute-start | bytes 393224 | tf_op jit(solution)/shard_map/ppermute | solution.py:290
  24.0 4.7 %collective-permute-start.3 = (bf16[8,8192]{1,0:T(8,128)(2,1)S(1)}, bf16[8,8192]{1,0:T(8,128)(2,1)S(1)}, u32[]{:S(2)}, u32[]{:S(2)}) collective-permute-start(bf16[8,8192]{1,0:T(8,128)(2,1)S(1)} %collective-permute-done.1.after_ref.refs_2_), channel_id=1, source_target_pairs={{0,1},{1,0},{2,3},{3,2},{4,5},{5,4},{6,7},{7,6},{8,9},{9,8},{10,11... | collective-permute-start | bytes 393224 | tf_op jit(solution)/shard_map/ppermute | solution.py:290
  24.0 5.1 %collective-permute-start.8 = (bf16[8,8192]{1,0:T(8,128)(2,1)S(1)}, bf16[8,8192]{1,0:T(8,128)(2,1)S(1)}, u32[]{:S(2)}, u32[]{:S(2)}) collective-permute-start(bf16[8,8192]{1,0:T(8,128)(2,1)S(1)} %collective-permute-done.6.refs_8_), channel_id=1, source_target_pairs={{0,1},{1,0},{2,3},{3,2},{4,5},{5,4},{6,7},{7,6},{8,9},{9,8},{10,11... | collective-permute-start | bytes 393224 | tf_op jit(solution)/shard_map/ppermute | solution.py:290
  28.0 1.4 %collective-permute-start.7 = (bf16[8,8192]{1,0:T(8,128)(2,1)S(1)}, bf16[8,8192]{1,0:T(8,128)(2,1)S(1)}, u32[]{:S(2)}, u32[]{:S(2)}) collective-permute-start(bf16[8,8192]{1,0:T(8,128)(2,1)S(1)} %collective-permute-done.5.after_ref.refs_6_), channel_id=1, source_target_pairs={{0,1},{1,0},{2,3},{3,2},{4,5},{5,4},{6,7},{7,6},{8,9},{9,8},{10,11... | collective-permute-start | bytes 393224 | tf_op jit(solution)/shard_map/ppermute | solution.py:290
  28.1 1.5 %collective-permute-start.12 = (bf16[8,8192]{1,0:T(8,128)(2,1)S(1)}, bf16[8,8192]{1,0:T(8,128)(2,1)S(1)}, u32[]{:S(2)}, u32[]{:S(2)}) collective-permute-start(bf16[8,8192]{1,0:T(8,128)(2,1)S(1)} %collective-permute-done.10.odd_ref.refs_12_), channel_id=1, source_target_pairs={{0,1},{1,0},{2,3},{3,2},{4,5},{5,4},{6,7},{7,6},{8,9},{9,8},{10,11... | collective-permute-start | bytes 393224 | tf_op jit(solution)/shard_map/ppermute | solution.py:290
  28.6 1.3 %collective-permute-start.11 = (bf16[8,8192]{1,0:T(8,128)(2,1)S(1)}, bf16[8,8192]{1,0:T(8,128)(2,1)S(1)}, u32[]{:S(2)}, u32[]{:S(2)}) collective-permute-start(bf16[8,8192]{1,0:T(8,128)(2,1)S(1)} %collective-permute-done.9.after_ref.even_ref.refs_10_), channel_id=1, source_target_pairs={{0,1},{1,0},{2,3},{3,2},{4,5},{5,4},{6,7},{7,6},{8,9},{9,8},{10,11... | collective-permute-start | bytes 393224 | tf_op jit(solution)/shard_map/ppermute | solution.py:290
  28.7 1.4 %collective-permute-start.14 = (bf16[8,8192]{1,0:T(8,128)(2,1)S(1)}, bf16[8,8192]{1,0:T(8,128)(2,1)S(1)}, u32[]{:S(2)}, u32[]{:S(2)}) collective-permute-start(bf16[8,8192]{1,0:T(8,128)(2,1)S(1)} %collective-permute-done.13.refs_14_), channel_id=1, source_target_pairs={{0,1},{1,0},{2,3},{3,2},{4,5},{5,4},{6,7},{7,6},{8,9},{9,8},{10,11... | collective-permute-start | bytes 393224 | tf_op jit(solution)/shard_map/ppermute | solution.py:290
  35.2 4.9 %collective-permute-start.16 = (bf16[128,512]{1,0:T(8,128)(2,1)S(1)}, bf16[128,512]{1,0:T(8,128)(2,1)S(1)}, u32[]{:S(2)}, u32[]{:S(2)}) collective-permute-start(bf16[128,512]{1,0:T(8,128)(2,1)S(1)} %get-tuple-element.44.value_ref), channel_id=1, source_target_pairs={{0,1},{1,0},{2,3},{3,2},{4,5},{5,4},{6,7},{7,6},{8,9},{9,8},{10,11... | collective-permute-start | bytes 393224 | tf_op jit(solution)/shard_map/ppermute | solution.py:290
  35.6 9.2 %collective-permute-start.15 = (bf16[128,512]{1,0:T(8,128)(2,1)S(1)}, bf16[128,512]{1,0:T(8,128)(2,1)S(1)}, u32[]{:S(2)}, u32[]{:S(2)}) collective-permute-start(bf16[128,512]{1,0:T(8,128)(2,1)S(1)} %get-tuple-element.43.after_ref.value_ref), channel_id=1, source_target_pairs={{0,8},{1,9},{2,10},{3,11},{4,12},{5,13},{6,14},{7,15},{8,0},{9,1},... | collective-permute-start | bytes 393224 | tf_op jit(solution)/shard_map/ppermute | solution.py:290
  44.9 20.2 %copy-start.3 = (f32[1024]{0:T(1024)S(1)}, f32[1024]{0:T(1024)}, u32[]{:S(2)}) copy-start(f32[1024]{0:T(1024)} %param.11) | copy-start | bytes 12292
  44.9 5.5 %collective-permute-start.18 = (bf16[128,512]{1,0:T(8,128)(2,1)S(1)}, bf16[128,512]{1,0:T(8,128)(2,1)S(1)}, u32[]{:S(2)}, u32[]{:S(2)}) collective-permute-start(bf16[128,512]{1,0:T(8,128)(2,1)S(1)} %turn.9.value_ref), channel_id=1, source_target_pairs={{0,2},{1,3},{2,0},{3,1},{4,6},{5,7},{6,4},{7,5},{8,10},{9,11},{10,... | collective-permute-start | bytes 393224 | tf_op jit(solution)/shard_map/ppermute | solution.py:290
  46.6 3.8 %collective-permute-start.17 = (bf16[128,512]{1,0:T(8,128)(2,1)S(1)}, bf16[128,512]{1,0:T(8,128)(2,1)S(1)}, u32[]{:S(2)}, u32[]{:S(2)}) collective-permute-start(bf16[128,512]{1,0:T(8,128)(2,1)S(1)} %turn.8.after_ref.value_ref), channel_id=1, source_target_pairs={{0,1},{1,0},{2,3},{3,2},{4,5},{5,4},{6,7},{7,6},{8,9},{9,8},{10,11... | collective-permute-start | bytes 393224 | tf_op jit(solution)/shard_map/ppermute | solution.py:290
  50.5 5.6 %collective-permute-start.19 = (bf16[128,512]{1,0:T(8,128)(2,1)S(1)}, bf16[128,512]{1,0:T(8,128)(2,1)S(1)}, u32[]{:S(2)}, u32[]{:S(2)}) collective-permute-start(bf16[128,512]{1,0:T(8,128)(2,1)S(1)} %turn.10.value_ref), channel_id=1, source_target_pairs={{0,2},{1,3},{2,0},{3,1},{4,6},{5,7},{6,4},{7,5},{8,10},{9,11},{10,... | collective-permute-start | bytes 393224 | tf_op jit(solution)/shard_map/ppermute | solution.py:290
  51.8 5.0 %collective-permute-start.21 = (bf16[128,512]{1,0:T(8,128)(2,1)S(1)}, bf16[128,512]{1,0:T(8,128)(2,1)S(1)}, u32[]{:S(2)}, u32[]{:S(2)}) collective-permute-start(bf16[128,512]{1,0:T(8,128)(2,1)S(1)} %turn.11.value_ref), channel_id=1, source_target_pairs={{0,4},{1,5},{2,6},{3,7},{4,0},{5,1},{6,2},{7,3},{8,12},{9,13},{10,... | collective-permute-start | bytes 393224 | tf_op jit(solution)/shard_map/ppermute | solution.py:290
  56.2 6.4 %collective-permute-start.20 = (bf16[128,512]{1,0:T(8,128)(2,1)S(1)}, bf16[128,512]{1,0:T(8,128)(2,1)S(1)}, u32[]{:S(2)}, u32[]{:S(2)}) collective-permute-start(bf16[128,512]{1,0:T(8,128)(2,1)S(1)} %turn.12.value_ref), channel_id=1, source_target_pairs={{0,4},{1,5},{2,6},{3,7},{4,0},{5,1},{6,2},{7,3},{8,12},{9,13},{10,... | collective-permute-start | bytes 393224 | tf_op jit(solution)/shard_map/ppermute | solution.py:290
  56.8 8.3 %collective-permute-start.22 = (bf16[128,512]{1,0:T(8,128)(2,1)S(1)}, bf16[128,512]{1,0:T(8,128)(2,1)S(1)}, u32[]{:S(2)}, u32[]{:S(2)}) collective-permute-start(bf16[128,512]{1,0:T(8,128)(2,1)S(1)} %turn.14.value_ref), channel_id=1, source_target_pairs={{0,8},{1,9},{2,10},{3,11},{4,12},{5,13},{6,14},{7,15},{8,0},{9,1},... | collective-permute-start | bytes 393224 | tf_op jit(solution)/shard_map/ppermute | solution.py:290
  66.6 27.5 %copy-start.1 = (bf16[8,8192]{1,0:T(8,128)(2,1)S(1)}, bf16[8,8192]{1,0:T(8,128)(2,1)}, u32[]{:S(2)}) copy-start(bf16[8,8192]{1,0:T(8,128)(2,1)} %tokens_ref.1) | copy-start | bytes 393220
  66.6 2.7 %collective-permute-start.23 = (bf16[128,4096]{1,0:T(8,128)(2,1)S(1)}, bf16[128,4096]{1,0:T(8,128)(2,1)S(1)}, u32[]{:S(2)}, u32[]{:S(2)}) collective-permute-start(bf16[128,4096]{1,0:T(8,128)(2,1)S(1)} %down_project.3), channel_id=1, source_target_pairs={{0,1},{1,0},{2,3},{3,2},{4,5},{5,4},{6,7},{7,6},{8,9},{9,8},{10,11... | collective-permute-start | bytes 3145736 | tf_op jit(solution)/shard_map/ppermute | solution.py:290
  69.3 5.0 %collective-permute-start.24 = (bf16[16,4096]{1,0:T(8,128)(2,1)S(1)}, bf16[16,4096]{1,0:T(8,128)(2,1)S(1)}, u32[]{:S(2)}, u32[]{:S(2)}) collective-permute-start(bf16[16,4096]{1,0:T(8,128)(2,1)S(1)} %far.1), channel_id=1, source_target_pairs={{0,4},{1,3},{4,8},{5,1},{8,12},{9,5},{12,14},{13,9},{14,10},{15,13... | collective-permute-start | bytes 393224 | tf_op jit(solution)/shard_map/ppermute | solution.py:281
  74.5 5.0 %collective-permute-start.25 = (bf16[16,4096]{1,0:T(8,128)(2,1)S(1)}, bf16[16,4096]{1,0:T(8,128)(2,1)S(1)}, u32[]{:S(2)}, u32[]{:S(2)}) collective-permute-start(bf16[16,4096]{1,0:T(8,128)(2,1)S(1)} %get-tuple-element.51), channel_id=1, source_target_pairs={{0,4},{1,5},{4,8},{5,9},{8,12},{9,13},{12,14},{13,15},{14,10},{15,... | collective-permute-start | bytes 393224 | tf_op jit(solution)/shard_map/ppermute | solution.py:281
  74.5 5.0 %collective-permute-start.26 = (bf16[16,4096]{1,0:T(8,128)(2,1)S(1)}, bf16[16,4096]{1,0:T(8,128)(2,1)S(1)}, u32[]{:S(2)}, u32[]{:S(2)}) collective-permute-start(bf16[16,4096]{1,0:T(8,128)(2,1)S(1)} %get-tuple-element.52), channel_id=1, source_target_pairs={{0,2},{1,3},{4,0},{5,1},{8,4},{9,5},{12,8},{13,9},{14,12},{15,13},... | collective-permute-start | bytes 393224 | tf_op jit(solution)/shard_map/ppermute | solution.py:281
  79.6 5.0 %collective-permute-start.27 = (bf16[16,4096]{1,0:T(8,128)(2,1)S(1)}, bf16[16,4096]{1,0:T(8,128)(2,1)S(1)}, u32[]{:S(2)}, u32[]{:S(2)}) collective-permute-start(bf16[16,4096]{1,0:T(8,128)(2,1)S(1)} %get-tuple-element.53), channel_id=1, source_target_pairs={{0,4},{1,5},{4,8},{5,9},{8,12},{9,13},{12,14},{13,15},{14,10},{15,... | collective-permute-start | bytes 393224 | tf_op jit(solution)/shard_map/ppermute | solution.py:281
  80.5 5.0 %collective-permute-start.28 = (bf16[16,4096]{1,0:T(8,128)(2,1)S(1)}, bf16[16,4096]{1,0:T(8,128)(2,1)S(1)}, u32[]{:S(2)}, u32[]{:S(2)}) collective-permute-start(bf16[16,4096]{1,0:T(8,128)(2,1)S(1)} %get-tuple-element.54), channel_id=1, source_target_pairs={{0,2},{1,3},{4,0},{5,1},{8,4},{9,5},{12,8},{13,9},{14,12},{15,13},... | collective-permute-start | bytes 393224 | tf_op jit(solution)/shard_map/ppermute | solution.py:281
  85.6 5.0 %collective-permute-start.29 = (bf16[16,4096]{1,0:T(8,128)(2,1)S(1)}, bf16[16,4096]{1,0:T(8,128)(2,1)S(1)}, u32[]{:S(2)}, u32[]{:S(2)}) collective-permute-start(bf16[16,4096]{1,0:T(8,128)(2,1)S(1)} %get-tuple-element.55), channel_id=1, source_target_pairs={{0,4},{1,5},{4,8},{5,9},{8,12},{9,13},{12,14},{13,15},{14,10},{15,... | collective-permute-start | bytes 393224 | tf_op jit(solution)/shard_map/ppermute | solution.py:281
  87.6 5.0 %collective-permute-start.30 = (bf16[16,4096]{1,0:T(8,128)(2,1)S(1)}, bf16[16,4096]{1,0:T(8,128)(2,1)S(1)}, u32[]{:S(2)}, u32[]{:S(2)}) collective-permute-start(bf16[16,4096]{1,0:T(8,128)(2,1)S(1)} %get-tuple-element.56), channel_id=1, source_target_pairs={{0,2},{1,3},{4,0},{5,1},{8,4},{9,5},{12,8},{13,9},{14,12},{15,13},... | collective-permute-start | bytes 393224 | tf_op jit(solution)/shard_map/ppermute | solution.py:281
  92.7 1.3 %collective-permute-start.31 = (bf16[8,4096]{1,0:T(8,128)(2,1)S(1)}, bf16[8,4096]{1,0:T(8,128)(2,1)S(1)}, u32[]{:S(2)}, u32[]{:S(2)}) collective-permute-start(bf16[8,4096]{1,0:T(8,128)(2,1)S(1)} %get-tuple-element.58), channel_id=1, source_target_pairs={{0,1},{1,0},{2,3},{3,2},{4,5},{5,4},{6,7},{7,6},{8,9},{9,8},{10,11... | collective-permute-start | bytes 196616 | tf_op jit(solution)/shard_map/ppermute | solution.py:290

commit v4 on v3

--- a/solution.py
+++ b/solution.py
@@ -21,23 +21,41 @@
     return jnp.where(parity % 2 == 0, 1.0, -1.0).astype(jnp.bfloat16)
 
 
-def normalize_kernel(rows_ref, gain_ref, out_ref):
+def normalize_kernel(rows_hbm, gain_hbm, out_ref, rows_ref, gain_ref, sems):
+    copies = [
+        pltpu.make_async_copy(rows_hbm, rows_ref, sems.at[0]),
+        pltpu.make_async_copy(gain_hbm, gain_ref, sems.at[1]),
+    ]
+    for copy in copies:
+        copy.start()
+    for copy in copies:
+        copy.wait()
     values = rows_ref[...].astype(jnp.float32)
     inverse = lax.rsqrt(jnp.mean(values * values, axis=-1, keepdims=True) + 1e-05)
     out_ref[...] = (values * inverse * gain_ref[...]).astype(jnp.bfloat16)
 
 
+def in_hbm(value):
+    return pltpu.with_memory_space_constraint(value, pltpu.HBM)
+
+
 def normalize(rows_in, norm_gain):
-    vmem = pl.BlockSpec(memory_space=pltpu.VMEM)
+    hbm = pl.BlockSpec(memory_space=pltpu.HBM)
+    gain = norm_gain.reshape(1, -1)
     return pl.pallas_call(
         normalize_kernel,
         out_shape=jax.ShapeDtypeStruct(rows_in.shape, jnp.bfloat16),
-        in_specs=[vmem, vmem],
-        out_specs=vmem,
+        in_specs=[hbm, hbm],
+        out_specs=pl.BlockSpec(memory_space=pltpu.VMEM),
+        scratch_shapes=[
+            pltpu.VMEM(rows_in.shape, rows_in.dtype),
+            pltpu.VMEM(gain.shape, gain.dtype),
+            pltpu.SemaphoreType.DMA((2,)),
+        ],
         compiler_params=pltpu.CompilerParams(vmem_limit_bytes=4 * MIB),
         cost_estimate=pl.CostEstimate(flops=8 * rows_in.size, bytes_accessed=4 * rows_in.size, transcendentals=0),
         name="normalize",
-    )(rows_in, norm_gain.reshape(1, -1))
+    )(in_hbm(rows_in), in_hbm(gain))
 
 
 def ring_of(chips):
@@ -50,25 +68,24 @@
     return jnp.where(spot < (chips + 1) // 2, 2 * spot, 2 * (chips - spot) - 1)
 
 
-def load_kernel(flip, at, weight_ref, after_ref, out_ref, sem):
+def once(value, *others):
+    return lax.optimization_barrier((value, *others))[0]
+
+
+def load_kernel(at, weight_ref, after_ref, out_ref, sem):
     cols = out_ref.shape[1]
-    wide = weight_ref.shape[1]
-    start = at * cols
-    if flip is not None:
-        side = lax.axis_index("hid") % 2
-        side = 1 - side if flip else side
-        start = start + side * (wide // 2)
-        start = pl.multiple_of(start, cols)
+    at = lax.axis_index("hid") % 2 if at is None else at
+    start = pl.multiple_of(at * cols, cols)
     copy = pltpu.make_async_copy(weight_ref.at[:, pl.ds(start, cols)], out_ref, sem)
     copy.start()
     copy.wait()
 
 
-def load(weight, after, cols, at, flip=None):
+def load(weight, after, cols, at):
     rows = weight.shape[0]
     hbm = pl.BlockSpec(memory_space=pltpu.HBM)
     return pl.pallas_call(
-        functools.partial(load_kernel, flip, at),
+        functools.partial(load_kernel, at),
         out_shape=jax.ShapeDtypeStruct((rows, cols), weight.dtype),
         in_specs=[hbm, hbm],
         out_specs=pl.BlockSpec(memory_space=pltpu.VMEM),
@@ -76,7 +93,7 @@
         compiler_params=pltpu.CompilerParams(vmem_limit_bytes=1 * MIB),
         cost_estimate=pl.CostEstimate(flops=0, bytes_accessed=2 * rows * cols, transcendentals=0),
         name="load",
-    )(pltpu.with_memory_space_constraint(weight, pltpu.HBM), after)
+    )(in_hbm(weight), after)
 
 
 def up_kernel(count, shifts, *refs):
@@ -86,8 +103,12 @@
     for shift in shifts:
         there = 2 * ring_place(chip, shift, count // 2)
         spots += [there + core, there + 1 - core]
-    parts, (out_a, out_b, rows_ref, hidden_ref) = refs[:count], refs[-4:]
-    gates, ups = refs[count:-4:2], refs[count + 1 : -4 : 2]
+    parts, (down_hbm, out_a, out_b, down_ref, rows_ref, hidden_ref, sem) = refs[:count], refs[-7:]
+    gates, ups = refs[count:-7:2], refs[count + 1 : -7 : 2]
+    cols = down_ref.shape[1]
+    start = pl.multiple_of((1 - core) * cols, cols)
+    fetch = pltpu.make_async_copy(down_hbm.at[:, pl.ds(start, cols)], down_ref, sem)
+    fetch.start()
     own = parts[0].shape[0]
     for pair in range(count // 2):
         both = [parts[2 * pair + k][...].astype(jnp.float32) for k in range(2)]
@@ -113,29 +134,35 @@
     half = out_a.shape[1]
     out_a[...] = hidden_ref[:, :half].astype(jnp.bfloat16)
     out_b[...] = hidden_ref[:, half:].astype(jnp.bfloat16)
-
-
-def up_project(shifts, parts, weights):
+    fetch.wait()
+
+
+def up_project(shifts, parts, weights, down_weight):
     count, own = len(parts), parts[0].shape[0]
     depth = weights[0].shape[0]
     width = weights[0].shape[1] * len(weights) // 2
     rows = count * own
     half = jax.ShapeDtypeStruct((rows, width // 2), jnp.bfloat16)
+    down = jax.ShapeDtypeStruct((down_weight.shape[0], down_weight.shape[1] // 2), down_weight.dtype)
     vmem = pl.BlockSpec(memory_space=pltpu.VMEM)
     return pl.pallas_call(
         functools.partial(up_kernel, count, shifts),
-        out_shape=(half, half),
-        in_specs=[vmem] * (count + len(weights)),
-        out_specs=(vmem, vmem),
-        scratch_shapes=[pltpu.VMEM((rows, depth), jnp.bfloat16), pltpu.VMEM((rows, width), jnp.float32)],
-        compiler_params=pltpu.CompilerParams(vmem_limit_bytes=12 * MIB),
+        out_shape=[half, half] + [down],
+        in_specs=[vmem] * (count + len(weights)) + [pl.BlockSpec(memory_space=pltpu.HBM)],
+        out_specs=[vmem] * 3,
+        scratch_shapes=[
+            pltpu.VMEM((rows, depth), jnp.bfloat16),
+            pltpu.VMEM((rows, width), jnp.float32),
+            pltpu.SemaphoreType.DMA,
+        ],
+        compiler_params=pltpu.CompilerParams(vmem_limit_bytes=6 * MIB),
         cost_estimate=pl.CostEstimate(flops=4 * rows * depth * width, bytes_accessed=0, transcendentals=rows * width),
         name="up_project",
-    )(*parts, *weights)
-
-
-def down_kernel(blocks, chips, scale, a_ref, b_ref, clip_ref, *refs):
-    weights, (out_ref, rows_ref, mixed_ref) = refs[:-3], refs[-3:]
+    )(*parts, *weights, in_hbm(down_weight))
+
+
+def down_kernel(blocks, chips, scale, a_ref, b_ref, clip_ref, weight_ref, *refs):
+    outs, (rows_ref, mixed_ref) = refs[:-2], refs[-2:]
     half = a_ref.shape[1]
     rows_ref[:, :half] = a_ref[...].astype(jnp.float32)
     rows_ref[:, half:] = b_ref[...].astype(jnp.float32)
@@ -154,29 +181,32 @@
     each = rows // chips
     me = lax.axis_index("hid")
     for chip in range(chips):
-        spot = pl.multiple_of(ring_place(me // 2, chip, chips) * each, each)
+        spot = pl.multiple_of(ring_place(me // 2, chip + chips // 2, chips) * each, each)
         mixed_ref[chip * each : (chip + 1) * each, :] = rows_ref[pl.ds(spot, each), :].astype(jnp.bfloat16)
-    step = weights[0].shape[1]
-    for at, weight_ref in enumerate(weights):
-        product = jnp.dot(mixed_ref[...], weight_ref[...], preferred_element_type=jnp.float32)
-        out_ref[:, at * step : (at + 1) * step] = product.astype(jnp.bfloat16)
-
-
-def down_project(a, b, clip_scale, weights, chips, total):
+    product = jnp.dot(mixed_ref[...], weight_ref[...], preferred_element_type=jnp.float32)
+    first = 0
+    for out_ref in outs:
+        out_ref[...] = product[first : first + out_ref.shape[0]].astype(jnp.bfloat16)
+        first += out_ref.shape[0]
+
+
+def down_project(a, b, clip_scale, weight, chips, total):
     rows = a.shape[0]
-    width = 2 * a.shape[1]
-    depth = len(weights) * weights[0].shape[1]
+    width, depth = weight.shape
     vmem = pl.BlockSpec(memory_space=pltpu.VMEM)
+    outs = [
+        jax.ShapeDtypeStruct((count, depth), jnp.bfloat16) for count in (rows // chips, rows - rows // chips)
+    ]
     return pl.pallas_call(
         functools.partial(down_kernel, width // BLOCK, chips, total**-0.5),
-        out_shape=jax.ShapeDtypeStruct((rows, depth), jnp.bfloat16),
-        in_specs=[vmem, vmem, vmem] + [vmem] * len(weights),
-        out_specs=vmem,
+        out_shape=outs,
+        in_specs=[vmem] * 4,
+        out_specs=[vmem] * 2,
         scratch_shapes=[pltpu.VMEM((rows, width), jnp.float32), pltpu.VMEM((rows, width), jnp.bfloat16)],
         compiler_params=pltpu.CompilerParams(vmem_limit_bytes=8 * MIB),
         cost_estimate=pl.CostEstimate(flops=2 * rows * depth * width, bytes_accessed=0, transcendentals=0),
         name="down_project",
-    )(a, b, clip_scale, *weights)
+    )(a, b, clip_scale, weight)
 
 
 def pick_kernel(even_ref, odd_ref, out_ref):
@@ -210,29 +240,21 @@
 
 
 def chunk(away, chips, own_ref, arrived_ref):
-    rows = own_ref.shape[0] // chips
-    at = slice(away % chips * rows, (away % chips + 1) * rows)
+    rows = own_ref.shape[0] // (chips - 1)
+    spot = (away + chips // 2 - 1) % chips
+    at = slice(spot * rows, (spot + 1) * rows)
     return own_ref[at, :].astype(jnp.float32) + arrived_ref[at, :].astype(jnp.float32)
 
 
-def far_kernel(away, chips, own_ref, arrived_ref, out_ref):
-    out_ref[...] = chunk(away, chips, own_ref, arrived_ref).astype(jnp.bfloat16)
-
-
-def split_kernel(away, chips, far_ref, own_ref, arrived_ref, ahead_ref, behind_ref):
-    ahead = chunk(away, chips, own_ref, arrived_ref)
-    behind = chunk(-away, chips, own_ref, arrived_ref)
-    core = lax.axis_index("hid") % 2
-    far = far_ref[...].astype(jnp.float32)
-    ahead_ref[...] = (ahead + jnp.where(core == 0, far, 0.0)).astype(jnp.bfloat16)
-    behind_ref[...] = (behind + jnp.where(core == 0, 0.0, far)).astype(jnp.bfloat16)
-
-
-def relay_kernel(away, chips, ahead_in, behind_in, own_ref, arrived_ref, ahead_ref, behind_ref):
-    ahead = chunk(away, chips, own_ref, arrived_ref) + ahead_in[...].astype(jnp.float32)
-    behind = chunk(-away, chips, own_ref, arrived_ref) + behind_in[...].astype(jnp.float32)
-    ahead_ref[...] = ahead.astype(jnp.bfloat16)
-    behind_ref[...] = behind.astype(jnp.bfloat16)
+def sum_kernel(one_ref, two_ref, out_ref):
+    out_ref[...] = (one_ref[...].astype(jnp.float32) + two_ref[...].astype(jnp.float32)).astype(jnp.bfloat16)
+
+
+def relay_kernel(away, chips, core, arrived_in, own_ref, arrived_ref, out_ref):
+    value = arrived_in[...].astype(jnp.float32)
+    if core is not None:
+        value = jnp.where(lax.axis_index("hid") % 2 == core, value, 0.0)
+    out_ref[...] = (chunk(away, chips, own_ref, arrived_ref) + value).astype(jnp.bfloat16)
 
 
 def last_kernel(chips, ahead_in, behind_in, own_ref, arrived_ref, keep_ref, give_ref, sum_ref):
@@ -295,57 +317,64 @@
     wanted = [(weight, at) for at in range(width // wide) for weight in (gate_weight, up_weight)]
     weights = []
 
-    def beside(after, *arrived):
-        if len(weights) == len(wanted):
-            return arrived
-        weight, at = wanted[len(weights)]
-        arrived = lax.optimization_barrier((load(weight, after, wide, at), *arrived))
-        weights.append(arrived[0])
-        return arrived[1:]
-
-    mine, shifts = [normed], [0]
+    def beside(after, arrived, *others):
+        if len(weights) < len(wanted):
+            weight, at = wanted[len(weights)]
+            weights.append(load(weight, after, wide, at))
+            others = (weights[-1], *others)
+        return once(arrived, *others) if others else arrived
+
+    parts, shifts = [normed, cross(normed)], [0]
     ahead = behind = normed
     for step in range(1, steps):
-        ahead, behind = beside(ahead, right(ahead), left(behind))
-        mine += [ahead, behind]
+        after, done = behind, parts[-1:] if step == 1 else parts[-3::2]
+        ahead, behind = right(ahead), left(behind)
+        behind = beside(after, behind, *done)
+        parts += [ahead, cross(ahead), behind, cross(behind)]
         shifts += [-step, step]
-    (far,) = beside(ahead, hop(both(pick_kernel, ahead, behind, "pick"), 1, -1))
-    mine.append(far)
+    far = beside(ahead, hop(both(pick_kernel, ahead, behind, "pick"), 1, -1), *parts[-3::2])
+    parts += [far, cross(far)]
     shifts.append(steps)
     while len(weights) < len(wanted):
-        (normed,) = beside(normed, normed)
-    parts = [block for own in mine for block in (own, cross(own))]
-    half_a, half_b = up_project(shifts, parts, weights)
-    wide = down_weight.shape[1] // 2
-    def butterfly(value, mask):
-        return both(functools.partial(turn_kernel, mask), value, cross(value, mask), "turn")
+        parts[0] = beside(parts[0], parts[0])
+
+    half_a, half_b, down_theirs = up_project(shifts, parts, weights, down_weight)
+
+    def turn(value, mask, *others):
+        return both(functools.partial(turn_kernel, mask), value, once(cross(value, mask), *others), "turn")
 
     masks = [1 << bit for bit in range(count.bit_length() - 1)]
-    orders = [masks[-1:] + masks[:-1], masks]
-    down_weights = []
     for stage in range(len(masks)):
-        before = half_a
-        half_a = butterfly(half_a, orders[0][stage])
-        half_b = butterfly(half_b, orders[1][stage])
-        if stage < 2:
-            columns = load(down_weight, before, wide, 0, stage == 0)
-            columns, half_a, half_b = lax.optimization_barrier((columns, half_a, half_b))
-            down_weights.append(columns)
-    total = count * gate_weight.shape[1]
+        first, second = masks[stage - 1], masks[stage]
+        if stage == 0:
+            half_b = turn(half_b, second)
+            down_own = load(down_weight, half_b, down_weight.shape[1] // 2, None)
+            half_a = turn(half_a, first, half_b, down_own)
+        elif stage < len(masks) - 1:
+            half_b = turn(half_b, second, half_a)
+            half_a = turn(half_a, first, half_b)
+        else:
+            half_a = turn(half_a, first, half_b)
+            half_b = turn(half_b, second, half_a)
+
+    total = count * width
     limits = clip_scale.reshape(1, -1)
-    theirs = down_project(half_a, half_b, limits, down_weights[:1], chips, total)
-    own = down_project(half_a, half_b, limits, down_weights[1:], chips, total)
-    arrived = cross(theirs)
-    rows, wide = own.shape[0] // chips, own.shape[1]
+    theirs_far, theirs = down_project(half_a, half_b, limits, down_theirs, chips, total)
+    arrived_far = cross(theirs_far)
+    own_far, own = down_project(half_a, half_b, limits, down_own, chips, total)
+    arrived = cross(once(theirs, own, arrived_far))
+    rows, wide = own_far.shape
     part = jax.ShapeDtypeStruct((rows, wide), jnp.bfloat16)
 
-    far = hop(small(functools.partial(far_kernel, steps, chips), part, (own, arrived), "far"), 1, -1)
+    ahead = behind = hop(small(sum_kernel, part, (own_far, arrived_far), "far"), 1, -1)
     for away in range(steps - 1, 0, -1):
-        if away == steps - 1:
-            body, operands = split_kernel, (far, own, arrived)
-        else:
-            body, operands = relay_kernel, (ahead, behind, own, arrived)
-        ahead, behind = small(functools.partial(body, away, chips), (part, part), operands, "relay")
+        cores = (0, 1) if away == steps - 1 else (None, None)
+        ahead = small(
+            functools.partial(relay_kernel, away, chips, cores[0]), part, (ahead, own, arrived), "relay"
+        )
+        behind = small(
+            functools.partial(relay_kernel, -away, chips, cores[1]), part, (behind, own, arrived), "relay"
+        )
         ahead, behind = right(ahead), left(behind)
     half = jax.ShapeDtypeStruct((rows // 2, wide), jnp.bfloat16)
     kept = jax.ShapeDtypeStruct((rows // 2, wide), jnp.float32)

time: 95.2 us -> 92.8 us (0.975)
  starting transfers between devices: 22.8 us -> 21 us
  local copies, waits for them, and re-layouts: 1.67 us -> 0.01 us
    ppermute x18 -> x19, starting transfers between devices: 8.82 us -> 6.81 us  [cross(): return lax.ppermute(value, 'hid', [(d, d ^ mask) for d in range(count)])]
    unnamed x8 -> x4, local copies, waits for them, and re-layouts: 1.67 us -> 0.01 us
    ppermute x18 -> x19, waiting for transfers between devices: 19.5 us -> 20.5 us  [cross(): return lax.ppermute(value, 'hid', [(d, d ^ mask) for d in range(count)])]
    pallas_call x7 -> x6, Pallas kernels: 26 us -> 25.7 us  [the longest x5 17.5 us: load(): pl.pallas_call(functools.partial(load_kernel, at), out_shape=jax.ShapeDty...]
  transfers between devices with their start and end apart: 32 -> 33, of which waited for: 22 -> 19; matrix products, arithmetic and copies ran while one was open for 0% -> 0% of each run, Pallas kernels for 24% -> 21%
where the time goes in v4:
time: 92.8 us; the launch traced here: 92.5 us
  waiting for transfers between devices  40 us (43%)
  Pallas kernels  31.2 us (34%)
  starting transfers between devices  21 us (23%)
    ppermute x19, waiting for transfers between devices, cross(): return lax.ppermute(value, 'hid', [(d, d ^ mask) for d in range(count)])  20.5 us
    ppermute x14, waiting for transfers between devices, hop(): return lax.ppermute(value, 'hid', pairs)  19.5 us
    pallas_call x5, Pallas kernels, load(): pl.pallas_call(functools.partial(load_kernel, at), out_shape=jax.ShapeDty...  17.5 us
    ppermute x14, starting transfers between devices, hop(): return lax.ppermute(value, 'hid', pairs)  14.2 us
    pallas_call x1, Pallas kernels, up_project(): pl.pallas_call(functools.partial(up_kernel, count, shifts), out_shape=[ha...  8.13 us
    ppermute x19, starting transfers between devices, cross(): return lax.ppermute(value, 'hid', [(d, d ^ mask) for d in range(count)])  6.81 us
    pallas_call x2, Pallas kernels, down_project(): pl.pallas_call(functools.partial(down_kernel, width // BLOCK, chips, tota...  2.85 us
  transfers between devices with their start and end apart: 33, of which 19 were waited for; matrix products, arithmetic and copies ran while one was open for 0% of the time, Pallas kernels for 21%

profile of v4, /device:TPU:0, one launch (start us, length us, event | category | flops | bytes accessed | tf_op | source)
XLA Modules:
  0.0 92.5 jit_solution(4404750056466305281)
XLA Ops:
  0.0 1.1 %normalize.1.after_ref.refs_0_ = bf16[8,8192]{1,0:T(8,128)(2,1)S(1)} custom-call(bf16[8,8192]{1,0:T(8,128)(2,1)} %tokens_ref.1, f32[1,8192]{1,0:T(1,128)} %bitcast.4), custom_call_target="tpu_custom_call" | custom-call | flops 524288 | bytes 262144 | tf_op jit(solution)/shard_map/normalize/pallas_call | solution.py:45
  1.1 3.0 %collective-permute-start.3 = (bf16[8,8192]{1,0:T(8,128)(2,1)S(1)}, bf16[8,8192]{1,0:T(8,128)(2,1)S(1)}, u32[]{:S(2)}, u32[]{:S(2)}) collective-permute-start(bf16[8,8192]{1,0:T(8,128)(2,1)S(1)} %normalize.1.after_ref.refs_0_), channel_id=1, source_target_pairs={{0,2},{1,3},{4,0},{5,1},{8,4},{9,5},{12,8},{13,9},{14,12},{15,13},... | collective-permute-start | bytes 393224 | tf_op jit(solution)/shard_map/ppermute | solution.py:303
  4.1 0.2 collective-permute-start.1
  4.3 3.6 %load.5.refs_16_ = bf16[8192,512]{1,0:T(8,128)(2,1)S(1)} custom-call(bf16[8192,1024]{1,0:T(8,128)(2,1)} %weight_ref.7, bf16[8,8192]{1,0:T(8,128)(2,1)S(1)} %normalize.1.after_ref.refs_0_), custom_call_target="tpu_custom_call" | custom-call | bytes 8388608 | tf_op jit(solution)/shard_map/load/pallas_call | solution.py:87
  7.9 2.1 %collective-permute-done.1.refs_2_ = bf16[8,8192]{1,0:T(8,128)(2,1)S(1)} collective-permute-done((bf16[8,8192]{1,0:T(8,128)(2,1)S(1)}, bf16[8,8192]{1,0:T(8,128)(2,1)S(1)}, u32[]{:S(2)}, u32[]{:S(2)}) %collective-permute-start.1) | collective-permute-done | bytes 131104 | tf_op jit(solution)/shard_map/ppermute | solution.py:303
  10.1 1.6 %collective-permute-start.7 = (bf16[8,8192]{1,0:T(8,128)(2,1)S(1)}, bf16[8,8192]{1,0:T(8,128)(2,1)S(1)}, u32[]{:S(2)}, u32[]{:S(2)}) collective-permute-start(bf16[8,8192]{1,0:T(8,128)(2,1)S(1)} %collective-permute-done.3.after_ref.refs_4_), channel_id=1, source_target_pairs={{0,2},{1,3},{4,0},{5,1},{8,4},{9,5},{12,8},{13,9},{14,12},{15,13},... | collective-permute-start | bytes 393224 | tf_op jit(solution)/shard_map/ppermute | solution.py:303
  11.6 0.2 collective-permute-start.4
  11.9 0.4 collective-permute-start.5
  12.3 3.6 %load.6.refs_17_ = bf16[8192,512]{1,0:T(8,128)(2,1)S(1)} custom-call(bf16[8192,1024]{1,0:T(8,128)(2,1)} %weight_ref.8, bf16[8,8192]{1,0:T(8,128)(2,1)S(1)} %collective-permute-done.3.after_ref.refs_4_), custom_call_target="tpu_custom_call" | custom-call | bytes 8388608 | tf_op jit(solution)/shard_map/load/pallas_call | solution.py:87
  15.9 0.1 collective-permute-done.7.after_ref.refs_8_
  16.0 1.6 %collective-permute-done.5.refs_6_ = bf16[8,8192]{1,0:T(8,128)(2,1)S(1)} collective-permute-done((bf16[8,8192]{1,0:T(8,128)(2,1)S(1)}, bf16[8,8192]{1,0:T(8,128)(2,1)S(1)}, u32[]{:S(2)}, u32[]{:S(2)}) %collective-permute-start.5) | collective-permute-done | bytes 131104 | tf_op jit(solution)/shard_map/ppermute | solution.py:303
  17.5 1.6 %collective-permute-start.11 = (bf16[8,8192]{1,0:T(8,128)(2,1)S(1)}, bf16[8,8192]{1,0:T(8,128)(2,1)S(1)}, u32[]{:S(2)}, u32[]{:S(2)}) collective-permute-start(bf16[8,8192]{1,0:T(8,128)(2,1)S(1)} %collective-permute-done.7.after_ref.refs_8_), channel_id=1, source_target_pairs={{0,2},{1,3},{4,0},{5,1},{8,4},{9,5},{12,8},{13,9},{14,12},{15,13},... | collective-permute-start | bytes 393224 | tf_op jit(solution)/shard_map/ppermute | solution.py:303
  19.1 0.2 collective-permute-start.8
  19.4 0.4 collective-permute-start.9
  19.8 3.5 %load.7.refs_18_ = bf16[8192,512]{1,0:T(8,128)(2,1)S(1)} custom-call(bf16[8192,1024]{1,0:T(8,128)(2,1)} %weight_ref.7, bf16[8,8192]{1,0:T(8,128)(2,1)S(1)} %collective-permute-done.7.after_ref.refs_8_), custom_call_target="tpu_custom_call" | custom-call | bytes 8388608 | tf_op jit(solution)/shard_map/load/pallas_call | solution.py:87
  23.3 0.1 collective-permute-done.11.odd_ref.refs_12_
  23.5 1.6 %collective-permute-done.9.even_ref.after_ref.refs_10_ = bf16[8,8192]{1,0:T(8,128)(2,1)S(1)} collective-permute-done((bf16[8,8192]{1,0:T(8,128)(2,1)S(1)}, bf16[8,8192]{1,0:T(8,128)(2,1)S(1)}, u32[]{:S(2)}, u32[]{:S(2)}) %collective-permute-start.9) | collective-permute-done | bytes 131104 | tf_op jit(solution)/shard_map/ppermute | solution.py:303
  25.1 0.5 collective-permute-start.13
  25.6 1.3 %collective-permute-start.12 = (bf16[8,8192]{1,0:T(8,128)(2,1)S(1)}, bf16[8,8192]{1,0:T(8,128)(2,1)S(1)}, u32[]{:S(2)}, u32[]{:S(2)}) collective-permute-start(bf16[8,8192]{1,0:T(8,128)(2,1)S(1)} %collective-permute-done.11.odd_ref.refs_12_), channel_id=1, source_target_pairs={{0,1},{1,0},{2,3},{3,2},{4,5},{5,4},{6,7},{7,6},{8,9},{9,8},{10,11... | collective-permute-start | bytes 393224 | tf_op jit(solution)/shard_map/ppermute | solution.py:312
  26.9 3.5 %load.8.refs_19_ = bf16[8192,512]{1,0:T(8,128)(2,1)S(1)} custom-call(bf16[8192,1024]{1,0:T(8,128)(2,1)} %weight_ref.8, bf16[8,8192]{1,0:T(8,128)(2,1)S(1)} %collective-permute-done.9.even_ref.after_ref.refs_10_), custom_call_target="tpu_custom_call" | custom-call | bytes 8388608 | tf_op jit(solution)/shard_map/load/pallas_call | solution.py:87
  30.5 0.1 collective-permute-start.14
  30.5 1.3 %collective-permute-done.14.refs_15_ = bf16[8,8192]{1,0:T(8,128)(2,1)S(1)} collective-permute-done((bf16[8,8192]{1,0:T(8,128)(2,1)S(1)}, bf16[8,8192]{1,0:T(8,128)(2,1)S(1)}, u32[]{:S(2)}, u32[]{:S(2)}) %collective-permute-start.14) | collective-permute-done | bytes 131104 | tf_op jit(solution)/shard_map/ppermute | solution.py:312
  31.9 8.1 %up_project.1 = (bf16[128,512]{1,0:T(8,128)(2,1)S(1)}, bf16[128,512]{1,0:T(8,128)(2,1)S(1)}, bf16[1024,4096]{1,0:T(8,128)(2,1)S(1)}) custom-call(bf16[8,8192]{1,0:T(8,128)(2,1)S(1)} %normalize.1.after_ref.refs_0_, bf16[8,8192]{1,0:T(8,128)(2,1)S(1)} %collective-permute-done.refs_1_, bf16[8,8192]{1,0:T(8,128)(2,1)S(1)} %collective-permute-done.1.refs_2_, ...), custom_call_target="tpu_custom_call" | custom-call | flops 4294967296 | tf_op jit(solution)/shard_map/up_project/pallas_call | solution.py:148
  40.0 0.2 collective-permute-start.16
  40.2 0.4 collective-permute-start.15
  40.6 0.8 collective-permute-done.16.other_ref
  41.5 1.2 %collective-permute-start.18 = (bf16[128,512]{1,0:T(8,128)(2,1)S(1)}, bf16[128,512]{1,0:T(8,128)(2,1)S(1)}, u32[]{:S(2)}, u32[]{:S(2)}) collective-permute-start(bf16[128,512]{1,0:T(8,128)(2,1)S(1)} %turn.8.after_ref.value_ref), channel_id=1, source_target_pairs={{0,2},{1,3},{2,0},{3,1},{4,6},{5,7},{6,4},{7,5},{8,10},{9,11},{10,... | collective-permute-start | bytes 393224 | tf_op jit(solution)/shard_map/ppermute | solution.py:312
  42.7 3.4 %load.9.weight_ref = bf16[1024,4096]{1,0:T(8,128)(2,1)S(1)} custom-call(bf16[1024,8192]{1,0:T(8,128)(2,1)} %weight_ref.9, bf16[128,512]{1,0:T(8,128)(2,1)S(1)} %turn.8.after_ref.value_ref), custom_call_target="tpu_custom_call" | custom-call | bytes 8388608 | tf_op jit(solution)/shard_map/load/pallas_call | solution.py:87
  46.1 3.5 %collective-permute-done.15.other_ref = bf16[128,512]{1,0:T(8,128)(2,1)S(1)} collective-permute-done((bf16[128,512]{1,0:T(8,128)(2,1)S(1)}, bf16[128,512]{1,0:T(8,128)(2,1)S(1)}, u32[]{:S(2)}, u32[]{:S(2)}) %collective-permute-start.15) | collective-permute-done | bytes 131104 | tf_op jit(solution)/shard_map/ppermute | solution.py:312
  49.6 0.1 collective-permute-start.17
  49.8 0.1 collective-permute-start.20
  49.9 1.2 %collective-permute-done.17.other_ref = bf16[128,512]{1,0:T(8,128)(2,1)S(1)} collective-permute-done((bf16[128,512]{1,0:T(8,128)(2,1)S(1)}, bf16[128,512]{1,0:T(8,128)(2,1)S(1)}, u32[]{:S(2)}, u32[]{:S(2)}) %collective-permute-start.17) | collective-permute-done | bytes 131104 | tf_op jit(solution)/shard_map/ppermute | solution.py:312
  51.1 1.3 %collective-permute-start.19 = (bf16[128,512]{1,0:T(8,128)(2,1)S(1)}, bf16[128,512]{1,0:T(8,128)(2,1)S(1)}, u32[]{:S(2)}, u32[]{:S(2)}) collective-permute-start(bf16[128,512]{1,0:T(8,128)(2,1)S(1)} %turn.11.value_ref), channel_id=1, source_target_pairs={{0,2},{1,3},{2,0},{3,1},{4,6},{5,7},{6,4},{7,5},{8,10},{9,11},{10,... | collective-permute-start | bytes 393224 | tf_op jit(solution)/shard_map/ppermute | solution.py:312
  52.4 3.3 %collective-permute-done.20.other_ref = bf16[128,512]{1,0:T(8,128)(2,1)S(1)} collective-permute-done((bf16[128,512]{1,0:T(8,128)(2,1)S(1)}, bf16[128,512]{1,0:T(8,128)(2,1)S(1)}, u32[]{:S(2)}, u32[]{:S(2)}) %collective-permute-start.20) | collective-permute-done | bytes 131104 | tf_op jit(solution)/shard_map/ppermute | solution.py:312
  55.8 0.9 %collective-permute-done.19.other_ref = bf16[128,512]{1,0:T(8,128)(2,1)S(1)} collective-permute-done((bf16[128,512]{1,0:T(8,128)(2,1)S(1)}, bf16[128,512]{1,0:T(8,128)(2,1)S(1)}, u32[]{:S(2)}, u32[]{:S(2)}) %collective-permute-start.19) | collective-permute-done | bytes 131104 | tf_op jit(solution)/shard_map/ppermute | solution.py:312
  56.8 0.9 %collective-permute-start.21 = (bf16[128,512]{1,0:T(8,128)(2,1)S(1)}, bf16[128,512]{1,0:T(8,128)(2,1)S(1)}, u32[]{:S(2)}, u32[]{:S(2)}) collective-permute-start(bf16[128,512]{1,0:T(8,128)(2,1)S(1)} %turn.13.value_ref), channel_id=1, source_target_pairs={{0,4},{1,5},{2,6},{3,7},{4,0},{5,1},{6,2},{7,3},{8,12},{9,13},{10,... | collective-permute-start | bytes 393224 | tf_op jit(solution)/shard_map/ppermute | solution.py:312
  57.7 4.8 %collective-permute-done.21.other_ref = bf16[128,512]{1,0:T(8,128)(2,1)S(1)} collective-permute-done((bf16[128,512]{1,0:T(8,128)(2,1)S(1)}, bf16[128,512]{1,0:T(8,128)(2,1)S(1)}, u32[]{:S(2)}, u32[]{:S(2)}) %collective-permute-start.21) | collective-permute-done | bytes 131104 | tf_op jit(solution)/shard_map/ppermute | solution.py:312
  62.5 3.4 %collective-permute-done.22.other_ref = bf16[128,512]{1,0:T(8,128)(2,1)S(1)} collective-permute-done((bf16[128,512]{1,0:T(8,128)(2,1)S(1)}, bf16[128,512]{1,0:T(8,128)(2,1)S(1)}, u32[]{:S(2)}, u32[]{:S(2)}) %collective-permute-start.22) | collective-permute-done | bytes 131104 | tf_op jit(solution)/shard_map/ppermute | solution.py:312
  66.0 1.4 %down_project.3 = (bf16[16,4096]{1,0:T(8,128)(2,1)S(1)}, bf16[112,4096]{1,0:T(8,128)(2,1)S(1)}) custom-call(bf16[128,512]{1,0:T(8,128)(2,1)S(1)} %turn.14.a_ref, bf16[128,512]{1,0:T(8,128)(2,1)S(1)} %turn.15.b_ref, f32[1,1024]{1,0:T(1,128)S(1)} %bitcast.2, bf16[1024,4096]{1,0:T(8,128)(2,1)S(1)} %get-tuple-element.40.weight_ref), custom_call_target="tpu_custom_call" | custom-call | flops 1073741824 | tf_op jit(solution)/shard_map/down_project/pallas_call | solution.py:200
  67.4 0.1 collective-permute-start.23
  67.5 1.4 %down_project.2 = (bf16[16,4096]{1,0:T(8,128)(2,1)S(1)}, bf16[112,4096]{1,0:T(8,128)(2,1)S(1)}) custom-call(bf16[128,512]{1,0:T(8,128)(2,1)S(1)} %turn.14.a_ref, bf16[128,512]{1,0:T(8,128)(2,1)S(1)} %turn.15.b_ref, f32[1,1024]{1,0:T(1,128)S(1)} %bitcast.3, bf16[1024,4096]{1,0:T(8,128)(2,1)S(1)} %load.9.weight_ref), custom_call_target="tpu_custom_call" | custom-call | flops 1073741824 | tf_op jit(solution)/shard_map/down_project/pallas_call | solution.py:200
  68.9 0.6 collective-permute-start.25
  69.5 0.1 collective-permute-start.24
  69.6 5.0 %collective-permute-done.24.arrived_in = bf16[16,4096]{1,0:T(8,128)(2,1)S(1)} collective-permute-done((bf16[16,4096]{1,0:T(8,128)(2,1)S(1)}, bf16[16,4096]{1,0:T(8,128)(2,1)S(1)}, u32[]{:S(2)}, u32[]{:S(2)}) %collective-permute-start.24) | collective-permute-done | bytes 131104 | tf_op jit(solution)/shard_map/ppermute | solution.py:303
  74.5 0.1 relay.6
  74.6 0.1 collective-permute-start.26
  74.7 0.1 relay.9
  74.7 2.1 %collective-permute-start.29 = (bf16[16,4096]{1,0:T(8,128)(2,1)S(1)}, bf16[16,4096]{1,0:T(8,128)(2,1)S(1)}, u32[]{:S(2)}, u32[]{:S(2)}) collective-permute-start(bf16[16,4096]{1,0:T(8,128)(2,1)S(1)} %relay.9), channel_id=1, source_target_pairs={{0,2},{1,3},{4,0},{5,1},{8,4},{9,5},{12,8},{13,9},{14,12},{15,13},... | collective-permute-start | bytes 393224 | tf_op jit(solution)/shard_map/ppermute | solution.py:303
  76.8 2.8 %collective-permute-done.26.arrived_in = bf16[16,4096]{1,0:T(8,128)(2,1)S(1)} collective-permute-done((bf16[16,4096]{1,0:T(8,128)(2,1)S(1)}, bf16[16,4096]{1,0:T(8,128)(2,1)S(1)}, u32[]{:S(2)}, u32[]{:S(2)}) %collective-permute-start.26) | collective-permute-done | bytes 131104 | tf_op jit(solution)/shard_map/ppermute | solution.py:303
  79.6 0.1 relay.7
  79.7 0.1 collective-permute-start.27
  79.8 0.1 relay.10
  79.8 2.1 %collective-permute-start.30 = (bf16[16,4096]{1,0:T(8,128)(2,1)S(1)}, bf16[16,4096]{1,0:T(8,128)(2,1)S(1)}, u32[]{:S(2)}, u32[]{:S(2)}) collective-permute-start(bf16[16,4096]{1,0:T(8,128)(2,1)S(1)} %relay.10), channel_id=1, source_target_pairs={{0,2},{1,3},{4,0},{5,1},{8,4},{9,5},{12,8},{13,9},{14,12},{15,13},... | collective-permute-start | bytes 393224 | tf_op jit(solution)/shard_map/ppermute | solution.py:303
  81.9 3.3 %collective-permute-done.27.arrived_in = bf16[16,4096]{1,0:T(8,128)(2,1)S(1)} collective-permute-done((bf16[16,4096]{1,0:T(8,128)(2,1)S(1)}, bf16[16,4096]{1,0:T(8,128)(2,1)S(1)}, u32[]{:S(2)}, u32[]{:S(2)}) %collective-permute-start.27) | collective-permute-done | bytes 131104 | tf_op jit(solution)/shard_map/ppermute | solution.py:303
  85.1 0.1 relay.8
  85.2 0.1 collective-permute-start.28
  85.3 0.1 relay.11
  85.3 2.1 %collective-permute-start.31 = (bf16[16,4096]{1,0:T(8,128)(2,1)S(1)}, bf16[16,4096]{1,0:T(8,128)(2,1)S(1)}, u32[]{:S(2)}, u32[]{:S(2)}) collective-permute-start(bf16[16,4096]{1,0:T(8,128)(2,1)S(1)} %relay.11), channel_id=1, source_target_pairs={{0,2},{1,3},{4,0},{5,1},{8,4},{9,5},{12,8},{13,9},{14,12},{15,13},... | collective-permute-start | bytes 393224 | tf_op jit(solution)/shard_map/ppermute | solution.py:303
  87.4 2.8 %collective-permute-done.28.ahead_in = bf16[16,4096]{1,0:T(8,128)(2,1)S(1)} collective-permute-done((bf16[16,4096]{1,0:T(8,128)(2,1)S(1)}, bf16[16,4096]{1,0:T(8,128)(2,1)S(1)}, u32[]{:S(2)}, u32[]{:S(2)}) %collective-permute-start.28) | collective-permute-done | bytes 131104 | tf_op jit(solution)/shard_map/ppermute | solution.py:303
  90.2 0.1 collective-permute-done.31.behind_in
  90.3 0.1 last.1
  90.5 0.1 collective-permute-start.32
  90.5 1.2 %collective-permute-done.32.take_ref = bf16[8,4096]{1,0:T(8,128)(2,1)S(1)} collective-permute-done((bf16[8,4096]{1,0:T(8,128)(2,1)S(1)}, bf16[8,4096]{1,0:T(8,128)(2,1)S(1)}, u32[]{:S(2)}, u32[]{:S(2)}) %collective-permute-start.32) | collective-permute-done | bytes 65568 | tf_op jit(solution)/shard_map/ppermute | solution.py:312
  91.8 0.7 mix.1
  (33 shorter events, 0.5 us)
Async XLA Ops:
  1.1 6.8 %collective-permute-start.3 = (bf16[8,8192]{1,0:T(8,128)(2,1)S(1)}, bf16[8,8192]{1,0:T(8,128)(2,1)S(1)}, u32[]{:S(2)}, u32[]{:S(2)}) collective-permute-start(bf16[8,8192]{1,0:T(8,128)(2,1)S(1)} %normalize.1.after_ref.refs_0_), channel_id=1, source_target_pairs={{0,2},{1,3},{4,0},{5,1},{8,4},{9,5},{12,8},{13,9},{14,12},{15,13},... | collective-permute-start | bytes 393224 | tf_op jit(solution)/shard_map/ppermute | solution.py:303
  4.1 3.8 %collective-permute-start = (bf16[8,8192]{1,0:T(8,128)(2,1)S(1)}, bf16[8,8192]{1,0:T(8,128)(2,1)S(1)}, u32[]{:S(2)}, u32[]{:S(2)}) collective-permute-start(bf16[8,8192]{1,0:T(8,128)(2,1)S(1)} %normalize.1.after_ref.refs_0_), channel_id=1, source_target_pairs={{0,1},{1,0},{2,3},{3,2},{4,5},{5,4},{6,7},{7,6},{8,9},{9,8},{10,11... | collective-permute-start | bytes 393224 | tf_op jit(solution)/shard_map/ppermute | solution.py:312
  4.1 5.9 %collective-permute-start.1 = (bf16[8,8192]{1,0:T(8,128)(2,1)S(1)}, bf16[8,8192]{1,0:T(8,128)(2,1)S(1)}, u32[]{:S(2)}, u32[]{:S(2)}) collective-permute-start(bf16[8,8192]{1,0:T(8,128)(2,1)S(1)} %normalize.1.after_ref.refs_0_), channel_id=1, source_target_pairs={{0,4},{1,5},{4,8},{5,9},{8,12},{9,13},{12,14},{13,15},{14,10},{15,... | collective-permute-start | bytes 393224 | tf_op jit(solution)/shard_map/ppermute | solution.py:303
  10.1 5.8 %collective-permute-start.2 = (bf16[8,8192]{1,0:T(8,128)(2,1)S(1)}, bf16[8,8192]{1,0:T(8,128)(2,1)S(1)}, u32[]{:S(2)}, u32[]{:S(2)}) collective-permute-start(bf16[8,8192]{1,0:T(8,128)(2,1)S(1)} %collective-permute-done.1.refs_2_), channel_id=1, source_target_pairs={{0,1},{1,0},{2,3},{3,2},{4,5},{5,4},{6,7},{7,6},{8,9},{9,8},{10,11... | collective-permute-start | bytes 393224 | tf_op jit(solution)/shard_map/ppermute | solution.py:312
  10.1 5.9 %collective-permute-start.7 = (bf16[8,8192]{1,0:T(8,128)(2,1)S(1)}, bf16[8,8192]{1,0:T(8,128)(2,1)S(1)}, u32[]{:S(2)}, u32[]{:S(2)}) collective-permute-start(bf16[8,8192]{1,0:T(8,128)(2,1)S(1)} %collective-permute-done.3.after_ref.refs_4_), channel_id=1, source_target_pairs={{0,2},{1,3},{4,0},{5,1},{8,4},{9,5},{12,8},{13,9},{14,12},{15,13},... | collective-permute-start | bytes 393224 | tf_op jit(solution)/shard_map/ppermute | solution.py:303
  11.6 4.3 %collective-permute-start.4 = (bf16[8,8192]{1,0:T(8,128)(2,1)S(1)}, bf16[8,8192]{1,0:T(8,128)(2,1)S(1)}, u32[]{:S(2)}, u32[]{:S(2)}) collective-permute-start(bf16[8,8192]{1,0:T(8,128)(2,1)S(1)} %collective-permute-done.3.after_ref.refs_4_), channel_id=1, source_target_pairs={{0,1},{1,0},{2,3},{3,2},{4,5},{5,4},{6,7},{7,6},{8,9},{9,8},{10,11... | collective-permute-start | bytes 393224 | tf_op jit(solution)/shard_map/ppermute | solution.py:312
  11.9 5.7 %collective-permute-start.5 = (bf16[8,8192]{1,0:T(8,128)(2,1)S(1)}, bf16[8,8192]{1,0:T(8,128)(2,1)S(1)}, u32[]{:S(2)}, u32[]{:S(2)}) collective-permute-start(bf16[8,8192]{1,0:T(8,128)(2,1)S(1)} %collective-permute-done.1.refs_2_), channel_id=1, source_target_pairs={{0,4},{1,5},{4,8},{5,9},{8,12},{9,13},{12,14},{13,15},{14,10},{15,... | collective-permute-start | bytes 393224 | tf_op jit(solution)/shard_map/ppermute | solution.py:303
  17.5 5.8 %collective-permute-start.6 = (bf16[8,8192]{1,0:T(8,128)(2,1)S(1)}, bf16[8,8192]{1,0:T(8,128)(2,1)S(1)}, u32[]{:S(2)}, u32[]{:S(2)}) collective-permute-start(bf16[8,8192]{1,0:T(8,128)(2,1)S(1)} %collective-permute-done.5.refs_6_), channel_id=1, source_target_pairs={{0,1},{1,0},{2,3},{3,2},{4,5},{5,4},{6,7},{7,6},{8,9},{9,8},{10,11... | collective-permute-start | bytes 393224 | tf_op jit(solution)/shard_map/ppermute | solution.py:312
  17.5 5.9 %collective-permute-start.11 = (bf16[8,8192]{1,0:T(8,128)(2,1)S(1)}, bf16[8,8192]{1,0:T(8,128)(2,1)S(1)}, u32[]{:S(2)}, u32[]{:S(2)}) collective-permute-start(bf16[8,8192]{1,0:T(8,128)(2,1)S(1)} %collective-permute-done.7.after_ref.refs_8_), channel_id=1, source_target_pairs={{0,2},{1,3},{4,0},{5,1},{8,4},{9,5},{12,8},{13,9},{14,12},{15,13},... | collective-permute-start | bytes 393224 | tf_op jit(solution)/shard_map/ppermute | solution.py:303
  19.1 4.3 %collective-permute-start.8 = (bf16[8,8192]{1,0:T(8,128)(2,1)S(1)}, bf16[8,8192]{1,0:T(8,128)(2,1)S(1)}, u32[]{:S(2)}, u32[]{:S(2)}) collective-permute-start(bf16[8,8192]{1,0:T(8,128)(2,1)S(1)} %collective-permute-done.7.after_ref.refs_8_), channel_id=1, source_target_pairs={{0,1},{1,0},{2,3},{3,2},{4,5},{5,4},{6,7},{7,6},{8,9},{9,8},{10,11... | collective-permute-start | bytes 393224 | tf_op jit(solution)/shard_map/ppermute | solution.py:312
  19.4 5.7 %collective-permute-start.9 = (bf16[8,8192]{1,0:T(8,128)(2,1)S(1)}, bf16[8,8192]{1,0:T(8,128)(2,1)S(1)}, u32[]{:S(2)}, u32[]{:S(2)}) collective-permute-start(bf16[8,8192]{1,0:T(8,128)(2,1)S(1)} %collective-permute-done.5.refs_6_), channel_id=1, source_target_pairs={{0,4},{1,5},{4,8},{5,9},{8,12},{9,13},{12,14},{13,15},{14,10},{15,... | collective-permute-start | bytes 393224 | tf_op jit(solution)/shard_map/ppermute | solution.py:303
  25.0 5.4 %collective-permute-start.10 = (bf16[8,8192]{1,0:T(8,128)(2,1)S(1)}, bf16[8,8192]{1,0:T(8,128)(2,1)S(1)}, u32[]{:S(2)}, u32[]{:S(2)}) collective-permute-start(bf16[8,8192]{1,0:T(8,128)(2,1)S(1)} %collective-permute-done.9.even_ref.after_ref.refs_10_), channel_id=1, source_target_pairs={{0,1},{1,0},{2,3},{3,2},{4,5},{5,4},{6,7},{7,6},{8,9},{9,8},{10,11... | collective-permute-start | bytes 393224 | tf_op jit(solution)/shard_map/ppermute | solution.py:312
  25.1 5.4 %collective-permute-start.13 = (bf16[8,8192]{1,0:T(8,128)(2,1)S(1)}, bf16[8,8192]{1,0:T(8,128)(2,1)S(1)}, u32[]{:S(2)}, u32[]{:S(2)}) collective-permute-start(bf16[8,8192]{1,0:T(8,128)(2,1)S(1)} %pick.1), channel_id=1, source_target_pairs={{0,4},{1,3},{4,8},{5,1},{8,12},{9,5},{12,14},{13,9},{14,10},{15,13... | collective-permute-start | bytes 393224 | tf_op jit(solution)/shard_map/ppermute | solution.py:303
  25.6 4.9 %collective-permute-start.12 = (bf16[8,8192]{1,0:T(8,128)(2,1)S(1)}, bf16[8,8192]{1,0:T(8,128)(2,1)S(1)}, u32[]{:S(2)}, u32[]{:S(2)}) collective-permute-start(bf16[8,8192]{1,0:T(8,128)(2,1)S(1)} %collective-permute-done.11.odd_ref.refs_12_), channel_id=1, source_target_pairs={{0,1},{1,0},{2,3},{3,2},{4,5},{5,4},{6,7},{7,6},{8,9},{9,8},{10,11... | collective-permute-start | bytes 393224 | tf_op jit(solution)/shard_map/ppermute | solution.py:312
  30.5 1.4 %collective-permute-start.14 = (bf16[8,8192]{1,0:T(8,128)(2,1)S(1)}, bf16[8,8192]{1,0:T(8,128)(2,1)S(1)}, u32[]{:S(2)}, u32[]{:S(2)}) collective-permute-start(bf16[8,8192]{1,0:T(8,128)(2,1)S(1)} %collective-permute-done.13.refs_14_), channel_id=1, source_target_pairs={{0,1},{1,0},{2,3},{3,2},{4,5},{5,4},{6,7},{7,6},{8,9},{9,8},{10,11... | collective-permute-start | bytes 393224 | tf_op jit(solution)/shard_map/ppermute | solution.py:312
  40.0 1.4 %collective-permute-start.16 = (bf16[128,512]{1,0:T(8,128)(2,1)S(1)}, bf16[128,512]{1,0:T(8,128)(2,1)S(1)}, u32[]{:S(2)}, u32[]{:S(2)}) collective-permute-start(bf16[128,512]{1,0:T(8,128)(2,1)S(1)} %get-tuple-element.31.value_ref), channel_id=1, source_target_pairs={{0,1},{1,0},{2,3},{3,2},{4,5},{5,4},{6,7},{7,6},{8,9},{9,8},{10,11... | collective-permute-start | bytes 393224 | tf_op jit(solution)/shard_map/ppermute | solution.py:312
  40.2 9.4 %collective-permute-start.15 = (bf16[128,512]{1,0:T(8,128)(2,1)S(1)}, bf16[128,512]{1,0:T(8,128)(2,1)S(1)}, u32[]{:S(2)}, u32[]{:S(2)}) collective-permute-start(bf16[128,512]{1,0:T(8,128)(2,1)S(1)} %get-tuple-element.30.value_ref), channel_id=1, source_target_pairs={{0,8},{1,9},{2,10},{3,11},{4,12},{5,13},{6,14},{7,15},{8,0},{9,1},... | collective-permute-start | bytes 393224 | tf_op jit(solution)/shard_map/ppermute | solution.py:312
  41.5 24.5 %copy-start.1 = (f32[1024]{0:T(1024)S(1)}, f32[1024]{0:T(1024)}, u32[]{:S(2)}) copy-start(f32[1024]{0:T(1024)} %param.11) | copy-start | bytes 12292
  41.5 8.3 %collective-permute-start.18 = (bf16[128,512]{1,0:T(8,128)(2,1)S(1)}, bf16[128,512]{1,0:T(8,128)(2,1)S(1)}, u32[]{:S(2)}, u32[]{:S(2)}) collective-permute-start(bf16[128,512]{1,0:T(8,128)(2,1)S(1)} %turn.8.after_ref.value_ref), channel_id=1, source_target_pairs={{0,2},{1,3},{2,0},{3,1},{4,6},{5,7},{6,4},{7,5},{8,10},{9,11},{10,... | collective-permute-start | bytes 393224 | tf_op jit(solution)/shard_map/ppermute | solution.py:312
  49.6 1.4 %collective-permute-start.17 = (bf16[128,512]{1,0:T(8,128)(2,1)S(1)}, bf16[128,512]{1,0:T(8,128)(2,1)S(1)}, u32[]{:S(2)}, u32[]{:S(2)}) collective-permute-start(bf16[128,512]{1,0:T(8,128)(2,1)S(1)} %turn.9.value_ref), channel_id=1, source_target_pairs={{0,1},{1,0},{2,3},{3,2},{4,5},{5,4},{6,7},{7,6},{8,9},{9,8},{10,11... | collective-permute-start | bytes 393224 | tf_op jit(solution)/shard_map/ppermute | solution.py:312
  49.8 5.9 %collective-permute-start.20 = (bf16[128,512]{1,0:T(8,128)(2,1)S(1)}, bf16[128,512]{1,0:T(8,128)(2,1)S(1)}, u32[]{:S(2)}, u32[]{:S(2)}) collective-permute-start(bf16[128,512]{1,0:T(8,128)(2,1)S(1)} %turn.10.value_ref), channel_id=1, source_target_pairs={{0,4},{1,5},{2,6},{3,7},{4,0},{5,1},{6,2},{7,3},{8,12},{9,13},{10,... | collective-permute-start | bytes 393224 | tf_op jit(solution)/shard_map/ppermute | solution.py:312
  51.1 5.6 %collective-permute-start.19 = (bf16[128,512]{1,0:T(8,128)(2,1)S(1)}, bf16[128,512]{1,0:T(8,128)(2,1)S(1)}, u32[]{:S(2)}, u32[]{:S(2)}) collective-permute-start(bf16[128,512]{1,0:T(8,128)(2,1)S(1)} %turn.11.value_ref), channel_id=1, source_target_pairs={{0,2},{1,3},{2,0},{3,1},{4,6},{5,7},{6,4},{7,5},{8,10},{9,11},{10,... | collective-permute-start | bytes 393224 | tf_op jit(solution)/shard_map/ppermute | solution.py:312
  56.8 5.7 %collective-permute-start.21 = (bf16[128,512]{1,0:T(8,128)(2,1)S(1)}, bf16[128,512]{1,0:T(8,128)(2,1)S(1)}, u32[]{:S(2)}, u32[]{:S(2)}) collective-permute-start(bf16[128,512]{1,0:T(8,128)(2,1)S(1)} %turn.13.value_ref), channel_id=1, source_target_pairs={{0,4},{1,5},{2,6},{3,7},{4,0},{5,1},{6,2},{7,3},{8,12},{9,13},{10,... | collective-permute-start | bytes 393224 | tf_op jit(solution)/shard_map/ppermute | solution.py:312
  57.7 8.2 %collective-permute-start.22 = (bf16[128,512]{1,0:T(8,128)(2,1)S(1)}, bf16[128,512]{1,0:T(8,128)(2,1)S(1)}, u32[]{:S(2)}, u32[]{:S(2)}) collective-permute-start(bf16[128,512]{1,0:T(8,128)(2,1)S(1)} %turn.12.value_ref), channel_id=1, source_target_pairs={{0,8},{1,9},{2,10},{3,11},{4,12},{5,13},{6,14},{7,15},{8,0},{9,1},... | collective-permute-start | bytes 393224 | tf_op jit(solution)/shard_map/ppermute | solution.py:312
  67.4 1.5 %collective-permute-start.23 = (bf16[16,4096]{1,0:T(8,128)(2,1)S(1)}, bf16[16,4096]{1,0:T(8,128)(2,1)S(1)}, u32[]{:S(2)}, u32[]{:S(2)}) collective-permute-start(bf16[16,4096]{1,0:T(8,128)(2,1)S(1)} %get-tuple-element.41), channel_id=1, source_target_pairs={{0,1},{1,0},{2,3},{3,2},{4,5},{5,4},{6,7},{7,6},{8,9},{9,8},{10,11... | collective-permute-start | bytes 393224 | tf_op jit(solution)/shard_map/ppermute | solution.py:312
  68.9 22.9 %copy-start = (bf16[8,8192]{1,0:T(8,128)(2,1)S(1)}, bf16[8,8192]{1,0:T(8,128)(2,1)}, u32[]{:S(2)}) copy-start(bf16[8,8192]{1,0:T(8,128)(2,1)} %tokens_ref.1) | copy-start | bytes 393220
  68.9 5.6 %collective-permute-start.25 = (bf16[112,4096]{1,0:T(8,128)(2,1)S(1)}, bf16[112,4096]{1,0:T(8,128)(2,1)S(1)}, u32[]{:S(2)}, u32[]{:S(2)}) collective-permute-start(bf16[112,4096]{1,0:T(8,128)(2,1)S(1)} %get-tuple-element.44), channel_id=1, source_target_pairs={{0,1},{1,0},{2,3},{3,2},{4,5},{5,4},{6,7},{7,6},{8,9},{9,8},{10,11... | collective-permute-start | bytes 2752520 | tf_op jit(solution)/shard_map/ppermute | solution.py:312
  69.5 5.0 %collective-permute-start.24 = (bf16[16,4096]{1,0:T(8,128)(2,1)S(1)}, bf16[16,4096]{1,0:T(8,128)(2,1)S(1)}, u32[]{:S(2)}, u32[]{:S(2)}) collective-permute-start(bf16[16,4096]{1,0:T(8,128)(2,1)S(1)} %far.1), channel_id=1, source_target_pairs={{0,4},{1,3},{4,8},{5,1},{8,12},{9,5},{12,14},{13,9},{14,10},{15,13... | collective-permute-start | bytes 393224 | tf_op jit(solution)/shard_map/ppermute | solution.py:303
  74.6 5.0 %collective-permute-start.26 = (bf16[16,4096]{1,0:T(8,128)(2,1)S(1)}, bf16[16,4096]{1,0:T(8,128)(2,1)S(1)}, u32[]{:S(2)}, u32[]{:S(2)}) collective-permute-start(bf16[16,4096]{1,0:T(8,128)(2,1)S(1)} %relay.6), channel_id=1, source_target_pairs={{0,4},{1,5},{4,8},{5,9},{8,12},{9,13},{12,14},{13,15},{14,10},{15,... | collective-permute-start | bytes 393224 | tf_op jit(solution)/shard_map/ppermute | solution.py:303
  74.7 5.0 %collective-permute-start.29 = (bf16[16,4096]{1,0:T(8,128)(2,1)S(1)}, bf16[16,4096]{1,0:T(8,128)(2,1)S(1)}, u32[]{:S(2)}, u32[]{:S(2)}) collective-permute-start(bf16[16,4096]{1,0:T(8,128)(2,1)S(1)} %relay.9), channel_id=1, source_target_pairs={{0,2},{1,3},{4,0},{5,1},{8,4},{9,5},{12,8},{13,9},{14,12},{15,13},... | collective-permute-start | bytes 393224 | tf_op jit(solution)/shard_map/ppermute | solution.py:303
  79.7 5.5 %collective-permute-start.27 = (bf16[16,4096]{1,0:T(8,128)(2,1)S(1)}, bf16[16,4096]{1,0:T(8,128)(2,1)S(1)}, u32[]{:S(2)}, u32[]{:S(2)}) collective-permute-start(bf16[16,4096]{1,0:T(8,128)(2,1)S(1)} %relay.7), channel_id=1, source_target_pairs={{0,4},{1,5},{4,8},{5,9},{8,12},{9,13},{12,14},{13,15},{14,10},{15,... | collective-permute-start | bytes 393224 | tf_op jit(solution)/shard_map/ppermute | solution.py:303
  79.8 5.5 %collective-permute-start.30 = (bf16[16,4096]{1,0:T(8,128)(2,1)S(1)}, bf16[16,4096]{1,0:T(8,128)(2,1)S(1)}, u32[]{:S(2)}, u32[]{:S(2)}) collective-permute-start(bf16[16,4096]{1,0:T(8,128)(2,1)S(1)} %relay.10), channel_id=1, source_target_pairs={{0,2},{1,3},{4,0},{5,1},{8,4},{9,5},{12,8},{13,9},{14,12},{15,13},... | collective-permute-start | bytes 393224 | tf_op jit(solution)/shard_map/ppermute | solution.py:303
  85.2 5.0 %collective-permute-start.28 = (bf16[16,4096]{1,0:T(8,128)(2,1)S(1)}, bf16[16,4096]{1,0:T(8,128)(2,1)S(1)}, u32[]{:S(2)}, u32[]{:S(2)}) collective-permute-start(bf16[16,4096]{1,0:T(8,128)(2,1)S(1)} %relay.8), channel_id=1, source_target_pairs={{0,4},{1,5},{4,8},{5,9},{8,12},{9,13},{12,14},{13,15},{14,10},{15,... | collective-permute-start | bytes 393224 | tf_op jit(solution)/shard_map/ppermute | solution.py:303
  85.3 5.0 %collective-permute-start.31 = (bf16[16,4096]{1,0:T(8,128)(2,1)S(1)}, bf16[16,4096]{1,0:T(8,128)(2,1)S(1)}, u32[]{:S(2)}, u32[]{:S(2)}) collective-permute-start(bf16[16,4096]{1,0:T(8,128)(2,1)S(1)} %relay.11), channel_id=1, source_target_pairs={{0,2},{1,3},{4,0},{5,1},{8,4},{9,5},{12,8},{13,9},{14,12},{15,13},... | collective-permute-start | bytes 393224 | tf_op jit(solution)/shard_map/ppermute | solution.py:303
  90.5 1.3 %collective-permute-start.32 = (bf16[8,4096]{1,0:T(8,128)(2,1)S(1)}, bf16[8,4096]{1,0:T(8,128)(2,1)S(1)}, u32[]{:S(2)}, u32[]{:S(2)}) collective-permute-start(bf16[8,4096]{1,0:T(8,128)(2,1)S(1)} %get-tuple-element.46), channel_id=1, source_target_pairs={{0,1},{1,0},{2,3},{3,2},{4,5},{5,4},{6,7},{7,6},{8,9},{9,8},{10,11... | collective-permute-start | bytes 196616 | tf_op jit(solution)/shard_map/ppermute | solution.py:312

commit v5 on v4

--- a/solution.py
+++ b/solution.py
@@ -72,97 +72,101 @@
     return lax.optimization_barrier((value, *others))[0]
 
 
-def load_kernel(at, weight_ref, after_ref, out_ref, sem):
-    cols = out_ref.shape[1]
-    at = lax.axis_index("hid") % 2 if at is None else at
-    start = pl.multiple_of(at * cols, cols)
-    copy = pltpu.make_async_copy(weight_ref.at[:, pl.ds(start, cols)], out_ref, sem)
-    copy.start()
-    copy.wait()
-
-
-def load(weight, after, cols, at):
-    rows = weight.shape[0]
+def load_kernel(places, after_ref, *refs):
+    count = len(places)
+    weights, outs, sems = refs[:count], refs[count:-1], refs[-1]
+    core = lax.axis_index("hid") % 2
+    copies = []
+    for piece, (own, pieces, at) in enumerate(places):
+        cols = outs[piece].shape[1]
+        side = 0 if own is None else core if own else 1 - core
+        start = pl.multiple_of((side * pieces + at) * cols, cols)
+        copies.append(
+            pltpu.make_async_copy(weights[piece].at[:, pl.ds(start, cols)], outs[piece], sems.at[piece])
+        )
+    for copy in copies:
+        copy.start()
+    for copy in copies:
+        copy.wait()
+
+
+def load(after, *wanted):
     hbm = pl.BlockSpec(memory_space=pltpu.HBM)
-    return pl.pallas_call(
-        functools.partial(load_kernel, at),
-        out_shape=jax.ShapeDtypeStruct((rows, cols), weight.dtype),
-        in_specs=[hbm, hbm],
-        out_specs=pl.BlockSpec(memory_space=pltpu.VMEM),
-        scratch_shapes=[pltpu.SemaphoreType.DMA],
+    shapes = []
+    for weight, own, pieces, _ in wanted:
+        cols = weight.shape[1] // (pieces if own is None else 2 * pieces)
+        shapes.append(jax.ShapeDtypeStruct((weight.shape[0], cols), weight.dtype))
+    return pl.pallas_call(
+        functools.partial(load_kernel, [place[1:] for place in wanted]),
+        out_shape=shapes,
+        in_specs=[hbm] * (1 + len(wanted)),
+        out_specs=[pl.BlockSpec(memory_space=pltpu.VMEM)] * len(wanted),
+        scratch_shapes=[pltpu.SemaphoreType.DMA((len(wanted),))],
         compiler_params=pltpu.CompilerParams(vmem_limit_bytes=1 * MIB),
-        cost_estimate=pl.CostEstimate(flops=0, bytes_accessed=2 * rows * cols, transcendentals=0),
+        cost_estimate=pl.CostEstimate(flops=0, bytes_accessed=2 * sum(s.size for s in shapes), transcendentals=0),
         name="load",
-    )(in_hbm(weight), after)
-
-
-def up_kernel(count, shifts, *refs):
+    )(after, *[in_hbm(place[0]) for place in wanted])
+
+
+def join_rows(parts, out_ref):
+    own = parts[0].shape[0]
+    for pair in range(len(parts) // 2):
+        both = [parts[2 * pair + k][...].astype(jnp.float32) for k in range(2)]
+        out_ref[2 * own * pair : 2 * own * (pair + 1), :] = jnp.concatenate(both, axis=0).astype(jnp.bfloat16)
+
+
+def up_kernel(shifts, first, *refs):
+    count = 2 * len(shifts)
+    if first:
+        gate_ref, up_ref, out_ref, rows_ref, hidden_ref = refs[count:]
+        join_rows(refs[:count], rows_ref)
+    else:
+        rows_ref, gate_ref, up_ref, out_ref, hidden_ref = refs
     me = lax.axis_index("hid")
     chip, core = me // 2, me % 2
-    spots = []
-    for shift in shifts:
-        there = 2 * ring_place(chip, shift, count // 2)
-        spots += [there + core, there + 1 - core]
-    parts, (down_hbm, out_a, out_b, down_ref, rows_ref, hidden_ref, sem) = refs[:count], refs[-7:]
-    gates, ups = refs[count:-7:2], refs[count + 1 : -7 : 2]
-    cols = down_ref.shape[1]
-    start = pl.multiple_of((1 - core) * cols, cols)
-    fetch = pltpu.make_async_copy(down_hbm.at[:, pl.ds(start, cols)], down_ref, sem)
-    fetch.start()
-    own = parts[0].shape[0]
-    for pair in range(count // 2):
-        both = [parts[2 * pair + k][...].astype(jnp.float32) for k in range(2)]
-        rows_ref[2 * own * pair : 2 * own * (pair + 1), :] = jnp.concatenate(both, axis=0).astype(jnp.bfloat16)
+    own = rows_ref.shape[0] // count
     turn = hadamard(BLOCK)
     values = rows_ref[...]
-    wide = gates[0].shape[1]
-    for at in range(len(gates)):
-        gate = jnp.dot(values, gates[at][...], preferred_element_type=jnp.float32)
-        up = jnp.dot(values, ups[at][...], preferred_element_type=jnp.float32)
-        hidden = gate / (1.0 + jnp.exp(-gate)) * up
-        high = hidden.astype(jnp.bfloat16)
-        low = (hidden - high.astype(jnp.float32)).astype(jnp.bfloat16)
-        for block in range(wide // BLOCK):
-            inner = slice(block * BLOCK, (block + 1) * BLOCK)
-            outer = slice(at * wide + block * BLOCK, at * wide + (block + 1) * BLOCK)
-            turned = jnp.dot(high[:, inner], turn, preferred_element_type=jnp.float32) + jnp.dot(
-                low[:, inner], turn, preferred_element_type=jnp.float32
-            )
-            for part in range(count):
-                spot = pl.multiple_of(spots[part] * own, own)
-                hidden_ref[pl.ds(spot, own), outer] = turned[part * own : (part + 1) * own]
-    half = out_a.shape[1]
-    out_a[...] = hidden_ref[:, :half].astype(jnp.bfloat16)
-    out_b[...] = hidden_ref[:, half:].astype(jnp.bfloat16)
-    fetch.wait()
-
-
-def up_project(shifts, parts, weights, down_weight):
-    count, own = len(parts), parts[0].shape[0]
-    depth = weights[0].shape[0]
-    width = weights[0].shape[1] * len(weights) // 2
-    rows = count * own
-    half = jax.ShapeDtypeStruct((rows, width // 2), jnp.bfloat16)
-    down = jax.ShapeDtypeStruct((down_weight.shape[0], down_weight.shape[1] // 2), down_weight.dtype)
+    gate = jnp.dot(values, gate_ref[...], preferred_element_type=jnp.float32)
+    up = jnp.dot(values, up_ref[...], preferred_element_type=jnp.float32)
+    hidden = gate / (1.0 + jnp.exp(-gate)) * up
+    high = hidden.astype(jnp.bfloat16)
+    low = (hidden - high.astype(jnp.float32)).astype(jnp.bfloat16)
+    for block in range(gate.shape[1] // BLOCK):
+        lanes = slice(block * BLOCK, (block + 1) * BLOCK)
+        turned = jnp.dot(high[:, lanes], turn, preferred_element_type=jnp.float32) + jnp.dot(
+            low[:, lanes], turn, preferred_element_type=jnp.float32
+        )
+        for part in range(count):
+            there = 2 * ring_place(chip, shifts[part // 2], count // 2)
+            there = there + core if part % 2 == 0 else there + 1 - core
+            spot = pl.multiple_of(there * own, own)
+            hidden_ref[pl.ds(spot, own), lanes] = turned[part * own : (part + 1) * own]
+    out_ref[...] = hidden_ref[...].astype(jnp.bfloat16)
+
+
+def up_project(shifts, parts, gate_weight, up_weight):
+    first = len(parts) > 1
+    depth, width = gate_weight.shape
+    rows = sum(part.shape[0] for part in parts)
     vmem = pl.BlockSpec(memory_space=pltpu.VMEM)
-    return pl.pallas_call(
-        functools.partial(up_kernel, count, shifts),
-        out_shape=[half, half] + [down],
-        in_specs=[vmem] * (count + len(weights)) + [pl.BlockSpec(memory_space=pltpu.HBM)],
-        out_specs=[vmem] * 3,
-        scratch_shapes=[
-            pltpu.VMEM((rows, depth), jnp.bfloat16),
-            pltpu.VMEM((rows, width), jnp.float32),
-            pltpu.SemaphoreType.DMA,
-        ],
-        compiler_params=pltpu.CompilerParams(vmem_limit_bytes=6 * MIB),
+    outs = [jax.ShapeDtypeStruct((rows, width), jnp.bfloat16)]
+    if first:
+        outs.append(jax.ShapeDtypeStruct((rows, depth), jnp.bfloat16))
+    return pl.pallas_call(
+        functools.partial(up_kernel, shifts, first),
+        out_shape=outs,
+        in_specs=[vmem] * (len(parts) + 2),
+        out_specs=[vmem] * len(outs),
+        scratch_shapes=[pltpu.VMEM((rows, width), jnp.float32)],
+        compiler_params=pltpu.CompilerParams(vmem_limit_bytes=4 * MIB + 2 * rows * depth),
         cost_estimate=pl.CostEstimate(flops=4 * rows * depth * width, bytes_accessed=0, transcendentals=rows * width),
         name="up_project",
-    )(*parts, *weights, in_hbm(down_weight))
-
-
-def down_kernel(blocks, chips, scale, a_ref, b_ref, clip_ref, weight_ref, *refs):
-    outs, (rows_ref, mixed_ref) = refs[:-2], refs[-2:]
+    )(*parts, gate_weight, up_weight)
+
+
+def down_kernel(blocks, chips, scale, a_ref, b_ref, clip_ref, *refs):
+    weights, outs, (rows_ref, mixed_ref) = refs[:-4], refs[-4:-2], refs[-2:]
     half = a_ref.shape[1]
     rows_ref[:, :half] = a_ref[...].astype(jnp.float32)
     rows_ref[:, half:] = b_ref[...].astype(jnp.float32)
@@ -183,16 +187,18 @@
     for chip in range(chips):
         spot = pl.multiple_of(ring_place(me // 2, chip + chips // 2, chips) * each, each)
         mixed_ref[chip * each : (chip + 1) * each, :] = rows_ref[pl.ds(spot, each), :].astype(jnp.bfloat16)
-    product = jnp.dot(mixed_ref[...], weight_ref[...], preferred_element_type=jnp.float32)
-    first = 0
-    for out_ref in outs:
-        out_ref[...] = product[first : first + out_ref.shape[0]].astype(jnp.bfloat16)
-        first += out_ref.shape[0]
-
-
-def down_project(a, b, clip_scale, weight, chips, total):
+    wide = weights[0].shape[1]
+    for at, weight_ref in enumerate(weights):
+        product = jnp.dot(mixed_ref[...], weight_ref[...], preferred_element_type=jnp.float32)
+        first = 0
+        for out_ref in outs:
+            out_ref[:, at * wide : (at + 1) * wide] = product[first : first + out_ref.shape[0]].astype(jnp.bfloat16)
+            first += out_ref.shape[0]
+
+
+def down_project(a, b, clip_scale, weights, chips, total):
     rows = a.shape[0]
-    width, depth = weight.shape
+    width, depth = weights[0].shape[0], weights[0].shape[1] * len(weights)
     vmem = pl.BlockSpec(memory_space=pltpu.VMEM)
     outs = [
         jax.ShapeDtypeStruct((count, depth), jnp.bfloat16) for count in (rows // chips, rows - rows // chips)
@@ -200,13 +206,13 @@
     return pl.pallas_call(
         functools.partial(down_kernel, width // BLOCK, chips, total**-0.5),
         out_shape=outs,
-        in_specs=[vmem] * 4,
+        in_specs=[vmem] * (3 + len(weights)),
         out_specs=[vmem] * 2,
         scratch_shapes=[pltpu.VMEM((rows, width), jnp.float32), pltpu.VMEM((rows, width), jnp.bfloat16)],
         compiler_params=pltpu.CompilerParams(vmem_limit_bytes=8 * MIB),
         cost_estimate=pl.CostEstimate(flops=2 * rows * depth * width, bytes_accessed=0, transcendentals=0),
         name="down_project",
-    )(a, b, clip_scale, weight)
+    )(a, b, clip_scale, *weights)
 
 
 def pick_kernel(even_ref, odd_ref, out_ref):
@@ -313,32 +319,38 @@
 
     normed = normalize(tokens, norm_gain)
     width = gate_weight.shape[1]
-    wide = max(BLOCK, width // 2)
-    wanted = [(weight, at) for at in range(width // wide) for weight in (gate_weight, up_weight)]
-    weights = []
-
-    def beside(after, arrived, *others):
+    pieces = width // max(BLOCK, width // 2)
+    wanted = [(weight, None, pieces, at) for at in range(pieces) for weight in (gate_weight, up_weight)]
+    weights, down_theirs = [], []
+
+    def beside(after, arrived):
         if len(weights) < len(wanted):
-            weight, at = wanted[len(weights)]
-            weights.append(load(weight, after, wide, at))
-            others = (weights[-1], *others)
-        return once(arrived, *others) if others else arrived
-
-    parts, shifts = [normed, cross(normed)], [0]
+            at = len(weights)
+            columns, below = load(after, wanted[at], (down_weight, False, len(wanted), at))
+            weights.append(columns)
+            down_theirs.append(below)
+            arrived = once(arrived, columns, below)
+        return arrived
+
+    mine, shifts = [normed], [0]
     ahead = behind = normed
     for step in range(1, steps):
-        after, done = behind, parts[-1:] if step == 1 else parts[-3::2]
+        after = behind
         ahead, behind = right(ahead), left(behind)
-        behind = beside(after, behind, *done)
-        parts += [ahead, cross(ahead), behind, cross(behind)]
+        behind = beside(after, behind)
+        mine += [ahead, behind]
         shifts += [-step, step]
-    far = beside(ahead, hop(both(pick_kernel, ahead, behind, "pick"), 1, -1), *parts[-3::2])
-    parts += [far, cross(far)]
+    mine.append(beside(ahead, hop(both(pick_kernel, ahead, behind, "pick"), 1, -1)))
     shifts.append(steps)
     while len(weights) < len(wanted):
-        parts[0] = beside(parts[0], parts[0])
-
-    half_a, half_b, down_theirs = up_project(shifts, parts, weights, down_weight)
+        mine[0] = beside(mine[0], mine[0])
+    parts = [block for own in mine for block in (own, cross(own))]
+
+    half_b, joined = up_project(shifts, parts, *weights[-2:])
+    if pieces == 1:
+        half_a, half_b = jnp.split(half_b, 2, axis=1)
+    else:
+        (half_a,) = up_project(shifts, [joined], *weights[:2])
 
     def turn(value, mask, *others):
         return both(functools.partial(turn_kernel, mask), value, once(cross(value, mask), *others), "turn")
@@ -348,8 +360,12 @@
         first, second = masks[stage - 1], masks[stage]
         if stage == 0:
             half_b = turn(half_b, second)
-            down_own = load(down_weight, half_b, down_weight.shape[1] // 2, None)
+            (down_own,) = load(half_b, (down_weight, True, 1, 0))
+            early = turn(half_b, masks[1], down_own)
             half_a = turn(half_a, first, half_b, down_own)
+        elif stage == 1:
+            half_b = early
+            half_a = turn(half_a, first, early)
         elif stage < len(masks) - 1:
             half_b = turn(half_b, second, half_a)
             half_a = turn(half_a, first, half_b)
@@ -361,7 +377,7 @@
     limits = clip_scale.reshape(1, -1)
     theirs_far, theirs = down_project(half_a, half_b, limits, down_theirs, chips, total)
     arrived_far = cross(theirs_far)
-    own_far, own = down_project(half_a, half_b, limits, down_own, chips, total)
+    own_far, own = down_project(half_a, half_b, limits, [down_own], chips, total)
     arrived = cross(once(theirs, own, arrived_far))
     rows, wide = own_far.shape
     part = jax.ShapeDtypeStruct((rows, wide), jnp.bfloat16)

time: 92.8 us -> 90 us (0.970)
  waiting for transfers between devices: 40 us -> 28.4 us
  starting transfers between devices: 21 us -> 30.2 us
    ppermute x19, waiting for transfers between devices: 20.5 us -> 14.3 us  [cross(): return lax.ppermute(value, 'hid', [(d, d ^ mask) for d in range(count)])]
    ppermute x19, starting transfers between devices: 6.81 us -> 12.4 us  [cross(): return lax.ppermute(value, 'hid', [(d, d ^ mask) for d in range(count)])]
    ppermute x14, waiting for transfers between devices: 19.5 us -> 14.1 us  [hop(): return lax.ppermute(value, 'hid', pairs)]
    ppermute x14, starting transfers between devices: 14.2 us -> 17.8 us  [hop(): return lax.ppermute(value, 'hid', pairs)]
    pallas_call x6 -> x7, Pallas kernels: 25.7 us -> 25.5 us  [the longest x5 20 us: load(): pl.pallas_call(functools.partial(load_kernel, [place[1:] for place in wan...]
  transfers between devices with their start and end apart: 33 -> 33, of which waited for: 19 -> 16; matrix products, arithmetic and copies ran while one was open for 0% -> 0% of each run, Pallas kernels for 21% -> 28%
where the time goes in v5:
time: 90 us; the launch traced here: 89.8 us
  Pallas kernels  31 us (34%)
  starting transfers between devices  30.2 us (34%)
  waiting for transfers between devices  28.4 us (32%)
    pallas_call x5, Pallas kernels, load(): pl.pallas_call(functools.partial(load_kernel, [place[1:] for place in wan...  20 us
    ppermute x14, starting transfers between devices, hop(): return lax.ppermute(value, 'hid', pairs)  17.8 us
    ppermute x19, waiting for transfers between devices, cross(): return lax.ppermute(value, 'hid', [(d, d ^ mask) for d in range(count)])  14.3 us
    ppermute x14, waiting for transfers between devices, hop(): return lax.ppermute(value, 'hid', pairs)  14.1 us
    ppermute x19, starting transfers between devices, cross(): return lax.ppermute(value, 'hid', [(d, d ^ mask) for d in range(count)])  12.4 us
    pallas_call x2, Pallas kernels, up_project(): pl.pallas_call(functools.partial(up_kernel, shifts, first), out_shape=out...  5.49 us
    pallas_call x2, Pallas kernels, down_project(): pl.pallas_call(functools.partial(down_kernel, width // BLOCK, chips, tota...  2.85 us
  transfers between devices with their start and end apart: 33, of which 16 were waited for; matrix products, arithmetic and copies ran while one was open for 0% of the time, Pallas kernels for 28%

profile of v5, /device:TPU:0, one launch (start us, length us, event | category | flops | bytes accessed | tf_op | source)
XLA Modules:
  0.0 89.8 jit_solution(5861973476360816139)
XLA Ops:
  0.0 1.1 %normalize.1.after_ref.refs_0_ = bf16[8,8192]{1,0:T(8,128)(2,1)S(1)} custom-call(bf16[8,8192]{1,0:T(8,128)(2,1)} %tokens_ref.1, f32[1,8192]{1,0:T(1,128)} %bitcast.4), custom_call_target="tpu_custom_call" | custom-call | flops 524288 | bytes 262144 | tf_op jit(solution)/shard_map/normalize/pallas_call | solution.py:45
  1.1 3.0 %collective-permute-start.3 = (bf16[8,8192]{1,0:T(8,128)(2,1)S(1)}, bf16[8,8192]{1,0:T(8,128)(2,1)S(1)}, u32[]{:S(2)}, u32[]{:S(2)}) collective-permute-start(bf16[8,8192]{1,0:T(8,128)(2,1)S(1)} %normalize.1.after_ref.refs_0_), channel_id=1, source_target_pairs={{0,2},{1,3},{4,0},{5,1},{8,4},{9,5},{12,8},{13,9},{14,12},{15,13},... | collective-permute-start | bytes 393224 | tf_op jit(solution)/shard_map/ppermute | solution.py:309
  4.1 0.1 collective-permute-start.1
  4.3 4.2 %load.5 = (bf16[8192,512]{1,0:T(8,128)(2,1)S(1)}, bf16[1024,1024]{1,0:T(8,128)(2,1)S(1)}) custom-call(bf16[8,8192]{1,0:T(8,128)(2,1)S(1)} %normalize.1.after_ref.refs_0_, bf16[8192,1024]{1,0:T(8,128)(2,1)} %refs_0_.7, bf16[1024,8192]{1,0:T(8,128)(2,1)} %refs_0_.9), custom_call_target="tpu_custom_call" | custom-call | bytes 10485760 | tf_op jit(solution)/shard_map/load/pallas_call | solution.py:99
  8.4 2.0 %collective-permute-start.7 = (bf16[8,8192]{1,0:T(8,128)(2,1)S(1)}, bf16[8,8192]{1,0:T(8,128)(2,1)S(1)}, u32[]{:S(2)}, u32[]{:S(2)}) collective-permute-start(bf16[8,8192]{1,0:T(8,128)(2,1)S(1)} %collective-permute-done.3.after_ref.refs_4_), channel_id=1, source_target_pairs={{0,2},{1,3},{4,0},{5,1},{8,4},{9,5},{12,8},{13,9},{14,12},{15,13},... | collective-permute-start | bytes 393224 | tf_op jit(solution)/shard_map/ppermute | solution.py:309
  10.4 0.1 collective-permute-start.5
  10.5 4.2 %load.6 = (bf16[8192,512]{1,0:T(8,128)(2,1)S(1)}, bf16[1024,1024]{1,0:T(8,128)(2,1)S(1)}) custom-call(bf16[8,8192]{1,0:T(8,128)(2,1)S(1)} %collective-permute-done.3.after_ref.refs_4_, bf16[8192,1024]{1,0:T(8,128)(2,1)} %refs_0_.8, bf16[1024,8192]{1,0:T(8,128)(2,1)} %refs_0_.9), custom_call_target="tpu_custom_call" | custom-call | bytes 10485760 | tf_op jit(solution)/shard_map/load/pallas_call | solution.py:99
  14.7 1.9 %collective-permute-start.11 = (bf16[8,8192]{1,0:T(8,128)(2,1)S(1)}, bf16[8,8192]{1,0:T(8,128)(2,1)S(1)}, u32[]{:S(2)}, u32[]{:S(2)}) collective-permute-start(bf16[8,8192]{1,0:T(8,128)(2,1)S(1)} %collective-permute-done.7.after_ref.refs_8_), channel_id=1, source_target_pairs={{0,2},{1,3},{4,0},{5,1},{8,4},{9,5},{12,8},{13,9},{14,12},{15,13},... | collective-permute-start | bytes 393224 | tf_op jit(solution)/shard_map/ppermute | solution.py:309
  16.7 0.1 collective-permute-start.9
  16.8 4.1 %load.7 = (bf16[8192,512]{1,0:T(8,128)(2,1)S(1)}, bf16[1024,1024]{1,0:T(8,128)(2,1)S(1)}) custom-call(bf16[8,8192]{1,0:T(8,128)(2,1)S(1)} %collective-permute-done.7.after_ref.refs_8_, bf16[8192,1024]{1,0:T(8,128)(2,1)} %refs_0_.7, bf16[1024,8192]{1,0:T(8,128)(2,1)} %refs_0_.9), custom_call_target="tpu_custom_call" | custom-call | bytes 10485760 | tf_op jit(solution)/shard_map/load/pallas_call | solution.py:99
  21.0 0.7 collective-permute-done.9.even_ref.after_ref.refs_10_
  21.7 1.3 %collective-permute-start.13 = (bf16[8,8192]{1,0:T(8,128)(2,1)S(1)}, bf16[8,8192]{1,0:T(8,128)(2,1)S(1)}, u32[]{:S(2)}, u32[]{:S(2)}) collective-permute-start(bf16[8,8192]{1,0:T(8,128)(2,1)S(1)} %pick.1), channel_id=1, source_target_pairs={{0,4},{1,3},{4,8},{5,1},{8,12},{9,5},{12,14},{13,9},{14,10},{15,13... | collective-permute-start | bytes 393224 | tf_op jit(solution)/shard_map/ppermute | solution.py:309
  23.0 0.5 collective-permute-start.2
  23.5 0.5 collective-permute-start.8
  24.0 4.1 %load.8 = (bf16[8192,512]{1,0:T(8,128)(2,1)S(1)}, bf16[1024,1024]{1,0:T(8,128)(2,1)S(1)}) custom-call(bf16[8,8192]{1,0:T(8,128)(2,1)S(1)} %collective-permute-done.9.even_ref.after_ref.refs_10_, bf16[8192,1024]{1,0:T(8,128)(2,1)} %refs_0_.8, bf16[1024,8192]{1,0:T(8,128)(2,1)} %refs_0_.9), custom_call_target="tpu_custom_call" | custom-call | bytes 10485760 | tf_op jit(solution)/shard_map/load/pallas_call | solution.py:99
  28.2 0.1 collective-permute-start.6
  28.2 0.5 collective-permute-start.12
  28.7 0.1 collective-permute-start.10
  28.8 0.4 collective-permute-start.14
  29.3 0.3 collective-permute-done.6.refs_7_
  29.6 0.5 collective-permute-done.10.refs_11_
  30.1 0.2 collective-permute-done.14.refs_15_
  30.3 2.8 %up_project.2 = (bf16[128,512]{1,0:T(8,128)(2,1)S(1)}, bf16[128,8192]{1,0:T(8,128)(2,1)S(1)}) custom-call(bf16[8,8192]{1,0:T(8,128)(2,1)S(1)} %normalize.1.after_ref.refs_0_, bf16[8,8192]{1,0:T(8,128)(2,1)S(1)} %collective-permute-done.refs_1_, bf16[8,8192]{1,0:T(8,128)(2,1)S(1)} %collective-permute-done.1.refs_2_, ...), custom_call_target="tpu_custom_call" | custom-call | flops 2147483648 | tf_op jit(solution)/shard_map/up_project/pallas_call | solution.py:156
  33.0 0.4 collective-permute-start.16
  33.4 2.7 %up_project.3.value_ref = bf16[128,512]{1,0:T(8,128)(2,1)S(1)} custom-call(bf16[128,8192]{1,0:T(8,128)(2,1)S(1)} %get-tuple-element.45.refs_0_, bf16[8192,512]{1,0:T(8,128)(2,1)S(1)} %get-tuple-element.33.refs_1_, bf16[8192,512]{1,0:T(8,128)(2,1)S(1)} %get-tuple-element.36.refs_2_), custom_call_target="tpu_custom_call" | custom-call | flops 2147483648 | tf_op jit(solution)/shard_map/up_project/pallas_call | solution.py:156
  36.2 2.7 %collective-permute-start.15 = (bf16[128,512]{1,0:T(8,128)(2,1)S(1)}, bf16[128,512]{1,0:T(8,128)(2,1)S(1)}, u32[]{:S(2)}, u32[]{:S(2)}) collective-permute-start(bf16[128,512]{1,0:T(8,128)(2,1)S(1)} %up_project.3.value_ref), channel_id=1, source_target_pairs={{0,8},{1,9},{2,10},{3,11},{4,12},{5,13},{6,14},{7,15},{8,0},{9,1},... | collective-permute-start | bytes 393224 | tf_op jit(solution)/shard_map/ppermute | solution.py:318
  38.9 0.8 collective-permute-start.18
  39.7 3.4 %load.9.refs_0_ = bf16[1024,4096]{1,0:T(8,128)(2,1)S(1)} custom-call(bf16[128,512]{1,0:T(8,128)(2,1)S(1)} %turn.8.after_ref.value_ref, bf16[1024,8192]{1,0:T(8,128)(2,1)} %refs_0_.9), custom_call_target="tpu_custom_call" | custom-call | bytes 8388608 | tf_op jit(solution)/shard_map/load/pallas_call | solution.py:99
  43.1 2.4 %collective-permute-done.15.other_ref = bf16[128,512]{1,0:T(8,128)(2,1)S(1)} collective-permute-done((bf16[128,512]{1,0:T(8,128)(2,1)S(1)}, bf16[128,512]{1,0:T(8,128)(2,1)S(1)}, u32[]{:S(2)}, u32[]{:S(2)}) %collective-permute-start.15) | collective-permute-done | bytes 131104 | tf_op jit(solution)/shard_map/ppermute | solution.py:318
  45.6 0.1 collective-permute-start.17
  45.7 0.8 collective-permute-start.20
  46.5 0.5 collective-permute-done.17.other_ref
  47.0 0.8 collective-permute-start.19
  47.8 3.8 %collective-permute-done.20.other_ref = bf16[128,512]{1,0:T(8,128)(2,1)S(1)} collective-permute-done((bf16[128,512]{1,0:T(8,128)(2,1)S(1)}, bf16[128,512]{1,0:T(8,128)(2,1)S(1)}, u32[]{:S(2)}, u32[]{:S(2)}) %collective-permute-start.20) | collective-permute-done | bytes 131104 | tf_op jit(solution)/shard_map/ppermute | solution.py:318
  51.7 0.9 %collective-permute-done.19.other_ref = bf16[128,512]{1,0:T(8,128)(2,1)S(1)} collective-permute-done((bf16[128,512]{1,0:T(8,128)(2,1)S(1)}, bf16[128,512]{1,0:T(8,128)(2,1)S(1)}, u32[]{:S(2)}, u32[]{:S(2)}) %collective-permute-start.19) | collective-permute-done | bytes 131104 | tf_op jit(solution)/shard_map/ppermute | solution.py:318
  52.7 0.9 %collective-permute-start.21 = (bf16[128,512]{1,0:T(8,128)(2,1)S(1)}, bf16[128,512]{1,0:T(8,128)(2,1)S(1)}, u32[]{:S(2)}, u32[]{:S(2)}) collective-permute-start(bf16[128,512]{1,0:T(8,128)(2,1)S(1)} %turn.13.value_ref), channel_id=1, source_target_pairs={{0,4},{1,5},{2,6},{3,7},{4,0},{5,1},{6,2},{7,3},{8,12},{9,13},{10,... | collective-permute-start | bytes 393224 | tf_op jit(solution)/shard_map/ppermute | solution.py:318
  53.7 3.2 %collective-permute-start.22 = (bf16[128,512]{1,0:T(8,128)(2,1)S(1)}, bf16[128,512]{1,0:T(8,128)(2,1)S(1)}, u32[]{:S(2)}, u32[]{:S(2)}) collective-permute-start(bf16[128,512]{1,0:T(8,128)(2,1)S(1)} %turn.12.value_ref), channel_id=1, source_target_pairs={{0,8},{1,9},{2,10},{3,11},{4,12},{5,13},{6,14},{7,15},{8,0},{9,1},... | collective-permute-start | bytes 393224 | tf_op jit(solution)/shard_map/ppermute | solution.py:318
  56.8 2.9 %collective-permute-done.21.other_ref = bf16[128,512]{1,0:T(8,128)(2,1)S(1)} collective-permute-done((bf16[128,512]{1,0:T(8,128)(2,1)S(1)}, bf16[128,512]{1,0:T(8,128)(2,1)S(1)}, u32[]{:S(2)}, u32[]{:S(2)}) %collective-permute-start.21) | collective-permute-done | bytes 131104 | tf_op jit(solution)/shard_map/ppermute | solution.py:318
  59.8 1.4 %collective-permute-done.22.other_ref = bf16[128,512]{1,0:T(8,128)(2,1)S(1)} collective-permute-done((bf16[128,512]{1,0:T(8,128)(2,1)S(1)}, bf16[128,512]{1,0:T(8,128)(2,1)S(1)}, u32[]{:S(2)}, u32[]{:S(2)}) %collective-permute-start.22) | collective-permute-done | bytes 131104 | tf_op jit(solution)/shard_map/ppermute | solution.py:318
  61.2 1.4 %down_project.3 = (bf16[16,4096]{1,0:T(8,128)(2,1)S(1)}, bf16[112,4096]{1,0:T(8,128)(2,1)S(1)}) custom-call(bf16[128,512]{1,0:T(8,128)(2,1)S(1)} %turn.14.a_ref, bf16[128,512]{1,0:T(8,128)(2,1)S(1)} %turn.15.b_ref, f32[1,1024]{1,0:T(1,128)S(1)} %bitcast.2, bf16[1024,1024]{1,0:T(8,128)(2,1)S(1)} %get-tuple-element.34.refs_0_, ...), custom_call_target="tpu_custom_call" | custom-call | flops 1073741824 | tf_op jit(solution)/shard_map/down_project/pallas_call | solution.py:206
  62.7 0.1 collective-permute-start.23
  62.7 1.4 %down_project.2 = (bf16[16,4096]{1,0:T(8,128)(2,1)S(1)}, bf16[112,4096]{1,0:T(8,128)(2,1)S(1)}) custom-call(bf16[128,512]{1,0:T(8,128)(2,1)S(1)} %turn.14.a_ref, bf16[128,512]{1,0:T(8,128)(2,1)S(1)} %turn.15.b_ref, f32[1,1024]{1,0:T(1,128)S(1)} %bitcast.3, bf16[1024,4096]{1,0:T(8,128)(2,1)S(1)} %load.9.refs_0_), custom_call_target="tpu_custom_call" | custom-call | flops 1073741824 | tf_op jit(solution)/shard_map/down_project/pallas_call | solution.py:206
  64.2 0.6 collective-permute-start.25
  64.8 2.1 %collective-permute-start.24 = (bf16[16,4096]{1,0:T(8,128)(2,1)S(1)}, bf16[16,4096]{1,0:T(8,128)(2,1)S(1)}, u32[]{:S(2)}, u32[]{:S(2)}) collective-permute-start(bf16[16,4096]{1,0:T(8,128)(2,1)S(1)} %far.1), channel_id=1, source_target_pairs={{0,4},{1,3},{4,8},{5,1},{8,12},{9,5},{12,14},{13,9},{14,10},{15,13... | collective-permute-start | bytes 393224 | tf_op jit(solution)/shard_map/ppermute | solution.py:309
  66.9 2.9 %collective-permute-done.24.arrived_in = bf16[16,4096]{1,0:T(8,128)(2,1)S(1)} collective-permute-done((bf16[16,4096]{1,0:T(8,128)(2,1)S(1)}, bf16[16,4096]{1,0:T(8,128)(2,1)S(1)}, u32[]{:S(2)}, u32[]{:S(2)}) %collective-permute-start.24) | collective-permute-done | bytes 131104 | tf_op jit(solution)/shard_map/ppermute | solution.py:309
  69.8 0.1 relay.6
  69.9 2.1 %collective-permute-start.26 = (bf16[16,4096]{1,0:T(8,128)(2,1)S(1)}, bf16[16,4096]{1,0:T(8,128)(2,1)S(1)}, u32[]{:S(2)}, u32[]{:S(2)}) collective-permute-start(bf16[16,4096]{1,0:T(8,128)(2,1)S(1)} %relay.6), channel_id=1, source_target_pairs={{0,4},{1,5},{4,8},{5,9},{8,12},{9,13},{12,14},{13,15},{14,10},{15,... | collective-permute-start | bytes 393224 | tf_op jit(solution)/shard_map/ppermute | solution.py:309
  72.0 0.1 relay.9
  72.1 0.1 collective-permute-start.29
  72.2 2.7 %collective-permute-done.26.arrived_in = bf16[16,4096]{1,0:T(8,128)(2,1)S(1)} collective-permute-done((bf16[16,4096]{1,0:T(8,128)(2,1)S(1)}, bf16[16,4096]{1,0:T(8,128)(2,1)S(1)}, u32[]{:S(2)}, u32[]{:S(2)}) %collective-permute-start.26) | collective-permute-done | bytes 131104 | tf_op jit(solution)/shard_map/ppermute | solution.py:309
  74.9 0.1 relay.7
  75.0 2.1 %collective-permute-start.27 = (bf16[16,4096]{1,0:T(8,128)(2,1)S(1)}, bf16[16,4096]{1,0:T(8,128)(2,1)S(1)}, u32[]{:S(2)}, u32[]{:S(2)}) collective-permute-start(bf16[16,4096]{1,0:T(8,128)(2,1)S(1)} %relay.7), channel_id=1, source_target_pairs={{0,4},{1,5},{4,8},{5,9},{8,12},{9,13},{12,14},{13,15},{14,10},{15,... | collective-permute-start | bytes 393224 | tf_op jit(solution)/shard_map/ppermute | solution.py:309
  77.1 0.1 relay.10
  77.2 0.1 collective-permute-start.30
  77.2 2.8 %collective-permute-done.27.arrived_in = bf16[16,4096]{1,0:T(8,128)(2,1)S(1)} collective-permute-done((bf16[16,4096]{1,0:T(8,128)(2,1)S(1)}, bf16[16,4096]{1,0:T(8,128)(2,1)S(1)}, u32[]{:S(2)}, u32[]{:S(2)}) %collective-permute-start.27) | collective-permute-done | bytes 131104 | tf_op jit(solution)/shard_map/ppermute | solution.py:309
  80.0 0.1 relay.8
  80.1 2.5 %collective-permute-start.28 = (bf16[16,4096]{1,0:T(8,128)(2,1)S(1)}, bf16[16,4096]{1,0:T(8,128)(2,1)S(1)}, u32[]{:S(2)}, u32[]{:S(2)}) collective-permute-start(bf16[16,4096]{1,0:T(8,128)(2,1)S(1)} %relay.8), channel_id=1, source_target_pairs={{0,4},{1,5},{4,8},{5,9},{8,12},{9,13},{12,14},{13,15},{14,10},{15,... | collective-permute-start | bytes 393224 | tf_op jit(solution)/shard_map/ppermute | solution.py:309
  82.7 0.1 collective-permute-start.31
  82.7 2.4 %collective-permute-done.28.ahead_in = bf16[16,4096]{1,0:T(8,128)(2,1)S(1)} collective-permute-done((bf16[16,4096]{1,0:T(8,128)(2,1)S(1)}, bf16[16,4096]{1,0:T(8,128)(2,1)S(1)}, u32[]{:S(2)}, u32[]{:S(2)}) %collective-permute-start.28) | collective-permute-done | bytes 131104 | tf_op jit(solution)/shard_map/ppermute | solution.py:309
  85.1 2.6 %collective-permute-done.31.behind_in = bf16[16,4096]{1,0:T(8,128)(2,1)S(1)} collective-permute-done((bf16[16,4096]{1,0:T(8,128)(2,1)S(1)}, bf16[16,4096]{1,0:T(8,128)(2,1)S(1)}, u32[]{:S(2)}, u32[]{:S(2)}) %collective-permute-start.31) | collective-permute-done | bytes 131104 | tf_op jit(solution)/shard_map/ppermute | solution.py:309
  87.7 0.1 last.1
  87.8 0.1 collective-permute-start.32
  87.9 1.2 %collective-permute-done.32.take_ref = bf16[8,4096]{1,0:T(8,128)(2,1)S(1)} collective-permute-done((bf16[8,4096]{1,0:T(8,128)(2,1)S(1)}, bf16[8,4096]{1,0:T(8,128)(2,1)S(1)}, u32[]{:S(2)}, u32[]{:S(2)}) %collective-permute-start.32) | collective-permute-done | bytes 65568 | tf_op jit(solution)/shard_map/ppermute | solution.py:318
  89.1 0.7 mix.1
  (34 shorter events, 0.5 us)
Async XLA Ops:
  1.1 7.3 %collective-permute-start.3 = (bf16[8,8192]{1,0:T(8,128)(2,1)S(1)}, bf16[8,8192]{1,0:T(8,128)(2,1)S(1)}, u32[]{:S(2)}, u32[]{:S(2)}) collective-permute-start(bf16[8,8192]{1,0:T(8,128)(2,1)S(1)} %normalize.1.after_ref.refs_0_), channel_id=1, source_target_pairs={{0,2},{1,3},{4,0},{5,1},{8,4},{9,5},{12,8},{13,9},{14,12},{15,13},... | collective-permute-start | bytes 393224 | tf_op jit(solution)/shard_map/ppermute | solution.py:309
  4.1 6.3 %collective-permute-start.1 = (bf16[8,8192]{1,0:T(8,128)(2,1)S(1)}, bf16[8,8192]{1,0:T(8,128)(2,1)S(1)}, u32[]{:S(2)}, u32[]{:S(2)}) collective-permute-start(bf16[8,8192]{1,0:T(8,128)(2,1)S(1)} %normalize.1.after_ref.refs_0_), channel_id=1, source_target_pairs={{0,4},{1,5},{4,8},{5,9},{8,12},{9,13},{12,14},{13,15},{14,10},{15,... | collective-permute-start | bytes 393224 | tf_op jit(solution)/shard_map/ppermute | solution.py:309
  8.4 6.3 %collective-permute-start.7 = (bf16[8,8192]{1,0:T(8,128)(2,1)S(1)}, bf16[8,8192]{1,0:T(8,128)(2,1)S(1)}, u32[]{:S(2)}, u32[]{:S(2)}) collective-permute-start(bf16[8,8192]{1,0:T(8,128)(2,1)S(1)} %collective-permute-done.3.after_ref.refs_4_), channel_id=1, source_target_pairs={{0,2},{1,3},{4,0},{5,1},{8,4},{9,5},{12,8},{13,9},{14,12},{15,13},... | collective-permute-start | bytes 393224 | tf_op jit(solution)/shard_map/ppermute | solution.py:309
  10.4 6.3 %collective-permute-start.5 = (bf16[8,8192]{1,0:T(8,128)(2,1)S(1)}, bf16[8,8192]{1,0:T(8,128)(2,1)S(1)}, u32[]{:S(2)}, u32[]{:S(2)}) collective-permute-start(bf16[8,8192]{1,0:T(8,128)(2,1)S(1)} %collective-permute-done.1.refs_2_), channel_id=1, source_target_pairs={{0,4},{1,5},{4,8},{5,9},{8,12},{9,13},{12,14},{13,15},{14,10},{15,... | collective-permute-start | bytes 393224 | tf_op jit(solution)/shard_map/ppermute | solution.py:309
  14.7 6.2 %collective-permute-start.11 = (bf16[8,8192]{1,0:T(8,128)(2,1)S(1)}, bf16[8,8192]{1,0:T(8,128)(2,1)S(1)}, u32[]{:S(2)}, u32[]{:S(2)}) collective-permute-start(bf16[8,8192]{1,0:T(8,128)(2,1)S(1)} %collective-permute-done.7.after_ref.refs_8_), channel_id=1, source_target_pairs={{0,2},{1,3},{4,0},{5,1},{8,4},{9,5},{12,8},{13,9},{14,12},{15,13},... | collective-permute-start | bytes 393224 | tf_op jit(solution)/shard_map/ppermute | solution.py:309
  16.7 5.0 %collective-permute-start.9 = (bf16[8,8192]{1,0:T(8,128)(2,1)S(1)}, bf16[8,8192]{1,0:T(8,128)(2,1)S(1)}, u32[]{:S(2)}, u32[]{:S(2)}) collective-permute-start(bf16[8,8192]{1,0:T(8,128)(2,1)S(1)} %collective-permute-done.5.refs_6_), channel_id=1, source_target_pairs={{0,4},{1,5},{4,8},{5,9},{8,12},{9,13},{12,14},{13,15},{14,10},{15,... | collective-permute-start | bytes 393224 | tf_op jit(solution)/shard_map/ppermute | solution.py:309
  21.7 6.5 %collective-permute-start.13 = (bf16[8,8192]{1,0:T(8,128)(2,1)S(1)}, bf16[8,8192]{1,0:T(8,128)(2,1)S(1)}, u32[]{:S(2)}, u32[]{:S(2)}) collective-permute-start(bf16[8,8192]{1,0:T(8,128)(2,1)S(1)} %pick.1), channel_id=1, source_target_pairs={{0,4},{1,3},{4,8},{5,1},{8,12},{9,5},{12,14},{13,9},{14,10},{15,13... | collective-permute-start | bytes 393224 | tf_op jit(solution)/shard_map/ppermute | solution.py:309
  23.0 5.2 %collective-permute-start = (bf16[8,8192]{1,0:T(8,128)(2,1)S(1)}, bf16[8,8192]{1,0:T(8,128)(2,1)S(1)}, u32[]{:S(2)}, u32[]{:S(2)}) collective-permute-start(bf16[8,8192]{1,0:T(8,128)(2,1)S(1)} %normalize.1.after_ref.refs_0_), channel_id=1, source_target_pairs={{0,1},{1,0},{2,3},{3,2},{4,5},{5,4},{6,7},{7,6},{8,9},{9,8},{10,11... | collective-permute-start | bytes 393224 | tf_op jit(solution)/shard_map/ppermute | solution.py:318
  23.0 5.7 %collective-permute-start.2 = (bf16[8,8192]{1,0:T(8,128)(2,1)S(1)}, bf16[8,8192]{1,0:T(8,128)(2,1)S(1)}, u32[]{:S(2)}, u32[]{:S(2)}) collective-permute-start(bf16[8,8192]{1,0:T(8,128)(2,1)S(1)} %collective-permute-done.1.refs_2_), channel_id=1, source_target_pairs={{0,1},{1,0},{2,3},{3,2},{4,5},{5,4},{6,7},{7,6},{8,9},{9,8},{10,11... | collective-permute-start | bytes 393224 | tf_op jit(solution)/shard_map/ppermute | solution.py:318
  23.5 5.3 %collective-permute-start.4 = (bf16[8,8192]{1,0:T(8,128)(2,1)S(1)}, bf16[8,8192]{1,0:T(8,128)(2,1)S(1)}, u32[]{:S(2)}, u32[]{:S(2)}) collective-permute-start(bf16[8,8192]{1,0:T(8,128)(2,1)S(1)} %collective-permute-done.3.after_ref.refs_4_), channel_id=1, source_target_pairs={{0,1},{1,0},{2,3},{3,2},{4,5},{5,4},{6,7},{7,6},{8,9},{9,8},{10,11... | collective-permute-start | bytes 393224 | tf_op jit(solution)/shard_map/ppermute | solution.py:318
  23.5 6.0 %collective-permute-start.8 = (bf16[8,8192]{1,0:T(8,128)(2,1)S(1)}, bf16[8,8192]{1,0:T(8,128)(2,1)S(1)}, u32[]{:S(2)}, u32[]{:S(2)}) collective-permute-start(bf16[8,8192]{1,0:T(8,128)(2,1)S(1)} %collective-permute-done.7.after_ref.refs_8_), channel_id=1, source_target_pairs={{0,1},{1,0},{2,3},{3,2},{4,5},{5,4},{6,7},{7,6},{8,9},{9,8},{10,11... | collective-permute-start | bytes 393224 | tf_op jit(solution)/shard_map/ppermute | solution.py:318
  28.2 1.4 %collective-permute-start.6 = (bf16[8,8192]{1,0:T(8,128)(2,1)S(1)}, bf16[8,8192]{1,0:T(8,128)(2,1)S(1)}, u32[]{:S(2)}, u32[]{:S(2)}) collective-permute-start(bf16[8,8192]{1,0:T(8,128)(2,1)S(1)} %collective-permute-done.5.refs_6_), channel_id=1, source_target_pairs={{0,1},{1,0},{2,3},{3,2},{4,5},{5,4},{6,7},{7,6},{8,9},{9,8},{10,11... | collective-permute-start | bytes 393224 | tf_op jit(solution)/shard_map/ppermute | solution.py:318
  28.2 1.8 %collective-permute-start.12 = (bf16[8,8192]{1,0:T(8,128)(2,1)S(1)}, bf16[8,8192]{1,0:T(8,128)(2,1)S(1)}, u32[]{:S(2)}, u32[]{:S(2)}) collective-permute-start(bf16[8,8192]{1,0:T(8,128)(2,1)S(1)} %collective-permute-done.11.odd_ref.refs_12_), channel_id=1, source_target_pairs={{0,1},{1,0},{2,3},{3,2},{4,5},{5,4},{6,7},{7,6},{8,9},{9,8},{10,11... | collective-permute-start | bytes 393224 | tf_op jit(solution)/shard_map/ppermute | solution.py:318
  28.7 1.3 %collective-permute-start.10 = (bf16[8,8192]{1,0:T(8,128)(2,1)S(1)}, bf16[8,8192]{1,0:T(8,128)(2,1)S(1)}, u32[]{:S(2)}, u32[]{:S(2)}) collective-permute-start(bf16[8,8192]{1,0:T(8,128)(2,1)S(1)} %collective-permute-done.9.even_ref.after_ref.refs_10_), channel_id=1, source_target_pairs={{0,1},{1,0},{2,3},{3,2},{4,5},{5,4},{6,7},{7,6},{8,9},{9,8},{10,11... | collective-permute-start | bytes 393224 | tf_op jit(solution)/shard_map/ppermute | solution.py:318
  28.8 1.4 %collective-permute-start.14 = (bf16[8,8192]{1,0:T(8,128)(2,1)S(1)}, bf16[8,8192]{1,0:T(8,128)(2,1)S(1)}, u32[]{:S(2)}, u32[]{:S(2)}) collective-permute-start(bf16[8,8192]{1,0:T(8,128)(2,1)S(1)} %collective-permute-done.13.refs_14_), channel_id=1, source_target_pairs={{0,1},{1,0},{2,3},{3,2},{4,5},{5,4},{6,7},{7,6},{8,9},{9,8},{10,11... | collective-permute-start | bytes 393224 | tf_op jit(solution)/shard_map/ppermute | solution.py:318
  33.0 5.8 %collective-permute-start.16 = (bf16[128,512]{1,0:T(8,128)(2,1)S(1)}, bf16[128,512]{1,0:T(8,128)(2,1)S(1)}, u32[]{:S(2)}, u32[]{:S(2)}) collective-permute-start(bf16[128,512]{1,0:T(8,128)(2,1)S(1)} %get-tuple-element.46.value_ref), channel_id=1, source_target_pairs={{0,1},{1,0},{2,3},{3,2},{4,5},{5,4},{6,7},{7,6},{8,9},{9,8},{10,11... | collective-permute-start | bytes 393224 | tf_op jit(solution)/shard_map/ppermute | solution.py:318
  36.2 9.4 %collective-permute-start.15 = (bf16[128,512]{1,0:T(8,128)(2,1)S(1)}, bf16[128,512]{1,0:T(8,128)(2,1)S(1)}, u32[]{:S(2)}, u32[]{:S(2)}) collective-permute-start(bf16[128,512]{1,0:T(8,128)(2,1)S(1)} %up_project.3.value_ref), channel_id=1, source_target_pairs={{0,8},{1,9},{2,10},{3,11},{4,12},{5,13},{6,14},{7,15},{8,0},{9,1},... | collective-permute-start | bytes 393224 | tf_op jit(solution)/shard_map/ppermute | solution.py:318
  38.9 22.3 %copy-start.1 = (f32[1024]{0:T(1024)S(1)}, f32[1024]{0:T(1024)}, u32[]{:S(2)}) copy-start(f32[1024]{0:T(1024)} %param.11) | copy-start | bytes 12292
  38.9 6.7 %collective-permute-start.18 = (bf16[128,512]{1,0:T(8,128)(2,1)S(1)}, bf16[128,512]{1,0:T(8,128)(2,1)S(1)}, u32[]{:S(2)}, u32[]{:S(2)}) collective-permute-start(bf16[128,512]{1,0:T(8,128)(2,1)S(1)} %turn.8.after_ref.value_ref), channel_id=1, source_target_pairs={{0,2},{1,3},{2,0},{3,1},{4,6},{5,7},{6,4},{7,5},{8,10},{9,11},{10,... | collective-permute-start | bytes 393224 | tf_op jit(solution)/shard_map/ppermute | solution.py:318
  45.6 1.4 %collective-permute-start.17 = (bf16[128,512]{1,0:T(8,128)(2,1)S(1)}, bf16[128,512]{1,0:T(8,128)(2,1)S(1)}, u32[]{:S(2)}, u32[]{:S(2)}) collective-permute-start(bf16[128,512]{1,0:T(8,128)(2,1)S(1)} %turn.9.value_ref), channel_id=1, source_target_pairs={{0,1},{1,0},{2,3},{3,2},{4,5},{5,4},{6,7},{7,6},{8,9},{9,8},{10,11... | collective-permute-start | bytes 393224 | tf_op jit(solution)/shard_map/ppermute | solution.py:318
  45.7 6.0 %collective-permute-start.20 = (bf16[128,512]{1,0:T(8,128)(2,1)S(1)}, bf16[128,512]{1,0:T(8,128)(2,1)S(1)}, u32[]{:S(2)}, u32[]{:S(2)}) collective-permute-start(bf16[128,512]{1,0:T(8,128)(2,1)S(1)} %turn.10.value_ref), channel_id=1, source_target_pairs={{0,4},{1,5},{2,6},{3,7},{4,0},{5,1},{6,2},{7,3},{8,12},{9,13},{10,... | collective-permute-start | bytes 393224 | tf_op jit(solution)/shard_map/ppermute | solution.py:318
  47.0 5.6 %collective-permute-start.19 = (bf16[128,512]{1,0:T(8,128)(2,1)S(1)}, bf16[128,512]{1,0:T(8,128)(2,1)S(1)}, u32[]{:S(2)}, u32[]{:S(2)}) collective-permute-start(bf16[128,512]{1,0:T(8,128)(2,1)S(1)} %turn.11.value_ref), channel_id=1, source_target_pairs={{0,2},{1,3},{2,0},{3,1},{4,6},{5,7},{6,4},{7,5},{8,10},{9,11},{10,... | collective-permute-start | bytes 393224 | tf_op jit(solution)/shard_map/ppermute | solution.py:318
  52.7 7.1 %collective-permute-start.21 = (bf16[128,512]{1,0:T(8,128)(2,1)S(1)}, bf16[128,512]{1,0:T(8,128)(2,1)S(1)}, u32[]{:S(2)}, u32[]{:S(2)}) collective-permute-start(bf16[128,512]{1,0:T(8,128)(2,1)S(1)} %turn.13.value_ref), channel_id=1, source_target_pairs={{0,4},{1,5},{2,6},{3,7},{4,0},{5,1},{6,2},{7,3},{8,12},{9,13},{10,... | collective-permute-start | bytes 393224 | tf_op jit(solution)/shard_map/ppermute | solution.py:318
  53.7 7.5 %collective-permute-start.22 = (bf16[128,512]{1,0:T(8,128)(2,1)S(1)}, bf16[128,512]{1,0:T(8,128)(2,1)S(1)}, u32[]{:S(2)}, u32[]{:S(2)}) collective-permute-start(bf16[128,512]{1,0:T(8,128)(2,1)S(1)} %turn.12.value_ref), channel_id=1, source_target_pairs={{0,8},{1,9},{2,10},{3,11},{4,12},{5,13},{6,14},{7,15},{8,0},{9,1},... | collective-permute-start | bytes 393224 | tf_op jit(solution)/shard_map/ppermute | solution.py:318
  62.7 1.5 %collective-permute-start.23 = (bf16[16,4096]{1,0:T(8,128)(2,1)S(1)}, bf16[16,4096]{1,0:T(8,128)(2,1)S(1)}, u32[]{:S(2)}, u32[]{:S(2)}) collective-permute-start(bf16[16,4096]{1,0:T(8,128)(2,1)S(1)} %get-tuple-element.55), channel_id=1, source_target_pairs={{0,1},{1,0},{2,3},{3,2},{4,5},{5,4},{6,7},{7,6},{8,9},{9,8},{10,11... | collective-permute-start | bytes 393224 | tf_op jit(solution)/shard_map/ppermute | solution.py:318
  64.2 24.9 %copy-start = (bf16[8,8192]{1,0:T(8,128)(2,1)S(1)}, bf16[8,8192]{1,0:T(8,128)(2,1)}, u32[]{:S(2)}) copy-start(bf16[8,8192]{1,0:T(8,128)(2,1)} %tokens_ref.1) | copy-start | bytes 393220
  64.2 5.6 %collective-permute-start.25 = (bf16[112,4096]{1,0:T(8,128)(2,1)S(1)}, bf16[112,4096]{1,0:T(8,128)(2,1)S(1)}, u32[]{:S(2)}, u32[]{:S(2)}) collective-permute-start(bf16[112,4096]{1,0:T(8,128)(2,1)S(1)} %get-tuple-element.58), channel_id=1, source_target_pairs={{0,1},{1,0},{2,3},{3,2},{4,5},{5,4},{6,7},{7,6},{8,9},{9,8},{10,11... | collective-permute-start | bytes 2752520 | tf_op jit(solution)/shard_map/ppermute | solution.py:318
  64.8 5.0 %collective-permute-start.24 = (bf16[16,4096]{1,0:T(8,128)(2,1)S(1)}, bf16[16,4096]{1,0:T(8,128)(2,1)S(1)}, u32[]{:S(2)}, u32[]{:S(2)}) collective-permute-start(bf16[16,4096]{1,0:T(8,128)(2,1)S(1)} %far.1), channel_id=1, source_target_pairs={{0,4},{1,3},{4,8},{5,1},{8,12},{9,5},{12,14},{13,9},{14,10},{15,13... | collective-permute-start | bytes 393224 | tf_op jit(solution)/shard_map/ppermute | solution.py:309
  69.9 5.0 %collective-permute-start.26 = (bf16[16,4096]{1,0:T(8,128)(2,1)S(1)}, bf16[16,4096]{1,0:T(8,128)(2,1)S(1)}, u32[]{:S(2)}, u32[]{:S(2)}) collective-permute-start(bf16[16,4096]{1,0:T(8,128)(2,1)S(1)} %relay.6), channel_id=1, source_target_pairs={{0,4},{1,5},{4,8},{5,9},{8,12},{9,13},{12,14},{13,15},{14,10},{15,... | collective-permute-start | bytes 393224 | tf_op jit(solution)/shard_map/ppermute | solution.py:309
  72.1 5.0 %collective-permute-start.29 = (bf16[16,4096]{1,0:T(8,128)(2,1)S(1)}, bf16[16,4096]{1,0:T(8,128)(2,1)S(1)}, u32[]{:S(2)}, u32[]{:S(2)}) collective-permute-start(bf16[16,4096]{1,0:T(8,128)(2,1)S(1)} %relay.9), channel_id=1, source_target_pairs={{0,2},{1,3},{4,0},{5,1},{8,4},{9,5},{12,8},{13,9},{14,12},{15,13},... | collective-permute-start | bytes 393224 | tf_op jit(solution)/shard_map/ppermute | solution.py:309
  75.0 5.1 %collective-permute-start.27 = (bf16[16,4096]{1,0:T(8,128)(2,1)S(1)}, bf16[16,4096]{1,0:T(8,128)(2,1)S(1)}, u32[]{:S(2)}, u32[]{:S(2)}) collective-permute-start(bf16[16,4096]{1,0:T(8,128)(2,1)S(1)} %relay.7), channel_id=1, source_target_pairs={{0,4},{1,5},{4,8},{5,9},{8,12},{9,13},{12,14},{13,15},{14,10},{15,... | collective-permute-start | bytes 393224 | tf_op jit(solution)/shard_map/ppermute | solution.py:309
  77.2 5.4 %collective-permute-start.30 = (bf16[16,4096]{1,0:T(8,128)(2,1)S(1)}, bf16[16,4096]{1,0:T(8,128)(2,1)S(1)}, u32[]{:S(2)}, u32[]{:S(2)}) collective-permute-start(bf16[16,4096]{1,0:T(8,128)(2,1)S(1)} %relay.10), channel_id=1, source_target_pairs={{0,2},{1,3},{4,0},{5,1},{8,4},{9,5},{12,8},{13,9},{14,12},{15,13},... | collective-permute-start | bytes 393224 | tf_op jit(solution)/shard_map/ppermute | solution.py:309
  80.1 5.1 %collective-permute-start.28 = (bf16[16,4096]{1,0:T(8,128)(2,1)S(1)}, bf16[16,4096]{1,0:T(8,128)(2,1)S(1)}, u32[]{:S(2)}, u32[]{:S(2)}) collective-permute-start(bf16[16,4096]{1,0:T(8,128)(2,1)S(1)} %relay.8), channel_id=1, source_target_pairs={{0,4},{1,5},{4,8},{5,9},{8,12},{9,13},{12,14},{13,15},{14,10},{15,... | collective-permute-start | bytes 393224 | tf_op jit(solution)/shard_map/ppermute | solution.py:309
  82.7 5.0 %collective-permute-start.31 = (bf16[16,4096]{1,0:T(8,128)(2,1)S(1)}, bf16[16,4096]{1,0:T(8,128)(2,1)S(1)}, u32[]{:S(2)}, u32[]{:S(2)}) collective-permute-start(bf16[16,4096]{1,0:T(8,128)(2,1)S(1)} %relay.11), channel_id=1, source_target_pairs={{0,2},{1,3},{4,0},{5,1},{8,4},{9,5},{12,8},{13,9},{14,12},{15,13},... | collective-permute-start | bytes 393224 | tf_op jit(solution)/shard_map/ppermute | solution.py:309
  87.8 1.3 %collective-permute-start.32 = (bf16[8,4096]{1,0:T(8,128)(2,1)S(1)}, bf16[8,4096]{1,0:T(8,128)(2,1)S(1)}, u32[]{:S(2)}, u32[]{:S(2)}) collective-permute-start(bf16[8,4096]{1,0:T(8,128)(2,1)S(1)} %get-tuple-element.60), channel_id=1, source_target_pairs={{0,1},{1,0},{2,3},{3,2},{4,5},{5,4},{6,7},{7,6},{8,9},{9,8},{10,11... | collective-permute-start | bytes 196616 | tf_op jit(solution)/shard_map/ppermute | solution.py:318

commit v6 on v5

--- a/solution.py
+++ b/solution.py
@@ -9,6 +9,8 @@
 
 BLOCK = 256
 MIB = 1 << 20
+TURN = 2_000_000_000
+COST = 20_000_000_000
 
 
 def hadamard(count):
@@ -53,7 +55,7 @@
             pltpu.SemaphoreType.DMA((2,)),
         ],
         compiler_params=pltpu.CompilerParams(vmem_limit_bytes=4 * MIB),
-        cost_estimate=pl.CostEstimate(flops=8 * rows_in.size, bytes_accessed=4 * rows_in.size, transcendentals=0),
+        cost_estimate=pl.CostEstimate(flops=COST, bytes_accessed=4 * rows_in.size, transcendentals=0),
         name="normalize",
     )(in_hbm(rows_in), in_hbm(gain))
 
@@ -70,42 +72,6 @@
 
 def once(value, *others):
     return lax.optimization_barrier((value, *others))[0]
-
-
-def load_kernel(places, after_ref, *refs):
-    count = len(places)
-    weights, outs, sems = refs[:count], refs[count:-1], refs[-1]
-    core = lax.axis_index("hid") % 2
-    copies = []
-    for piece, (own, pieces, at) in enumerate(places):
-        cols = outs[piece].shape[1]
-        side = 0 if own is None else core if own else 1 - core
-        start = pl.multiple_of((side * pieces + at) * cols, cols)
-        copies.append(
-            pltpu.make_async_copy(weights[piece].at[:, pl.ds(start, cols)], outs[piece], sems.at[piece])
-        )
-    for copy in copies:
-        copy.start()
-    for copy in copies:
-        copy.wait()
-
-
-def load(after, *wanted):
-    hbm = pl.BlockSpec(memory_space=pltpu.HBM)
-    shapes = []
-    for weight, own, pieces, _ in wanted:
-        cols = weight.shape[1] // (pieces if own is None else 2 * pieces)
-        shapes.append(jax.ShapeDtypeStruct((weight.shape[0], cols), weight.dtype))
-    return pl.pallas_call(
-        functools.partial(load_kernel, [place[1:] for place in wanted]),
-        out_shape=shapes,
-        in_specs=[hbm] * (1 + len(wanted)),
-        out_specs=[pl.BlockSpec(memory_space=pltpu.VMEM)] * len(wanted),
-        scratch_shapes=[pltpu.SemaphoreType.DMA((len(wanted),))],
-        compiler_params=pltpu.CompilerParams(vmem_limit_bytes=1 * MIB),
-        cost_estimate=pl.CostEstimate(flops=0, bytes_accessed=2 * sum(s.size for s in shapes), transcendentals=0),
-        name="load",
-    )(after, *[in_hbm(place[0]) for place in wanted])
 
 
 def join_rows(parts, out_ref):
@@ -115,7 +81,7 @@
         out_ref[2 * own * pair : 2 * own * (pair + 1), :] = jnp.concatenate(both, axis=0).astype(jnp.bfloat16)
 
 
-def up_kernel(shifts, first, *refs):
+def up_kernel(shifts, first, lanes_of, *refs):
     count = 2 * len(shifts)
     if first:
         gate_ref, up_ref, out_ref, rows_ref, hidden_ref = refs[count:]
@@ -127,8 +93,8 @@
     own = rows_ref.shape[0] // count
     turn = hadamard(BLOCK)
     values = rows_ref[...]
-    gate = jnp.dot(values, gate_ref[...], preferred_element_type=jnp.float32)
-    up = jnp.dot(values, up_ref[...], preferred_element_type=jnp.float32)
+    gate = jnp.dot(values, gate_ref[:, lanes_of], preferred_element_type=jnp.float32)
+    up = jnp.dot(values, up_ref[:, lanes_of], preferred_element_type=jnp.float32)
     hidden = gate / (1.0 + jnp.exp(-gate)) * up
     high = hidden.astype(jnp.bfloat16)
     low = (hidden - high.astype(jnp.float32)).astype(jnp.bfloat16)
@@ -145,16 +111,17 @@
     out_ref[...] = hidden_ref[...].astype(jnp.bfloat16)
 
 
-def up_project(shifts, parts, gate_weight, up_weight):
+def up_project(shifts, parts, gate_weight, up_weight, at, pieces):
     first = len(parts) > 1
     depth, width = gate_weight.shape
+    width = width // pieces
     rows = sum(part.shape[0] for part in parts)
     vmem = pl.BlockSpec(memory_space=pltpu.VMEM)
     outs = [jax.ShapeDtypeStruct((rows, width), jnp.bfloat16)]
     if first:
         outs.append(jax.ShapeDtypeStruct((rows, depth), jnp.bfloat16))
     return pl.pallas_call(
-        functools.partial(up_kernel, shifts, first),
+        functools.partial(up_kernel, shifts, first, slice(at * width, (at + 1) * width)),
         out_shape=outs,
         in_specs=[vmem] * (len(parts) + 2),
         out_specs=[vmem] * len(outs),
@@ -165,8 +132,8 @@
     )(*parts, gate_weight, up_weight)
 
 
-def down_kernel(blocks, chips, scale, a_ref, b_ref, clip_ref, *refs):
-    weights, outs, (rows_ref, mixed_ref) = refs[:-4], refs[-4:-2], refs[-2:]
+def down_kernel(blocks, chips, scale, flip, a_ref, b_ref, clip_ref, weight_ref, *refs):
+    outs, (rows_ref, mixed_ref) = refs[:-2], refs[-2:]
     half = a_ref.shape[1]
     rows_ref[:, :half] = a_ref[...].astype(jnp.float32)
     rows_ref[:, half:] = b_ref[...].astype(jnp.float32)
@@ -187,32 +154,33 @@
     for chip in range(chips):
         spot = pl.multiple_of(ring_place(me // 2, chip + chips // 2, chips) * each, each)
         mixed_ref[chip * each : (chip + 1) * each, :] = rows_ref[pl.ds(spot, each), :].astype(jnp.bfloat16)
-    wide = weights[0].shape[1]
-    for at, weight_ref in enumerate(weights):
-        product = jnp.dot(mixed_ref[...], weight_ref[...], preferred_element_type=jnp.float32)
-        first = 0
-        for out_ref in outs:
-            out_ref[:, at * wide : (at + 1) * wide] = product[first : first + out_ref.shape[0]].astype(jnp.bfloat16)
-            first += out_ref.shape[0]
-
-
-def down_project(a, b, clip_scale, weights, chips, total):
+    wide = weight_ref.shape[1] // 2
+    side = 1 - me % 2 if flip else me % 2
+    lanes = pl.ds(pl.multiple_of(side * wide, wide), wide)
+    product = jnp.dot(mixed_ref[...], weight_ref[:, lanes], preferred_element_type=jnp.float32)
+    first = 0
+    for out_ref in outs:
+        out_ref[...] = product[first : first + out_ref.shape[0]].astype(jnp.bfloat16)
+        first += out_ref.shape[0]
+
+
+def down_project(a, b, clip_scale, weight, flip, chips, total):
     rows = a.shape[0]
-    width, depth = weights[0].shape[0], weights[0].shape[1] * len(weights)
+    width, depth = weight.shape[0], weight.shape[1] // 2
     vmem = pl.BlockSpec(memory_space=pltpu.VMEM)
     outs = [
         jax.ShapeDtypeStruct((count, depth), jnp.bfloat16) for count in (rows // chips, rows - rows // chips)
     ]
     return pl.pallas_call(
-        functools.partial(down_kernel, width // BLOCK, chips, total**-0.5),
+        functools.partial(down_kernel, width // BLOCK, chips, total**-0.5, flip),
         out_shape=outs,
-        in_specs=[vmem] * (3 + len(weights)),
+        in_specs=[vmem] * 4,
         out_specs=[vmem] * 2,
         scratch_shapes=[pltpu.VMEM((rows, width), jnp.float32), pltpu.VMEM((rows, width), jnp.bfloat16)],
         compiler_params=pltpu.CompilerParams(vmem_limit_bytes=8 * MIB),
         cost_estimate=pl.CostEstimate(flops=2 * rows * depth * width, bytes_accessed=0, transcendentals=0),
         name="down_project",
-    )(a, b, clip_scale, *weights)
+    )(a, b, clip_scale, weight)
 
 
 def pick_kernel(even_ref, odd_ref, out_ref):
@@ -240,7 +208,7 @@
         in_specs=[vmem, vmem],
         out_specs=vmem,
         compiler_params=pltpu.CompilerParams(vmem_limit_bytes=2 * MIB),
-        cost_estimate=pl.CostEstimate(flops=2 * first.size, bytes_accessed=0, transcendentals=0),
+        cost_estimate=pl.CostEstimate(flops=TURN, bytes_accessed=0, transcendentals=0),
         name=name,
     )(first, second)
 
@@ -320,37 +288,21 @@
     normed = normalize(tokens, norm_gain)
     width = gate_weight.shape[1]
     pieces = width // max(BLOCK, width // 2)
-    wanted = [(weight, None, pieces, at) for at in range(pieces) for weight in (gate_weight, up_weight)]
-    weights, down_theirs = [], []
-
-    def beside(after, arrived):
-        if len(weights) < len(wanted):
-            at = len(weights)
-            columns, below = load(after, wanted[at], (down_weight, False, len(wanted), at))
-            weights.append(columns)
-            down_theirs.append(below)
-            arrived = once(arrived, columns, below)
-        return arrived
-
     mine, shifts = [normed], [0]
     ahead = behind = normed
     for step in range(1, steps):
-        after = behind
         ahead, behind = right(ahead), left(behind)
-        behind = beside(after, behind)
         mine += [ahead, behind]
         shifts += [-step, step]
-    mine.append(beside(ahead, hop(both(pick_kernel, ahead, behind, "pick"), 1, -1)))
+    mine.append(hop(both(pick_kernel, ahead, behind, "pick"), 1, -1))
     shifts.append(steps)
-    while len(weights) < len(wanted):
-        mine[0] = beside(mine[0], mine[0])
     parts = [block for own in mine for block in (own, cross(own))]
 
-    half_b, joined = up_project(shifts, parts, *weights[-2:])
+    half_b, joined = up_project(shifts, parts, gate_weight, up_weight, pieces - 1, pieces)
     if pieces == 1:
         half_a, half_b = jnp.split(half_b, 2, axis=1)
     else:
-        (half_a,) = up_project(shifts, [joined], *weights[:2])
+        (half_a,) = up_project(shifts, [joined], gate_weight, up_weight, 0, pieces)
 
     def turn(value, mask, *others):
         return both(functools.partial(turn_kernel, mask), value, once(cross(value, mask), *others), "turn")
@@ -360,9 +312,8 @@
         first, second = masks[stage - 1], masks[stage]
         if stage == 0:
             half_b = turn(half_b, second)
-            (down_own,) = load(half_b, (down_weight, True, 1, 0))
-            early = turn(half_b, masks[1], down_own)
-            half_a = turn(half_a, first, half_b, down_own)
+            early = turn(half_b, masks[1])
+            half_a = turn(half_a, first, half_b)
         elif stage == 1:
             half_b = early
             half_a = turn(half_a, first, early)
@@ -375,9 +326,9 @@
 
     total = count * width
     limits = clip_scale.reshape(1, -1)
-    theirs_far, theirs = down_project(half_a, half_b, limits, down_theirs, chips, total)
+    theirs_far, theirs = down_project(half_a, half_b, limits, down_weight, True, chips, total)
     arrived_far = cross(theirs_far)
-    own_far, own = down_project(half_a, half_b, limits, [down_own], chips, total)
+    own_far, own = down_project(half_a, half_b, limits, down_weight, False, chips, total)
     arrived = cross(once(theirs, own, arrived_far))
     rows, wide = own_far.shape
     part = jax.ShapeDtypeStruct((rows, wide), jnp.bfloat16)

time: 90 us -> 84.8 us (0.942)
  Pallas kernels: 31 us -> 11.2 us
  waiting for transfers between devices: 28.4 us -> 46.4 us
  starting transfers between devices: 30.2 us -> 26.6 us
    pallas_call x7 -> x2, Pallas kernels: 25.5 us -> 5.53 us  [up_project(): pl.pallas_call(functools.partial(up_kernel, shifts, first, slice(at * wid...]
    ppermute x14, waiting for transfers between devices: 14.1 us -> 27.8 us  [hop(): return lax.ppermute(value, 'hid', pairs)]
    ppermute x19, waiting for transfers between devices: 14.3 us -> 18.6 us  [cross(): return lax.ppermute(value, 'hid', [(d, d ^ mask) for d in range(count)])]
    ppermute x14, starting transfers between devices: 17.8 us -> 14.8 us  [hop(): return lax.ppermute(value, 'hid', pairs)]
  transfers between devices with their start and end apart: 33 -> 33, of which waited for: 16 -> 18; matrix products, arithmetic and copies ran while one was open for 0% -> 0% of each run, Pallas kernels for 28% -> 6%
where the time goes in v6:
time: 84.8 us; the launch traced here: 84.7 us
  waiting for transfers between devices  46.4 us (55%)
  starting transfers between devices  26.6 us (31%)
  Pallas kernels  11.2 us (13%)
    ppermute x14, waiting for transfers between devices, hop(): return lax.ppermute(value, 'hid', pairs)  27.8 us
    ppermute x19, waiting for transfers between devices, cross(): return lax.ppermute(value, 'hid', [(d, d ^ mask) for d in range(count)])  18.6 us
    ppermute x14, starting transfers between devices, hop(): return lax.ppermute(value, 'hid', pairs)  14.8 us
    ppermute x19, starting transfers between devices, cross(): return lax.ppermute(value, 'hid', [(d, d ^ mask) for d in range(count)])  11.8 us
    pallas_call x2, Pallas kernels, up_project(): pl.pallas_call(functools.partial(up_kernel, shifts, first, slice(at * wid...  5.53 us
    pallas_call x2, Pallas kernels, down_project(): pl.pallas_call(functools.partial(down_kernel, width // BLOCK, chips, tota...  2.91 us
  transfers between devices with their start and end apart: 33, of which 18 were waited for; matrix products, arithmetic and copies ran while one was open for 0% of the time, Pallas kernels for 6%

profile of v6, /device:TPU:0, one launch (start us, length us, event | category | flops | bytes accessed | tf_op | source)
XLA Modules:
  0.0 84.7 jit_solution(415176341946325092)
XLA Ops:
  0.0 1.3 %normalize.1.refs_0_ = bf16[8,8192]{1,0:T(8,128)(2,1)S(1)} custom-call(bf16[8,8192]{1,0:T(8,128)(2,1)} %tokens_ref.1, f32[1,8192]{1,0:T(1,128)} %bitcast.10), custom_call_target="tpu_custom_call" | custom-call | flops 20000000000 | bytes 262144 | tf_op jit(solution)/shard_map/normalize/pallas_call | solution.py:47
  1.3 3.0 %collective-permute-start.3 = (bf16[8,8192]{1,0:T(8,128)(2,1)S(1)}, bf16[8,8192]{1,0:T(8,128)(2,1)S(1)}, u32[]{:S(2)}, u32[]{:S(2)}) collective-permute-start(bf16[8,8192]{1,0:T(8,128)(2,1)S(1)} %normalize.1.refs_0_), channel_id=1, source_target_pairs={{0,2},{1,3},{4,0},{5,1},{8,4},{9,5},{12,8},{13,9},{14,12},{15,13},... | collective-permute-start | bytes 393224 | tf_op jit(solution)/shard_map/ppermute | solution.py:277
  4.4 0.1 collective-permute-start.1
  4.5 3.4 %collective-permute-done.3.refs_4_ = bf16[8,8192]{1,0:T(8,128)(2,1)S(1)} collective-permute-done((bf16[8,8192]{1,0:T(8,128)(2,1)S(1)}, bf16[8,8192]{1,0:T(8,128)(2,1)S(1)}, u32[]{:S(2)}, u32[]{:S(2)}) %collective-permute-start.3) | collective-permute-done | bytes 131104 | tf_op jit(solution)/shard_map/ppermute | solution.py:277
  7.9 1.7 %collective-permute-start.7 = (bf16[8,8192]{1,0:T(8,128)(2,1)S(1)}, bf16[8,8192]{1,0:T(8,128)(2,1)S(1)}, u32[]{:S(2)}, u32[]{:S(2)}) collective-permute-start(bf16[8,8192]{1,0:T(8,128)(2,1)S(1)} %collective-permute-done.3.refs_4_), channel_id=1, source_target_pairs={{0,2},{1,3},{4,0},{5,1},{8,4},{9,5},{12,8},{13,9},{14,12},{15,13},... | collective-permute-start | bytes 393224 | tf_op jit(solution)/shard_map/ppermute | solution.py:277
  9.6 0.3 collective-permute-start.5
  9.9 2.9 %collective-permute-done.7.refs_8_ = bf16[8,8192]{1,0:T(8,128)(2,1)S(1)} collective-permute-done((bf16[8,8192]{1,0:T(8,128)(2,1)S(1)}, bf16[8,8192]{1,0:T(8,128)(2,1)S(1)}, u32[]{:S(2)}, u32[]{:S(2)}) %collective-permute-start.7) | collective-permute-done | bytes 131104 | tf_op jit(solution)/shard_map/ppermute | solution.py:277
  12.9 1.7 %collective-permute-start.11 = (bf16[8,8192]{1,0:T(8,128)(2,1)S(1)}, bf16[8,8192]{1,0:T(8,128)(2,1)S(1)}, u32[]{:S(2)}, u32[]{:S(2)}) collective-permute-start(bf16[8,8192]{1,0:T(8,128)(2,1)S(1)} %collective-permute-done.7.refs_8_), channel_id=1, source_target_pairs={{0,2},{1,3},{4,0},{5,1},{8,4},{9,5},{12,8},{13,9},{14,12},{15,13},... | collective-permute-start | bytes 393224 | tf_op jit(solution)/shard_map/ppermute | solution.py:277
  14.6 0.3 collective-permute-start.9
  14.9 0.5 collective-permute-start.4
  15.4 2.4 %collective-permute-done.11.odd_ref.refs_12_ = bf16[8,8192]{1,0:T(8,128)(2,1)S(1)} collective-permute-done((bf16[8,8192]{1,0:T(8,128)(2,1)S(1)}, bf16[8,8192]{1,0:T(8,128)(2,1)S(1)}, u32[]{:S(2)}, u32[]{:S(2)}) %collective-permute-start.11) | collective-permute-done | bytes 131104 | tf_op jit(solution)/shard_map/ppermute | solution.py:277
  17.8 1.7 %collective-permute-done.9.even_ref.refs_10_ = bf16[8,8192]{1,0:T(8,128)(2,1)S(1)} collective-permute-done((bf16[8,8192]{1,0:T(8,128)(2,1)S(1)}, bf16[8,8192]{1,0:T(8,128)(2,1)S(1)}, u32[]{:S(2)}, u32[]{:S(2)}) %collective-permute-start.9) | collective-permute-done | bytes 131104 | tf_op jit(solution)/shard_map/ppermute | solution.py:277
  19.6 0.4 collective-permute-start.13
  20.0 0.5 collective-permute-start.6
  20.5 0.1 collective-permute-start.12
  20.5 0.4 collective-permute-start.10
  21.0 3.6 %collective-permute-done.13.refs_14_ = bf16[8,8192]{1,0:T(8,128)(2,1)S(1)} collective-permute-done((bf16[8,8192]{1,0:T(8,128)(2,1)S(1)}, bf16[8,8192]{1,0:T(8,128)(2,1)S(1)}, u32[]{:S(2)}, u32[]{:S(2)}) %collective-permute-start.13) | collective-permute-done | bytes 131104 | tf_op jit(solution)/shard_map/ppermute | solution.py:277
  24.6 1.3 %collective-permute-done.14.refs_15_ = bf16[8,8192]{1,0:T(8,128)(2,1)S(1)} collective-permute-done((bf16[8,8192]{1,0:T(8,128)(2,1)S(1)}, bf16[8,8192]{1,0:T(8,128)(2,1)S(1)}, u32[]{:S(2)}, u32[]{:S(2)}) %collective-permute-start.14) | collective-permute-done | bytes 131104 | tf_op jit(solution)/shard_map/ppermute | solution.py:286
  26.0 2.8 %up_project.2 = (bf16[128,512]{1,0:T(8,128)(2,1)S(1)}, bf16[128,8192]{1,0:T(8,128)(2,1)S(1)}) custom-call(bf16[8,8192]{1,0:T(8,128)(2,1)S(1)} %normalize.1.refs_0_, bf16[8,8192]{1,0:T(8,128)(2,1)S(1)} %collective-permute-done.refs_1_, bf16[8,8192]{1,0:T(8,128)(2,1)S(1)} %collective-permute-done.1.refs_2_, ...), custom_call_target="tpu_custom_call" | custom-call | flops 2147483648 | tf_op jit(solution)/shard_map/up_project/pallas_call | solution.py:123
  28.8 0.2 collective-permute-start.16
  29.0 2.8 %up_project.3.value_ref = bf16[128,512]{1,0:T(8,128)(2,1)S(1)} custom-call(bf16[128,8192]{1,0:T(8,128)(2,1)S(1)} %get-tuple-element.20.refs_0_, bf16[8192,1024]{1,0:T(8,128)(2,1)S(1)} %bitcast.5, bf16[8192,1024]{1,0:T(8,128)(2,1)S(1)} %bitcast.7), custom_call_target="tpu_custom_call" | custom-call | flops 2147483648 | tf_op jit(solution)/shard_map/up_project/pallas_call | solution.py:123
  31.8 1.6 %collective-permute-start.15 = (bf16[128,512]{1,0:T(8,128)(2,1)S(1)}, bf16[128,512]{1,0:T(8,128)(2,1)S(1)}, u32[]{:S(2)}, u32[]{:S(2)}) collective-permute-start(bf16[128,512]{1,0:T(8,128)(2,1)S(1)} %up_project.3.value_ref), channel_id=1, source_target_pairs={{0,8},{1,9},{2,10},{3,11},{4,12},{5,13},{6,14},{7,15},{8,0},{9,1},... | collective-permute-start | bytes 393224 | tf_op jit(solution)/shard_map/ppermute | solution.py:286
  33.4 2.7 %collective-permute-start.18 = (bf16[128,512]{1,0:T(8,128)(2,1)S(1)}, bf16[128,512]{1,0:T(8,128)(2,1)S(1)}, u32[]{:S(2)}, u32[]{:S(2)}) collective-permute-start(bf16[128,512]{1,0:T(8,128)(2,1)S(1)} %turn.8.value_ref), channel_id=1, source_target_pairs={{0,2},{1,3},{2,0},{3,1},{4,6},{5,7},{6,4},{7,5},{8,10},{9,11},{10,... | collective-permute-start | bytes 393224 | tf_op jit(solution)/shard_map/ppermute | solution.py:286
  36.1 5.1 %collective-permute-done.15.other_ref = bf16[128,512]{1,0:T(8,128)(2,1)S(1)} collective-permute-done((bf16[128,512]{1,0:T(8,128)(2,1)S(1)}, bf16[128,512]{1,0:T(8,128)(2,1)S(1)}, u32[]{:S(2)}, u32[]{:S(2)}) %collective-permute-start.15) | collective-permute-done | bytes 131104 | tf_op jit(solution)/shard_map/ppermute | solution.py:286
  41.3 0.1 collective-permute-start.17
  41.5 0.1 collective-permute-start.20
  41.5 1.1 %collective-permute-done.17.other_ref = bf16[128,512]{1,0:T(8,128)(2,1)S(1)} collective-permute-done((bf16[128,512]{1,0:T(8,128)(2,1)S(1)}, bf16[128,512]{1,0:T(8,128)(2,1)S(1)}, u32[]{:S(2)}, u32[]{:S(2)}) %collective-permute-start.17) | collective-permute-done | bytes 131104 | tf_op jit(solution)/shard_map/ppermute | solution.py:286
  42.7 0.0 slice-start.1
  42.7 1.7 %collective-permute-start.19 = (bf16[128,512]{1,0:T(8,128)(2,1)S(1)}, bf16[128,512]{1,0:T(8,128)(2,1)S(1)}, u32[]{:S(2)}, u32[]{:S(2)}) collective-permute-start(bf16[128,512]{1,0:T(8,128)(2,1)S(1)} %turn.11.value_ref), channel_id=1, source_target_pairs={{0,2},{1,3},{2,0},{3,1},{4,6},{5,7},{6,4},{7,5},{8,10},{9,11},{10,... | collective-permute-start | bytes 393224 | tf_op jit(solution)/shard_map/ppermute | solution.py:286
  44.5 2.9 %collective-permute-done.20.other_ref = bf16[128,512]{1,0:T(8,128)(2,1)S(1)} collective-permute-done((bf16[128,512]{1,0:T(8,128)(2,1)S(1)}, bf16[128,512]{1,0:T(8,128)(2,1)S(1)}, u32[]{:S(2)}, u32[]{:S(2)}) %collective-permute-start.20) | collective-permute-done | bytes 131104 | tf_op jit(solution)/shard_map/ppermute | solution.py:286
  47.4 0.0 slice-start.2
  47.4 0.9 %collective-permute-done.19.other_ref = bf16[128,512]{1,0:T(8,128)(2,1)S(1)} collective-permute-done((bf16[128,512]{1,0:T(8,128)(2,1)S(1)}, bf16[128,512]{1,0:T(8,128)(2,1)S(1)}, u32[]{:S(2)}, u32[]{:S(2)}) %collective-permute-start.19) | collective-permute-done | bytes 131104 | tf_op jit(solution)/shard_map/ppermute | solution.py:286
  48.4 0.0 slice-start.3
  48.4 1.0 %collective-permute-start.21 = (bf16[128,512]{1,0:T(8,128)(2,1)S(1)}, bf16[128,512]{1,0:T(8,128)(2,1)S(1)}, u32[]{:S(2)}, u32[]{:S(2)}) collective-permute-start(bf16[128,512]{1,0:T(8,128)(2,1)S(1)} %turn.13.value_ref), channel_id=1, source_target_pairs={{0,4},{1,5},{2,6},{3,7},{4,0},{5,1},{6,2},{7,3},{8,12},{9,13},{10,... | collective-permute-start | bytes 393224 | tf_op jit(solution)/shard_map/ppermute | solution.py:286
  49.4 2.2 %collective-permute-start.22 = (bf16[128,512]{1,0:T(8,128)(2,1)S(1)}, bf16[128,512]{1,0:T(8,128)(2,1)S(1)}, u32[]{:S(2)}, u32[]{:S(2)}) collective-permute-start(bf16[128,512]{1,0:T(8,128)(2,1)S(1)} %turn.12.value_ref), channel_id=1, source_target_pairs={{0,8},{1,9},{2,10},{3,11},{4,12},{5,13},{6,14},{7,15},{8,0},{9,1},... | collective-permute-start | bytes 393224 | tf_op jit(solution)/shard_map/ppermute | solution.py:286
  51.6 4.1 %collective-permute-done.21.other_ref = bf16[128,512]{1,0:T(8,128)(2,1)S(1)} collective-permute-done((bf16[128,512]{1,0:T(8,128)(2,1)S(1)}, bf16[128,512]{1,0:T(8,128)(2,1)S(1)}, u32[]{:S(2)}, u32[]{:S(2)}) %collective-permute-start.21) | collective-permute-done | bytes 131104 | tf_op jit(solution)/shard_map/ppermute | solution.py:286
  55.7 1.9 %collective-permute-done.22.other_ref = bf16[128,512]{1,0:T(8,128)(2,1)S(1)} collective-permute-done((bf16[128,512]{1,0:T(8,128)(2,1)S(1)}, bf16[128,512]{1,0:T(8,128)(2,1)S(1)}, u32[]{:S(2)}, u32[]{:S(2)}) %collective-permute-start.22) | collective-permute-done | bytes 131104 | tf_op jit(solution)/shard_map/ppermute | solution.py:286
  57.7 1.5 %down_project.3 = (bf16[16,4096]{1,0:T(8,128)(2,1)S(1)}, bf16[112,4096]{1,0:T(8,128)(2,1)S(1)}) custom-call(bf16[128,512]{1,0:T(8,128)(2,1)S(1)} %turn.14.a_ref, bf16[128,512]{1,0:T(8,128)(2,1)S(1)} %turn.15.b_ref, f32[1,1024]{1,0:T(1,128)S(1)} %bitcast.8, bf16[1024,8192]{1,0:T(8,128)(2,1)S(1)} %bitcast.3), custom_call_target="tpu_custom_call" | custom-call | flops 1073741824 | tf_op jit(solution)/shard_map/down_project/pallas_call | solution.py:174
  59.2 0.1 collective-permute-start.23
  59.3 1.5 %down_project.2 = (bf16[16,4096]{1,0:T(8,128)(2,1)S(1)}, bf16[112,4096]{1,0:T(8,128)(2,1)S(1)}) custom-call(bf16[128,512]{1,0:T(8,128)(2,1)S(1)} %turn.14.a_ref, bf16[128,512]{1,0:T(8,128)(2,1)S(1)} %turn.15.b_ref, f32[1,1024]{1,0:T(1,128)S(1)} %bitcast.9, bf16[1024,8192]{1,0:T(8,128)(2,1)S(1)} %bitcast.3), custom_call_target="tpu_custom_call" | custom-call | flops 1073741824 | tf_op jit(solution)/shard_map/down_project/pallas_call | solution.py:174
  60.7 0.6 collective-permute-start.25
  61.3 0.4 collective-permute-start.24
  61.8 4.6 %collective-permute-done.24.arrived_in = bf16[16,4096]{1,0:T(8,128)(2,1)S(1)} collective-permute-done((bf16[16,4096]{1,0:T(8,128)(2,1)S(1)}, bf16[16,4096]{1,0:T(8,128)(2,1)S(1)}, u32[]{:S(2)}, u32[]{:S(2)}) %collective-permute-start.24) | collective-permute-done | bytes 131104 | tf_op jit(solution)/shard_map/ppermute | solution.py:277
  66.4 0.1 relay.6
  66.4 0.4 collective-permute-start.26
  66.9 0.1 relay.9
  66.9 1.7 %collective-permute-start.29 = (bf16[16,4096]{1,0:T(8,128)(2,1)S(1)}, bf16[16,4096]{1,0:T(8,128)(2,1)S(1)}, u32[]{:S(2)}, u32[]{:S(2)}) collective-permute-start(bf16[16,4096]{1,0:T(8,128)(2,1)S(1)} %relay.9), channel_id=1, source_target_pairs={{0,2},{1,3},{4,0},{5,1},{8,4},{9,5},{12,8},{13,9},{14,12},{15,13},... | collective-permute-start | bytes 393224 | tf_op jit(solution)/shard_map/ppermute | solution.py:277
  68.6 2.8 %collective-permute-done.26.arrived_in = bf16[16,4096]{1,0:T(8,128)(2,1)S(1)} collective-permute-done((bf16[16,4096]{1,0:T(8,128)(2,1)S(1)}, bf16[16,4096]{1,0:T(8,128)(2,1)S(1)}, u32[]{:S(2)}, u32[]{:S(2)}) %collective-permute-start.26) | collective-permute-done | bytes 131104 | tf_op jit(solution)/shard_map/ppermute | solution.py:277
  71.4 0.1 relay.7
  71.5 0.4 collective-permute-start.27
  71.9 0.0 collective-permute-done.29.arrived_in
  71.9 0.1 relay.10
  72.0 1.7 %collective-permute-start.30 = (bf16[16,4096]{1,0:T(8,128)(2,1)S(1)}, bf16[16,4096]{1,0:T(8,128)(2,1)S(1)}, u32[]{:S(2)}, u32[]{:S(2)}) collective-permute-start(bf16[16,4096]{1,0:T(8,128)(2,1)S(1)} %relay.10), channel_id=1, source_target_pairs={{0,2},{1,3},{4,0},{5,1},{8,4},{9,5},{12,8},{13,9},{14,12},{15,13},... | collective-permute-start | bytes 393224 | tf_op jit(solution)/shard_map/ppermute | solution.py:277
  73.7 3.3 %collective-permute-done.27.arrived_in = bf16[16,4096]{1,0:T(8,128)(2,1)S(1)} collective-permute-done((bf16[16,4096]{1,0:T(8,128)(2,1)S(1)}, bf16[16,4096]{1,0:T(8,128)(2,1)S(1)}, u32[]{:S(2)}, u32[]{:S(2)}) %collective-permute-start.27) | collective-permute-done | bytes 131104 | tf_op jit(solution)/shard_map/ppermute | solution.py:277
  77.0 0.1 relay.8
  77.0 0.4 collective-permute-start.28
  77.5 0.1 relay.11
  77.5 2.0 %collective-permute-start.31 = (bf16[16,4096]{1,0:T(8,128)(2,1)S(1)}, bf16[16,4096]{1,0:T(8,128)(2,1)S(1)}, u32[]{:S(2)}, u32[]{:S(2)}) collective-permute-start(bf16[16,4096]{1,0:T(8,128)(2,1)S(1)} %relay.11), channel_id=1, source_target_pairs={{0,2},{1,3},{4,0},{5,1},{8,4},{9,5},{12,8},{13,9},{14,12},{15,13},... | collective-permute-start | bytes 393224 | tf_op jit(solution)/shard_map/ppermute | solution.py:277
  79.5 2.5 %collective-permute-done.28.ahead_in = bf16[16,4096]{1,0:T(8,128)(2,1)S(1)} collective-permute-done((bf16[16,4096]{1,0:T(8,128)(2,1)S(1)}, bf16[16,4096]{1,0:T(8,128)(2,1)S(1)}, u32[]{:S(2)}, u32[]{:S(2)}) %collective-permute-start.28) | collective-permute-done | bytes 131104 | tf_op jit(solution)/shard_map/ppermute | solution.py:277
  82.0 0.5 collective-permute-done.31.behind_in
  82.5 0.1 last.1
  82.6 0.1 collective-permute-start.32
  82.7 1.2 %collective-permute-done.32.take_ref = bf16[8,4096]{1,0:T(8,128)(2,1)S(1)} collective-permute-done((bf16[8,4096]{1,0:T(8,128)(2,1)S(1)}, bf16[8,4096]{1,0:T(8,128)(2,1)S(1)}, u32[]{:S(2)}, u32[]{:S(2)}) %collective-permute-start.32) | collective-permute-done | bytes 65568 | tf_op jit(solution)/shard_map/ppermute | solution.py:286
  84.0 0.7 mix.1
  (56 shorter events, 0.5 us)
Async XLA Ops:
  0.0 25.9 %slice-start.4 = ((s8[16777216]{0:T(1024)(128)(4,1)}), s8[4194304]{0:T(1024)(128)(4,1)S(1)}, s32[]{:S(2)}) async-start(s8[16777216]{0:T(1024)(128)(4,1)} %bitcast.4), calls=%async_computation.4 | async-start | bytes 8388608
  0.0 25.9 %slice-start.8 = ((s8[16777216]{0:T(1024)(128)(4,1)}), s8[4194304]{0:T(1024)(128)(4,1)S(1)}, s32[]{:S(2)}) async-start(s8[16777216]{0:T(1024)(128)(4,1)} %bitcast.6), calls=%async_computation.8 | async-start | bytes 8388608
  0.0 25.9 %slice-start.5 = ((s8[16777216]{0:T(1024)(128)(4,1)}), s8[4194304]{0:T(1024)(128)(4,1)S(1)}, s32[]{:S(2)}) async-start(s8[16777216]{0:T(1024)(128)(4,1)} %bitcast.4), calls=%async_computation.5 | async-start | bytes 8388608
  0.0 25.9 %slice-start.6 = ((s8[16777216]{0:T(1024)(128)(4,1)}), s8[4194304]{0:T(1024)(128)(4,1)S(1)}, s32[]{:S(2)}) async-start(s8[16777216]{0:T(1024)(128)(4,1)} %bitcast.4), calls=%async_computation.6 | async-start | bytes 8388608
  0.0 25.9 %slice-start.7 = ((s8[16777216]{0:T(1024)(128)(4,1)}), s8[4194304]{0:T(1024)(128)(4,1)S(1)}, s32[]{:S(2)}) async-start(s8[16777216]{0:T(1024)(128)(4,1)} %bitcast.4), calls=%async_computation.7 | async-start | bytes 8388608
  0.0 25.9 %slice-start.9 = ((s8[16777216]{0:T(1024)(128)(4,1)}), s8[4194304]{0:T(1024)(128)(4,1)S(1)}, s32[]{:S(2)}) async-start(s8[16777216]{0:T(1024)(128)(4,1)} %bitcast.6), calls=%async_computation.9 | async-start | bytes 8388608
  0.0 25.9 %slice-start.10 = ((s8[16777216]{0:T(1024)(128)(4,1)}), s8[4194304]{0:T(1024)(128)(4,1)S(1)}, s32[]{:S(2)}) async-start(s8[16777216]{0:T(1024)(128)(4,1)} %bitcast.6), calls=%async_computation.10 | async-start | bytes 8388608
  0.0 25.9 %slice-start.11 = ((s8[16777216]{0:T(1024)(128)(4,1)}), s8[4194304]{0:T(1024)(128)(4,1)S(1)}, s32[]{:S(2)}) async-start(s8[16777216]{0:T(1024)(128)(4,1)} %bitcast.6), calls=%async_computation.11 | async-start | bytes 8388608
  1.3 6.6 %collective-permute-start.3 = (bf16[8,8192]{1,0:T(8,128)(2,1)S(1)}, bf16[8,8192]{1,0:T(8,128)(2,1)S(1)}, u32[]{:S(2)}, u32[]{:S(2)}) collective-permute-start(bf16[8,8192]{1,0:T(8,128)(2,1)S(1)} %normalize.1.refs_0_), channel_id=1, source_target_pairs={{0,2},{1,3},{4,0},{5,1},{8,4},{9,5},{12,8},{13,9},{14,12},{15,13},... | collective-permute-start | bytes 393224 | tf_op jit(solution)/shard_map/ppermute | solution.py:277
  4.4 5.2 %collective-permute-start.1 = (bf16[8,8192]{1,0:T(8,128)(2,1)S(1)}, bf16[8,8192]{1,0:T(8,128)(2,1)S(1)}, u32[]{:S(2)}, u32[]{:S(2)}) collective-permute-start(bf16[8,8192]{1,0:T(8,128)(2,1)S(1)} %normalize.1.refs_0_), channel_id=1, source_target_pairs={{0,4},{1,5},{4,8},{5,9},{8,12},{9,13},{12,14},{13,15},{14,10},{15,... | collective-permute-start | bytes 393224 | tf_op jit(solution)/shard_map/ppermute | solution.py:277
  7.9 5.0 %collective-permute-start.7 = (bf16[8,8192]{1,0:T(8,128)(2,1)S(1)}, bf16[8,8192]{1,0:T(8,128)(2,1)S(1)}, u32[]{:S(2)}, u32[]{:S(2)}) collective-permute-start(bf16[8,8192]{1,0:T(8,128)(2,1)S(1)} %collective-permute-done.3.refs_4_), channel_id=1, source_target_pairs={{0,2},{1,3},{4,0},{5,1},{8,4},{9,5},{12,8},{13,9},{14,12},{15,13},... | collective-permute-start | bytes 393224 | tf_op jit(solution)/shard_map/ppermute | solution.py:277
  9.6 5.0 %collective-permute-start.5 = (bf16[8,8192]{1,0:T(8,128)(2,1)S(1)}, bf16[8,8192]{1,0:T(8,128)(2,1)S(1)}, u32[]{:S(2)}, u32[]{:S(2)}) collective-permute-start(bf16[8,8192]{1,0:T(8,128)(2,1)S(1)} %collective-permute-done.1.refs_2_), channel_id=1, source_target_pairs={{0,4},{1,5},{4,8},{5,9},{8,12},{9,13},{12,14},{13,15},{14,10},{15,... | collective-permute-start | bytes 393224 | tf_op jit(solution)/shard_map/ppermute | solution.py:277
  12.9 5.0 %collective-permute-start.11 = (bf16[8,8192]{1,0:T(8,128)(2,1)S(1)}, bf16[8,8192]{1,0:T(8,128)(2,1)S(1)}, u32[]{:S(2)}, u32[]{:S(2)}) collective-permute-start(bf16[8,8192]{1,0:T(8,128)(2,1)S(1)} %collective-permute-done.7.refs_8_), channel_id=1, source_target_pairs={{0,2},{1,3},{4,0},{5,1},{8,4},{9,5},{12,8},{13,9},{14,12},{15,13},... | collective-permute-start | bytes 393224 | tf_op jit(solution)/shard_map/ppermute | solution.py:277
  14.6 5.0 %collective-permute-start.9 = (bf16[8,8192]{1,0:T(8,128)(2,1)S(1)}, bf16[8,8192]{1,0:T(8,128)(2,1)S(1)}, u32[]{:S(2)}, u32[]{:S(2)}) collective-permute-start(bf16[8,8192]{1,0:T(8,128)(2,1)S(1)} %collective-permute-done.5.refs_6_), channel_id=1, source_target_pairs={{0,4},{1,5},{4,8},{5,9},{8,12},{9,13},{12,14},{13,15},{14,10},{15,... | collective-permute-start | bytes 393224 | tf_op jit(solution)/shard_map/ppermute | solution.py:277
  14.9 5.0 %collective-permute-start = (bf16[8,8192]{1,0:T(8,128)(2,1)S(1)}, bf16[8,8192]{1,0:T(8,128)(2,1)S(1)}, u32[]{:S(2)}, u32[]{:S(2)}) collective-permute-start(bf16[8,8192]{1,0:T(8,128)(2,1)S(1)} %normalize.1.refs_0_), channel_id=1, source_target_pairs={{0,1},{1,0},{2,3},{3,2},{4,5},{5,4},{6,7},{7,6},{8,9},{9,8},{10,11... | collective-permute-start | bytes 393224 | tf_op jit(solution)/shard_map/ppermute | solution.py:286
  14.9 5.6 %collective-permute-start.4 = (bf16[8,8192]{1,0:T(8,128)(2,1)S(1)}, bf16[8,8192]{1,0:T(8,128)(2,1)S(1)}, u32[]{:S(2)}, u32[]{:S(2)}) collective-permute-start(bf16[8,8192]{1,0:T(8,128)(2,1)S(1)} %collective-permute-done.3.refs_4_), channel_id=1, source_target_pairs={{0,1},{1,0},{2,3},{3,2},{4,5},{5,4},{6,7},{7,6},{8,9},{9,8},{10,11... | collective-permute-start | bytes 393224 | tf_op jit(solution)/shard_map/ppermute | solution.py:286
  15.4 5.1 %collective-permute-start.2 = (bf16[8,8192]{1,0:T(8,128)(2,1)S(1)}, bf16[8,8192]{1,0:T(8,128)(2,1)S(1)}, u32[]{:S(2)}, u32[]{:S(2)}) collective-permute-start(bf16[8,8192]{1,0:T(8,128)(2,1)S(1)} %collective-permute-done.1.refs_2_), channel_id=1, source_target_pairs={{0,1},{1,0},{2,3},{3,2},{4,5},{5,4},{6,7},{7,6},{8,9},{9,8},{10,11... | collective-permute-start | bytes 393224 | tf_op jit(solution)/shard_map/ppermute | solution.py:286
  19.6 5.0 %collective-permute-start.13 = (bf16[8,8192]{1,0:T(8,128)(2,1)S(1)}, bf16[8,8192]{1,0:T(8,128)(2,1)S(1)}, u32[]{:S(2)}, u32[]{:S(2)}) collective-permute-start(bf16[8,8192]{1,0:T(8,128)(2,1)S(1)} %pick.1), channel_id=1, source_target_pairs={{0,4},{1,3},{4,8},{5,1},{8,12},{9,5},{12,14},{13,9},{14,10},{15,13... | collective-permute-start | bytes 393224 | tf_op jit(solution)/shard_map/ppermute | solution.py:277
  19.9 4.6 %collective-permute-start.8 = (bf16[8,8192]{1,0:T(8,128)(2,1)S(1)}, bf16[8,8192]{1,0:T(8,128)(2,1)S(1)}, u32[]{:S(2)}, u32[]{:S(2)}) collective-permute-start(bf16[8,8192]{1,0:T(8,128)(2,1)S(1)} %collective-permute-done.7.refs_8_), channel_id=1, source_target_pairs={{0,1},{1,0},{2,3},{3,2},{4,5},{5,4},{6,7},{7,6},{8,9},{9,8},{10,11... | collective-permute-start | bytes 393224 | tf_op jit(solution)/shard_map/ppermute | solution.py:286
  20.0 4.6 %collective-permute-start.6 = (bf16[8,8192]{1,0:T(8,128)(2,1)S(1)}, bf16[8,8192]{1,0:T(8,128)(2,1)S(1)}, u32[]{:S(2)}, u32[]{:S(2)}) collective-permute-start(bf16[8,8192]{1,0:T(8,128)(2,1)S(1)} %collective-permute-done.5.refs_6_), channel_id=1, source_target_pairs={{0,1},{1,0},{2,3},{3,2},{4,5},{5,4},{6,7},{7,6},{8,9},{9,8},{10,11... | collective-permute-start | bytes 393224 | tf_op jit(solution)/shard_map/ppermute | solution.py:286
  20.5 4.1 %collective-permute-start.12 = (bf16[8,8192]{1,0:T(8,128)(2,1)S(1)}, bf16[8,8192]{1,0:T(8,128)(2,1)S(1)}, u32[]{:S(2)}, u32[]{:S(2)}) collective-permute-start(bf16[8,8192]{1,0:T(8,128)(2,1)S(1)} %collective-permute-done.11.odd_ref.refs_12_), channel_id=1, source_target_pairs={{0,1},{1,0},{2,3},{3,2},{4,5},{5,4},{6,7},{7,6},{8,9},{9,8},{10,11... | collective-permute-start | bytes 393224 | tf_op jit(solution)/shard_map/ppermute | solution.py:286
  20.5 4.1 %collective-permute-start.10 = (bf16[8,8192]{1,0:T(8,128)(2,1)S(1)}, bf16[8,8192]{1,0:T(8,128)(2,1)S(1)}, u32[]{:S(2)}, u32[]{:S(2)}) collective-permute-start(bf16[8,8192]{1,0:T(8,128)(2,1)S(1)} %collective-permute-done.9.even_ref.refs_10_), channel_id=1, source_target_pairs={{0,1},{1,0},{2,3},{3,2},{4,5},{5,4},{6,7},{7,6},{8,9},{9,8},{10,11... | collective-permute-start | bytes 393224 | tf_op jit(solution)/shard_map/ppermute | solution.py:286
  24.6 1.3 %collective-permute-start.14 = (bf16[8,8192]{1,0:T(8,128)(2,1)S(1)}, bf16[8,8192]{1,0:T(8,128)(2,1)S(1)}, u32[]{:S(2)}, u32[]{:S(2)}) collective-permute-start(bf16[8,8192]{1,0:T(8,128)(2,1)S(1)} %collective-permute-done.13.refs_14_), channel_id=1, source_target_pairs={{0,1},{1,0},{2,3},{3,2},{4,5},{5,4},{6,7},{7,6},{8,9},{9,8},{10,11... | collective-permute-start | bytes 393224 | tf_op jit(solution)/shard_map/ppermute | solution.py:286
  28.8 4.6 %collective-permute-start.16 = (bf16[128,512]{1,0:T(8,128)(2,1)S(1)}, bf16[128,512]{1,0:T(8,128)(2,1)S(1)}, u32[]{:S(2)}, u32[]{:S(2)}) collective-permute-start(bf16[128,512]{1,0:T(8,128)(2,1)S(1)} %get-tuple-element.21.value_ref), channel_id=1, source_target_pairs={{0,1},{1,0},{2,3},{3,2},{4,5},{5,4},{6,7},{7,6},{8,9},{9,8},{10,11... | collective-permute-start | bytes 393224 | tf_op jit(solution)/shard_map/ppermute | solution.py:286
  31.8 9.4 %collective-permute-start.15 = (bf16[128,512]{1,0:T(8,128)(2,1)S(1)}, bf16[128,512]{1,0:T(8,128)(2,1)S(1)}, u32[]{:S(2)}, u32[]{:S(2)}) collective-permute-start(bf16[128,512]{1,0:T(8,128)(2,1)S(1)} %up_project.3.value_ref), channel_id=1, source_target_pairs={{0,8},{1,9},{2,10},{3,11},{4,12},{5,13},{6,14},{7,15},{8,0},{9,1},... | collective-permute-start | bytes 393224 | tf_op jit(solution)/shard_map/ppermute | solution.py:286
  33.4 8.0 %collective-permute-start.18 = (bf16[128,512]{1,0:T(8,128)(2,1)S(1)}, bf16[128,512]{1,0:T(8,128)(2,1)S(1)}, u32[]{:S(2)}, u32[]{:S(2)}) collective-permute-start(bf16[128,512]{1,0:T(8,128)(2,1)S(1)} %turn.8.value_ref), channel_id=1, source_target_pairs={{0,2},{1,3},{2,0},{3,1},{4,6},{5,7},{6,4},{7,5},{8,10},{9,11},{10,... | collective-permute-start | bytes 393224 | tf_op jit(solution)/shard_map/ppermute | solution.py:286
  41.3 1.4 %collective-permute-start.17 = (bf16[128,512]{1,0:T(8,128)(2,1)S(1)}, bf16[128,512]{1,0:T(8,128)(2,1)S(1)}, u32[]{:S(2)}, u32[]{:S(2)}) collective-permute-start(bf16[128,512]{1,0:T(8,128)(2,1)S(1)} %turn.9.value_ref), channel_id=1, source_target_pairs={{0,1},{1,0},{2,3},{3,2},{4,5},{5,4},{6,7},{7,6},{8,9},{9,8},{10,11... | collective-permute-start | bytes 393224 | tf_op jit(solution)/shard_map/ppermute | solution.py:286
  41.4 16.2 %slice-start = ((s8[16777216]{0:T(1024)(128)(4,1)}), s8[4194304]{0:T(1024)(128)(4,1)S(1)}, s32[]{:S(2)}) async-start(s8[16777216]{0:T(1024)(128)(4,1)} %bitcast.2), calls=%async_computation | async-start | bytes 8388608
  41.4 16.2 %copy-start.1 = (f32[1024]{0:T(1024)S(1)}, f32[1024]{0:T(1024)}, u32[]{:S(2)}) copy-start(f32[1024]{0:T(1024)} %param.11) | copy-start | bytes 12292
  41.5 5.9 %collective-permute-start.20 = (bf16[128,512]{1,0:T(8,128)(2,1)S(1)}, bf16[128,512]{1,0:T(8,128)(2,1)S(1)}, u32[]{:S(2)}, u32[]{:S(2)}) collective-permute-start(bf16[128,512]{1,0:T(8,128)(2,1)S(1)} %turn.10.value_ref), channel_id=1, source_target_pairs={{0,4},{1,5},{2,6},{3,7},{4,0},{5,1},{6,2},{7,3},{8,12},{9,13},{10,... | collective-permute-start | bytes 393224 | tf_op jit(solution)/shard_map/ppermute | solution.py:286
  42.7 15.0 %slice-start.1 = ((s8[16777216]{0:T(1024)(128)(4,1)}), s8[4194304]{0:T(1024)(128)(4,1)S(1)}, s32[]{:S(2)}) async-start(s8[16777216]{0:T(1024)(128)(4,1)} %bitcast.2), calls=%async_computation.1 | async-start | bytes 8388608
  42.7 5.6 %collective-permute-start.19 = (bf16[128,512]{1,0:T(8,128)(2,1)S(1)}, bf16[128,512]{1,0:T(8,128)(2,1)S(1)}, u32[]{:S(2)}, u32[]{:S(2)}) collective-permute-start(bf16[128,512]{1,0:T(8,128)(2,1)S(1)} %turn.11.value_ref), channel_id=1, source_target_pairs={{0,2},{1,3},{2,0},{3,1},{4,6},{5,7},{6,4},{7,5},{8,10},{9,11},{10,... | collective-permute-start | bytes 393224 | tf_op jit(solution)/shard_map/ppermute | solution.py:286
  47.4 10.3 %slice-start.2 = ((s8[16777216]{0:T(1024)(128)(4,1)}), s8[4194304]{0:T(1024)(128)(4,1)S(1)}, s32[]{:S(2)}) async-start(s8[16777216]{0:T(1024)(128)(4,1)} %bitcast.2), calls=%async_computation.2 | async-start | bytes 8388608
  48.4 9.3 %slice-start.3 = ((s8[16777216]{0:T(1024)(128)(4,1)}), s8[4194304]{0:T(1024)(128)(4,1)S(1)}, s32[]{:S(2)}) async-start(s8[16777216]{0:T(1024)(128)(4,1)} %bitcast.2), calls=%async_computation.3 | async-start | bytes 8388608
  48.4 7.3 %collective-permute-start.21 = (bf16[128,512]{1,0:T(8,128)(2,1)S(1)}, bf16[128,512]{1,0:T(8,128)(2,1)S(1)}, u32[]{:S(2)}, u32[]{:S(2)}) collective-permute-start(bf16[128,512]{1,0:T(8,128)(2,1)S(1)} %turn.13.value_ref), channel_id=1, source_target_pairs={{0,4},{1,5},{2,6},{3,7},{4,0},{5,1},{6,2},{7,3},{8,12},{9,13},{10,... | collective-permute-start | bytes 393224 | tf_op jit(solution)/shard_map/ppermute | solution.py:286
  49.4 8.2 %collective-permute-start.22 = (bf16[128,512]{1,0:T(8,128)(2,1)S(1)}, bf16[128,512]{1,0:T(8,128)(2,1)S(1)}, u32[]{:S(2)}, u32[]{:S(2)}) collective-permute-start(bf16[128,512]{1,0:T(8,128)(2,1)S(1)} %turn.12.value_ref), channel_id=1, source_target_pairs={{0,8},{1,9},{2,10},{3,11},{4,12},{5,13},{6,14},{7,15},{8,0},{9,1},... | collective-permute-start | bytes 393224 | tf_op jit(solution)/shard_map/ppermute | solution.py:286
  59.2 24.8 %copy-start = (bf16[8,8192]{1,0:T(8,128)(2,1)S(1)}, bf16[8,8192]{1,0:T(8,128)(2,1)}, u32[]{:S(2)}) copy-start(bf16[8,8192]{1,0:T(8,128)(2,1)} %tokens_ref.1) | copy-start | bytes 393220
  59.2 1.5 %collective-permute-start.23 = (bf16[16,4096]{1,0:T(8,128)(2,1)S(1)}, bf16[16,4096]{1,0:T(8,128)(2,1)S(1)}, u32[]{:S(2)}, u32[]{:S(2)}) collective-permute-start(bf16[16,4096]{1,0:T(8,128)(2,1)S(1)} %get-tuple-element.29), channel_id=1, source_target_pairs={{0,1},{1,0},{2,3},{3,2},{4,5},{5,4},{6,7},{7,6},{8,9},{9,8},{10,11... | collective-permute-start | bytes 393224 | tf_op jit(solution)/shard_map/ppermute | solution.py:286
  60.7 5.6 %collective-permute-start.25 = (bf16[112,4096]{1,0:T(8,128)(2,1)S(1)}, bf16[112,4096]{1,0:T(8,128)(2,1)S(1)}, u32[]{:S(2)}, u32[]{:S(2)}) collective-permute-start(bf16[112,4096]{1,0:T(8,128)(2,1)S(1)} %get-tuple-element.32), channel_id=1, source_target_pairs={{0,1},{1,0},{2,3},{3,2},{4,5},{5,4},{6,7},{7,6},{8,9},{9,8},{10,11... | collective-permute-start | bytes 2752520 | tf_op jit(solution)/shard_map/ppermute | solution.py:286
  61.3 5.0 %collective-permute-start.24 = (bf16[16,4096]{1,0:T(8,128)(2,1)S(1)}, bf16[16,4096]{1,0:T(8,128)(2,1)S(1)}, u32[]{:S(2)}, u32[]{:S(2)}) collective-permute-start(bf16[16,4096]{1,0:T(8,128)(2,1)S(1)} %far.1), channel_id=1, source_target_pairs={{0,4},{1,3},{4,8},{5,1},{8,12},{9,5},{12,14},{13,9},{14,10},{15,13... | collective-permute-start | bytes 393224 | tf_op jit(solution)/shard_map/ppermute | solution.py:277
  66.4 5.0 %collective-permute-start.26 = (bf16[16,4096]{1,0:T(8,128)(2,1)S(1)}, bf16[16,4096]{1,0:T(8,128)(2,1)S(1)}, u32[]{:S(2)}, u32[]{:S(2)}) collective-permute-start(bf16[16,4096]{1,0:T(8,128)(2,1)S(1)} %relay.6), channel_id=1, source_target_pairs={{0,4},{1,5},{4,8},{5,9},{8,12},{9,13},{12,14},{13,15},{14,10},{15,... | collective-permute-start | bytes 393224 | tf_op jit(solution)/shard_map/ppermute | solution.py:277
  66.9 5.0 %collective-permute-start.29 = (bf16[16,4096]{1,0:T(8,128)(2,1)S(1)}, bf16[16,4096]{1,0:T(8,128)(2,1)S(1)}, u32[]{:S(2)}, u32[]{:S(2)}) collective-permute-start(bf16[16,4096]{1,0:T(8,128)(2,1)S(1)} %relay.9), channel_id=1, source_target_pairs={{0,2},{1,3},{4,0},{5,1},{8,4},{9,5},{12,8},{13,9},{14,12},{15,13},... | collective-permute-start | bytes 393224 | tf_op jit(solution)/shard_map/ppermute | solution.py:277
  71.5 5.5 %collective-permute-start.27 = (bf16[16,4096]{1,0:T(8,128)(2,1)S(1)}, bf16[16,4096]{1,0:T(8,128)(2,1)S(1)}, u32[]{:S(2)}, u32[]{:S(2)}) collective-permute-start(bf16[16,4096]{1,0:T(8,128)(2,1)S(1)} %relay.7), channel_id=1, source_target_pairs={{0,4},{1,5},{4,8},{5,9},{8,12},{9,13},{12,14},{13,15},{14,10},{15,... | collective-permute-start | bytes 393224 | tf_op jit(solution)/shard_map/ppermute | solution.py:277
  72.0 5.5 %collective-permute-start.30 = (bf16[16,4096]{1,0:T(8,128)(2,1)S(1)}, bf16[16,4096]{1,0:T(8,128)(2,1)S(1)}, u32[]{:S(2)}, u32[]{:S(2)}) collective-permute-start(bf16[16,4096]{1,0:T(8,128)(2,1)S(1)} %relay.10), channel_id=1, source_target_pairs={{0,2},{1,3},{4,0},{5,1},{8,4},{9,5},{12,8},{13,9},{14,12},{15,13},... | collective-permute-start | bytes 393224 | tf_op jit(solution)/shard_map/ppermute | solution.py:277
  77.0 5.0 %collective-permute-start.28 = (bf16[16,4096]{1,0:T(8,128)(2,1)S(1)}, bf16[16,4096]{1,0:T(8,128)(2,1)S(1)}, u32[]{:S(2)}, u32[]{:S(2)}) collective-permute-start(bf16[16,4096]{1,0:T(8,128)(2,1)S(1)} %relay.8), channel_id=1, source_target_pairs={{0,4},{1,5},{4,8},{5,9},{8,12},{9,13},{12,14},{13,15},{14,10},{15,... | collective-permute-start | bytes 393224 | tf_op jit(solution)/shard_map/ppermute | solution.py:277
  77.5 5.0 %collective-permute-start.31 = (bf16[16,4096]{1,0:T(8,128)(2,1)S(1)}, bf16[16,4096]{1,0:T(8,128)(2,1)S(1)}, u32[]{:S(2)}, u32[]{:S(2)}) collective-permute-start(bf16[16,4096]{1,0:T(8,128)(2,1)S(1)} %relay.11), channel_id=1, source_target_pairs={{0,2},{1,3},{4,0},{5,1},{8,4},{9,5},{12,8},{13,9},{14,12},{15,13},... | collective-permute-start | bytes 393224 | tf_op jit(solution)/shard_map/ppermute | solution.py:277
  82.6 1.3 %collective-permute-start.32 = (bf16[8,4096]{1,0:T(8,128)(2,1)S(1)}, bf16[8,4096]{1,0:T(8,128)(2,1)S(1)}, u32[]{:S(2)}, u32[]{:S(2)}) collective-permute-start(bf16[8,4096]{1,0:T(8,128)(2,1)S(1)} %get-tuple-element.34), channel_id=1, source_target_pairs={{0,1},{1,0},{2,3},{3,2},{4,5},{5,4},{6,7},{7,6},{8,9},{9,8},{10,11... | collective-permute-start | bytes 196616 | tf_op jit(solution)/shard_map/ppermute | solution.py:286

commit v7 on v6

--- a/solution.py
+++ b/solution.py
@@ -132,6 +132,15 @@
     )(*parts, gate_weight, up_weight)
 
 
+def ring_order(chips):
+    steps = chips // 2
+    early = [steps - 1, chips + 1 - steps, steps]
+    return early + [away for away in range(chips) if away not in early]
+
+
+EARLY = 3
+
+
 def down_kernel(blocks, chips, scale, flip, a_ref, b_ref, clip_ref, weight_ref, *refs):
     outs, (rows_ref, mixed_ref) = refs[:-2], refs[-2:]
     half = a_ref.shape[1]
@@ -152,7 +161,7 @@
     each = rows // chips
     me = lax.axis_index("hid")
     for chip in range(chips):
-        spot = pl.multiple_of(ring_place(me // 2, chip + chips // 2, chips) * each, each)
+        spot = pl.multiple_of(ring_place(me // 2, ring_order(chips)[chip], chips) * each, each)
         mixed_ref[chip * each : (chip + 1) * each, :] = rows_ref[pl.ds(spot, each), :].astype(jnp.bfloat16)
     wide = weight_ref.shape[1] // 2
     side = 1 - me % 2 if flip else me % 2
@@ -169,7 +178,7 @@
     width, depth = weight.shape[0], weight.shape[1] // 2
     vmem = pl.BlockSpec(memory_space=pltpu.VMEM)
     outs = [
-        jax.ShapeDtypeStruct((count, depth), jnp.bfloat16) for count in (rows // chips, rows - rows // chips)
+        jax.ShapeDtypeStruct((count, depth), jnp.bfloat16) for count in (EARLY * (rows // chips), rows - EARLY * (rows // chips))
     ]
     return pl.pallas_call(
         functools.partial(down_kernel, width // BLOCK, chips, total**-0.5, flip),
@@ -214,21 +223,25 @@
 
 
 def chunk(away, chips, own_ref, arrived_ref):
-    rows = own_ref.shape[0] // (chips - 1)
-    spot = (away + chips // 2 - 1) % chips
+    spot = ring_order(chips).index(away % chips)
+    if spot < EARLY:
+        rows = own_ref.shape[0] // EARLY
+    else:
+        rows, spot = own_ref.shape[0] // (chips - EARLY), spot - EARLY
     at = slice(spot * rows, (spot + 1) * rows)
     return own_ref[at, :].astype(jnp.float32) + arrived_ref[at, :].astype(jnp.float32)
 
 
-def sum_kernel(one_ref, two_ref, out_ref):
-    out_ref[...] = (one_ref[...].astype(jnp.float32) + two_ref[...].astype(jnp.float32)).astype(jnp.bfloat16)
-
-
-def relay_kernel(away, chips, core, arrived_in, own_ref, arrived_ref, out_ref):
-    value = arrived_in[...].astype(jnp.float32)
-    if core is not None:
-        value = jnp.where(lax.axis_index("hid") % 2 == core, value, 0.0)
-    out_ref[...] = (chunk(away, chips, own_ref, arrived_ref) + value).astype(jnp.bfloat16)
+def sum_kernel(away, chips, own_ref, arrived_ref, out_ref):
+    out_ref[...] = chunk(away, chips, own_ref, arrived_ref).astype(jnp.bfloat16)
+
+
+def relay_kernel(away, chips, core, own_ref, arrived_ref, *refs):
+    out_ref = refs[-1]
+    value = chunk(away, chips, own_ref, arrived_ref) + refs[0][...].astype(jnp.float32)
+    if len(refs) == 3:
+        value = value + jnp.where(lax.axis_index("hid") % 2 == core, refs[1][...].astype(jnp.float32), 0.0)
+    out_ref[...] = value.astype(jnp.bfloat16)
 
 
 def last_kernel(chips, ahead_in, behind_in, own_ref, arrived_ref, keep_ref, give_ref, sum_ref):
@@ -291,10 +304,12 @@
     mine, shifts = [normed], [0]
     ahead = behind = normed
     for step in range(1, steps):
+        if step == steps - 1:
+            far = hop(both(pick_kernel, ahead, behind, "pick"), 2, -2)
         ahead, behind = right(ahead), left(behind)
         mine += [ahead, behind]
         shifts += [-step, step]
-    mine.append(hop(both(pick_kernel, ahead, behind, "pick"), 1, -1))
+    mine.append(far)
     shifts.append(steps)
     parts = [block for own in mine for block in (own, cross(own))]
 
@@ -326,21 +341,25 @@
 
     total = count * width
     limits = clip_scale.reshape(1, -1)
-    theirs_far, theirs = down_project(half_a, half_b, limits, down_weight, True, chips, total)
-    arrived_far = cross(theirs_far)
-    own_far, own = down_project(half_a, half_b, limits, down_weight, False, chips, total)
-    arrived = cross(once(theirs, own, arrived_far))
-    rows, wide = own_far.shape
+    theirs_early, theirs = down_project(half_a, half_b, limits, down_weight, True, chips, total)
+    arrived_early = cross(theirs_early)
+    own_early, own = down_project(half_a, half_b, limits, down_weight, False, chips, total)
+    arrived = cross(once(theirs, own, arrived_early))
+    rows, wide = own_early.shape[0] // EARLY, own_early.shape[1]
     part = jax.ShapeDtypeStruct((rows, wide), jnp.bfloat16)
 
-    ahead = behind = hop(small(sum_kernel, part, (own_far, arrived_far), "far"), 1, -1)
-    for away in range(steps - 1, 0, -1):
-        cores = (0, 1) if away == steps - 1 else (None, None)
+    first = [
+        small(functools.partial(sum_kernel, away, chips), part, (own_early, arrived_early), "sum")
+        for away in (steps - 1, 1 - steps, steps)
+    ]
+    ahead, behind, far = right(first[0]), left(first[1]), hop(first[2], 2, -2)
+    for away in range(steps - 2, 0, -1):
+        more = (far,) if away == steps - 2 else ()
         ahead = small(
-            functools.partial(relay_kernel, away, chips, cores[0]), part, (ahead, own, arrived), "relay"
+            functools.partial(relay_kernel, away, chips, 0), part, (own, arrived, ahead, *more), "relay"
         )
         behind = small(
-            functools.partial(relay_kernel, -away, chips, cores[1]), part, (behind, own, arrived), "relay"
+            functools.partial(relay_kernel, -away, chips, 1), part, (own, arrived, behind, *more), "relay"
         )
         ahead, behind = right(ahead), left(behind)
     half = jax.ShapeDtypeStruct((rows // 2, wide), jnp.bfloat16)

time: 84.8 us -> 82.9 us (0.978)
  waiting for transfers between devices: 46.4 us -> 41.1 us
  starting transfers between devices: 26.6 us -> 29.9 us
    ppermute x14, waiting for transfers between devices: 27.8 us -> 22.7 us  [hop(): return lax.ppermute(value, 'hid', pairs)]
    ppermute x14, starting transfers between devices: 14.8 us -> 17.3 us  [hop(): return lax.ppermute(value, 'hid', pairs)]
  transfers between devices with their start and end apart: 33 -> 33, of which waited for: 18 -> 21; matrix products, arithmetic and copies ran while one was open for 0% -> 0% of each run, Pallas kernels for 6% -> 6%
where the time goes in v7:
time: 82.9 us; the launch traced here: 82.7 us
  waiting for transfers between devices  41.1 us (50%)
  starting transfers between devices  29.9 us (36%)
  Pallas kernels  11.2 us (14%)
    ppermute x14, waiting for transfers between devices, hop(): return lax.ppermute(value, 'hid', pairs)  22.7 us
    ppermute x19, waiting for transfers between devices, cross(): return lax.ppermute(value, 'hid', [(d, d ^ mask) for d in range(count)])  18.4 us
    ppermute x14, starting transfers between devices, hop(): return lax.ppermute(value, 'hid', pairs)  17.3 us
    ppermute x19, starting transfers between devices, cross(): return lax.ppermute(value, 'hid', [(d, d ^ mask) for d in range(count)])  12.6 us
    pallas_call x2, Pallas kernels, up_project(): pl.pallas_call(functools.partial(up_kernel, shifts, first, slice(at * wid...  5.53 us
    pallas_call x2, Pallas kernels, down_project(): pl.pallas_call(functools.partial(down_kernel, width // BLOCK, chips, tota...  2.9 us
  transfers between devices with their start and end apart: 33, of which 21 were waited for; matrix products, arithmetic and copies ran while one was open for 0% of the time, Pallas kernels for 6%

profile of v7, /device:TPU:0, one launch (start us, length us, event | category | flops | bytes accessed | tf_op | source)
XLA Modules:
  0.0 82.7 jit_solution(6355831631398342153)
XLA Ops:
  0.0 1.3 %normalize.1.refs_0_ = bf16[8,8192]{1,0:T(8,128)(2,1)S(1)} custom-call(bf16[8,8192]{1,0:T(8,128)(2,1)} %tokens_ref.1, f32[1,8192]{1,0:T(1,128)} %bitcast.10), custom_call_target="tpu_custom_call" | custom-call | flops 20000000000 | bytes 262144 | tf_op jit(solution)/shard_map/normalize/pallas_call | solution.py:47
  1.3 3.0 %collective-permute-start.3 = (bf16[8,8192]{1,0:T(8,128)(2,1)S(1)}, bf16[8,8192]{1,0:T(8,128)(2,1)S(1)}, u32[]{:S(2)}, u32[]{:S(2)}) collective-permute-start(bf16[8,8192]{1,0:T(8,128)(2,1)S(1)} %normalize.1.refs_0_), channel_id=1, source_target_pairs={{0,2},{1,3},{4,0},{5,1},{8,4},{9,5},{12,8},{13,9},{14,12},{15,13},... | collective-permute-start | bytes 393224 | tf_op jit(solution)/shard_map/ppermute | solution.py:290
  4.4 0.1 collective-permute-start.1
  4.5 3.4 %collective-permute-done.3.refs_4_ = bf16[8,8192]{1,0:T(8,128)(2,1)S(1)} collective-permute-done((bf16[8,8192]{1,0:T(8,128)(2,1)S(1)}, bf16[8,8192]{1,0:T(8,128)(2,1)S(1)}, u32[]{:S(2)}, u32[]{:S(2)}) %collective-permute-start.3) | collective-permute-done | bytes 131104 | tf_op jit(solution)/shard_map/ppermute | solution.py:290
  7.9 1.7 %collective-permute-start.7 = (bf16[8,8192]{1,0:T(8,128)(2,1)S(1)}, bf16[8,8192]{1,0:T(8,128)(2,1)S(1)}, u32[]{:S(2)}, u32[]{:S(2)}) collective-permute-start(bf16[8,8192]{1,0:T(8,128)(2,1)S(1)} %collective-permute-done.3.refs_4_), channel_id=1, source_target_pairs={{0,2},{1,3},{4,0},{5,1},{8,4},{9,5},{12,8},{13,9},{14,12},{15,13},... | collective-permute-start | bytes 393224 | tf_op jit(solution)/shard_map/ppermute | solution.py:290
  9.6 0.3 collective-permute-start.5
  9.9 0.5 collective-permute-start.4
  10.5 2.4 %collective-permute-done.7.odd_ref.refs_8_ = bf16[8,8192]{1,0:T(8,128)(2,1)S(1)} collective-permute-done((bf16[8,8192]{1,0:T(8,128)(2,1)S(1)}, bf16[8,8192]{1,0:T(8,128)(2,1)S(1)}, u32[]{:S(2)}, u32[]{:S(2)}) %collective-permute-start.7) | collective-permute-done | bytes 131104 | tf_op jit(solution)/shard_map/ppermute | solution.py:290
  12.9 1.7 %collective-permute-start.11 = (bf16[8,8192]{1,0:T(8,128)(2,1)S(1)}, bf16[8,8192]{1,0:T(8,128)(2,1)S(1)}, u32[]{:S(2)}, u32[]{:S(2)}) collective-permute-start(bf16[8,8192]{1,0:T(8,128)(2,1)S(1)} %collective-permute-done.7.odd_ref.refs_8_), channel_id=1, source_target_pairs={{0,2},{1,3},{4,0},{5,1},{8,4},{9,5},{12,8},{13,9},{14,12},{15,13},... | collective-permute-start | bytes 393224 | tf_op jit(solution)/shard_map/ppermute | solution.py:290
  14.6 1.6 %collective-permute-start.13 = (bf16[8,8192]{1,0:T(8,128)(2,1)S(1)}, bf16[8,8192]{1,0:T(8,128)(2,1)S(1)}, u32[]{:S(2)}, u32[]{:S(2)}) collective-permute-start(bf16[8,8192]{1,0:T(8,128)(2,1)S(1)} %pick.1), channel_id=1, source_target_pairs={{0,8},{1,7},{4,12},{5,3},{8,14},{9,1},{12,10},{13,5},{14,6},{15,9}... | collective-permute-start | bytes 393224 | tf_op jit(solution)/shard_map/ppermute | solution.py:290
  16.2 1.6 %collective-permute-start.9 = (bf16[8,8192]{1,0:T(8,128)(2,1)S(1)}, bf16[8,8192]{1,0:T(8,128)(2,1)S(1)}, u32[]{:S(2)}, u32[]{:S(2)}) collective-permute-start(bf16[8,8192]{1,0:T(8,128)(2,1)S(1)} %collective-permute-done.5.even_ref.refs_6_), channel_id=1, source_target_pairs={{0,4},{1,5},{4,8},{5,9},{8,12},{9,13},{12,14},{13,15},{14,10},{15,... | collective-permute-start | bytes 393224 | tf_op jit(solution)/shard_map/ppermute | solution.py:290
  17.7 0.5 collective-permute-start.6
  18.3 2.0 %collective-permute-done.11.refs_12_ = bf16[8,8192]{1,0:T(8,128)(2,1)S(1)} collective-permute-done((bf16[8,8192]{1,0:T(8,128)(2,1)S(1)}, bf16[8,8192]{1,0:T(8,128)(2,1)S(1)}, u32[]{:S(2)}, u32[]{:S(2)}) %collective-permute-start.11) | collective-permute-done | bytes 131104 | tf_op jit(solution)/shard_map/ppermute | solution.py:290
  20.3 1.7 %collective-permute-done.13.refs_14_ = bf16[8,8192]{1,0:T(8,128)(2,1)S(1)} collective-permute-done((bf16[8,8192]{1,0:T(8,128)(2,1)S(1)}, bf16[8,8192]{1,0:T(8,128)(2,1)S(1)}, u32[]{:S(2)}, u32[]{:S(2)}) %collective-permute-start.13) | collective-permute-done | bytes 131104 | tf_op jit(solution)/shard_map/ppermute | solution.py:290
  22.0 0.2 collective-permute-done.9.refs_10_
  22.2 0.3 collective-permute-start.10
  22.5 0.8 collective-permute-done.14.refs_15_
  23.3 0.2 collective-permute-done.10.refs_11_
  23.6 2.8 %up_project.2 = (bf16[128,512]{1,0:T(8,128)(2,1)S(1)}, bf16[128,8192]{1,0:T(8,128)(2,1)S(1)}) custom-call(bf16[8,8192]{1,0:T(8,128)(2,1)S(1)} %normalize.1.refs_0_, bf16[8,8192]{1,0:T(8,128)(2,1)S(1)} %collective-permute-done.refs_1_, bf16[8,8192]{1,0:T(8,128)(2,1)S(1)} %collective-permute-done.1.refs_2_, ...), custom_call_target="tpu_custom_call" | custom-call | flops 2147483648 | tf_op jit(solution)/shard_map/up_project/pallas_call | solution.py:123
  26.4 0.4 collective-permute-start.16
  26.8 2.8 %up_project.3.value_ref = bf16[128,512]{1,0:T(8,128)(2,1)S(1)} custom-call(bf16[128,8192]{1,0:T(8,128)(2,1)S(1)} %get-tuple-element.20.refs_0_, bf16[8192,1024]{1,0:T(8,128)(2,1)S(1)} %bitcast.5, bf16[8192,1024]{1,0:T(8,128)(2,1)S(1)} %bitcast.7), custom_call_target="tpu_custom_call" | custom-call | flops 2147483648 | tf_op jit(solution)/shard_map/up_project/pallas_call | solution.py:123
  29.5 2.6 %collective-permute-start.15 = (bf16[128,512]{1,0:T(8,128)(2,1)S(1)}, bf16[128,512]{1,0:T(8,128)(2,1)S(1)}, u32[]{:S(2)}, u32[]{:S(2)}) collective-permute-start(bf16[128,512]{1,0:T(8,128)(2,1)S(1)} %up_project.3.value_ref), channel_id=1, source_target_pairs={{0,8},{1,9},{2,10},{3,11},{4,12},{5,13},{6,14},{7,15},{8,0},{9,1},... | collective-permute-start | bytes 393224 | tf_op jit(solution)/shard_map/ppermute | solution.py:299
  32.2 0.9 %collective-permute-start.18 = (bf16[128,512]{1,0:T(8,128)(2,1)S(1)}, bf16[128,512]{1,0:T(8,128)(2,1)S(1)}, u32[]{:S(2)}, u32[]{:S(2)}) collective-permute-start(bf16[128,512]{1,0:T(8,128)(2,1)S(1)} %turn.8.value_ref), channel_id=1, source_target_pairs={{0,2},{1,3},{2,0},{3,1},{4,6},{5,7},{6,4},{7,5},{8,10},{9,11},{10,... | collective-permute-start | bytes 393224 | tf_op jit(solution)/shard_map/ppermute | solution.py:299
  33.2 5.8 %collective-permute-done.15.other_ref = bf16[128,512]{1,0:T(8,128)(2,1)S(1)} collective-permute-done((bf16[128,512]{1,0:T(8,128)(2,1)S(1)}, bf16[128,512]{1,0:T(8,128)(2,1)S(1)}, u32[]{:S(2)}, u32[]{:S(2)}) %collective-permute-start.15) | collective-permute-done | bytes 131104 | tf_op jit(solution)/shard_map/ppermute | solution.py:299
  39.1 0.1 collective-permute-start.17
  39.2 0.0 slice-start
  39.2 0.8 collective-permute-start.20
  40.0 0.4 collective-permute-done.17.other_ref
  40.5 0.0 slice-start.1
  40.5 2.3 %collective-permute-start.19 = (bf16[128,512]{1,0:T(8,128)(2,1)S(1)}, bf16[128,512]{1,0:T(8,128)(2,1)S(1)}, u32[]{:S(2)}, u32[]{:S(2)}) collective-permute-start(bf16[128,512]{1,0:T(8,128)(2,1)S(1)} %turn.11.value_ref), channel_id=1, source_target_pairs={{0,2},{1,3},{2,0},{3,1},{4,6},{5,7},{6,4},{7,5},{8,10},{9,11},{10,... | collective-permute-start | bytes 393224 | tf_op jit(solution)/shard_map/ppermute | solution.py:299
  42.9 2.3 %collective-permute-done.20.other_ref = bf16[128,512]{1,0:T(8,128)(2,1)S(1)} collective-permute-done((bf16[128,512]{1,0:T(8,128)(2,1)S(1)}, bf16[128,512]{1,0:T(8,128)(2,1)S(1)}, u32[]{:S(2)}, u32[]{:S(2)}) %collective-permute-start.20) | collective-permute-done | bytes 131104 | tf_op jit(solution)/shard_map/ppermute | solution.py:299
  45.2 0.0 slice-start.2
  45.2 1.4 %collective-permute-done.19.other_ref = bf16[128,512]{1,0:T(8,128)(2,1)S(1)} collective-permute-done((bf16[128,512]{1,0:T(8,128)(2,1)S(1)}, bf16[128,512]{1,0:T(8,128)(2,1)S(1)}, u32[]{:S(2)}, u32[]{:S(2)}) %collective-permute-start.19) | collective-permute-done | bytes 131104 | tf_op jit(solution)/shard_map/ppermute | solution.py:299
  46.7 0.0 slice-start.3
  46.8 1.0 %collective-permute-start.21 = (bf16[128,512]{1,0:T(8,128)(2,1)S(1)}, bf16[128,512]{1,0:T(8,128)(2,1)S(1)}, u32[]{:S(2)}, u32[]{:S(2)}) collective-permute-start(bf16[128,512]{1,0:T(8,128)(2,1)S(1)} %turn.13.value_ref), channel_id=1, source_target_pairs={{0,4},{1,5},{2,6},{3,7},{4,0},{5,1},{6,2},{7,3},{8,12},{9,13},{10,... | collective-permute-start | bytes 393224 | tf_op jit(solution)/shard_map/ppermute | solution.py:299
  47.7 2.7 %collective-permute-start.22 = (bf16[128,512]{1,0:T(8,128)(2,1)S(1)}, bf16[128,512]{1,0:T(8,128)(2,1)S(1)}, u32[]{:S(2)}, u32[]{:S(2)}) collective-permute-start(bf16[128,512]{1,0:T(8,128)(2,1)S(1)} %turn.12.value_ref), channel_id=1, source_target_pairs={{0,8},{1,9},{2,10},{3,11},{4,12},{5,13},{6,14},{7,15},{8,0},{9,1},... | collective-permute-start | bytes 393224 | tf_op jit(solution)/shard_map/ppermute | solution.py:299
  50.4 3.7 %collective-permute-done.21.other_ref = bf16[128,512]{1,0:T(8,128)(2,1)S(1)} collective-permute-done((bf16[128,512]{1,0:T(8,128)(2,1)S(1)}, bf16[128,512]{1,0:T(8,128)(2,1)S(1)}, u32[]{:S(2)}, u32[]{:S(2)}) %collective-permute-start.21) | collective-permute-done | bytes 131104 | tf_op jit(solution)/shard_map/ppermute | solution.py:299
  54.2 2.1 %collective-permute-done.22.other_ref = bf16[128,512]{1,0:T(8,128)(2,1)S(1)} collective-permute-done((bf16[128,512]{1,0:T(8,128)(2,1)S(1)}, bf16[128,512]{1,0:T(8,128)(2,1)S(1)}, u32[]{:S(2)}, u32[]{:S(2)}) %collective-permute-start.22) | collective-permute-done | bytes 131104 | tf_op jit(solution)/shard_map/ppermute | solution.py:299
  56.4 1.4 %down_project.3 = (bf16[48,4096]{1,0:T(8,128)(2,1)S(1)}, bf16[80,4096]{1,0:T(8,128)(2,1)S(1)}) custom-call(bf16[128,512]{1,0:T(8,128)(2,1)S(1)} %turn.14.a_ref, bf16[128,512]{1,0:T(8,128)(2,1)S(1)} %turn.15.b_ref, f32[1,1024]{1,0:T(1,128)S(1)} %bitcast.8, bf16[1024,8192]{1,0:T(8,128)(2,1)S(1)} %bitcast.3), custom_call_target="tpu_custom_call" | custom-call | flops 1073741824 | tf_op jit(solution)/shard_map/down_project/pallas_call | solution.py:183
  57.9 0.1 collective-permute-start.23
  58.0 1.4 %down_project.2 = (bf16[48,4096]{1,0:T(8,128)(2,1)S(1)}, bf16[80,4096]{1,0:T(8,128)(2,1)S(1)}) custom-call(bf16[128,512]{1,0:T(8,128)(2,1)S(1)} %turn.14.a_ref, bf16[128,512]{1,0:T(8,128)(2,1)S(1)} %turn.15.b_ref, f32[1,1024]{1,0:T(1,128)S(1)} %bitcast.9, bf16[1024,8192]{1,0:T(8,128)(2,1)S(1)} %bitcast.3), custom_call_target="tpu_custom_call" | custom-call | flops 1073741824 | tf_op jit(solution)/shard_map/down_project/pallas_call | solution.py:183
  59.4 0.3 collective-permute-done.23.arrived_ref
  59.7 0.3 collective-permute-start.24
  60.0 0.6 collective-permute-start.25
  60.6 2.7 %collective-permute-start.26 = (bf16[16,4096]{1,0:T(8,128)(2,1)S(1)}, bf16[16,4096]{1,0:T(8,128)(2,1)S(1)}, u32[]{:S(2)}, u32[]{:S(2)}) collective-permute-start(bf16[16,4096]{1,0:T(8,128)(2,1)S(1)} %sum.4), channel_id=1, source_target_pairs={{0,8},{1,7},{4,12},{5,3},{8,14},{9,1},{12,10},{13,5},{14,6},{15,9}... | collective-permute-start | bytes 393224 | tf_op jit(solution)/shard_map/ppermute | solution.py:290
  63.4 0.1 collective-permute-start.29
  63.4 2.2 %collective-permute-done.25.refs_0_ = bf16[16,4096]{1,0:T(8,128)(2,1)S(1)} collective-permute-done((bf16[16,4096]{1,0:T(8,128)(2,1)S(1)}, bf16[16,4096]{1,0:T(8,128)(2,1)S(1)}, u32[]{:S(2)}, u32[]{:S(2)}) %collective-permute-start.25) | collective-permute-done | bytes 131104 | tf_op jit(solution)/shard_map/ppermute | solution.py:290
  65.7 3.6 %collective-permute-done.26.refs_1_ = bf16[16,4096]{1,0:T(8,128)(2,1)S(1)} collective-permute-done((bf16[16,4096]{1,0:T(8,128)(2,1)S(1)}, bf16[16,4096]{1,0:T(8,128)(2,1)S(1)}, u32[]{:S(2)}, u32[]{:S(2)}) %collective-permute-start.26) | collective-permute-done | bytes 131104 | tf_op jit(solution)/shard_map/ppermute | solution.py:290
  69.3 0.1 relay.4
  69.4 0.1 collective-permute-start.27
  69.4 0.3 collective-permute-done.29.refs_0_
  69.7 0.1 relay.6
  69.8 1.8 %collective-permute-start.30 = (bf16[16,4096]{1,0:T(8,128)(2,1)S(1)}, bf16[16,4096]{1,0:T(8,128)(2,1)S(1)}, u32[]{:S(2)}, u32[]{:S(2)}) collective-permute-start(bf16[16,4096]{1,0:T(8,128)(2,1)S(1)} %relay.6), channel_id=1, source_target_pairs={{0,2},{1,3},{4,0},{5,1},{8,4},{9,5},{12,8},{13,9},{14,12},{15,13},... | collective-permute-start | bytes 393224 | tf_op jit(solution)/shard_map/ppermute | solution.py:290
  71.6 3.8 %collective-permute-done.27.refs_0_ = bf16[16,4096]{1,0:T(8,128)(2,1)S(1)} collective-permute-done((bf16[16,4096]{1,0:T(8,128)(2,1)S(1)}, bf16[16,4096]{1,0:T(8,128)(2,1)S(1)}, u32[]{:S(2)}, u32[]{:S(2)}) %collective-permute-start.27) | collective-permute-done | bytes 131104 | tf_op jit(solution)/shard_map/ppermute | solution.py:290
  75.4 0.1 relay.5
  75.4 0.1 collective-permute-start.28
  75.5 0.1 relay.7
  75.6 2.1 %collective-permute-start.31 = (bf16[16,4096]{1,0:T(8,128)(2,1)S(1)}, bf16[16,4096]{1,0:T(8,128)(2,1)S(1)}, u32[]{:S(2)}, u32[]{:S(2)}) collective-permute-start(bf16[16,4096]{1,0:T(8,128)(2,1)S(1)} %relay.7), channel_id=1, source_target_pairs={{0,2},{1,3},{4,0},{5,1},{8,4},{9,5},{12,8},{13,9},{14,12},{15,13},... | collective-permute-start | bytes 393224 | tf_op jit(solution)/shard_map/ppermute | solution.py:290
  77.6 2.8 %collective-permute-done.28.ahead_in = bf16[16,4096]{1,0:T(8,128)(2,1)S(1)} collective-permute-done((bf16[16,4096]{1,0:T(8,128)(2,1)S(1)}, bf16[16,4096]{1,0:T(8,128)(2,1)S(1)}, u32[]{:S(2)}, u32[]{:S(2)}) %collective-permute-start.28) | collective-permute-done | bytes 131104 | tf_op jit(solution)/shard_map/ppermute | solution.py:290
  80.4 0.1 collective-permute-done.31.behind_in
  80.6 0.1 last.1
  80.7 0.1 collective-permute-start.32
  80.8 1.2 %collective-permute-done.32.take_ref = bf16[8,4096]{1,0:T(8,128)(2,1)S(1)} collective-permute-done((bf16[8,4096]{1,0:T(8,128)(2,1)S(1)}, bf16[8,4096]{1,0:T(8,128)(2,1)S(1)}, u32[]{:S(2)}, u32[]{:S(2)}) %collective-permute-start.32) | collective-permute-done | bytes 65568 | tf_op jit(solution)/shard_map/ppermute | solution.py:299
  82.0 0.7 mix.1
  (56 shorter events, 0.6 us)
Async XLA Ops:
  0.0 23.5 %slice-start.4 = ((s8[16777216]{0:T(1024)(128)(4,1)}), s8[4194304]{0:T(1024)(128)(4,1)S(1)}, s32[]{:S(2)}) async-start(s8[16777216]{0:T(1024)(128)(4,1)} %bitcast.4), calls=%async_computation.4 | async-start | bytes 8388608
  0.0 23.5 %slice-start.8 = ((s8[16777216]{0:T(1024)(128)(4,1)}), s8[4194304]{0:T(1024)(128)(4,1)S(1)}, s32[]{:S(2)}) async-start(s8[16777216]{0:T(1024)(128)(4,1)} %bitcast.6), calls=%async_computation.8 | async-start | bytes 8388608
  0.0 23.5 %slice-start.5 = ((s8[16777216]{0:T(1024)(128)(4,1)}), s8[4194304]{0:T(1024)(128)(4,1)S(1)}, s32[]{:S(2)}) async-start(s8[16777216]{0:T(1024)(128)(4,1)} %bitcast.4), calls=%async_computation.5 | async-start | bytes 8388608
  0.0 23.6 %slice-start.6 = ((s8[16777216]{0:T(1024)(128)(4,1)}), s8[4194304]{0:T(1024)(128)(4,1)S(1)}, s32[]{:S(2)}) async-start(s8[16777216]{0:T(1024)(128)(4,1)} %bitcast.4), calls=%async_computation.6 | async-start | bytes 8388608
  0.0 23.6 %slice-start.7 = ((s8[16777216]{0:T(1024)(128)(4,1)}), s8[4194304]{0:T(1024)(128)(4,1)S(1)}, s32[]{:S(2)}) async-start(s8[16777216]{0:T(1024)(128)(4,1)} %bitcast.4), calls=%async_computation.7 | async-start | bytes 8388608
  0.0 23.6 %slice-start.9 = ((s8[16777216]{0:T(1024)(128)(4,1)}), s8[4194304]{0:T(1024)(128)(4,1)S(1)}, s32[]{:S(2)}) async-start(s8[16777216]{0:T(1024)(128)(4,1)} %bitcast.6), calls=%async_computation.9 | async-start | bytes 8388608
  0.0 23.6 %slice-start.10 = ((s8[16777216]{0:T(1024)(128)(4,1)}), s8[4194304]{0:T(1024)(128)(4,1)S(1)}, s32[]{:S(2)}) async-start(s8[16777216]{0:T(1024)(128)(4,1)} %bitcast.6), calls=%async_computation.10 | async-start | bytes 8388608
  0.0 23.6 %slice-start.11 = ((s8[16777216]{0:T(1024)(128)(4,1)}), s8[4194304]{0:T(1024)(128)(4,1)S(1)}, s32[]{:S(2)}) async-start(s8[16777216]{0:T(1024)(128)(4,1)} %bitcast.6), calls=%async_computation.11 | async-start | bytes 8388608
  1.3 6.6 %collective-permute-start.3 = (bf16[8,8192]{1,0:T(8,128)(2,1)S(1)}, bf16[8,8192]{1,0:T(8,128)(2,1)S(1)}, u32[]{:S(2)}, u32[]{:S(2)}) collective-permute-start(bf16[8,8192]{1,0:T(8,128)(2,1)S(1)} %normalize.1.refs_0_), channel_id=1, source_target_pairs={{0,2},{1,3},{4,0},{5,1},{8,4},{9,5},{12,8},{13,9},{14,12},{15,13},... | collective-permute-start | bytes 393224 | tf_op jit(solution)/shard_map/ppermute | solution.py:290
  4.4 5.2 %collective-permute-start.1 = (bf16[8,8192]{1,0:T(8,128)(2,1)S(1)}, bf16[8,8192]{1,0:T(8,128)(2,1)S(1)}, u32[]{:S(2)}, u32[]{:S(2)}) collective-permute-start(bf16[8,8192]{1,0:T(8,128)(2,1)S(1)} %normalize.1.refs_0_), channel_id=1, source_target_pairs={{0,4},{1,5},{4,8},{5,9},{8,12},{9,13},{12,14},{13,15},{14,10},{15,... | collective-permute-start | bytes 393224 | tf_op jit(solution)/shard_map/ppermute | solution.py:290
  7.9 5.0 %collective-permute-start.7 = (bf16[8,8192]{1,0:T(8,128)(2,1)S(1)}, bf16[8,8192]{1,0:T(8,128)(2,1)S(1)}, u32[]{:S(2)}, u32[]{:S(2)}) collective-permute-start(bf16[8,8192]{1,0:T(8,128)(2,1)S(1)} %collective-permute-done.3.refs_4_), channel_id=1, source_target_pairs={{0,2},{1,3},{4,0},{5,1},{8,4},{9,5},{12,8},{13,9},{14,12},{15,13},... | collective-permute-start | bytes 393224 | tf_op jit(solution)/shard_map/ppermute | solution.py:290
  9.6 5.0 %collective-permute-start.5 = (bf16[8,8192]{1,0:T(8,128)(2,1)S(1)}, bf16[8,8192]{1,0:T(8,128)(2,1)S(1)}, u32[]{:S(2)}, u32[]{:S(2)}) collective-permute-start(bf16[8,8192]{1,0:T(8,128)(2,1)S(1)} %collective-permute-done.1.refs_2_), channel_id=1, source_target_pairs={{0,4},{1,5},{4,8},{5,9},{8,12},{9,13},{12,14},{13,15},{14,10},{15,... | collective-permute-start | bytes 393224 | tf_op jit(solution)/shard_map/ppermute | solution.py:290
  9.9 6.2 %collective-permute-start = (bf16[8,8192]{1,0:T(8,128)(2,1)S(1)}, bf16[8,8192]{1,0:T(8,128)(2,1)S(1)}, u32[]{:S(2)}, u32[]{:S(2)}) collective-permute-start(bf16[8,8192]{1,0:T(8,128)(2,1)S(1)} %normalize.1.refs_0_), channel_id=1, source_target_pairs={{0,1},{1,0},{2,3},{3,2},{4,5},{5,4},{6,7},{7,6},{8,9},{9,8},{10,11... | collective-permute-start | bytes 393224 | tf_op jit(solution)/shard_map/ppermute | solution.py:299
  9.9 7.8 %collective-permute-start.4 = (bf16[8,8192]{1,0:T(8,128)(2,1)S(1)}, bf16[8,8192]{1,0:T(8,128)(2,1)S(1)}, u32[]{:S(2)}, u32[]{:S(2)}) collective-permute-start(bf16[8,8192]{1,0:T(8,128)(2,1)S(1)} %collective-permute-done.3.refs_4_), channel_id=1, source_target_pairs={{0,1},{1,0},{2,3},{3,2},{4,5},{5,4},{6,7},{7,6},{8,9},{9,8},{10,11... | collective-permute-start | bytes 393224 | tf_op jit(solution)/shard_map/ppermute | solution.py:299
  10.4 7.3 %collective-permute-start.2 = (bf16[8,8192]{1,0:T(8,128)(2,1)S(1)}, bf16[8,8192]{1,0:T(8,128)(2,1)S(1)}, u32[]{:S(2)}, u32[]{:S(2)}) collective-permute-start(bf16[8,8192]{1,0:T(8,128)(2,1)S(1)} %collective-permute-done.1.refs_2_), channel_id=1, source_target_pairs={{0,1},{1,0},{2,3},{3,2},{4,5},{5,4},{6,7},{7,6},{8,9},{9,8},{10,11... | collective-permute-start | bytes 393224 | tf_op jit(solution)/shard_map/ppermute | solution.py:299
  12.9 7.4 %collective-permute-start.11 = (bf16[8,8192]{1,0:T(8,128)(2,1)S(1)}, bf16[8,8192]{1,0:T(8,128)(2,1)S(1)}, u32[]{:S(2)}, u32[]{:S(2)}) collective-permute-start(bf16[8,8192]{1,0:T(8,128)(2,1)S(1)} %collective-permute-done.7.odd_ref.refs_8_), channel_id=1, source_target_pairs={{0,2},{1,3},{4,0},{5,1},{8,4},{9,5},{12,8},{13,9},{14,12},{15,13},... | collective-permute-start | bytes 393224 | tf_op jit(solution)/shard_map/ppermute | solution.py:290
  14.6 7.4 %collective-permute-start.13 = (bf16[8,8192]{1,0:T(8,128)(2,1)S(1)}, bf16[8,8192]{1,0:T(8,128)(2,1)S(1)}, u32[]{:S(2)}, u32[]{:S(2)}) collective-permute-start(bf16[8,8192]{1,0:T(8,128)(2,1)S(1)} %pick.1), channel_id=1, source_target_pairs={{0,8},{1,7},{4,12},{5,3},{8,14},{9,1},{12,10},{13,5},{14,6},{15,9}... | collective-permute-start | bytes 393224 | tf_op jit(solution)/shard_map/ppermute | solution.py:290
  16.2 6.0 %collective-permute-start.9 = (bf16[8,8192]{1,0:T(8,128)(2,1)S(1)}, bf16[8,8192]{1,0:T(8,128)(2,1)S(1)}, u32[]{:S(2)}, u32[]{:S(2)}) collective-permute-start(bf16[8,8192]{1,0:T(8,128)(2,1)S(1)} %collective-permute-done.5.even_ref.refs_6_), channel_id=1, source_target_pairs={{0,4},{1,5},{4,8},{5,9},{8,12},{9,13},{12,14},{13,15},{14,10},{15,... | collective-permute-start | bytes 393224 | tf_op jit(solution)/shard_map/ppermute | solution.py:290
  17.7 4.8 %collective-permute-start.8 = (bf16[8,8192]{1,0:T(8,128)(2,1)S(1)}, bf16[8,8192]{1,0:T(8,128)(2,1)S(1)}, u32[]{:S(2)}, u32[]{:S(2)}) collective-permute-start(bf16[8,8192]{1,0:T(8,128)(2,1)S(1)} %collective-permute-done.7.odd_ref.refs_8_), channel_id=1, source_target_pairs={{0,1},{1,0},{2,3},{3,2},{4,5},{5,4},{6,7},{7,6},{8,9},{9,8},{10,11... | collective-permute-start | bytes 393224 | tf_op jit(solution)/shard_map/ppermute | solution.py:299
  17.7 4.8 %collective-permute-start.6 = (bf16[8,8192]{1,0:T(8,128)(2,1)S(1)}, bf16[8,8192]{1,0:T(8,128)(2,1)S(1)}, u32[]{:S(2)}, u32[]{:S(2)}) collective-permute-start(bf16[8,8192]{1,0:T(8,128)(2,1)S(1)} %collective-permute-done.5.even_ref.refs_6_), channel_id=1, source_target_pairs={{0,1},{1,0},{2,3},{3,2},{4,5},{5,4},{6,7},{7,6},{8,9},{9,8},{10,11... | collective-permute-start | bytes 393224 | tf_op jit(solution)/shard_map/ppermute | solution.py:299
  20.3 2.2 %collective-permute-start.12 = (bf16[8,8192]{1,0:T(8,128)(2,1)S(1)}, bf16[8,8192]{1,0:T(8,128)(2,1)S(1)}, u32[]{:S(2)}, u32[]{:S(2)}) collective-permute-start(bf16[8,8192]{1,0:T(8,128)(2,1)S(1)} %collective-permute-done.11.refs_12_), channel_id=1, source_target_pairs={{0,1},{1,0},{2,3},{3,2},{4,5},{5,4},{6,7},{7,6},{8,9},{9,8},{10,11... | collective-permute-start | bytes 393224 | tf_op jit(solution)/shard_map/ppermute | solution.py:299
  22.0 1.3 %collective-permute-start.14 = (bf16[8,8192]{1,0:T(8,128)(2,1)S(1)}, bf16[8,8192]{1,0:T(8,128)(2,1)S(1)}, u32[]{:S(2)}, u32[]{:S(2)}) collective-permute-start(bf16[8,8192]{1,0:T(8,128)(2,1)S(1)} %collective-permute-done.13.refs_14_), channel_id=1, source_target_pairs={{0,1},{1,0},{2,3},{3,2},{4,5},{5,4},{6,7},{7,6},{8,9},{9,8},{10,11... | collective-permute-start | bytes 393224 | tf_op jit(solution)/shard_map/ppermute | solution.py:299
  22.2 1.3 %collective-permute-start.10 = (bf16[8,8192]{1,0:T(8,128)(2,1)S(1)}, bf16[8,8192]{1,0:T(8,128)(2,1)S(1)}, u32[]{:S(2)}, u32[]{:S(2)}) collective-permute-start(bf16[8,8192]{1,0:T(8,128)(2,1)S(1)} %collective-permute-done.9.refs_10_), channel_id=1, source_target_pairs={{0,1},{1,0},{2,3},{3,2},{4,5},{5,4},{6,7},{7,6},{8,9},{9,8},{10,11... | collective-permute-start | bytes 393224 | tf_op jit(solution)/shard_map/ppermute | solution.py:299
  26.4 5.8 %collective-permute-start.16 = (bf16[128,512]{1,0:T(8,128)(2,1)S(1)}, bf16[128,512]{1,0:T(8,128)(2,1)S(1)}, u32[]{:S(2)}, u32[]{:S(2)}) collective-permute-start(bf16[128,512]{1,0:T(8,128)(2,1)S(1)} %get-tuple-element.21.value_ref), channel_id=1, source_target_pairs={{0,1},{1,0},{2,3},{3,2},{4,5},{5,4},{6,7},{7,6},{8,9},{9,8},{10,11... | collective-permute-start | bytes 393224 | tf_op jit(solution)/shard_map/ppermute | solution.py:299
  29.5 9.5 %collective-permute-start.15 = (bf16[128,512]{1,0:T(8,128)(2,1)S(1)}, bf16[128,512]{1,0:T(8,128)(2,1)S(1)}, u32[]{:S(2)}, u32[]{:S(2)}) collective-permute-start(bf16[128,512]{1,0:T(8,128)(2,1)S(1)} %up_project.3.value_ref), channel_id=1, source_target_pairs={{0,8},{1,9},{2,10},{3,11},{4,12},{5,13},{6,14},{7,15},{8,0},{9,1},... | collective-permute-start | bytes 393224 | tf_op jit(solution)/shard_map/ppermute | solution.py:299
  32.2 6.9 %collective-permute-start.18 = (bf16[128,512]{1,0:T(8,128)(2,1)S(1)}, bf16[128,512]{1,0:T(8,128)(2,1)S(1)}, u32[]{:S(2)}, u32[]{:S(2)}) collective-permute-start(bf16[128,512]{1,0:T(8,128)(2,1)S(1)} %turn.8.value_ref), channel_id=1, source_target_pairs={{0,2},{1,3},{2,0},{3,1},{4,6},{5,7},{6,4},{7,5},{8,10},{9,11},{10,... | collective-permute-start | bytes 393224 | tf_op jit(solution)/shard_map/ppermute | solution.py:299
  39.1 1.4 %collective-permute-start.17 = (bf16[128,512]{1,0:T(8,128)(2,1)S(1)}, bf16[128,512]{1,0:T(8,128)(2,1)S(1)}, u32[]{:S(2)}, u32[]{:S(2)}) collective-permute-start(bf16[128,512]{1,0:T(8,128)(2,1)S(1)} %turn.9.value_ref), channel_id=1, source_target_pairs={{0,1},{1,0},{2,3},{3,2},{4,5},{5,4},{6,7},{7,6},{8,9},{9,8},{10,11... | collective-permute-start | bytes 393224 | tf_op jit(solution)/shard_map/ppermute | solution.py:299
  39.2 17.2 %slice-start = ((s8[16777216]{0:T(1024)(128)(4,1)}), s8[4194304]{0:T(1024)(128)(4,1)S(1)}, s32[]{:S(2)}) async-start(s8[16777216]{0:T(1024)(128)(4,1)} %bitcast.2), calls=%async_computation | async-start | bytes 8388608
  39.2 17.1 %copy-start.1 = (f32[1024]{0:T(1024)S(1)}, f32[1024]{0:T(1024)}, u32[]{:S(2)}) copy-start(f32[1024]{0:T(1024)} %param.11) | copy-start | bytes 12292
  39.2 6.0 %collective-permute-start.20 = (bf16[128,512]{1,0:T(8,128)(2,1)S(1)}, bf16[128,512]{1,0:T(8,128)(2,1)S(1)}, u32[]{:S(2)}, u32[]{:S(2)}) collective-permute-start(bf16[128,512]{1,0:T(8,128)(2,1)S(1)} %turn.10.value_ref), channel_id=1, source_target_pairs={{0,4},{1,5},{2,6},{3,7},{4,0},{5,1},{6,2},{7,3},{8,12},{9,13},{10,... | collective-permute-start | bytes 393224 | tf_op jit(solution)/shard_map/ppermute | solution.py:299
  40.5 15.9 %slice-start.1 = ((s8[16777216]{0:T(1024)(128)(4,1)}), s8[4194304]{0:T(1024)(128)(4,1)S(1)}, s32[]{:S(2)}) async-start(s8[16777216]{0:T(1024)(128)(4,1)} %bitcast.2), calls=%async_computation.1 | async-start | bytes 8388608
  40.5 6.2 %collective-permute-start.19 = (bf16[128,512]{1,0:T(8,128)(2,1)S(1)}, bf16[128,512]{1,0:T(8,128)(2,1)S(1)}, u32[]{:S(2)}, u32[]{:S(2)}) collective-permute-start(bf16[128,512]{1,0:T(8,128)(2,1)S(1)} %turn.11.value_ref), channel_id=1, source_target_pairs={{0,2},{1,3},{2,0},{3,1},{4,6},{5,7},{6,4},{7,5},{8,10},{9,11},{10,... | collective-permute-start | bytes 393224 | tf_op jit(solution)/shard_map/ppermute | solution.py:299
  45.2 11.2 %slice-start.2 = ((s8[16777216]{0:T(1024)(128)(4,1)}), s8[4194304]{0:T(1024)(128)(4,1)S(1)}, s32[]{:S(2)}) async-start(s8[16777216]{0:T(1024)(128)(4,1)} %bitcast.2), calls=%async_computation.2 | async-start | bytes 8388608
  46.7 9.7 %slice-start.3 = ((s8[16777216]{0:T(1024)(128)(4,1)}), s8[4194304]{0:T(1024)(128)(4,1)S(1)}, s32[]{:S(2)}) async-start(s8[16777216]{0:T(1024)(128)(4,1)} %bitcast.2), calls=%async_computation.3 | async-start | bytes 8388608
  46.8 7.4 %collective-permute-start.21 = (bf16[128,512]{1,0:T(8,128)(2,1)S(1)}, bf16[128,512]{1,0:T(8,128)(2,1)S(1)}, u32[]{:S(2)}, u32[]{:S(2)}) collective-permute-start(bf16[128,512]{1,0:T(8,128)(2,1)S(1)} %turn.13.value_ref), channel_id=1, source_target_pairs={{0,4},{1,5},{2,6},{3,7},{4,0},{5,1},{6,2},{7,3},{8,12},{9,13},{10,... | collective-permute-start | bytes 393224 | tf_op jit(solution)/shard_map/ppermute | solution.py:299
  47.7 8.6 %collective-permute-start.22 = (bf16[128,512]{1,0:T(8,128)(2,1)S(1)}, bf16[128,512]{1,0:T(8,128)(2,1)S(1)}, u32[]{:S(2)}, u32[]{:S(2)}) collective-permute-start(bf16[128,512]{1,0:T(8,128)(2,1)S(1)} %turn.12.value_ref), channel_id=1, source_target_pairs={{0,8},{1,9},{2,10},{3,11},{4,12},{5,13},{6,14},{7,15},{8,0},{9,1},... | collective-permute-start | bytes 393224 | tf_op jit(solution)/shard_map/ppermute | solution.py:299
  57.9 24.1 %copy-start = (bf16[8,8192]{1,0:T(8,128)(2,1)S(1)}, bf16[8,8192]{1,0:T(8,128)(2,1)}, u32[]{:S(2)}) copy-start(bf16[8,8192]{1,0:T(8,128)(2,1)} %tokens_ref.1) | copy-start | bytes 393220
  57.9 1.8 %collective-permute-start.23 = (bf16[48,4096]{1,0:T(8,128)(2,1)S(1)}, bf16[48,4096]{1,0:T(8,128)(2,1)S(1)}, u32[]{:S(2)}, u32[]{:S(2)}) collective-permute-start(bf16[48,4096]{1,0:T(8,128)(2,1)S(1)} %get-tuple-element.30), channel_id=1, source_target_pairs={{0,1},{1,0},{2,3},{3,2},{4,5},{5,4},{6,7},{7,6},{8,9},{9,8},{10,11... | collective-permute-start | bytes 1179656 | tf_op jit(solution)/shard_map/ppermute | solution.py:299
  59.7 9.6 %collective-permute-start.24 = (bf16[80,4096]{1,0:T(8,128)(2,1)S(1)}, bf16[80,4096]{1,0:T(8,128)(2,1)S(1)}, u32[]{:S(2)}, u32[]{:S(2)}) collective-permute-start(bf16[80,4096]{1,0:T(8,128)(2,1)S(1)} %get-tuple-element.31), channel_id=1, source_target_pairs={{0,1},{1,0},{2,3},{3,2},{4,5},{5,4},{6,7},{7,6},{8,9},{9,8},{10,11... | collective-permute-start | bytes 1966088 | tf_op jit(solution)/shard_map/ppermute | solution.py:299
  60.0 5.6 %collective-permute-start.25 = (bf16[16,4096]{1,0:T(8,128)(2,1)S(1)}, bf16[16,4096]{1,0:T(8,128)(2,1)S(1)}, u32[]{:S(2)}, u32[]{:S(2)}) collective-permute-start(bf16[16,4096]{1,0:T(8,128)(2,1)S(1)} %sum.3), channel_id=1, source_target_pairs={{0,4},{1,5},{4,8},{5,9},{8,12},{9,13},{12,14},{13,15},{14,10},{15,... | collective-permute-start | bytes 393224 | tf_op jit(solution)/shard_map/ppermute | solution.py:290
  60.6 8.6 %collective-permute-start.26 = (bf16[16,4096]{1,0:T(8,128)(2,1)S(1)}, bf16[16,4096]{1,0:T(8,128)(2,1)S(1)}, u32[]{:S(2)}, u32[]{:S(2)}) collective-permute-start(bf16[16,4096]{1,0:T(8,128)(2,1)S(1)} %sum.4), channel_id=1, source_target_pairs={{0,8},{1,7},{4,12},{5,3},{8,14},{9,1},{12,10},{13,5},{14,6},{15,9}... | collective-permute-start | bytes 393224 | tf_op jit(solution)/shard_map/ppermute | solution.py:290
  63.4 6.4 %collective-permute-start.29 = (bf16[16,4096]{1,0:T(8,128)(2,1)S(1)}, bf16[16,4096]{1,0:T(8,128)(2,1)S(1)}, u32[]{:S(2)}, u32[]{:S(2)}) collective-permute-start(bf16[16,4096]{1,0:T(8,128)(2,1)S(1)} %sum.5), channel_id=1, source_target_pairs={{0,2},{1,3},{4,0},{5,1},{8,4},{9,5},{12,8},{13,9},{14,12},{15,13},... | collective-permute-start | bytes 393224 | tf_op jit(solution)/shard_map/ppermute | solution.py:290
  69.4 6.0 %collective-permute-start.27 = (bf16[16,4096]{1,0:T(8,128)(2,1)S(1)}, bf16[16,4096]{1,0:T(8,128)(2,1)S(1)}, u32[]{:S(2)}, u32[]{:S(2)}) collective-permute-start(bf16[16,4096]{1,0:T(8,128)(2,1)S(1)} %relay.4), channel_id=1, source_target_pairs={{0,4},{1,5},{4,8},{5,9},{8,12},{9,13},{12,14},{13,15},{14,10},{15,... | collective-permute-start | bytes 393224 | tf_op jit(solution)/shard_map/ppermute | solution.py:290
  69.8 5.7 %collective-permute-start.30 = (bf16[16,4096]{1,0:T(8,128)(2,1)S(1)}, bf16[16,4096]{1,0:T(8,128)(2,1)S(1)}, u32[]{:S(2)}, u32[]{:S(2)}) collective-permute-start(bf16[16,4096]{1,0:T(8,128)(2,1)S(1)} %relay.6), channel_id=1, source_target_pairs={{0,2},{1,3},{4,0},{5,1},{8,4},{9,5},{12,8},{13,9},{14,12},{15,13},... | collective-permute-start | bytes 393224 | tf_op jit(solution)/shard_map/ppermute | solution.py:290
  75.4 5.0 %collective-permute-start.28 = (bf16[16,4096]{1,0:T(8,128)(2,1)S(1)}, bf16[16,4096]{1,0:T(8,128)(2,1)S(1)}, u32[]{:S(2)}, u32[]{:S(2)}) collective-permute-start(bf16[16,4096]{1,0:T(8,128)(2,1)S(1)} %relay.5), channel_id=1, source_target_pairs={{0,4},{1,5},{4,8},{5,9},{8,12},{9,13},{12,14},{13,15},{14,10},{15,... | collective-permute-start | bytes 393224 | tf_op jit(solution)/shard_map/ppermute | solution.py:290
  75.6 5.0 %collective-permute-start.31 = (bf16[16,4096]{1,0:T(8,128)(2,1)S(1)}, bf16[16,4096]{1,0:T(8,128)(2,1)S(1)}, u32[]{:S(2)}, u32[]{:S(2)}) collective-permute-start(bf16[16,4096]{1,0:T(8,128)(2,1)S(1)} %relay.7), channel_id=1, source_target_pairs={{0,2},{1,3},{4,0},{5,1},{8,4},{9,5},{12,8},{13,9},{14,12},{15,13},... | collective-permute-start | bytes 393224 | tf_op jit(solution)/shard_map/ppermute | solution.py:290
  80.7 1.3 %collective-permute-start.32 = (bf16[8,4096]{1,0:T(8,128)(2,1)S(1)}, bf16[8,4096]{1,0:T(8,128)(2,1)S(1)}, u32[]{:S(2)}, u32[]{:S(2)}) collective-permute-start(bf16[8,4096]{1,0:T(8,128)(2,1)S(1)} %get-tuple-element.34), channel_id=1, source_target_pairs={{0,1},{1,0},{2,3},{3,2},{4,5},{5,4},{6,7},{7,6},{8,9},{9,8},{10,11... | collective-permute-start | bytes 196616 | tf_op jit(solution)/shard_map/ppermute | solution.py:299

commit v8 on v7

--- a/solution.py
+++ b/solution.py
@@ -209,7 +209,7 @@
     out_ref[...] = (other_ref[...].astype(jnp.float32) + sign * value_ref[...].astype(jnp.float32)).astype(jnp.bfloat16)
 
 
-def both(body, first, second, name):
+def both(body, first, second, name, flops=TURN):
     vmem = pl.BlockSpec(memory_space=pltpu.VMEM)
     return pl.pallas_call(
         body,
@@ -217,7 +217,7 @@
         in_specs=[vmem, vmem],
         out_specs=vmem,
         compiler_params=pltpu.CompilerParams(vmem_limit_bytes=2 * MIB),
-        cost_estimate=pl.CostEstimate(flops=TURN, bytes_accessed=0, transcendentals=0),
+        cost_estimate=pl.CostEstimate(flops=flops, bytes_accessed=0, transcendentals=0),
         name=name,
     )(first, second)
 
@@ -319,25 +319,22 @@
     else:
         (half_a,) = up_project(shifts, [joined], gate_weight, up_weight, 0, pieces)
 
-    def turn(value, mask, *others):
-        return both(functools.partial(turn_kernel, mask), value, once(cross(value, mask), *others), "turn")
+    def turn(value, mask, *others, flops=TURN):
+        arrived = once(cross(value, mask), *others) if others else cross(value, mask)
+        return both(functools.partial(turn_kernel, mask), value, arrived, "turn", flops)
 
     masks = [1 << bit for bit in range(count.bit_length() - 1)]
-    for stage in range(len(masks)):
-        first, second = masks[stage - 1], masks[stage]
-        if stage == 0:
-            half_b = turn(half_b, second)
-            early = turn(half_b, masks[1])
-            half_a = turn(half_a, first, half_b)
-        elif stage == 1:
-            half_b = early
-            half_a = turn(half_a, first, early)
-        elif stage < len(masks) - 1:
-            half_b = turn(half_b, second, half_a)
-            half_a = turn(half_a, first, half_b)
-        else:
-            half_a = turn(half_a, first, half_b)
-            half_b = turn(half_b, second, half_a)
+    top, first, second, *rest = masks[-1], masks[1], masks[0], *masks[2:-1]
+    half_b = turn(half_b, first, half_a, flops=0)
+    early = turn(half_b, second, flops=0)
+    half_a = turn(half_a, top, early, flops=2 * TURN)
+    half_b = early
+    half_a = turn(half_a, second)
+    for place, mask in enumerate(rest):
+        half_b = turn(half_b, mask)
+        half_a = turn(half_a, first if place == 0 else rest[place - 1], half_b)
+    half_a = turn(half_a, rest[-1] if rest else first)
+    half_b = turn(half_b, top)
 
     total = count * width
     limits = clip_scale.reshape(1, -1)

time: 82.9 us -> 84.3 us (1.017)
  waiting for transfers between devices: 41.1 us -> 43 us
    ppermute x19, waiting for transfers between devices: 18.4 us -> 20.3 us  [cross(): return lax.ppermute(value, 'hid', [(d, d ^ mask) for d in range(count)])]
where the time goes in v8:
time: 84.3 us; the launch traced here: 84.1 us
  waiting for transfers between devices  43 us (51%)
  starting transfers between devices  29.5 us (35%)
  Pallas kernels  11.2 us (13%)
    ppermute x14, waiting for transfers between devices, hop(): return lax.ppermute(value, 'hid', pairs)  22.7 us
    ppermute x19, waiting for transfers between devices, cross(): return lax.ppermute(value, 'hid', [(d, d ^ mask) for d in range(count)])  20.3 us
    ppermute x14, starting transfers between devices, hop(): return lax.ppermute(value, 'hid', pairs)  17.2 us
    ppermute x19, starting transfers between devices, cross(): return lax.ppermute(value, 'hid', [(d, d ^ mask) for d in range(count)])  12.3 us
    pallas_call x2, Pallas kernels, up_project(): pl.pallas_call(functools.partial(up_kernel, shifts, first, slice(at * wid...  5.53 us
    pallas_call x2, Pallas kernels, down_project(): pl.pallas_call(functools.partial(down_kernel, width // BLOCK, chips, tota...  2.9 us
  transfers between devices with their start and end apart: 33, of which 21 were waited for; matrix products, arithmetic and copies ran while one was open for 0% of the time, Pallas kernels for 6%

profile of v8, /device:TPU:0, one launch (start us, length us, event | category | flops | bytes accessed | tf_op | source)
XLA Modules:
  0.0 84.1 jit_solution(11360394192477896428)
XLA Ops:
  0.0 1.3 %normalize.1.refs_0_ = bf16[8,8192]{1,0:T(8,128)(2,1)S(1)} custom-call(bf16[8,8192]{1,0:T(8,128)(2,1)} %tokens_ref.1, f32[1,8192]{1,0:T(1,128)} %bitcast.10), custom_call_target="tpu_custom_call" | custom-call | flops 20000000000 | bytes 262144 | tf_op jit(solution)/shard_map/normalize/pallas_call | solution.py:47
  1.3 3.0 %collective-permute-start.3 = (bf16[8,8192]{1,0:T(8,128)(2,1)S(1)}, bf16[8,8192]{1,0:T(8,128)(2,1)S(1)}, u32[]{:S(2)}, u32[]{:S(2)}) collective-permute-start(bf16[8,8192]{1,0:T(8,128)(2,1)S(1)} %normalize.1.refs_0_), channel_id=1, source_target_pairs={{0,2},{1,3},{4,0},{5,1},{8,4},{9,5},{12,8},{13,9},{14,12},{15,13},... | collective-permute-start | bytes 393224 | tf_op jit(solution)/shard_map/ppermute | solution.py:290
  4.4 0.1 collective-permute-start.1
  4.5 3.4 %collective-permute-done.3.refs_4_ = bf16[8,8192]{1,0:T(8,128)(2,1)S(1)} collective-permute-done((bf16[8,8192]{1,0:T(8,128)(2,1)S(1)}, bf16[8,8192]{1,0:T(8,128)(2,1)S(1)}, u32[]{:S(2)}, u32[]{:S(2)}) %collective-permute-start.3) | collective-permute-done | bytes 131104 | tf_op jit(solution)/shard_map/ppermute | solution.py:290
  7.9 1.7 %collective-permute-start.7 = (bf16[8,8192]{1,0:T(8,128)(2,1)S(1)}, bf16[8,8192]{1,0:T(8,128)(2,1)S(1)}, u32[]{:S(2)}, u32[]{:S(2)}) collective-permute-start(bf16[8,8192]{1,0:T(8,128)(2,1)S(1)} %collective-permute-done.3.refs_4_), channel_id=1, source_target_pairs={{0,2},{1,3},{4,0},{5,1},{8,4},{9,5},{12,8},{13,9},{14,12},{15,13},... | collective-permute-start | bytes 393224 | tf_op jit(solution)/shard_map/ppermute | solution.py:290
  9.6 0.3 collective-permute-start.5
  9.9 0.5 collective-permute-start.4
  10.5 2.4 %collective-permute-done.7.odd_ref.refs_8_ = bf16[8,8192]{1,0:T(8,128)(2,1)S(1)} collective-permute-done((bf16[8,8192]{1,0:T(8,128)(2,1)S(1)}, bf16[8,8192]{1,0:T(8,128)(2,1)S(1)}, u32[]{:S(2)}, u32[]{:S(2)}) %collective-permute-start.7) | collective-permute-done | bytes 131104 | tf_op jit(solution)/shard_map/ppermute | solution.py:290
  12.9 1.7 %collective-permute-start.11 = (bf16[8,8192]{1,0:T(8,128)(2,1)S(1)}, bf16[8,8192]{1,0:T(8,128)(2,1)S(1)}, u32[]{:S(2)}, u32[]{:S(2)}) collective-permute-start(bf16[8,8192]{1,0:T(8,128)(2,1)S(1)} %collective-permute-done.7.odd_ref.refs_8_), channel_id=1, source_target_pairs={{0,2},{1,3},{4,0},{5,1},{8,4},{9,5},{12,8},{13,9},{14,12},{15,13},... | collective-permute-start | bytes 393224 | tf_op jit(solution)/shard_map/ppermute | solution.py:290
  14.6 1.6 %collective-permute-start.13 = (bf16[8,8192]{1,0:T(8,128)(2,1)S(1)}, bf16[8,8192]{1,0:T(8,128)(2,1)S(1)}, u32[]{:S(2)}, u32[]{:S(2)}) collective-permute-start(bf16[8,8192]{1,0:T(8,128)(2,1)S(1)} %pick.1), channel_id=1, source_target_pairs={{0,8},{1,7},{4,12},{5,3},{8,14},{9,1},{12,10},{13,5},{14,6},{15,9}... | collective-permute-start | bytes 393224 | tf_op jit(solution)/shard_map/ppermute | solution.py:290
  16.2 1.6 %collective-permute-start.9 = (bf16[8,8192]{1,0:T(8,128)(2,1)S(1)}, bf16[8,8192]{1,0:T(8,128)(2,1)S(1)}, u32[]{:S(2)}, u32[]{:S(2)}) collective-permute-start(bf16[8,8192]{1,0:T(8,128)(2,1)S(1)} %collective-permute-done.5.even_ref.refs_6_), channel_id=1, source_target_pairs={{0,4},{1,5},{4,8},{5,9},{8,12},{9,13},{12,14},{13,15},{14,10},{15,... | collective-permute-start | bytes 393224 | tf_op jit(solution)/shard_map/ppermute | solution.py:290
  17.7 0.5 collective-permute-start.6
  18.3 2.0 %collective-permute-done.11.refs_12_ = bf16[8,8192]{1,0:T(8,128)(2,1)S(1)} collective-permute-done((bf16[8,8192]{1,0:T(8,128)(2,1)S(1)}, bf16[8,8192]{1,0:T(8,128)(2,1)S(1)}, u32[]{:S(2)}, u32[]{:S(2)}) %collective-permute-start.11) | collective-permute-done | bytes 131104 | tf_op jit(solution)/shard_map/ppermute | solution.py:290
  20.3 1.7 %collective-permute-done.13.refs_14_ = bf16[8,8192]{1,0:T(8,128)(2,1)S(1)} collective-permute-done((bf16[8,8192]{1,0:T(8,128)(2,1)S(1)}, bf16[8,8192]{1,0:T(8,128)(2,1)S(1)}, u32[]{:S(2)}, u32[]{:S(2)}) %collective-permute-start.13) | collective-permute-done | bytes 131104 | tf_op jit(solution)/shard_map/ppermute | solution.py:290
  22.0 0.2 collective-permute-done.9.refs_10_
  22.2 0.3 collective-permute-start.10
  22.5 0.8 collective-permute-done.14.refs_15_
  23.3 0.2 collective-permute-done.10.refs_11_
  23.6 2.8 %up_project.2 = (bf16[128,512]{1,0:T(8,128)(2,1)S(1)}, bf16[128,8192]{1,0:T(8,128)(2,1)S(1)}) custom-call(bf16[8,8192]{1,0:T(8,128)(2,1)S(1)} %normalize.1.refs_0_, bf16[8,8192]{1,0:T(8,128)(2,1)S(1)} %collective-permute-done.refs_1_, bf16[8,8192]{1,0:T(8,128)(2,1)S(1)} %collective-permute-done.1.refs_2_, ...), custom_call_target="tpu_custom_call" | custom-call | flops 2147483648 | tf_op jit(solution)/shard_map/up_project/pallas_call | solution.py:123
  26.4 2.4 %collective-permute-start.16 = (bf16[128,512]{1,0:T(8,128)(2,1)S(1)}, bf16[128,512]{1,0:T(8,128)(2,1)S(1)}, u32[]{:S(2)}, u32[]{:S(2)}) collective-permute-start(bf16[128,512]{1,0:T(8,128)(2,1)S(1)} %get-tuple-element.18.value_ref), channel_id=1, source_target_pairs={{0,2},{1,3},{2,0},{3,1},{4,6},{5,7},{6,4},{7,5},{8,10},{9,11},{10,... | collective-permute-start | bytes 393224 | tf_op jit(solution)/shard_map/ppermute | solution.py:299
  28.8 2.8 %up_project.3.value_ref = bf16[128,512]{1,0:T(8,128)(2,1)S(1)} custom-call(bf16[128,8192]{1,0:T(8,128)(2,1)S(1)} %get-tuple-element.17.refs_0_, bf16[8192,1024]{1,0:T(8,128)(2,1)S(1)} %bitcast.5, bf16[8192,1024]{1,0:T(8,128)(2,1)S(1)} %bitcast.7), custom_call_target="tpu_custom_call" | custom-call | flops 2147483648 | tf_op jit(solution)/shard_map/up_project/pallas_call | solution.py:123
  31.6 1.0 %collective-permute-done.16.other_ref = bf16[128,512]{1,0:T(8,128)(2,1)S(1)} collective-permute-done((bf16[128,512]{1,0:T(8,128)(2,1)S(1)}, bf16[128,512]{1,0:T(8,128)(2,1)S(1)}, u32[]{:S(2)}, u32[]{:S(2)}) %collective-permute-start.16) | collective-permute-done | bytes 131104 | tf_op jit(solution)/shard_map/ppermute | solution.py:299
  32.7 0.1 collective-permute-start.17
  32.8 2.2 %collective-permute-start.15 = (bf16[128,512]{1,0:T(8,128)(2,1)S(1)}, bf16[128,512]{1,0:T(8,128)(2,1)S(1)}, u32[]{:S(2)}, u32[]{:S(2)}) collective-permute-start(bf16[128,512]{1,0:T(8,128)(2,1)S(1)} %up_project.3.value_ref), channel_id=1, source_target_pairs={{0,8},{1,9},{2,10},{3,11},{4,12},{5,13},{6,14},{7,15},{8,0},{9,1},... | collective-permute-start | bytes 393224 | tf_op jit(solution)/shard_map/ppermute | solution.py:299
  35.0 7.4 %collective-permute-done.15.other_ref = bf16[128,512]{1,0:T(8,128)(2,1)S(1)} collective-permute-done((bf16[128,512]{1,0:T(8,128)(2,1)S(1)}, bf16[128,512]{1,0:T(8,128)(2,1)S(1)}, u32[]{:S(2)}, u32[]{:S(2)}) %collective-permute-start.15) | collective-permute-done | bytes 131104 | tf_op jit(solution)/shard_map/ppermute | solution.py:299
  42.4 0.0 slice-start
  42.5 0.1 collective-permute-start.18
  42.5 0.3 collective-permute-start.20
  42.8 1.1 %collective-permute-done.18.other_ref = bf16[128,512]{1,0:T(8,128)(2,1)S(1)} collective-permute-done((bf16[128,512]{1,0:T(8,128)(2,1)S(1)}, bf16[128,512]{1,0:T(8,128)(2,1)S(1)}, u32[]{:S(2)}, u32[]{:S(2)}) %collective-permute-start.18) | collective-permute-done | bytes 131104 | tf_op jit(solution)/shard_map/ppermute | solution.py:299
  43.9 0.0 slice-start.1
  43.9 1.8 %collective-permute-start.19 = (bf16[128,512]{1,0:T(8,128)(2,1)S(1)}, bf16[128,512]{1,0:T(8,128)(2,1)S(1)}, u32[]{:S(2)}, u32[]{:S(2)}) collective-permute-start(bf16[128,512]{1,0:T(8,128)(2,1)S(1)} %turn.11.value_ref), channel_id=1, source_target_pairs={{0,2},{1,3},{2,0},{3,1},{4,6},{5,7},{6,4},{7,5},{8,10},{9,11},{10,... | collective-permute-start | bytes 393224 | tf_op jit(solution)/shard_map/ppermute | solution.py:299
  45.8 2.7 %collective-permute-done.20.other_ref = bf16[128,512]{1,0:T(8,128)(2,1)S(1)} collective-permute-done((bf16[128,512]{1,0:T(8,128)(2,1)S(1)}, bf16[128,512]{1,0:T(8,128)(2,1)S(1)}, u32[]{:S(2)}, u32[]{:S(2)}) %collective-permute-start.20) | collective-permute-done | bytes 131104 | tf_op jit(solution)/shard_map/ppermute | solution.py:299
  48.5 0.0 slice-start.2
  48.5 1.9 %collective-permute-start.22 = (bf16[128,512]{1,0:T(8,128)(2,1)S(1)}, bf16[128,512]{1,0:T(8,128)(2,1)S(1)}, u32[]{:S(2)}, u32[]{:S(2)}) collective-permute-start(bf16[128,512]{1,0:T(8,128)(2,1)S(1)} %turn.12.value_ref), channel_id=1, source_target_pairs={{0,8},{1,9},{2,10},{3,11},{4,12},{5,13},{6,14},{7,15},{8,0},{9,1},... | collective-permute-start | bytes 393224 | tf_op jit(solution)/shard_map/ppermute | solution.py:299
  50.4 0.0 slice-start.3
  50.5 1.8 %collective-permute-start.21 = (bf16[128,512]{1,0:T(8,128)(2,1)S(1)}, bf16[128,512]{1,0:T(8,128)(2,1)S(1)}, u32[]{:S(2)}, u32[]{:S(2)}) collective-permute-start(bf16[128,512]{1,0:T(8,128)(2,1)S(1)} %turn.13.value_ref), channel_id=1, source_target_pairs={{0,4},{1,5},{2,6},{3,7},{4,0},{5,1},{6,2},{7,3},{8,12},{9,13},{10,... | collective-permute-start | bytes 393224 | tf_op jit(solution)/shard_map/ppermute | solution.py:299
  52.3 5.2 %collective-permute-done.22.other_ref = bf16[128,512]{1,0:T(8,128)(2,1)S(1)} collective-permute-done((bf16[128,512]{1,0:T(8,128)(2,1)S(1)}, bf16[128,512]{1,0:T(8,128)(2,1)S(1)}, u32[]{:S(2)}, u32[]{:S(2)}) %collective-permute-start.22) | collective-permute-done | bytes 131104 | tf_op jit(solution)/shard_map/ppermute | solution.py:299
  57.5 0.3 collective-permute-done.21.other_ref
  58.0 1.5 %down_project.3 = (bf16[48,4096]{1,0:T(8,128)(2,1)S(1)}, bf16[80,4096]{1,0:T(8,128)(2,1)S(1)}) custom-call(bf16[128,512]{1,0:T(8,128)(2,1)S(1)} %turn.14.a_ref, bf16[128,512]{1,0:T(8,128)(2,1)S(1)} %turn.15.b_ref, f32[1,1024]{1,0:T(1,128)S(1)} %bitcast.8, bf16[1024,8192]{1,0:T(8,128)(2,1)S(1)} %bitcast.3), custom_call_target="tpu_custom_call" | custom-call | flops 1073741824 | tf_op jit(solution)/shard_map/down_project/pallas_call | solution.py:183
  59.4 0.1 collective-permute-start.23
  59.5 1.4 %down_project.2 = (bf16[48,4096]{1,0:T(8,128)(2,1)S(1)}, bf16[80,4096]{1,0:T(8,128)(2,1)S(1)}) custom-call(bf16[128,512]{1,0:T(8,128)(2,1)S(1)} %turn.14.a_ref, bf16[128,512]{1,0:T(8,128)(2,1)S(1)} %turn.15.b_ref, f32[1,1024]{1,0:T(1,128)S(1)} %bitcast.9, bf16[1024,8192]{1,0:T(8,128)(2,1)S(1)} %bitcast.3), custom_call_target="tpu_custom_call" | custom-call | flops 1073741824 | tf_op jit(solution)/shard_map/down_project/pallas_call | solution.py:183
  61.0 0.3 collective-permute-done.23.arrived_ref
  61.2 0.3 collective-permute-start.24
  61.6 0.7 collective-permute-start.25
  62.3 2.6 %collective-permute-start.26 = (bf16[16,4096]{1,0:T(8,128)(2,1)S(1)}, bf16[16,4096]{1,0:T(8,128)(2,1)S(1)}, u32[]{:S(2)}, u32[]{:S(2)}) collective-permute-start(bf16[16,4096]{1,0:T(8,128)(2,1)S(1)} %sum.4), channel_id=1, source_target_pairs={{0,8},{1,7},{4,12},{5,3},{8,14},{9,1},{12,10},{13,5},{14,6},{15,9}... | collective-permute-start | bytes 393224 | tf_op jit(solution)/shard_map/ppermute | solution.py:290
  64.9 0.1 collective-permute-start.29
  65.0 2.3 %collective-permute-done.25.refs_0_ = bf16[16,4096]{1,0:T(8,128)(2,1)S(1)} collective-permute-done((bf16[16,4096]{1,0:T(8,128)(2,1)S(1)}, bf16[16,4096]{1,0:T(8,128)(2,1)S(1)}, u32[]{:S(2)}, u32[]{:S(2)}) %collective-permute-start.25) | collective-permute-done | bytes 131104 | tf_op jit(solution)/shard_map/ppermute | solution.py:290
  67.2 3.6 %collective-permute-done.26.refs_1_ = bf16[16,4096]{1,0:T(8,128)(2,1)S(1)} collective-permute-done((bf16[16,4096]{1,0:T(8,128)(2,1)S(1)}, bf16[16,4096]{1,0:T(8,128)(2,1)S(1)}, u32[]{:S(2)}, u32[]{:S(2)}) %collective-permute-start.26) | collective-permute-done | bytes 131104 | tf_op jit(solution)/shard_map/ppermute | solution.py:290
  70.8 0.1 relay.4
  70.9 0.1 collective-permute-start.27
  70.9 0.4 collective-permute-done.29.refs_0_
  71.3 0.1 relay.6
  71.4 1.7 %collective-permute-start.30 = (bf16[16,4096]{1,0:T(8,128)(2,1)S(1)}, bf16[16,4096]{1,0:T(8,128)(2,1)S(1)}, u32[]{:S(2)}, u32[]{:S(2)}) collective-permute-start(bf16[16,4096]{1,0:T(8,128)(2,1)S(1)} %relay.6), channel_id=1, source_target_pairs={{0,2},{1,3},{4,0},{5,1},{8,4},{9,5},{12,8},{13,9},{14,12},{15,13},... | collective-permute-start | bytes 393224 | tf_op jit(solution)/shard_map/ppermute | solution.py:290
  73.1 3.7 %collective-permute-done.27.refs_0_ = bf16[16,4096]{1,0:T(8,128)(2,1)S(1)} collective-permute-done((bf16[16,4096]{1,0:T(8,128)(2,1)S(1)}, bf16[16,4096]{1,0:T(8,128)(2,1)S(1)}, u32[]{:S(2)}, u32[]{:S(2)}) %collective-permute-start.27) | collective-permute-done | bytes 131104 | tf_op jit(solution)/shard_map/ppermute | solution.py:290
  76.8 0.1 relay.5
  76.8 0.1 collective-permute-start.28
  76.9 0.1 relay.7
  77.0 2.1 %collective-permute-start.31 = (bf16[16,4096]{1,0:T(8,128)(2,1)S(1)}, bf16[16,4096]{1,0:T(8,128)(2,1)S(1)}, u32[]{:S(2)}, u32[]{:S(2)}) collective-permute-start(bf16[16,4096]{1,0:T(8,128)(2,1)S(1)} %relay.7), channel_id=1, source_target_pairs={{0,2},{1,3},{4,0},{5,1},{8,4},{9,5},{12,8},{13,9},{14,12},{15,13},... | collective-permute-start | bytes 393224 | tf_op jit(solution)/shard_map/ppermute | solution.py:290
  79.0 2.8 %collective-permute-done.28.ahead_in = bf16[16,4096]{1,0:T(8,128)(2,1)S(1)} collective-permute-done((bf16[16,4096]{1,0:T(8,128)(2,1)S(1)}, bf16[16,4096]{1,0:T(8,128)(2,1)S(1)}, u32[]{:S(2)}, u32[]{:S(2)}) %collective-permute-start.28) | collective-permute-done | bytes 131104 | tf_op jit(solution)/shard_map/ppermute | solution.py:290
  81.9 0.1 collective-permute-done.31.behind_in
  82.0 0.1 last.1
  82.1 0.1 collective-permute-start.32
  82.2 1.2 %collective-permute-done.32.take_ref = bf16[8,4096]{1,0:T(8,128)(2,1)S(1)} collective-permute-done((bf16[8,4096]{1,0:T(8,128)(2,1)S(1)}, bf16[8,4096]{1,0:T(8,128)(2,1)S(1)}, u32[]{:S(2)}, u32[]{:S(2)}) %collective-permute-start.32) | collective-permute-done | bytes 65568 | tf_op jit(solution)/shard_map/ppermute | solution.py:299
  83.4 0.7 mix.1
  (56 shorter events, 0.6 us)
Async XLA Ops:
  0.0 23.5 %slice-start.4 = ((s8[16777216]{0:T(1024)(128)(4,1)}), s8[4194304]{0:T(1024)(128)(4,1)S(1)}, s32[]{:S(2)}) async-start(s8[16777216]{0:T(1024)(128)(4,1)} %bitcast.4), calls=%async_computation.4 | async-start | bytes 8388608
  0.0 23.5 %slice-start.8 = ((s8[16777216]{0:T(1024)(128)(4,1)}), s8[4194304]{0:T(1024)(128)(4,1)S(1)}, s32[]{:S(2)}) async-start(s8[16777216]{0:T(1024)(128)(4,1)} %bitcast.6), calls=%async_computation.8 | async-start | bytes 8388608
  0.0 23.5 %slice-start.5 = ((s8[16777216]{0:T(1024)(128)(4,1)}), s8[4194304]{0:T(1024)(128)(4,1)S(1)}, s32[]{:S(2)}) async-start(s8[16777216]{0:T(1024)(128)(4,1)} %bitcast.4), calls=%async_computation.5 | async-start | bytes 8388608
  0.0 23.6 %slice-start.6 = ((s8[16777216]{0:T(1024)(128)(4,1)}), s8[4194304]{0:T(1024)(128)(4,1)S(1)}, s32[]{:S(2)}) async-start(s8[16777216]{0:T(1024)(128)(4,1)} %bitcast.4), calls=%async_computation.6 | async-start | bytes 8388608
  0.0 23.6 %slice-start.7 = ((s8[16777216]{0:T(1024)(128)(4,1)}), s8[4194304]{0:T(1024)(128)(4,1)S(1)}, s32[]{:S(2)}) async-start(s8[16777216]{0:T(1024)(128)(4,1)} %bitcast.4), calls=%async_computation.7 | async-start | bytes 8388608
  0.0 23.6 %slice-start.9 = ((s8[16777216]{0:T(1024)(128)(4,1)}), s8[4194304]{0:T(1024)(128)(4,1)S(1)}, s32[]{:S(2)}) async-start(s8[16777216]{0:T(1024)(128)(4,1)} %bitcast.6), calls=%async_computation.9 | async-start | bytes 8388608
  0.0 23.6 %slice-start.10 = ((s8[16777216]{0:T(1024)(128)(4,1)}), s8[4194304]{0:T(1024)(128)(4,1)S(1)}, s32[]{:S(2)}) async-start(s8[16777216]{0:T(1024)(128)(4,1)} %bitcast.6), calls=%async_computation.10 | async-start | bytes 8388608
  0.0 23.6 %slice-start.11 = ((s8[16777216]{0:T(1024)(128)(4,1)}), s8[4194304]{0:T(1024)(128)(4,1)S(1)}, s32[]{:S(2)}) async-start(s8[16777216]{0:T(1024)(128)(4,1)} %bitcast.6), calls=%async_computation.11 | async-start | bytes 8388608
  1.3 6.6 %collective-permute-start.3 = (bf16[8,8192]{1,0:T(8,128)(2,1)S(1)}, bf16[8,8192]{1,0:T(8,128)(2,1)S(1)}, u32[]{:S(2)}, u32[]{:S(2)}) collective-permute-start(bf16[8,8192]{1,0:T(8,128)(2,1)S(1)} %normalize.1.refs_0_), channel_id=1, source_target_pairs={{0,2},{1,3},{4,0},{5,1},{8,4},{9,5},{12,8},{13,9},{14,12},{15,13},... | collective-permute-start | bytes 393224 | tf_op jit(solution)/shard_map/ppermute | solution.py:290
  4.4 5.2 %collective-permute-start.1 = (bf16[8,8192]{1,0:T(8,128)(2,1)S(1)}, bf16[8,8192]{1,0:T(8,128)(2,1)S(1)}, u32[]{:S(2)}, u32[]{:S(2)}) collective-permute-start(bf16[8,8192]{1,0:T(8,128)(2,1)S(1)} %normalize.1.refs_0_), channel_id=1, source_target_pairs={{0,4},{1,5},{4,8},{5,9},{8,12},{9,13},{12,14},{13,15},{14,10},{15,... | collective-permute-start | bytes 393224 | tf_op jit(solution)/shard_map/ppermute | solution.py:290
  7.9 5.0 %collective-permute-start.7 = (bf16[8,8192]{1,0:T(8,128)(2,1)S(1)}, bf16[8,8192]{1,0:T(8,128)(2,1)S(1)}, u32[]{:S(2)}, u32[]{:S(2)}) collective-permute-start(bf16[8,8192]{1,0:T(8,128)(2,1)S(1)} %collective-permute-done.3.refs_4_), channel_id=1, source_target_pairs={{0,2},{1,3},{4,0},{5,1},{8,4},{9,5},{12,8},{13,9},{14,12},{15,13},... | collective-permute-start | bytes 393224 | tf_op jit(solution)/shard_map/ppermute | solution.py:290
  9.6 5.0 %collective-permute-start.5 = (bf16[8,8192]{1,0:T(8,128)(2,1)S(1)}, bf16[8,8192]{1,0:T(8,128)(2,1)S(1)}, u32[]{:S(2)}, u32[]{:S(2)}) collective-permute-start(bf16[8,8192]{1,0:T(8,128)(2,1)S(1)} %collective-permute-done.1.refs_2_), channel_id=1, source_target_pairs={{0,4},{1,5},{4,8},{5,9},{8,12},{9,13},{12,14},{13,15},{14,10},{15,... | collective-permute-start | bytes 393224 | tf_op jit(solution)/shard_map/ppermute | solution.py:290
  9.9 6.2 %collective-permute-start = (bf16[8,8192]{1,0:T(8,128)(2,1)S(1)}, bf16[8,8192]{1,0:T(8,128)(2,1)S(1)}, u32[]{:S(2)}, u32[]{:S(2)}) collective-permute-start(bf16[8,8192]{1,0:T(8,128)(2,1)S(1)} %normalize.1.refs_0_), channel_id=1, source_target_pairs={{0,1},{1,0},{2,3},{3,2},{4,5},{5,4},{6,7},{7,6},{8,9},{9,8},{10,11... | collective-permute-start | bytes 393224 | tf_op jit(solution)/shard_map/ppermute | solution.py:299
  9.9 7.8 %collective-permute-start.4 = (bf16[8,8192]{1,0:T(8,128)(2,1)S(1)}, bf16[8,8192]{1,0:T(8,128)(2,1)S(1)}, u32[]{:S(2)}, u32[]{:S(2)}) collective-permute-start(bf16[8,8192]{1,0:T(8,128)(2,1)S(1)} %collective-permute-done.3.refs_4_), channel_id=1, source_target_pairs={{0,1},{1,0},{2,3},{3,2},{4,5},{5,4},{6,7},{7,6},{8,9},{9,8},{10,11... | collective-permute-start | bytes 393224 | tf_op jit(solution)/shard_map/ppermute | solution.py:299
  10.4 7.3 %collective-permute-start.2 = (bf16[8,8192]{1,0:T(8,128)(2,1)S(1)}, bf16[8,8192]{1,0:T(8,128)(2,1)S(1)}, u32[]{:S(2)}, u32[]{:S(2)}) collective-permute-start(bf16[8,8192]{1,0:T(8,128)(2,1)S(1)} %collective-permute-done.1.refs_2_), channel_id=1, source_target_pairs={{0,1},{1,0},{2,3},{3,2},{4,5},{5,4},{6,7},{7,6},{8,9},{9,8},{10,11... | collective-permute-start | bytes 393224 | tf_op jit(solution)/shard_map/ppermute | solution.py:299
  12.9 7.4 %collective-permute-start.11 = (bf16[8,8192]{1,0:T(8,128)(2,1)S(1)}, bf16[8,8192]{1,0:T(8,128)(2,1)S(1)}, u32[]{:S(2)}, u32[]{:S(2)}) collective-permute-start(bf16[8,8192]{1,0:T(8,128)(2,1)S(1)} %collective-permute-done.7.odd_ref.refs_8_), channel_id=1, source_target_pairs={{0,2},{1,3},{4,0},{5,1},{8,4},{9,5},{12,8},{13,9},{14,12},{15,13},... | collective-permute-start | bytes 393224 | tf_op jit(solution)/shard_map/ppermute | solution.py:290
  14.6 7.4 %collective-permute-start.13 = (bf16[8,8192]{1,0:T(8,128)(2,1)S(1)}, bf16[8,8192]{1,0:T(8,128)(2,1)S(1)}, u32[]{:S(2)}, u32[]{:S(2)}) collective-permute-start(bf16[8,8192]{1,0:T(8,128)(2,1)S(1)} %pick.1), channel_id=1, source_target_pairs={{0,8},{1,7},{4,12},{5,3},{8,14},{9,1},{12,10},{13,5},{14,6},{15,9}... | collective-permute-start | bytes 393224 | tf_op jit(solution)/shard_map/ppermute | solution.py:290
  16.2 6.0 %collective-permute-start.9 = (bf16[8,8192]{1,0:T(8,128)(2,1)S(1)}, bf16[8,8192]{1,0:T(8,128)(2,1)S(1)}, u32[]{:S(2)}, u32[]{:S(2)}) collective-permute-start(bf16[8,8192]{1,0:T(8,128)(2,1)S(1)} %collective-permute-done.5.even_ref.refs_6_), channel_id=1, source_target_pairs={{0,4},{1,5},{4,8},{5,9},{8,12},{9,13},{12,14},{13,15},{14,10},{15,... | collective-permute-start | bytes 393224 | tf_op jit(solution)/shard_map/ppermute | solution.py:290
  17.7 4.8 %collective-permute-start.8 = (bf16[8,8192]{1,0:T(8,128)(2,1)S(1)}, bf16[8,8192]{1,0:T(8,128)(2,1)S(1)}, u32[]{:S(2)}, u32[]{:S(2)}) collective-permute-start(bf16[8,8192]{1,0:T(8,128)(2,1)S(1)} %collective-permute-done.7.odd_ref.refs_8_), channel_id=1, source_target_pairs={{0,1},{1,0},{2,3},{3,2},{4,5},{5,4},{6,7},{7,6},{8,9},{9,8},{10,11... | collective-permute-start | bytes 393224 | tf_op jit(solution)/shard_map/ppermute | solution.py:299
  17.7 4.8 %collective-permute-start.6 = (bf16[8,8192]{1,0:T(8,128)(2,1)S(1)}, bf16[8,8192]{1,0:T(8,128)(2,1)S(1)}, u32[]{:S(2)}, u32[]{:S(2)}) collective-permute-start(bf16[8,8192]{1,0:T(8,128)(2,1)S(1)} %collective-permute-done.5.even_ref.refs_6_), channel_id=1, source_target_pairs={{0,1},{1,0},{2,3},{3,2},{4,5},{5,4},{6,7},{7,6},{8,9},{9,8},{10,11... | collective-permute-start | bytes 393224 | tf_op jit(solution)/shard_map/ppermute | solution.py:299
  20.3 2.2 %collective-permute-start.12 = (bf16[8,8192]{1,0:T(8,128)(2,1)S(1)}, bf16[8,8192]{1,0:T(8,128)(2,1)S(1)}, u32[]{:S(2)}, u32[]{:S(2)}) collective-permute-start(bf16[8,8192]{1,0:T(8,128)(2,1)S(1)} %collective-permute-done.11.refs_12_), channel_id=1, source_target_pairs={{0,1},{1,0},{2,3},{3,2},{4,5},{5,4},{6,7},{7,6},{8,9},{9,8},{10,11... | collective-permute-start | bytes 393224 | tf_op jit(solution)/shard_map/ppermute | solution.py:299
  22.0 1.3 %collective-permute-start.14 = (bf16[8,8192]{1,0:T(8,128)(2,1)S(1)}, bf16[8,8192]{1,0:T(8,128)(2,1)S(1)}, u32[]{:S(2)}, u32[]{:S(2)}) collective-permute-start(bf16[8,8192]{1,0:T(8,128)(2,1)S(1)} %collective-permute-done.13.refs_14_), channel_id=1, source_target_pairs={{0,1},{1,0},{2,3},{3,2},{4,5},{5,4},{6,7},{7,6},{8,9},{9,8},{10,11... | collective-permute-start | bytes 393224 | tf_op jit(solution)/shard_map/ppermute | solution.py:299
  22.2 1.3 %collective-permute-start.10 = (bf16[8,8192]{1,0:T(8,128)(2,1)S(1)}, bf16[8,8192]{1,0:T(8,128)(2,1)S(1)}, u32[]{:S(2)}, u32[]{:S(2)}) collective-permute-start(bf16[8,8192]{1,0:T(8,128)(2,1)S(1)} %collective-permute-done.9.refs_10_), channel_id=1, source_target_pairs={{0,1},{1,0},{2,3},{3,2},{4,5},{5,4},{6,7},{7,6},{8,9},{9,8},{10,11... | collective-permute-start | bytes 393224 | tf_op jit(solution)/shard_map/ppermute | solution.py:299
  26.4 6.2 %collective-permute-start.16 = (bf16[128,512]{1,0:T(8,128)(2,1)S(1)}, bf16[128,512]{1,0:T(8,128)(2,1)S(1)}, u32[]{:S(2)}, u32[]{:S(2)}) collective-permute-start(bf16[128,512]{1,0:T(8,128)(2,1)S(1)} %get-tuple-element.18.value_ref), channel_id=1, source_target_pairs={{0,2},{1,3},{2,0},{3,1},{4,6},{5,7},{6,4},{7,5},{8,10},{9,11},{10,... | collective-permute-start | bytes 393224 | tf_op jit(solution)/shard_map/ppermute | solution.py:299
  32.7 2.2 %collective-permute-start.17 = (bf16[128,512]{1,0:T(8,128)(2,1)S(1)}, bf16[128,512]{1,0:T(8,128)(2,1)S(1)}, u32[]{:S(2)}, u32[]{:S(2)}) collective-permute-start(bf16[128,512]{1,0:T(8,128)(2,1)S(1)} %turn.8.value_ref), channel_id=1, source_target_pairs={{0,1},{1,0},{2,3},{3,2},{4,5},{5,4},{6,7},{7,6},{8,9},{9,8},{10,11... | collective-permute-start | bytes 393224 | tf_op jit(solution)/shard_map/ppermute | solution.py:299
  32.8 9.6 %collective-permute-start.15 = (bf16[128,512]{1,0:T(8,128)(2,1)S(1)}, bf16[128,512]{1,0:T(8,128)(2,1)S(1)}, u32[]{:S(2)}, u32[]{:S(2)}) collective-permute-start(bf16[128,512]{1,0:T(8,128)(2,1)S(1)} %up_project.3.value_ref), channel_id=1, source_target_pairs={{0,8},{1,9},{2,10},{3,11},{4,12},{5,13},{6,14},{7,15},{8,0},{9,1},... | collective-permute-start | bytes 393224 | tf_op jit(solution)/shard_map/ppermute | solution.py:299
  42.4 15.5 %slice-start = ((s8[16777216]{0:T(1024)(128)(4,1)}), s8[4194304]{0:T(1024)(128)(4,1)S(1)}, s32[]{:S(2)}) async-start(s8[16777216]{0:T(1024)(128)(4,1)} %bitcast.2), calls=%async_computation | async-start | bytes 8388608
  42.5 15.5 %copy-start.1 = (f32[1024]{0:T(1024)S(1)}, f32[1024]{0:T(1024)}, u32[]{:S(2)}) copy-start(f32[1024]{0:T(1024)} %param.11) | copy-start | bytes 12292
  42.5 1.4 %collective-permute-start.18 = (bf16[128,512]{1,0:T(8,128)(2,1)S(1)}, bf16[128,512]{1,0:T(8,128)(2,1)S(1)}, u32[]{:S(2)}, u32[]{:S(2)}) collective-permute-start(bf16[128,512]{1,0:T(8,128)(2,1)S(1)} %turn.10.value_ref), channel_id=1, source_target_pairs={{0,1},{1,0},{2,3},{3,2},{4,5},{5,4},{6,7},{7,6},{8,9},{9,8},{10,11... | collective-permute-start | bytes 393224 | tf_op jit(solution)/shard_map/ppermute | solution.py:299
  42.5 5.9 %collective-permute-start.20 = (bf16[128,512]{1,0:T(8,128)(2,1)S(1)}, bf16[128,512]{1,0:T(8,128)(2,1)S(1)}, u32[]{:S(2)}, u32[]{:S(2)}) collective-permute-start(bf16[128,512]{1,0:T(8,128)(2,1)S(1)} %turn.9.value_ref), channel_id=1, source_target_pairs={{0,4},{1,5},{2,6},{3,7},{4,0},{5,1},{6,2},{7,3},{8,12},{9,13},{10,... | collective-permute-start | bytes 393224 | tf_op jit(solution)/shard_map/ppermute | solution.py:299
  43.9 14.0 %slice-start.1 = ((s8[16777216]{0:T(1024)(128)(4,1)}), s8[4194304]{0:T(1024)(128)(4,1)S(1)}, s32[]{:S(2)}) async-start(s8[16777216]{0:T(1024)(128)(4,1)} %bitcast.2), calls=%async_computation.1 | async-start | bytes 8388608
  43.9 6.4 %collective-permute-start.19 = (bf16[128,512]{1,0:T(8,128)(2,1)S(1)}, bf16[128,512]{1,0:T(8,128)(2,1)S(1)}, u32[]{:S(2)}, u32[]{:S(2)}) collective-permute-start(bf16[128,512]{1,0:T(8,128)(2,1)S(1)} %turn.11.value_ref), channel_id=1, source_target_pairs={{0,2},{1,3},{2,0},{3,1},{4,6},{5,7},{6,4},{7,5},{8,10},{9,11},{10,... | collective-permute-start | bytes 393224 | tf_op jit(solution)/shard_map/ppermute | solution.py:299
  48.5 9.4 %slice-start.2 = ((s8[16777216]{0:T(1024)(128)(4,1)}), s8[4194304]{0:T(1024)(128)(4,1)S(1)}, s32[]{:S(2)}) async-start(s8[16777216]{0:T(1024)(128)(4,1)} %bitcast.2), calls=%async_computation.2 | async-start | bytes 8388608
  48.5 8.9 %collective-permute-start.22 = (bf16[128,512]{1,0:T(8,128)(2,1)S(1)}, bf16[128,512]{1,0:T(8,128)(2,1)S(1)}, u32[]{:S(2)}, u32[]{:S(2)}) collective-permute-start(bf16[128,512]{1,0:T(8,128)(2,1)S(1)} %turn.12.value_ref), channel_id=1, source_target_pairs={{0,8},{1,9},{2,10},{3,11},{4,12},{5,13},{6,14},{7,15},{8,0},{9,1},... | collective-permute-start | bytes 393224 | tf_op jit(solution)/shard_map/ppermute | solution.py:299
  50.4 7.5 %slice-start.3 = ((s8[16777216]{0:T(1024)(128)(4,1)}), s8[4194304]{0:T(1024)(128)(4,1)S(1)}, s32[]{:S(2)}) async-start(s8[16777216]{0:T(1024)(128)(4,1)} %bitcast.2), calls=%async_computation.3 | async-start | bytes 8388608
  50.5 7.4 %collective-permute-start.21 = (bf16[128,512]{1,0:T(8,128)(2,1)S(1)}, bf16[128,512]{1,0:T(8,128)(2,1)S(1)}, u32[]{:S(2)}, u32[]{:S(2)}) collective-permute-start(bf16[128,512]{1,0:T(8,128)(2,1)S(1)} %turn.13.value_ref), channel_id=1, source_target_pairs={{0,4},{1,5},{2,6},{3,7},{4,0},{5,1},{6,2},{7,3},{8,12},{9,13},{10,... | collective-permute-start | bytes 393224 | tf_op jit(solution)/shard_map/ppermute | solution.py:299
  59.4 24.0 %copy-start = (bf16[8,8192]{1,0:T(8,128)(2,1)S(1)}, bf16[8,8192]{1,0:T(8,128)(2,1)}, u32[]{:S(2)}) copy-start(bf16[8,8192]{1,0:T(8,128)(2,1)} %tokens_ref.1) | copy-start | bytes 393220
  59.4 1.8 %collective-permute-start.23 = (bf16[48,4096]{1,0:T(8,128)(2,1)S(1)}, bf16[48,4096]{1,0:T(8,128)(2,1)S(1)}, u32[]{:S(2)}, u32[]{:S(2)}) collective-permute-start(bf16[48,4096]{1,0:T(8,128)(2,1)S(1)} %get-tuple-element.24), channel_id=1, source_target_pairs={{0,1},{1,0},{2,3},{3,2},{4,5},{5,4},{6,7},{7,6},{8,9},{9,8},{10,11... | collective-permute-start | bytes 1179656 | tf_op jit(solution)/shard_map/ppermute | solution.py:299
  61.2 9.6 %collective-permute-start.24 = (bf16[80,4096]{1,0:T(8,128)(2,1)S(1)}, bf16[80,4096]{1,0:T(8,128)(2,1)S(1)}, u32[]{:S(2)}, u32[]{:S(2)}) collective-permute-start(bf16[80,4096]{1,0:T(8,128)(2,1)S(1)} %get-tuple-element.25), channel_id=1, source_target_pairs={{0,1},{1,0},{2,3},{3,2},{4,5},{5,4},{6,7},{7,6},{8,9},{9,8},{10,11... | collective-permute-start | bytes 1966088 | tf_op jit(solution)/shard_map/ppermute | solution.py:299
  61.6 5.7 %collective-permute-start.25 = (bf16[16,4096]{1,0:T(8,128)(2,1)S(1)}, bf16[16,4096]{1,0:T(8,128)(2,1)S(1)}, u32[]{:S(2)}, u32[]{:S(2)}) collective-permute-start(bf16[16,4096]{1,0:T(8,128)(2,1)S(1)} %sum.3), channel_id=1, source_target_pairs={{0,4},{1,5},{4,8},{5,9},{8,12},{9,13},{12,14},{13,15},{14,10},{15,... | collective-permute-start | bytes 393224 | tf_op jit(solution)/shard_map/ppermute | solution.py:290
  62.3 8.5 %collective-permute-start.26 = (bf16[16,4096]{1,0:T(8,128)(2,1)S(1)}, bf16[16,4096]{1,0:T(8,128)(2,1)S(1)}, u32[]{:S(2)}, u32[]{:S(2)}) collective-permute-start(bf16[16,4096]{1,0:T(8,128)(2,1)S(1)} %sum.4), channel_id=1, source_target_pairs={{0,8},{1,7},{4,12},{5,3},{8,14},{9,1},{12,10},{13,5},{14,6},{15,9}... | collective-permute-start | bytes 393224 | tf_op jit(solution)/shard_map/ppermute | solution.py:290
  64.9 6.4 %collective-permute-start.29 = (bf16[16,4096]{1,0:T(8,128)(2,1)S(1)}, bf16[16,4096]{1,0:T(8,128)(2,1)S(1)}, u32[]{:S(2)}, u32[]{:S(2)}) collective-permute-start(bf16[16,4096]{1,0:T(8,128)(2,1)S(1)} %sum.5), channel_id=1, source_target_pairs={{0,2},{1,3},{4,0},{5,1},{8,4},{9,5},{12,8},{13,9},{14,12},{15,13},... | collective-permute-start | bytes 393224 | tf_op jit(solution)/shard_map/ppermute | solution.py:290
  70.9 5.9 %collective-permute-start.27 = (bf16[16,4096]{1,0:T(8,128)(2,1)S(1)}, bf16[16,4096]{1,0:T(8,128)(2,1)S(1)}, u32[]{:S(2)}, u32[]{:S(2)}) collective-permute-start(bf16[16,4096]{1,0:T(8,128)(2,1)S(1)} %relay.4), channel_id=1, source_target_pairs={{0,4},{1,5},{4,8},{5,9},{8,12},{9,13},{12,14},{13,15},{14,10},{15,... | collective-permute-start | bytes 393224 | tf_op jit(solution)/shard_map/ppermute | solution.py:290
  71.4 5.5 %collective-permute-start.30 = (bf16[16,4096]{1,0:T(8,128)(2,1)S(1)}, bf16[16,4096]{1,0:T(8,128)(2,1)S(1)}, u32[]{:S(2)}, u32[]{:S(2)}) collective-permute-start(bf16[16,4096]{1,0:T(8,128)(2,1)S(1)} %relay.6), channel_id=1, source_target_pairs={{0,2},{1,3},{4,0},{5,1},{8,4},{9,5},{12,8},{13,9},{14,12},{15,13},... | collective-permute-start | bytes 393224 | tf_op jit(solution)/shard_map/ppermute | solution.py:290
  76.8 5.0 %collective-permute-start.28 = (bf16[16,4096]{1,0:T(8,128)(2,1)S(1)}, bf16[16,4096]{1,0:T(8,128)(2,1)S(1)}, u32[]{:S(2)}, u32[]{:S(2)}) collective-permute-start(bf16[16,4096]{1,0:T(8,128)(2,1)S(1)} %relay.5), channel_id=1, source_target_pairs={{0,4},{1,5},{4,8},{5,9},{8,12},{9,13},{12,14},{13,15},{14,10},{15,... | collective-permute-start | bytes 393224 | tf_op jit(solution)/shard_map/ppermute | solution.py:290
  77.0 5.0 %collective-permute-start.31 = (bf16[16,4096]{1,0:T(8,128)(2,1)S(1)}, bf16[16,4096]{1,0:T(8,128)(2,1)S(1)}, u32[]{:S(2)}, u32[]{:S(2)}) collective-permute-start(bf16[16,4096]{1,0:T(8,128)(2,1)S(1)} %relay.7), channel_id=1, source_target_pairs={{0,2},{1,3},{4,0},{5,1},{8,4},{9,5},{12,8},{13,9},{14,12},{15,13},... | collective-permute-start | bytes 393224 | tf_op jit(solution)/shard_map/ppermute | solution.py:290
  82.1 1.3 %collective-permute-start.32 = (bf16[8,4096]{1,0:T(8,128)(2,1)S(1)}, bf16[8,4096]{1,0:T(8,128)(2,1)S(1)}, u32[]{:S(2)}, u32[]{:S(2)}) collective-permute-start(bf16[8,4096]{1,0:T(8,128)(2,1)S(1)} %get-tuple-element.28), channel_id=1, source_target_pairs={{0,1},{1,0},{2,3},{3,2},{4,5},{5,4},{6,7},{7,6},{8,9},{9,8},{10,11... | collective-permute-start | bytes 196616 | tf_op jit(solution)/shard_map/ppermute | solution.py:299

commit v9 on v7

--- a/solution.py
+++ b/solution.py
@@ -9,7 +9,8 @@
 
 BLOCK = 256
 MIB = 1 << 20
-TURN = 2_000_000_000
+OFFSETS = (3, 1, 0, 2)
+TURN = 1_000_000_000
 COST = 20_000_000_000
 
 
@@ -84,10 +85,10 @@
 def up_kernel(shifts, first, lanes_of, *refs):
     count = 2 * len(shifts)
     if first:
-        gate_ref, up_ref, out_ref, rows_ref, hidden_ref = refs[count:]
+        gate_ref, up_ref, *outs, rows_ref, hidden_ref = refs[count:]
         join_rows(refs[:count], rows_ref)
     else:
-        rows_ref, gate_ref, up_ref, out_ref, hidden_ref = refs
+        rows_ref, gate_ref, up_ref, *outs, hidden_ref = refs
     me = lax.axis_index("hid")
     chip, core = me // 2, me % 2
     own = rows_ref.shape[0] // count
@@ -108,7 +109,9 @@
             there = there + core if part % 2 == 0 else there + 1 - core
             spot = pl.multiple_of(there * own, own)
             hidden_ref[pl.ds(spot, own), lanes] = turned[part * own : (part + 1) * own]
-    out_ref[...] = hidden_ref[...].astype(jnp.bfloat16)
+    cols = outs[0].shape[1]
+    for at, out_ref in enumerate(outs):
+        out_ref[...] = hidden_ref[:, at * cols : (at + 1) * cols].astype(jnp.bfloat16)
 
 
 def up_project(shifts, parts, gate_weight, up_weight, at, pieces):
@@ -117,7 +120,7 @@
     width = width // pieces
     rows = sum(part.shape[0] for part in parts)
     vmem = pl.BlockSpec(memory_space=pltpu.VMEM)
-    outs = [jax.ShapeDtypeStruct((rows, width), jnp.bfloat16)]
+    outs = [jax.ShapeDtypeStruct((rows, width // 2), jnp.bfloat16)] * 2
     if first:
         outs.append(jax.ShapeDtypeStruct((rows, depth), jnp.bfloat16))
     return pl.pallas_call(
@@ -141,11 +144,11 @@
 EARLY = 3
 
 
-def down_kernel(blocks, chips, scale, flip, a_ref, b_ref, clip_ref, weight_ref, *refs):
-    outs, (rows_ref, mixed_ref) = refs[:-2], refs[-2:]
-    half = a_ref.shape[1]
-    rows_ref[:, :half] = a_ref[...].astype(jnp.float32)
-    rows_ref[:, half:] = b_ref[...].astype(jnp.float32)
+def down_kernel(blocks, chips, scale, flip, clip_ref, weight_ref, *refs):
+    slices, outs, (rows_ref, mixed_ref) = refs[:-4], refs[-4:-2], refs[-2:]
+    cols = slices[0].shape[1]
+    for at, slice_ref in enumerate(slices):
+        rows_ref[:, at * cols : (at + 1) * cols] = slice_ref[...].astype(jnp.float32)
     parts = [rows_ref[:, b * BLOCK : (b + 1) * BLOCK] for b in range(blocks)]
     span = 1
     while span < blocks:
@@ -173,8 +176,8 @@
         first += out_ref.shape[0]
 
 
-def down_project(a, b, clip_scale, weight, flip, chips, total):
-    rows = a.shape[0]
+def down_project(slices, clip_scale, weight, flip, chips, total):
+    rows = slices[0].shape[0]
     width, depth = weight.shape[0], weight.shape[1] // 2
     vmem = pl.BlockSpec(memory_space=pltpu.VMEM)
     outs = [
@@ -183,13 +186,13 @@
     return pl.pallas_call(
         functools.partial(down_kernel, width // BLOCK, chips, total**-0.5, flip),
         out_shape=outs,
-        in_specs=[vmem] * 4,
+        in_specs=[vmem] * (2 + len(slices)),
         out_specs=[vmem] * 2,
         scratch_shapes=[pltpu.VMEM((rows, width), jnp.float32), pltpu.VMEM((rows, width), jnp.bfloat16)],
         compiler_params=pltpu.CompilerParams(vmem_limit_bytes=8 * MIB),
         cost_estimate=pl.CostEstimate(flops=2 * rows * depth * width, bytes_accessed=0, transcendentals=0),
         name="down_project",
-    )(a, b, clip_scale, weight)
+    )(clip_scale, weight, *slices)
 
 
 def pick_kernel(even_ref, odd_ref, out_ref):
@@ -313,37 +316,24 @@
     shifts.append(steps)
     parts = [block for own in mine for block in (own, cross(own))]
 
-    half_b, joined = up_project(shifts, parts, gate_weight, up_weight, pieces - 1, pieces)
-    if pieces == 1:
-        half_a, half_b = jnp.split(half_b, 2, axis=1)
-    else:
-        (half_a,) = up_project(shifts, [joined], gate_weight, up_weight, 0, pieces)
+    *slices, joined = up_project(shifts, parts, gate_weight, up_weight, 0, pieces)
+    for at in range(1, pieces):
+        slices += up_project(shifts, [joined], gate_weight, up_weight, at, pieces)
 
     def turn(value, mask, *others):
         return both(functools.partial(turn_kernel, mask), value, once(cross(value, mask), *others), "turn")
 
     masks = [1 << bit for bit in range(count.bit_length() - 1)]
     for stage in range(len(masks)):
-        first, second = masks[stage - 1], masks[stage]
-        if stage == 0:
-            half_b = turn(half_b, second)
-            early = turn(half_b, masks[1])
-            half_a = turn(half_a, first, half_b)
-        elif stage == 1:
-            half_b = early
-            half_a = turn(half_a, first, early)
-        elif stage < len(masks) - 1:
-            half_b = turn(half_b, second, half_a)
-            half_a = turn(half_a, first, half_b)
-        else:
-            half_a = turn(half_a, first, half_b)
-            half_b = turn(half_b, second, half_a)
+        for at in range(len(slices)):
+            place = OFFSETS[at % 4] * len(masks) // 4 + stage
+            slices[at] = turn(slices[at], masks[place % len(masks)])
 
     total = count * width
     limits = clip_scale.reshape(1, -1)
-    theirs_early, theirs = down_project(half_a, half_b, limits, down_weight, True, chips, total)
+    theirs_early, theirs = down_project(slices, limits, down_weight, True, chips, total)
     arrived_early = cross(theirs_early)
-    own_early, own = down_project(half_a, half_b, limits, down_weight, False, chips, total)
+    own_early, own = down_project(slices, limits, down_weight, False, chips, total)
     arrived = cross(once(theirs, own, arrived_early))
     rows, wide = own_early.shape[0] // EARLY, own_early.shape[1]
     part = jax.ShapeDtypeStruct((rows, wide), jnp.bfloat16)

time: 82.9 us -> 80.2 us (0.967)
  waiting for transfers between devices: 41.1 us -> 32.9 us
  starting transfers between devices: 29.9 us -> 34 us
  local copies, waits for them, and re-layouts: 0.08 us -> 1.47 us
    ppermute x19 -> x27, waiting for transfers between devices: 18.4 us -> 10.3 us  [cross(): return lax.ppermute(value, 'hid', [(d, d ^ mask) for d in range(count)])]
    ppermute x19 -> x27, starting transfers between devices: 12.6 us -> 16.9 us  [cross(): return lax.ppermute(value, 'hid', [(d, d ^ mask) for d in range(count)])]
    unnamed x28 -> x16, local copies, waits for them, and re-layouts: 0.08 us -> 1.47 us
  transfers between devices with their start and end apart: 33 -> 41, of which waited for: 21 -> 22; matrix products, arithmetic and copies ran while one was open for 0% -> 0% of each run, Pallas kernels for 6% -> 3%
where the time goes in v9:
time: 80.2 us; the launch traced here: 80 us
  starting transfers between devices  34 us (42%)
  waiting for transfers between devices  32.9 us (41%)
  Pallas kernels  11.3 us (14%)
  local copies, waits for them, and re-layouts  1.47 us (2%)
    ppermute x14, waiting for transfers between devices, hop(): return lax.ppermute(value, 'hid', pairs)  22.6 us
    ppermute x14, starting transfers between devices, hop(): return lax.ppermute(value, 'hid', pairs)  17.1 us
    ppermute x27, starting transfers between devices, cross(): return lax.ppermute(value, 'hid', [(d, d ^ mask) for d in range(count)])  16.9 us
    ppermute x27, waiting for transfers between devices, cross(): return lax.ppermute(value, 'hid', [(d, d ^ mask) for d in range(count)])  10.3 us
    pallas_call x2, Pallas kernels, up_project(): pl.pallas_call(functools.partial(up_kernel, shifts, first, slice(at * wid...  5.54 us
    pallas_call x2, Pallas kernels, down_project(): pl.pallas_call(functools.partial(down_kernel, width // BLOCK, chips, tota...  2.9 us
  transfers between devices with their start and end apart: 41, of which 22 were waited for; matrix products, arithmetic and copies ran while one was open for 0% of the time, Pallas kernels for 3%

profile of v9, /device:TPU:0, one launch (start us, length us, event | category | flops | bytes accessed | tf_op | source)
XLA Modules:
  0.0 80.0 jit_solution(15506858033736178726)
XLA Ops:
  0.0 1.3 %normalize.1.refs_0_ = bf16[8,8192]{1,0:T(8,128)(2,1)S(1)} custom-call(bf16[8,8192]{1,0:T(8,128)(2,1)} %tokens_ref.1, f32[1,8192]{1,0:T(1,128)} %bitcast.6), custom_call_target="tpu_custom_call" | custom-call | flops 20000000000 | bytes 262144 | tf_op jit(solution)/shard_map/normalize/pallas_call | solution.py:48
  1.3 3.0 %collective-permute-start.3 = (bf16[8,8192]{1,0:T(8,128)(2,1)S(1)}, bf16[8,8192]{1,0:T(8,128)(2,1)S(1)}, u32[]{:S(2)}, u32[]{:S(2)}) collective-permute-start(bf16[8,8192]{1,0:T(8,128)(2,1)S(1)} %normalize.1.refs_0_), channel_id=1, source_target_pairs={{0,2},{1,3},{4,0},{5,1},{8,4},{9,5},{12,8},{13,9},{14,12},{15,13},... | collective-permute-start | bytes 393224 | tf_op jit(solution)/shard_map/ppermute | solution.py:293
  4.3 0.1 collective-permute-start.1
  4.4 3.4 %collective-permute-done.3.refs_4_ = bf16[8,8192]{1,0:T(8,128)(2,1)S(1)} collective-permute-done((bf16[8,8192]{1,0:T(8,128)(2,1)S(1)}, bf16[8,8192]{1,0:T(8,128)(2,1)S(1)}, u32[]{:S(2)}, u32[]{:S(2)}) %collective-permute-start.3) | collective-permute-done | bytes 131104 | tf_op jit(solution)/shard_map/ppermute | solution.py:293
  7.8 1.7 %collective-permute-start.7 = (bf16[8,8192]{1,0:T(8,128)(2,1)S(1)}, bf16[8,8192]{1,0:T(8,128)(2,1)S(1)}, u32[]{:S(2)}, u32[]{:S(2)}) collective-permute-start(bf16[8,8192]{1,0:T(8,128)(2,1)S(1)} %collective-permute-done.3.refs_4_), channel_id=1, source_target_pairs={{0,2},{1,3},{4,0},{5,1},{8,4},{9,5},{12,8},{13,9},{14,12},{15,13},... | collective-permute-start | bytes 393224 | tf_op jit(solution)/shard_map/ppermute | solution.py:293
  9.5 0.3 collective-permute-start.5
  9.9 0.5 collective-permute-start.4
  10.4 2.4 %collective-permute-done.7.odd_ref.refs_8_ = bf16[8,8192]{1,0:T(8,128)(2,1)S(1)} collective-permute-done((bf16[8,8192]{1,0:T(8,128)(2,1)S(1)}, bf16[8,8192]{1,0:T(8,128)(2,1)S(1)}, u32[]{:S(2)}, u32[]{:S(2)}) %collective-permute-start.7) | collective-permute-done | bytes 131104 | tf_op jit(solution)/shard_map/ppermute | solution.py:293
  12.8 1.7 %collective-permute-start.11 = (bf16[8,8192]{1,0:T(8,128)(2,1)S(1)}, bf16[8,8192]{1,0:T(8,128)(2,1)S(1)}, u32[]{:S(2)}, u32[]{:S(2)}) collective-permute-start(bf16[8,8192]{1,0:T(8,128)(2,1)S(1)} %collective-permute-done.7.odd_ref.refs_8_), channel_id=1, source_target_pairs={{0,2},{1,3},{4,0},{5,1},{8,4},{9,5},{12,8},{13,9},{14,12},{15,13},... | collective-permute-start | bytes 393224 | tf_op jit(solution)/shard_map/ppermute | solution.py:293
  14.5 1.6 %collective-permute-start.13 = (bf16[8,8192]{1,0:T(8,128)(2,1)S(1)}, bf16[8,8192]{1,0:T(8,128)(2,1)S(1)}, u32[]{:S(2)}, u32[]{:S(2)}) collective-permute-start(bf16[8,8192]{1,0:T(8,128)(2,1)S(1)} %pick.1), channel_id=1, source_target_pairs={{0,8},{1,7},{4,12},{5,3},{8,14},{9,1},{12,10},{13,5},{14,6},{15,9}... | collective-permute-start | bytes 393224 | tf_op jit(solution)/shard_map/ppermute | solution.py:293
  16.1 1.6 %collective-permute-start.9 = (bf16[8,8192]{1,0:T(8,128)(2,1)S(1)}, bf16[8,8192]{1,0:T(8,128)(2,1)S(1)}, u32[]{:S(2)}, u32[]{:S(2)}) collective-permute-start(bf16[8,8192]{1,0:T(8,128)(2,1)S(1)} %collective-permute-done.5.even_ref.refs_6_), channel_id=1, source_target_pairs={{0,4},{1,5},{4,8},{5,9},{8,12},{9,13},{12,14},{13,15},{14,10},{15,... | collective-permute-start | bytes 393224 | tf_op jit(solution)/shard_map/ppermute | solution.py:293
  17.7 0.5 collective-permute-start.6
  18.2 2.0 %collective-permute-done.11.refs_12_ = bf16[8,8192]{1,0:T(8,128)(2,1)S(1)} collective-permute-done((bf16[8,8192]{1,0:T(8,128)(2,1)S(1)}, bf16[8,8192]{1,0:T(8,128)(2,1)S(1)}, u32[]{:S(2)}, u32[]{:S(2)}) %collective-permute-start.11) | collective-permute-done | bytes 131104 | tf_op jit(solution)/shard_map/ppermute | solution.py:293
  20.2 1.7 %collective-permute-done.13.refs_14_ = bf16[8,8192]{1,0:T(8,128)(2,1)S(1)} collective-permute-done((bf16[8,8192]{1,0:T(8,128)(2,1)S(1)}, bf16[8,8192]{1,0:T(8,128)(2,1)S(1)}, u32[]{:S(2)}, u32[]{:S(2)}) %collective-permute-start.13) | collective-permute-done | bytes 131104 | tf_op jit(solution)/shard_map/ppermute | solution.py:293
  21.9 0.2 collective-permute-done.9.refs_10_
  22.1 0.3 collective-permute-start.10
  22.4 0.8 %collective-permute-done.14.refs_15_ = bf16[8,8192]{1,0:T(8,128)(2,1)S(1)} collective-permute-done((bf16[8,8192]{1,0:T(8,128)(2,1)S(1)}, bf16[8,8192]{1,0:T(8,128)(2,1)S(1)}, u32[]{:S(2)}, u32[]{:S(2)}) %collective-permute-start.14) | collective-permute-done | bytes 131104 | tf_op jit(solution)/shard_map/ppermute | solution.py:302
  23.3 0.2 collective-permute-done.10.refs_11_
  23.5 2.8 %up_project.2 = (bf16[128,256]{1,0:T(8,128)(2,1)S(1)}, bf16[128,256]{1,0:T(8,128)(2,1)S(1)}, bf16[128,8192]{1,0:T(8,128)(2,1)S(1)}) custom-call(bf16[8,8192]{1,0:T(8,128)(2,1)S(1)} %normalize.1.refs_0_, bf16[8,8192]{1,0:T(8,128)(2,1)S(1)} %collective-permute-done.refs_1_, bf16[8,8192]{1,0:T(8,128)(2,1)S(1)} %collective-permute-done.1.refs_2_, ...), custom_call_target="tpu_custom_call" | custom-call | flops 2147483648 | tf_op jit(solution)/shard_map/up_project/pallas_call | solution.py:126
  26.3 2.8 %up_project.3 = (bf16[128,256]{1,0:T(8,128)(2,1)S(1)}, bf16[128,256]{1,0:T(8,128)(2,1)S(1)}) custom-call(bf16[128,8192]{1,0:T(8,128)(2,1)S(1)} %get-tuple-element.19.refs_0_, bf16[8192,1024]{1,0:T(8,128)(2,1)S(1)} %copy-done, bf16[8192,1024]{1,0:T(8,128)(2,1)S(1)} %copy-done.1), custom_call_target="tpu_custom_call" | custom-call | flops 2147483648 | tf_op jit(solution)/shard_map/up_project/pallas_call | solution.py:126
  29.0 0.4 collective-permute-start.23
  29.4 0.9 %collective-permute-start.27 = (bf16[128,256]{1,0:T(8,128)(2,1)S(1)}, bf16[128,256]{1,0:T(8,128)(2,1)S(1)}, u32[]{:S(2)}, u32[]{:S(2)}) collective-permute-start(bf16[128,256]{1,0:T(8,128)(2,1)S(1)} %get-tuple-element.21.value_ref), channel_id=1, source_target_pairs={{0,4},{1,5},{2,6},{3,7},{4,0},{5,1},{6,2},{7,3},{8,12},{9,13},{10,... | collective-permute-start | bytes 196616 | tf_op jit(solution)/shard_map/ppermute | solution.py:302
  30.3 3.2 %collective-permute-start.15 = (bf16[128,256]{1,0:T(8,128)(2,1)S(1)}, bf16[128,256]{1,0:T(8,128)(2,1)S(1)}, u32[]{:S(2)}, u32[]{:S(2)}) collective-permute-start(bf16[128,256]{1,0:T(8,128)(2,1)S(1)} %get-tuple-element.17.value_ref), channel_id=1, source_target_pairs={{0,8},{1,9},{2,10},{3,11},{4,12},{5,13},{6,14},{7,15},{8,0},{9,1},... | collective-permute-start | bytes 196616 | tf_op jit(solution)/shard_map/ppermute | solution.py:302
  33.6 0.5 collective-permute-start.19
  34.1 1.6 %collective-permute-start.24 = (bf16[128,256]{1,0:T(8,128)(2,1)S(1)}, bf16[128,256]{1,0:T(8,128)(2,1)S(1)}, u32[]{:S(2)}, u32[]{:S(2)}) collective-permute-start(bf16[128,256]{1,0:T(8,128)(2,1)S(1)} %turn.24.value_ref), channel_id=1, source_target_pairs={{0,2},{1,3},{2,0},{3,1},{4,6},{5,7},{6,4},{7,5},{8,10},{9,11},{10,... | collective-permute-start | bytes 196616 | tf_op jit(solution)/shard_map/ppermute | solution.py:302
  35.7 1.3 %collective-permute-start.28 = (bf16[128,256]{1,0:T(8,128)(2,1)S(1)}, bf16[128,256]{1,0:T(8,128)(2,1)S(1)}, u32[]{:S(2)}, u32[]{:S(2)}) collective-permute-start(bf16[128,256]{1,0:T(8,128)(2,1)S(1)} %turn.28.value_ref), channel_id=1, source_target_pairs={{0,8},{1,9},{2,10},{3,11},{4,12},{5,13},{6,14},{7,15},{8,0},{9,1},... | collective-permute-start | bytes 196616 | tf_op jit(solution)/shard_map/ppermute | solution.py:302
  37.0 0.1 collective-permute-start.16
  37.1 0.9 %collective-permute-done.19.other_ref = bf16[128,256]{1,0:T(8,128)(2,1)S(1)} collective-permute-done((bf16[128,256]{1,0:T(8,128)(2,1)S(1)}, bf16[128,256]{1,0:T(8,128)(2,1)S(1)}, u32[]{:S(2)}, u32[]{:S(2)}) %collective-permute-start.19) | collective-permute-done | bytes 65568 | tf_op jit(solution)/shard_map/ppermute | solution.py:302
  38.1 1.0 %collective-permute-start.20 = (bf16[128,256]{1,0:T(8,128)(2,1)S(1)}, bf16[128,256]{1,0:T(8,128)(2,1)S(1)}, u32[]{:S(2)}, u32[]{:S(2)}) collective-permute-start(bf16[128,256]{1,0:T(8,128)(2,1)S(1)} %turn.20.value_ref), channel_id=1, source_target_pairs={{0,4},{1,5},{2,6},{3,7},{4,0},{5,1},{6,2},{7,3},{8,12},{9,13},{10,... | collective-permute-start | bytes 196616 | tf_op jit(solution)/shard_map/ppermute | solution.py:302
  39.1 1.1 %collective-permute-start.25 = (bf16[128,256]{1,0:T(8,128)(2,1)S(1)}, bf16[128,256]{1,0:T(8,128)(2,1)S(1)}, u32[]{:S(2)}, u32[]{:S(2)}) collective-permute-start(bf16[128,256]{1,0:T(8,128)(2,1)S(1)} %turn.25.value_ref), channel_id=1, source_target_pairs={{0,4},{1,5},{2,6},{3,7},{4,0},{5,1},{6,2},{7,3},{8,12},{9,13},{10,... | collective-permute-start | bytes 196616 | tf_op jit(solution)/shard_map/ppermute | solution.py:302
  40.3 1.4 %collective-permute-done.28.other_ref = bf16[128,256]{1,0:T(8,128)(2,1)S(1)} collective-permute-done((bf16[128,256]{1,0:T(8,128)(2,1)S(1)}, bf16[128,256]{1,0:T(8,128)(2,1)S(1)}, u32[]{:S(2)}, u32[]{:S(2)}) %collective-permute-start.28) | collective-permute-done | bytes 65568 | tf_op jit(solution)/shard_map/ppermute | solution.py:302
  41.7 0.1 collective-permute-start.29
  41.8 0.2 collective-permute-start.17
  42.1 1.0 %collective-permute-done.20.other_ref = bf16[128,256]{1,0:T(8,128)(2,1)S(1)} collective-permute-done((bf16[128,256]{1,0:T(8,128)(2,1)S(1)}, bf16[128,256]{1,0:T(8,128)(2,1)S(1)}, u32[]{:S(2)}, u32[]{:S(2)}) %collective-permute-start.20) | collective-permute-done | bytes 65568 | tf_op jit(solution)/shard_map/ppermute | solution.py:302
  43.1 0.6 collective-permute-start.21
  43.7 0.2 collective-permute-done.25.other_ref
  44.0 2.2 %collective-permute-start.26 = (bf16[128,256]{1,0:T(8,128)(2,1)S(1)}, bf16[128,256]{1,0:T(8,128)(2,1)S(1)}, u32[]{:S(2)}, u32[]{:S(2)}) collective-permute-start(bf16[128,256]{1,0:T(8,128)(2,1)S(1)} %turn.26.value_ref), channel_id=1, source_target_pairs={{0,8},{1,9},{2,10},{3,11},{4,12},{5,13},{6,14},{7,15},{8,0},{9,1},... | collective-permute-start | bytes 196616 | tf_op jit(solution)/shard_map/ppermute | solution.py:302
  46.2 1.6 %collective-permute-start.30 = (bf16[128,256]{1,0:T(8,128)(2,1)S(1)}, bf16[128,256]{1,0:T(8,128)(2,1)S(1)}, u32[]{:S(2)}, u32[]{:S(2)}) collective-permute-start(bf16[128,256]{1,0:T(8,128)(2,1)S(1)} %turn.30.value_ref), channel_id=1, source_target_pairs={{0,2},{1,3},{2,0},{3,1},{4,6},{5,7},{6,4},{7,5},{8,10},{9,11},{10,... | collective-permute-start | bytes 196616 | tf_op jit(solution)/shard_map/ppermute | solution.py:302
  47.9 0.1 collective-permute-start.18
  48.0 2.8 %collective-permute-done.21.other_ref = bf16[128,256]{1,0:T(8,128)(2,1)S(1)} collective-permute-done((bf16[128,256]{1,0:T(8,128)(2,1)S(1)}, bf16[128,256]{1,0:T(8,128)(2,1)S(1)}, u32[]{:S(2)}, u32[]{:S(2)}) %collective-permute-start.21) | collective-permute-done | bytes 65568 | tf_op jit(solution)/shard_map/ppermute | solution.py:302
  50.8 0.1 collective-permute-start.22
  50.9 0.8 collective-permute-done.26.other_ref
  51.8 0.6 collective-permute-done.18.other_ref
  52.5 1.4 %slice-done.3 = s8[4194304]{0:T(1024)(128)(4,1)S(1)} async-done(((s8[16777216]{0:T(1024)(128)(4,1)}), s8[4194304]{0:T(1024)(128)(4,1)S(1)}, s32[]{:S(2)}) %slice-start.3) | async-done | bytes 4194328
  53.9 1.4 %down_project.3 = (bf16[48,4096]{1,0:T(8,128)(2,1)S(1)}, bf16[80,4096]{1,0:T(8,128)(2,1)S(1)}) custom-call(f32[1,1024]{1,0:T(1,128)S(1)} %bitcast.4, bf16[1024,8192]{1,0:T(8,128)(2,1)S(1)} %bitcast.3, bf16[128,256]{1,0:T(8,128)(2,1)S(1)} %turn.19.refs_0_, bf16[128,256]{1,0:T(8,128)(2,1)S(1)} %turn.23.refs_1_, bf16[128,256]{1,0:T(8,128)(2,1)S(1)} %turn.27.refs_2_, ...), custom_call_target="tpu_custom_call" | custom-call | flops 1073741824 | tf_op jit(solution)/shard_map/down_project/pallas_call | solution.py:186
  55.4 0.1 collective-permute-start.31
  55.5 1.5 %down_project.2 = (bf16[48,4096]{1,0:T(8,128)(2,1)S(1)}, bf16[80,4096]{1,0:T(8,128)(2,1)S(1)}) custom-call(f32[1,1024]{1,0:T(1,128)S(1)} %bitcast.5, bf16[1024,8192]{1,0:T(8,128)(2,1)S(1)} %bitcast.3, bf16[128,256]{1,0:T(8,128)(2,1)S(1)} %turn.19.refs_0_, bf16[128,256]{1,0:T(8,128)(2,1)S(1)} %turn.23.refs_1_, bf16[128,256]{1,0:T(8,128)(2,1)S(1)} %turn.27.refs_2_, ...), custom_call_target="tpu_custom_call" | custom-call | flops 1073741824 | tf_op jit(solution)/shard_map/down_project/pallas_call | solution.py:186
  56.9 0.2 collective-permute-done.31.arrived_ref
  57.2 0.3 collective-permute-start.32
  57.5 0.1 collective-permute-start.33
  57.7 2.9 %collective-permute-start.34 = (bf16[16,4096]{1,0:T(8,128)(2,1)S(1)}, bf16[16,4096]{1,0:T(8,128)(2,1)S(1)}, u32[]{:S(2)}, u32[]{:S(2)}) collective-permute-start(bf16[16,4096]{1,0:T(8,128)(2,1)S(1)} %sum.4), channel_id=1, source_target_pairs={{0,8},{1,7},{4,12},{5,3},{8,14},{9,1},{12,10},{13,5},{14,6},{15,9}... | collective-permute-start | bytes 393224 | tf_op jit(solution)/shard_map/ppermute | solution.py:293
  60.6 2.5 %collective-permute-done.33.refs_0_ = bf16[16,4096]{1,0:T(8,128)(2,1)S(1)} collective-permute-done((bf16[16,4096]{1,0:T(8,128)(2,1)S(1)}, bf16[16,4096]{1,0:T(8,128)(2,1)S(1)}, u32[]{:S(2)}, u32[]{:S(2)}) %collective-permute-start.33) | collective-permute-done | bytes 131104 | tf_op jit(solution)/shard_map/ppermute | solution.py:293
  63.2 3.6 %collective-permute-done.34.refs_1_ = bf16[16,4096]{1,0:T(8,128)(2,1)S(1)} collective-permute-done((bf16[16,4096]{1,0:T(8,128)(2,1)S(1)}, bf16[16,4096]{1,0:T(8,128)(2,1)S(1)}, u32[]{:S(2)}, u32[]{:S(2)}) %collective-permute-start.34) | collective-permute-done | bytes 131104 | tf_op jit(solution)/shard_map/ppermute | solution.py:293
  66.8 0.1 relay.4
  66.9 0.1 collective-permute-done.37.refs_0_
  67.0 0.1 relay.6
  67.1 2.0 %collective-permute-start.38 = (bf16[16,4096]{1,0:T(8,128)(2,1)S(1)}, bf16[16,4096]{1,0:T(8,128)(2,1)S(1)}, u32[]{:S(2)}, u32[]{:S(2)}) collective-permute-start(bf16[16,4096]{1,0:T(8,128)(2,1)S(1)} %relay.6), channel_id=1, source_target_pairs={{0,2},{1,3},{4,0},{5,1},{8,4},{9,5},{12,8},{13,9},{14,12},{15,13},... | collective-permute-start | bytes 393224 | tf_op jit(solution)/shard_map/ppermute | solution.py:293
  69.1 3.6 %collective-permute-done.35.refs_0_ = bf16[16,4096]{1,0:T(8,128)(2,1)S(1)} collective-permute-done((bf16[16,4096]{1,0:T(8,128)(2,1)S(1)}, bf16[16,4096]{1,0:T(8,128)(2,1)S(1)}, u32[]{:S(2)}, u32[]{:S(2)}) %collective-permute-start.35) | collective-permute-done | bytes 131104 | tf_op jit(solution)/shard_map/ppermute | solution.py:293
  72.9 2.1 %collective-permute-start.39 = (bf16[16,4096]{1,0:T(8,128)(2,1)S(1)}, bf16[16,4096]{1,0:T(8,128)(2,1)S(1)}, u32[]{:S(2)}, u32[]{:S(2)}) collective-permute-start(bf16[16,4096]{1,0:T(8,128)(2,1)S(1)} %relay.7), channel_id=1, source_target_pairs={{0,2},{1,3},{4,0},{5,1},{8,4},{9,5},{12,8},{13,9},{14,12},{15,13},... | collective-permute-start | bytes 393224 | tf_op jit(solution)/shard_map/ppermute | solution.py:293
  74.9 2.8 %collective-permute-done.36.ahead_in = bf16[16,4096]{1,0:T(8,128)(2,1)S(1)} collective-permute-done((bf16[16,4096]{1,0:T(8,128)(2,1)S(1)}, bf16[16,4096]{1,0:T(8,128)(2,1)S(1)}, u32[]{:S(2)}, u32[]{:S(2)}) %collective-permute-start.36) | collective-permute-done | bytes 131104 | tf_op jit(solution)/shard_map/ppermute | solution.py:293
  77.8 0.1 collective-permute-done.39.behind_in
  77.9 0.1 last.1
  78.1 1.2 %collective-permute-done.40.take_ref = bf16[8,4096]{1,0:T(8,128)(2,1)S(1)} collective-permute-done((bf16[8,4096]{1,0:T(8,128)(2,1)S(1)}, bf16[8,4096]{1,0:T(8,128)(2,1)S(1)}, u32[]{:S(2)}, u32[]{:S(2)}) %collective-permute-start.40) | collective-permute-done | bytes 65568 | tf_op jit(solution)/shard_map/ppermute | solution.py:302
  79.3 0.7 mix.1
  (66 shorter events, 1.0 us)
Async XLA Ops:
  0.0 23.5 %copy-start = (bf16[8192,1024]{1,0:T(8,128)(2,1)S(1)}, bf16[8192,1024]{1,0:T(8,128)(2,1)}, u32[]{:S(2)}) copy-start(bf16[8192,1024]{1,0:T(8,128)(2,1)} %refs_1_.1) | copy-start | bytes 50331652
  0.0 23.5 %copy-start.1 = (bf16[8192,1024]{1,0:T(8,128)(2,1)S(1)}, bf16[8192,1024]{1,0:T(8,128)(2,1)}, u32[]{:S(2)}) copy-start(bf16[8192,1024]{1,0:T(8,128)(2,1)} %refs_2_.1) | copy-start | bytes 50331652
  1.3 6.6 %collective-permute-start.3 = (bf16[8,8192]{1,0:T(8,128)(2,1)S(1)}, bf16[8,8192]{1,0:T(8,128)(2,1)S(1)}, u32[]{:S(2)}, u32[]{:S(2)}) collective-permute-start(bf16[8,8192]{1,0:T(8,128)(2,1)S(1)} %normalize.1.refs_0_), channel_id=1, source_target_pairs={{0,2},{1,3},{4,0},{5,1},{8,4},{9,5},{12,8},{13,9},{14,12},{15,13},... | collective-permute-start | bytes 393224 | tf_op jit(solution)/shard_map/ppermute | solution.py:293
  4.3 5.2 %collective-permute-start.1 = (bf16[8,8192]{1,0:T(8,128)(2,1)S(1)}, bf16[8,8192]{1,0:T(8,128)(2,1)S(1)}, u32[]{:S(2)}, u32[]{:S(2)}) collective-permute-start(bf16[8,8192]{1,0:T(8,128)(2,1)S(1)} %normalize.1.refs_0_), channel_id=1, source_target_pairs={{0,4},{1,5},{4,8},{5,9},{8,12},{9,13},{12,14},{13,15},{14,10},{15,... | collective-permute-start | bytes 393224 | tf_op jit(solution)/shard_map/ppermute | solution.py:293
  7.8 5.0 %collective-permute-start.7 = (bf16[8,8192]{1,0:T(8,128)(2,1)S(1)}, bf16[8,8192]{1,0:T(8,128)(2,1)S(1)}, u32[]{:S(2)}, u32[]{:S(2)}) collective-permute-start(bf16[8,8192]{1,0:T(8,128)(2,1)S(1)} %collective-permute-done.3.refs_4_), channel_id=1, source_target_pairs={{0,2},{1,3},{4,0},{5,1},{8,4},{9,5},{12,8},{13,9},{14,12},{15,13},... | collective-permute-start | bytes 393224 | tf_op jit(solution)/shard_map/ppermute | solution.py:293
  9.5 5.0 %collective-permute-start.5 = (bf16[8,8192]{1,0:T(8,128)(2,1)S(1)}, bf16[8,8192]{1,0:T(8,128)(2,1)S(1)}, u32[]{:S(2)}, u32[]{:S(2)}) collective-permute-start(bf16[8,8192]{1,0:T(8,128)(2,1)S(1)} %collective-permute-done.1.refs_2_), channel_id=1, source_target_pairs={{0,4},{1,5},{4,8},{5,9},{8,12},{9,13},{12,14},{13,15},{14,10},{15,... | collective-permute-start | bytes 393224 | tf_op jit(solution)/shard_map/ppermute | solution.py:293
  9.9 6.2 %collective-permute-start = (bf16[8,8192]{1,0:T(8,128)(2,1)S(1)}, bf16[8,8192]{1,0:T(8,128)(2,1)S(1)}, u32[]{:S(2)}, u32[]{:S(2)}) collective-permute-start(bf16[8,8192]{1,0:T(8,128)(2,1)S(1)} %normalize.1.refs_0_), channel_id=1, source_target_pairs={{0,1},{1,0},{2,3},{3,2},{4,5},{5,4},{6,7},{7,6},{8,9},{9,8},{10,11... | collective-permute-start | bytes 393224 | tf_op jit(solution)/shard_map/ppermute | solution.py:302
  9.9 7.8 %collective-permute-start.4 = (bf16[8,8192]{1,0:T(8,128)(2,1)S(1)}, bf16[8,8192]{1,0:T(8,128)(2,1)S(1)}, u32[]{:S(2)}, u32[]{:S(2)}) collective-permute-start(bf16[8,8192]{1,0:T(8,128)(2,1)S(1)} %collective-permute-done.3.refs_4_), channel_id=1, source_target_pairs={{0,1},{1,0},{2,3},{3,2},{4,5},{5,4},{6,7},{7,6},{8,9},{9,8},{10,11... | collective-permute-start | bytes 393224 | tf_op jit(solution)/shard_map/ppermute | solution.py:302
  10.4 7.3 %collective-permute-start.2 = (bf16[8,8192]{1,0:T(8,128)(2,1)S(1)}, bf16[8,8192]{1,0:T(8,128)(2,1)S(1)}, u32[]{:S(2)}, u32[]{:S(2)}) collective-permute-start(bf16[8,8192]{1,0:T(8,128)(2,1)S(1)} %collective-permute-done.1.refs_2_), channel_id=1, source_target_pairs={{0,1},{1,0},{2,3},{3,2},{4,5},{5,4},{6,7},{7,6},{8,9},{9,8},{10,11... | collective-permute-start | bytes 393224 | tf_op jit(solution)/shard_map/ppermute | solution.py:302
  12.8 7.4 %collective-permute-start.11 = (bf16[8,8192]{1,0:T(8,128)(2,1)S(1)}, bf16[8,8192]{1,0:T(8,128)(2,1)S(1)}, u32[]{:S(2)}, u32[]{:S(2)}) collective-permute-start(bf16[8,8192]{1,0:T(8,128)(2,1)S(1)} %collective-permute-done.7.odd_ref.refs_8_), channel_id=1, source_target_pairs={{0,2},{1,3},{4,0},{5,1},{8,4},{9,5},{12,8},{13,9},{14,12},{15,13},... | collective-permute-start | bytes 393224 | tf_op jit(solution)/shard_map/ppermute | solution.py:293
  14.5 7.4 %collective-permute-start.13 = (bf16[8,8192]{1,0:T(8,128)(2,1)S(1)}, bf16[8,8192]{1,0:T(8,128)(2,1)S(1)}, u32[]{:S(2)}, u32[]{:S(2)}) collective-permute-start(bf16[8,8192]{1,0:T(8,128)(2,1)S(1)} %pick.1), channel_id=1, source_target_pairs={{0,8},{1,7},{4,12},{5,3},{8,14},{9,1},{12,10},{13,5},{14,6},{15,9}... | collective-permute-start | bytes 393224 | tf_op jit(solution)/shard_map/ppermute | solution.py:293
  16.1 6.0 %collective-permute-start.9 = (bf16[8,8192]{1,0:T(8,128)(2,1)S(1)}, bf16[8,8192]{1,0:T(8,128)(2,1)S(1)}, u32[]{:S(2)}, u32[]{:S(2)}) collective-permute-start(bf16[8,8192]{1,0:T(8,128)(2,1)S(1)} %collective-permute-done.5.even_ref.refs_6_), channel_id=1, source_target_pairs={{0,4},{1,5},{4,8},{5,9},{8,12},{9,13},{12,14},{13,15},{14,10},{15,... | collective-permute-start | bytes 393224 | tf_op jit(solution)/shard_map/ppermute | solution.py:293
  17.7 4.8 %collective-permute-start.8 = (bf16[8,8192]{1,0:T(8,128)(2,1)S(1)}, bf16[8,8192]{1,0:T(8,128)(2,1)S(1)}, u32[]{:S(2)}, u32[]{:S(2)}) collective-permute-start(bf16[8,8192]{1,0:T(8,128)(2,1)S(1)} %collective-permute-done.7.odd_ref.refs_8_), channel_id=1, source_target_pairs={{0,1},{1,0},{2,3},{3,2},{4,5},{5,4},{6,7},{7,6},{8,9},{9,8},{10,11... | collective-permute-start | bytes 393224 | tf_op jit(solution)/shard_map/ppermute | solution.py:302
  17.7 4.8 %collective-permute-start.6 = (bf16[8,8192]{1,0:T(8,128)(2,1)S(1)}, bf16[8,8192]{1,0:T(8,128)(2,1)S(1)}, u32[]{:S(2)}, u32[]{:S(2)}) collective-permute-start(bf16[8,8192]{1,0:T(8,128)(2,1)S(1)} %collective-permute-done.5.even_ref.refs_6_), channel_id=1, source_target_pairs={{0,1},{1,0},{2,3},{3,2},{4,5},{5,4},{6,7},{7,6},{8,9},{9,8},{10,11... | collective-permute-start | bytes 393224 | tf_op jit(solution)/shard_map/ppermute | solution.py:302
  20.2 2.2 %collective-permute-start.12 = (bf16[8,8192]{1,0:T(8,128)(2,1)S(1)}, bf16[8,8192]{1,0:T(8,128)(2,1)S(1)}, u32[]{:S(2)}, u32[]{:S(2)}) collective-permute-start(bf16[8,8192]{1,0:T(8,128)(2,1)S(1)} %collective-permute-done.11.refs_12_), channel_id=1, source_target_pairs={{0,1},{1,0},{2,3},{3,2},{4,5},{5,4},{6,7},{7,6},{8,9},{9,8},{10,11... | collective-permute-start | bytes 393224 | tf_op jit(solution)/shard_map/ppermute | solution.py:302
  21.9 1.3 %collective-permute-start.14 = (bf16[8,8192]{1,0:T(8,128)(2,1)S(1)}, bf16[8,8192]{1,0:T(8,128)(2,1)S(1)}, u32[]{:S(2)}, u32[]{:S(2)}) collective-permute-start(bf16[8,8192]{1,0:T(8,128)(2,1)S(1)} %collective-permute-done.13.refs_14_), channel_id=1, source_target_pairs={{0,1},{1,0},{2,3},{3,2},{4,5},{5,4},{6,7},{7,6},{8,9},{9,8},{10,11... | collective-permute-start | bytes 393224 | tf_op jit(solution)/shard_map/ppermute | solution.py:302
  22.1 1.3 %collective-permute-start.10 = (bf16[8,8192]{1,0:T(8,128)(2,1)S(1)}, bf16[8,8192]{1,0:T(8,128)(2,1)S(1)}, u32[]{:S(2)}, u32[]{:S(2)}) collective-permute-start(bf16[8,8192]{1,0:T(8,128)(2,1)S(1)} %collective-permute-done.9.refs_10_), channel_id=1, source_target_pairs={{0,1},{1,0},{2,3},{3,2},{4,5},{5,4},{6,7},{7,6},{8,9},{9,8},{10,11... | collective-permute-start | bytes 393224 | tf_op jit(solution)/shard_map/ppermute | solution.py:302
  29.0 5.0 %collective-permute-start.23 = (bf16[128,256]{1,0:T(8,128)(2,1)S(1)}, bf16[128,256]{1,0:T(8,128)(2,1)S(1)}, u32[]{:S(2)}, u32[]{:S(2)}) collective-permute-start(bf16[128,256]{1,0:T(8,128)(2,1)S(1)} %get-tuple-element.20.value_ref), channel_id=1, source_target_pairs={{0,1},{1,0},{2,3},{3,2},{4,5},{5,4},{6,7},{7,6},{8,9},{9,8},{10,11... | collective-permute-start | bytes 196616 | tf_op jit(solution)/shard_map/ppermute | solution.py:302
  29.4 6.3 %collective-permute-start.27 = (bf16[128,256]{1,0:T(8,128)(2,1)S(1)}, bf16[128,256]{1,0:T(8,128)(2,1)S(1)}, u32[]{:S(2)}, u32[]{:S(2)}) collective-permute-start(bf16[128,256]{1,0:T(8,128)(2,1)S(1)} %get-tuple-element.21.value_ref), channel_id=1, source_target_pairs={{0,4},{1,5},{2,6},{3,7},{4,0},{5,1},{6,2},{7,3},{8,12},{9,13},{10,... | collective-permute-start | bytes 196616 | tf_op jit(solution)/shard_map/ppermute | solution.py:302
  30.3 6.7 %collective-permute-start.15 = (bf16[128,256]{1,0:T(8,128)(2,1)S(1)}, bf16[128,256]{1,0:T(8,128)(2,1)S(1)}, u32[]{:S(2)}, u32[]{:S(2)}) collective-permute-start(bf16[128,256]{1,0:T(8,128)(2,1)S(1)} %get-tuple-element.17.value_ref), channel_id=1, source_target_pairs={{0,8},{1,9},{2,10},{3,11},{4,12},{5,13},{6,14},{7,15},{8,0},{9,1},... | collective-permute-start | bytes 196616 | tf_op jit(solution)/shard_map/ppermute | solution.py:302
  33.6 4.5 %collective-permute-start.19 = (bf16[128,256]{1,0:T(8,128)(2,1)S(1)}, bf16[128,256]{1,0:T(8,128)(2,1)S(1)}, u32[]{:S(2)}, u32[]{:S(2)}) collective-permute-start(bf16[128,256]{1,0:T(8,128)(2,1)S(1)} %get-tuple-element.18.value_ref), channel_id=1, source_target_pairs={{0,2},{1,3},{2,0},{3,1},{4,6},{5,7},{6,4},{7,5},{8,10},{9,11},{10,... | collective-permute-start | bytes 196616 | tf_op jit(solution)/shard_map/ppermute | solution.py:302
  34.1 5.0 %collective-permute-start.24 = (bf16[128,256]{1,0:T(8,128)(2,1)S(1)}, bf16[128,256]{1,0:T(8,128)(2,1)S(1)}, u32[]{:S(2)}, u32[]{:S(2)}) collective-permute-start(bf16[128,256]{1,0:T(8,128)(2,1)S(1)} %turn.24.value_ref), channel_id=1, source_target_pairs={{0,2},{1,3},{2,0},{3,1},{4,6},{5,7},{6,4},{7,5},{8,10},{9,11},{10,... | collective-permute-start | bytes 196616 | tf_op jit(solution)/shard_map/ppermute | solution.py:302
  35.7 5.9 %collective-permute-start.28 = (bf16[128,256]{1,0:T(8,128)(2,1)S(1)}, bf16[128,256]{1,0:T(8,128)(2,1)S(1)}, u32[]{:S(2)}, u32[]{:S(2)}) collective-permute-start(bf16[128,256]{1,0:T(8,128)(2,1)S(1)} %turn.28.value_ref), channel_id=1, source_target_pairs={{0,8},{1,9},{2,10},{3,11},{4,12},{5,13},{6,14},{7,15},{8,0},{9,1},... | collective-permute-start | bytes 196616 | tf_op jit(solution)/shard_map/ppermute | solution.py:302
  37.0 4.7 %collective-permute-start.16 = (bf16[128,256]{1,0:T(8,128)(2,1)S(1)}, bf16[128,256]{1,0:T(8,128)(2,1)S(1)}, u32[]{:S(2)}, u32[]{:S(2)}) collective-permute-start(bf16[128,256]{1,0:T(8,128)(2,1)S(1)} %turn.16.value_ref), channel_id=1, source_target_pairs={{0,1},{1,0},{2,3},{3,2},{4,5},{5,4},{6,7},{7,6},{8,9},{9,8},{10,11... | collective-permute-start | bytes 196616 | tf_op jit(solution)/shard_map/ppermute | solution.py:302
  38.1 5.0 %collective-permute-start.20 = (bf16[128,256]{1,0:T(8,128)(2,1)S(1)}, bf16[128,256]{1,0:T(8,128)(2,1)S(1)}, u32[]{:S(2)}, u32[]{:S(2)}) collective-permute-start(bf16[128,256]{1,0:T(8,128)(2,1)S(1)} %turn.20.value_ref), channel_id=1, source_target_pairs={{0,4},{1,5},{2,6},{3,7},{4,0},{5,1},{6,2},{7,3},{8,12},{9,13},{10,... | collective-permute-start | bytes 196616 | tf_op jit(solution)/shard_map/ppermute | solution.py:302
  39.1 4.8 %collective-permute-start.25 = (bf16[128,256]{1,0:T(8,128)(2,1)S(1)}, bf16[128,256]{1,0:T(8,128)(2,1)S(1)}, u32[]{:S(2)}, u32[]{:S(2)}) collective-permute-start(bf16[128,256]{1,0:T(8,128)(2,1)S(1)} %turn.25.value_ref), channel_id=1, source_target_pairs={{0,4},{1,5},{2,6},{3,7},{4,0},{5,1},{6,2},{7,3},{8,12},{9,13},{10,... | collective-permute-start | bytes 196616 | tf_op jit(solution)/shard_map/ppermute | solution.py:302
  41.7 4.5 %collective-permute-start.29 = (bf16[128,256]{1,0:T(8,128)(2,1)S(1)}, bf16[128,256]{1,0:T(8,128)(2,1)S(1)}, u32[]{:S(2)}, u32[]{:S(2)}) collective-permute-start(bf16[128,256]{1,0:T(8,128)(2,1)S(1)} %turn.29.value_ref), channel_id=1, source_target_pairs={{0,1},{1,0},{2,3},{3,2},{4,5},{5,4},{6,7},{7,6},{8,9},{9,8},{10,11... | collective-permute-start | bytes 196616 | tf_op jit(solution)/shard_map/ppermute | solution.py:302
  41.8 10.7 %slice-start = ((s8[16777216]{0:T(1024)(128)(4,1)}), s8[4194304]{0:T(1024)(128)(4,1)S(1)}, s32[]{:S(2)}) async-start(s8[16777216]{0:T(1024)(128)(4,1)} %bitcast.2), calls=%async_computation | async-start | bytes 8388608
  41.8 10.7 %copy-start.3 = (f32[1024]{0:T(1024)S(1)}, f32[1024]{0:T(1024)}, u32[]{:S(2)}) copy-start(f32[1024]{0:T(1024)} %param.11) | copy-start | bytes 12292
  41.8 6.0 %collective-permute-start.17 = (bf16[128,256]{1,0:T(8,128)(2,1)S(1)}, bf16[128,256]{1,0:T(8,128)(2,1)S(1)}, u32[]{:S(2)}, u32[]{:S(2)}) collective-permute-start(bf16[128,256]{1,0:T(8,128)(2,1)S(1)} %turn.17.value_ref), channel_id=1, source_target_pairs={{0,2},{1,3},{2,0},{3,1},{4,6},{5,7},{6,4},{7,5},{8,10},{9,11},{10,... | collective-permute-start | bytes 196616 | tf_op jit(solution)/shard_map/ppermute | solution.py:302
  43.1 7.7 %collective-permute-start.21 = (bf16[128,256]{1,0:T(8,128)(2,1)S(1)}, bf16[128,256]{1,0:T(8,128)(2,1)S(1)}, u32[]{:S(2)}, u32[]{:S(2)}) collective-permute-start(bf16[128,256]{1,0:T(8,128)(2,1)S(1)} %turn.21.value_ref), channel_id=1, source_target_pairs={{0,8},{1,9},{2,10},{3,11},{4,12},{5,13},{6,14},{7,15},{8,0},{9,1},... | collective-permute-start | bytes 196616 | tf_op jit(solution)/shard_map/ppermute | solution.py:302
  44.0 8.5 %slice-start.1 = ((s8[16777216]{0:T(1024)(128)(4,1)}), s8[4194304]{0:T(1024)(128)(4,1)S(1)}, s32[]{:S(2)}) async-start(s8[16777216]{0:T(1024)(128)(4,1)} %bitcast.2), calls=%async_computation.1 | async-start | bytes 8388608
  44.0 7.7 %collective-permute-start.26 = (bf16[128,256]{1,0:T(8,128)(2,1)S(1)}, bf16[128,256]{1,0:T(8,128)(2,1)S(1)}, u32[]{:S(2)}, u32[]{:S(2)}) collective-permute-start(bf16[128,256]{1,0:T(8,128)(2,1)S(1)} %turn.26.value_ref), channel_id=1, source_target_pairs={{0,8},{1,9},{2,10},{3,11},{4,12},{5,13},{6,14},{7,15},{8,0},{9,1},... | collective-permute-start | bytes 196616 | tf_op jit(solution)/shard_map/ppermute | solution.py:302
  46.2 5.5 %collective-permute-start.30 = (bf16[128,256]{1,0:T(8,128)(2,1)S(1)}, bf16[128,256]{1,0:T(8,128)(2,1)S(1)}, u32[]{:S(2)}, u32[]{:S(2)}) collective-permute-start(bf16[128,256]{1,0:T(8,128)(2,1)S(1)} %turn.30.value_ref), channel_id=1, source_target_pairs={{0,2},{1,3},{2,0},{3,1},{4,6},{5,7},{6,4},{7,5},{8,10},{9,11},{10,... | collective-permute-start | bytes 196616 | tf_op jit(solution)/shard_map/ppermute | solution.py:302
  47.9 4.6 %slice-start.2 = ((s8[16777216]{0:T(1024)(128)(4,1)}), s8[4194304]{0:T(1024)(128)(4,1)S(1)}, s32[]{:S(2)}) async-start(s8[16777216]{0:T(1024)(128)(4,1)} %bitcast.2), calls=%async_computation.2 | async-start | bytes 8388608
  47.9 4.5 %collective-permute-start.18 = (bf16[128,256]{1,0:T(8,128)(2,1)S(1)}, bf16[128,256]{1,0:T(8,128)(2,1)S(1)}, u32[]{:S(2)}, u32[]{:S(2)}) collective-permute-start(bf16[128,256]{1,0:T(8,128)(2,1)S(1)} %turn.18.value_ref), channel_id=1, source_target_pairs={{0,4},{1,5},{2,6},{3,7},{4,0},{5,1},{6,2},{7,3},{8,12},{9,13},{10,... | collective-permute-start | bytes 196616 | tf_op jit(solution)/shard_map/ppermute | solution.py:302
  50.8 1.6 %collective-permute-start.22 = (bf16[128,256]{1,0:T(8,128)(2,1)S(1)}, bf16[128,256]{1,0:T(8,128)(2,1)S(1)}, u32[]{:S(2)}, u32[]{:S(2)}) collective-permute-start(bf16[128,256]{1,0:T(8,128)(2,1)S(1)} %turn.22.value_ref), channel_id=1, source_target_pairs={{0,1},{1,0},{2,3},{3,2},{4,5},{5,4},{6,7},{7,6},{8,9},{9,8},{10,11... | collective-permute-start | bytes 196616 | tf_op jit(solution)/shard_map/ppermute | solution.py:302
  51.7 2.2 %slice-start.3 = ((s8[16777216]{0:T(1024)(128)(4,1)}), s8[4194304]{0:T(1024)(128)(4,1)S(1)}, s32[]{:S(2)}) async-start(s8[16777216]{0:T(1024)(128)(4,1)} %bitcast.2), calls=%async_computation.3 | async-start | bytes 8388608
  55.4 23.9 %copy-start.2 = (bf16[8,8192]{1,0:T(8,128)(2,1)S(1)}, bf16[8,8192]{1,0:T(8,128)(2,1)}, u32[]{:S(2)}) copy-start(bf16[8,8192]{1,0:T(8,128)(2,1)} %tokens_ref.1) | copy-start | bytes 393220
  55.4 1.8 %collective-permute-start.31 = (bf16[48,4096]{1,0:T(8,128)(2,1)S(1)}, bf16[48,4096]{1,0:T(8,128)(2,1)S(1)}, u32[]{:S(2)}, u32[]{:S(2)}) collective-permute-start(bf16[48,4096]{1,0:T(8,128)(2,1)S(1)} %get-tuple-element.24), channel_id=1, source_target_pairs={{0,1},{1,0},{2,3},{3,2},{4,5},{5,4},{6,7},{7,6},{8,9},{9,8},{10,11... | collective-permute-start | bytes 1179656 | tf_op jit(solution)/shard_map/ppermute | solution.py:302
  57.2 9.6 %collective-permute-start.32 = (bf16[80,4096]{1,0:T(8,128)(2,1)S(1)}, bf16[80,4096]{1,0:T(8,128)(2,1)S(1)}, u32[]{:S(2)}, u32[]{:S(2)}) collective-permute-start(bf16[80,4096]{1,0:T(8,128)(2,1)S(1)} %get-tuple-element.25), channel_id=1, source_target_pairs={{0,1},{1,0},{2,3},{3,2},{4,5},{5,4},{6,7},{7,6},{8,9},{9,8},{10,11... | collective-permute-start | bytes 1966088 | tf_op jit(solution)/shard_map/ppermute | solution.py:302
  57.5 5.6 %collective-permute-start.33 = (bf16[16,4096]{1,0:T(8,128)(2,1)S(1)}, bf16[16,4096]{1,0:T(8,128)(2,1)S(1)}, u32[]{:S(2)}, u32[]{:S(2)}) collective-permute-start(bf16[16,4096]{1,0:T(8,128)(2,1)S(1)} %sum.3), channel_id=1, source_target_pairs={{0,4},{1,5},{4,8},{5,9},{8,12},{9,13},{12,14},{13,15},{14,10},{15,... | collective-permute-start | bytes 393224 | tf_op jit(solution)/shard_map/ppermute | solution.py:293
  57.7 9.1 %collective-permute-start.34 = (bf16[16,4096]{1,0:T(8,128)(2,1)S(1)}, bf16[16,4096]{1,0:T(8,128)(2,1)S(1)}, u32[]{:S(2)}, u32[]{:S(2)}) collective-permute-start(bf16[16,4096]{1,0:T(8,128)(2,1)S(1)} %sum.4), channel_id=1, source_target_pairs={{0,8},{1,7},{4,12},{5,3},{8,14},{9,1},{12,10},{13,5},{14,6},{15,9}... | collective-permute-start | bytes 393224 | tf_op jit(solution)/shard_map/ppermute | solution.py:293
  60.6 6.5 %collective-permute-start.37 = (bf16[16,4096]{1,0:T(8,128)(2,1)S(1)}, bf16[16,4096]{1,0:T(8,128)(2,1)S(1)}, u32[]{:S(2)}, u32[]{:S(2)}) collective-permute-start(bf16[16,4096]{1,0:T(8,128)(2,1)S(1)} %sum.5), channel_id=1, source_target_pairs={{0,2},{1,3},{4,0},{5,1},{8,4},{9,5},{12,8},{13,9},{14,12},{15,13},... | collective-permute-start | bytes 393224 | tf_op jit(solution)/shard_map/ppermute | solution.py:293
  66.8 5.8 %collective-permute-start.35 = (bf16[16,4096]{1,0:T(8,128)(2,1)S(1)}, bf16[16,4096]{1,0:T(8,128)(2,1)S(1)}, u32[]{:S(2)}, u32[]{:S(2)}) collective-permute-start(bf16[16,4096]{1,0:T(8,128)(2,1)S(1)} %relay.4), channel_id=1, source_target_pairs={{0,4},{1,5},{4,8},{5,9},{8,12},{9,13},{12,14},{13,15},{14,10},{15,... | collective-permute-start | bytes 393224 | tf_op jit(solution)/shard_map/ppermute | solution.py:293
  67.1 5.7 %collective-permute-start.38 = (bf16[16,4096]{1,0:T(8,128)(2,1)S(1)}, bf16[16,4096]{1,0:T(8,128)(2,1)S(1)}, u32[]{:S(2)}, u32[]{:S(2)}) collective-permute-start(bf16[16,4096]{1,0:T(8,128)(2,1)S(1)} %relay.6), channel_id=1, source_target_pairs={{0,2},{1,3},{4,0},{5,1},{8,4},{9,5},{12,8},{13,9},{14,12},{15,13},... | collective-permute-start | bytes 393224 | tf_op jit(solution)/shard_map/ppermute | solution.py:293
  72.8 5.0 %collective-permute-start.36 = (bf16[16,4096]{1,0:T(8,128)(2,1)S(1)}, bf16[16,4096]{1,0:T(8,128)(2,1)S(1)}, u32[]{:S(2)}, u32[]{:S(2)}) collective-permute-start(bf16[16,4096]{1,0:T(8,128)(2,1)S(1)} %relay.5), channel_id=1, source_target_pairs={{0,4},{1,5},{4,8},{5,9},{8,12},{9,13},{12,14},{13,15},{14,10},{15,... | collective-permute-start | bytes 393224 | tf_op jit(solution)/shard_map/ppermute | solution.py:293
  72.9 5.0 %collective-permute-start.39 = (bf16[16,4096]{1,0:T(8,128)(2,1)S(1)}, bf16[16,4096]{1,0:T(8,128)(2,1)S(1)}, u32[]{:S(2)}, u32[]{:S(2)}) collective-permute-start(bf16[16,4096]{1,0:T(8,128)(2,1)S(1)} %relay.7), channel_id=1, source_target_pairs={{0,2},{1,3},{4,0},{5,1},{8,4},{9,5},{12,8},{13,9},{14,12},{15,13},... | collective-permute-start | bytes 393224 | tf_op jit(solution)/shard_map/ppermute | solution.py:293
  78.0 1.3 %collective-permute-start.40 = (bf16[8,4096]{1,0:T(8,128)(2,1)S(1)}, bf16[8,4096]{1,0:T(8,128)(2,1)S(1)}, u32[]{:S(2)}, u32[]{:S(2)}) collective-permute-start(bf16[8,4096]{1,0:T(8,128)(2,1)S(1)} %get-tuple-element.28), channel_id=1, source_target_pairs={{0,1},{1,0},{2,3},{3,2},{4,5},{5,4},{6,7},{7,6},{8,9},{9,8},{10,11... | collective-permute-start | bytes 196616 | tf_op jit(solution)/shard_map/ppermute | solution.py:302

commit v10 on v9

--- a/solution.py
+++ b/solution.py
@@ -10,7 +10,7 @@
 BLOCK = 256
 MIB = 1 << 20
 OFFSETS = (3, 1, 0, 2)
-TURN = 1_000_000_000
+TURN = 700_000_000
 COST = 20_000_000_000
 
 
@@ -225,34 +225,38 @@
     )(first, second)
 
 
-def chunk(away, chips, own_ref, arrived_ref):
+def chunk(away, chips, own_ref, arrived_ref, lanes):
     spot = ring_order(chips).index(away % chips)
     if spot < EARLY:
         rows = own_ref.shape[0] // EARLY
     else:
         rows, spot = own_ref.shape[0] // (chips - EARLY), spot - EARLY
     at = slice(spot * rows, (spot + 1) * rows)
-    return own_ref[at, :].astype(jnp.float32) + arrived_ref[at, :].astype(jnp.float32)
-
-
-def sum_kernel(away, chips, own_ref, arrived_ref, out_ref):
-    out_ref[...] = chunk(away, chips, own_ref, arrived_ref).astype(jnp.bfloat16)
-
-
-def relay_kernel(away, chips, core, own_ref, arrived_ref, *refs):
+    return own_ref[at, lanes].astype(jnp.float32) + arrived_ref[at, lanes].astype(jnp.float32)
+
+
+def sum_kernel(away, chips, lanes, own_ref, arrived_ref, out_ref):
+    out_ref[...] = chunk(away, chips, own_ref, arrived_ref, lanes).astype(jnp.bfloat16)
+
+
+def relay_kernel(away, chips, lanes, core, own_ref, arrived_ref, *refs):
     out_ref = refs[-1]
-    value = chunk(away, chips, own_ref, arrived_ref) + refs[0][...].astype(jnp.float32)
+    value = chunk(away, chips, own_ref, arrived_ref, lanes) + refs[0][...].astype(jnp.float32)
     if len(refs) == 3:
         value = value + jnp.where(lax.axis_index("hid") % 2 == core, refs[1][...].astype(jnp.float32), 0.0)
     out_ref[...] = value.astype(jnp.bfloat16)
 
 
-def last_kernel(chips, ahead_in, behind_in, own_ref, arrived_ref, keep_ref, give_ref, sum_ref):
+def last_kernel(chips, parts, own_ref, arrived_ref, *refs):
+    sums, (keep_ref, give_ref, sum_ref) = refs[:-3], refs[-3:]
     part = keep_ref.shape[0]
     core = lax.axis_index("hid") % 2
-    sum_ref[...] = (
-        chunk(0, chips, own_ref, arrived_ref) + ahead_in[...].astype(jnp.float32) + behind_in[...].astype(jnp.float32)
-    )
+    for at, lanes in enumerate(parts):
+        sum_ref[:, lanes] = (
+            chunk(0, chips, own_ref, arrived_ref, lanes)
+            + sums[2 * at][...].astype(jnp.float32)
+            + sums[2 * at + 1][...].astype(jnp.float32)
+        )
     keep_ref[...] = sum_ref[pl.ds(pl.multiple_of(core * part, part), part), :]
     give_ref[...] = sum_ref[pl.ds(pl.multiple_of((1 - core) * part, part), part), :].astype(jnp.bfloat16)
 
@@ -336,28 +340,32 @@
     own_early, own = down_project(slices, limits, down_weight, False, chips, total)
     arrived = cross(once(theirs, own, arrived_early))
     rows, wide = own_early.shape[0] // EARLY, own_early.shape[1]
-    part = jax.ShapeDtypeStruct((rows, wide), jnp.bfloat16)
-
-    first = [
-        small(functools.partial(sum_kernel, away, chips), part, (own_early, arrived_early), "sum")
-        for away in (steps - 1, 1 - steps, steps)
-    ]
-    ahead, behind, far = right(first[0]), left(first[1]), hop(first[2], 2, -2)
+    part = jax.ShapeDtypeStruct((rows, wide // 2), jnp.bfloat16)
+    parts = [slice(at * wide // 2, (at + 1) * wide // 2) for at in range(2)]
+
+    sums = []
+    for lanes in parts:
+        first = [
+            small(functools.partial(sum_kernel, away, chips, lanes), part, (own_early, arrived_early), "sum")
+            for away in (steps - 1, 1 - steps, steps)
+        ]
+        sums.append([right(first[0]), left(first[1]), hop(first[2], 2, -2)])
     for away in range(steps - 2, 0, -1):
-        more = (far,) if away == steps - 2 else ()
-        ahead = small(
-            functools.partial(relay_kernel, away, chips, 0), part, (own, arrived, ahead, *more), "relay"
-        )
-        behind = small(
-            functools.partial(relay_kernel, -away, chips, 1), part, (own, arrived, behind, *more), "relay"
-        )
-        ahead, behind = right(ahead), left(behind)
+        for at, lanes in enumerate(parts):
+            ahead, behind, *more = sums[at]
+            ahead = small(
+                functools.partial(relay_kernel, away, chips, lanes, 0), part, (own, arrived, ahead, *more), "relay"
+            )
+            behind = small(
+                functools.partial(relay_kernel, -away, chips, lanes, 1), part, (own, arrived, behind, *more), "relay"
+            )
+            sums[at] = [right(ahead), left(behind)]
     half = jax.ShapeDtypeStruct((rows // 2, wide), jnp.bfloat16)
     kept = jax.ShapeDtypeStruct((rows // 2, wide), jnp.float32)
     keep, give = small(
-        functools.partial(last_kernel, chips),
+        functools.partial(last_kernel, chips, parts),
         (kept, half),
-        (ahead, behind, own, arrived),
+        (own, arrived, *sums[0], *sums[1]),
         "last",
         [pltpu.VMEM((rows, wide), jnp.float32)],
     )

time: 80.2 us -> 79 us (0.985)
  waiting for transfers between devices: 32.9 us -> 24.1 us
  starting transfers between devices: 34 us -> 42.6 us
  local copies, waits for them, and re-layouts: 1.47 us -> 0.5 us
    ppermute x14 -> x21, waiting for transfers between devices: 22.6 us -> 13.9 us  [hop(): return lax.ppermute(value, 'hid', pairs)]
    ppermute x14 -> x21, starting transfers between devices: 17.1 us -> 25.7 us  [hop(): return lax.ppermute(value, 'hid', pairs)]
    unnamed x16, local copies, waits for them, and re-layouts: 1.47 us -> 0.5 us
  transfers between devices with their start and end apart: 41 -> 48, of which waited for: 22 -> 21; matrix products, arithmetic and copies ran while one was open for 0% -> 0% of each run, Pallas kernels for 3% -> 3%
where the time goes in v10:
time: 79 us; the launch traced here: 78.9 us
  starting transfers between devices  42.6 us (54%)
  waiting for transfers between devices  24.1 us (31%)
  Pallas kernels  11.3 us (14%)
    ppermute x21, starting transfers between devices, hop(): return lax.ppermute(value, 'hid', pairs)  25.7 us
    ppermute x27, starting transfers between devices, cross(): return lax.ppermute(value, 'hid', [(d, d ^ mask) for d in range(count)])  16.9 us
    ppermute x21, waiting for transfers between devices, hop(): return lax.ppermute(value, 'hid', pairs)  13.9 us
    ppermute x27, waiting for transfers between devices, cross(): return lax.ppermute(value, 'hid', [(d, d ^ mask) for d in range(count)])  10.2 us
    pallas_call x2, Pallas kernels, up_project(): pl.pallas_call(functools.partial(up_kernel, shifts, first, slice(at * wid...  5.54 us
    pallas_call x2, Pallas kernels, down_project(): pl.pallas_call(functools.partial(down_kernel, width // BLOCK, chips, tota...  2.89 us
  transfers between devices with their start and end apart: 48, of which 21 were waited for; matrix products, arithmetic and copies ran while one was open for 0% of the time, Pallas kernels for 3%

profile of v10, /device:TPU:0, one launch (start us, length us, event | category | flops | bytes accessed | tf_op | source)
XLA Modules:
  0.0 78.9 jit_solution(8524028897400473952)
XLA Ops:
  0.0 1.3 %normalize.1.refs_0_ = bf16[8,8192]{1,0:T(8,128)(2,1)S(1)} custom-call(bf16[8,8192]{1,0:T(8,128)(2,1)} %tokens_ref.1, f32[1,8192]{1,0:T(1,128)} %bitcast.6), custom_call_target="tpu_custom_call" | custom-call | flops 20000000000 | bytes 262144 | tf_op jit(solution)/shard_map/normalize/pallas_call | solution.py:48
  1.3 3.0 %collective-permute-start.3 = (bf16[8,8192]{1,0:T(8,128)(2,1)S(1)}, bf16[8,8192]{1,0:T(8,128)(2,1)S(1)}, u32[]{:S(2)}, u32[]{:S(2)}) collective-permute-start(bf16[8,8192]{1,0:T(8,128)(2,1)S(1)} %normalize.1.refs_0_), channel_id=1, source_target_pairs={{0,2},{1,3},{4,0},{5,1},{8,4},{9,5},{12,8},{13,9},{14,12},{15,13},... | collective-permute-start | bytes 393224 | tf_op jit(solution)/shard_map/ppermute | solution.py:297
  4.3 0.1 collective-permute-start.1
  4.4 3.4 %collective-permute-done.3.refs_4_ = bf16[8,8192]{1,0:T(8,128)(2,1)S(1)} collective-permute-done((bf16[8,8192]{1,0:T(8,128)(2,1)S(1)}, bf16[8,8192]{1,0:T(8,128)(2,1)S(1)}, u32[]{:S(2)}, u32[]{:S(2)}) %collective-permute-start.3) | collective-permute-done | bytes 131104 | tf_op jit(solution)/shard_map/ppermute | solution.py:297
  7.8 1.7 %collective-permute-start.7 = (bf16[8,8192]{1,0:T(8,128)(2,1)S(1)}, bf16[8,8192]{1,0:T(8,128)(2,1)S(1)}, u32[]{:S(2)}, u32[]{:S(2)}) collective-permute-start(bf16[8,8192]{1,0:T(8,128)(2,1)S(1)} %collective-permute-done.3.refs_4_), channel_id=1, source_target_pairs={{0,2},{1,3},{4,0},{5,1},{8,4},{9,5},{12,8},{13,9},{14,12},{15,13},... | collective-permute-start | bytes 393224 | tf_op jit(solution)/shard_map/ppermute | solution.py:297
  9.5 0.3 collective-permute-start.5
  9.9 0.5 collective-permute-start.4
  10.4 2.4 %collective-permute-done.7.odd_ref.refs_8_ = bf16[8,8192]{1,0:T(8,128)(2,1)S(1)} collective-permute-done((bf16[8,8192]{1,0:T(8,128)(2,1)S(1)}, bf16[8,8192]{1,0:T(8,128)(2,1)S(1)}, u32[]{:S(2)}, u32[]{:S(2)}) %collective-permute-start.7) | collective-permute-done | bytes 131104 | tf_op jit(solution)/shard_map/ppermute | solution.py:297
  12.8 1.7 %collective-permute-start.11 = (bf16[8,8192]{1,0:T(8,128)(2,1)S(1)}, bf16[8,8192]{1,0:T(8,128)(2,1)S(1)}, u32[]{:S(2)}, u32[]{:S(2)}) collective-permute-start(bf16[8,8192]{1,0:T(8,128)(2,1)S(1)} %collective-permute-done.7.odd_ref.refs_8_), channel_id=1, source_target_pairs={{0,2},{1,3},{4,0},{5,1},{8,4},{9,5},{12,8},{13,9},{14,12},{15,13},... | collective-permute-start | bytes 393224 | tf_op jit(solution)/shard_map/ppermute | solution.py:297
  14.5 1.6 %collective-permute-start.13 = (bf16[8,8192]{1,0:T(8,128)(2,1)S(1)}, bf16[8,8192]{1,0:T(8,128)(2,1)S(1)}, u32[]{:S(2)}, u32[]{:S(2)}) collective-permute-start(bf16[8,8192]{1,0:T(8,128)(2,1)S(1)} %pick.1), channel_id=1, source_target_pairs={{0,8},{1,7},{4,12},{5,3},{8,14},{9,1},{12,10},{13,5},{14,6},{15,9}... | collective-permute-start | bytes 393224 | tf_op jit(solution)/shard_map/ppermute | solution.py:297
  16.1 1.6 %collective-permute-start.9 = (bf16[8,8192]{1,0:T(8,128)(2,1)S(1)}, bf16[8,8192]{1,0:T(8,128)(2,1)S(1)}, u32[]{:S(2)}, u32[]{:S(2)}) collective-permute-start(bf16[8,8192]{1,0:T(8,128)(2,1)S(1)} %collective-permute-done.5.even_ref.refs_6_), channel_id=1, source_target_pairs={{0,4},{1,5},{4,8},{5,9},{8,12},{9,13},{12,14},{13,15},{14,10},{15,... | collective-permute-start | bytes 393224 | tf_op jit(solution)/shard_map/ppermute | solution.py:297
  17.7 0.5 collective-permute-start.6
  18.2 2.0 %collective-permute-done.11.refs_12_ = bf16[8,8192]{1,0:T(8,128)(2,1)S(1)} collective-permute-done((bf16[8,8192]{1,0:T(8,128)(2,1)S(1)}, bf16[8,8192]{1,0:T(8,128)(2,1)S(1)}, u32[]{:S(2)}, u32[]{:S(2)}) %collective-permute-start.11) | collective-permute-done | bytes 131104 | tf_op jit(solution)/shard_map/ppermute | solution.py:297
  20.2 1.7 %collective-permute-done.13.refs_14_ = bf16[8,8192]{1,0:T(8,128)(2,1)S(1)} collective-permute-done((bf16[8,8192]{1,0:T(8,128)(2,1)S(1)}, bf16[8,8192]{1,0:T(8,128)(2,1)S(1)}, u32[]{:S(2)}, u32[]{:S(2)}) %collective-permute-start.13) | collective-permute-done | bytes 131104 | tf_op jit(solution)/shard_map/ppermute | solution.py:297
  21.9 0.2 collective-permute-done.9.refs_10_
  22.1 0.3 collective-permute-start.10
  22.4 0.8 %collective-permute-done.14.refs_15_ = bf16[8,8192]{1,0:T(8,128)(2,1)S(1)} collective-permute-done((bf16[8,8192]{1,0:T(8,128)(2,1)S(1)}, bf16[8,8192]{1,0:T(8,128)(2,1)S(1)}, u32[]{:S(2)}, u32[]{:S(2)}) %collective-permute-start.14) | collective-permute-done | bytes 131104 | tf_op jit(solution)/shard_map/ppermute | solution.py:306
  23.3 0.2 collective-permute-done.10.refs_11_
  23.5 2.8 %up_project.2 = (bf16[128,256]{1,0:T(8,128)(2,1)S(1)}, bf16[128,256]{1,0:T(8,128)(2,1)S(1)}, bf16[128,8192]{1,0:T(8,128)(2,1)S(1)}) custom-call(bf16[8,8192]{1,0:T(8,128)(2,1)S(1)} %normalize.1.refs_0_, bf16[8,8192]{1,0:T(8,128)(2,1)S(1)} %collective-permute-done.refs_1_, bf16[8,8192]{1,0:T(8,128)(2,1)S(1)} %collective-permute-done.1.refs_2_, ...), custom_call_target="tpu_custom_call" | custom-call | flops 2147483648 | tf_op jit(solution)/shard_map/up_project/pallas_call | solution.py:126
  26.3 2.8 %up_project.3 = (bf16[128,256]{1,0:T(8,128)(2,1)S(1)}, bf16[128,256]{1,0:T(8,128)(2,1)S(1)}) custom-call(bf16[128,8192]{1,0:T(8,128)(2,1)S(1)} %get-tuple-element.19.refs_0_, bf16[8192,1024]{1,0:T(8,128)(2,1)S(1)} %copy-done, bf16[8192,1024]{1,0:T(8,128)(2,1)S(1)} %copy-done.1), custom_call_target="tpu_custom_call" | custom-call | flops 2147483648 | tf_op jit(solution)/shard_map/up_project/pallas_call | solution.py:126
  29.0 0.4 collective-permute-start.23
  29.4 0.9 %collective-permute-start.27 = (bf16[128,256]{1,0:T(8,128)(2,1)S(1)}, bf16[128,256]{1,0:T(8,128)(2,1)S(1)}, u32[]{:S(2)}, u32[]{:S(2)}) collective-permute-start(bf16[128,256]{1,0:T(8,128)(2,1)S(1)} %get-tuple-element.21.value_ref), channel_id=1, source_target_pairs={{0,4},{1,5},{2,6},{3,7},{4,0},{5,1},{6,2},{7,3},{8,12},{9,13},{10,... | collective-permute-start | bytes 196616 | tf_op jit(solution)/shard_map/ppermute | solution.py:306
  30.3 3.2 %collective-permute-start.15 = (bf16[128,256]{1,0:T(8,128)(2,1)S(1)}, bf16[128,256]{1,0:T(8,128)(2,1)S(1)}, u32[]{:S(2)}, u32[]{:S(2)}) collective-permute-start(bf16[128,256]{1,0:T(8,128)(2,1)S(1)} %get-tuple-element.17.value_ref), channel_id=1, source_target_pairs={{0,8},{1,9},{2,10},{3,11},{4,12},{5,13},{6,14},{7,15},{8,0},{9,1},... | collective-permute-start | bytes 196616 | tf_op jit(solution)/shard_map/ppermute | solution.py:306
  33.6 0.5 collective-permute-start.19
  34.1 1.6 %collective-permute-start.24 = (bf16[128,256]{1,0:T(8,128)(2,1)S(1)}, bf16[128,256]{1,0:T(8,128)(2,1)S(1)}, u32[]{:S(2)}, u32[]{:S(2)}) collective-permute-start(bf16[128,256]{1,0:T(8,128)(2,1)S(1)} %turn.24.value_ref), channel_id=1, source_target_pairs={{0,2},{1,3},{2,0},{3,1},{4,6},{5,7},{6,4},{7,5},{8,10},{9,11},{10,... | collective-permute-start | bytes 196616 | tf_op jit(solution)/shard_map/ppermute | solution.py:306
  35.7 1.3 %collective-permute-start.28 = (bf16[128,256]{1,0:T(8,128)(2,1)S(1)}, bf16[128,256]{1,0:T(8,128)(2,1)S(1)}, u32[]{:S(2)}, u32[]{:S(2)}) collective-permute-start(bf16[128,256]{1,0:T(8,128)(2,1)S(1)} %turn.28.value_ref), channel_id=1, source_target_pairs={{0,8},{1,9},{2,10},{3,11},{4,12},{5,13},{6,14},{7,15},{8,0},{9,1},... | collective-permute-start | bytes 196616 | tf_op jit(solution)/shard_map/ppermute | solution.py:306
  37.1 0.9 %collective-permute-done.19.other_ref = bf16[128,256]{1,0:T(8,128)(2,1)S(1)} collective-permute-done((bf16[128,256]{1,0:T(8,128)(2,1)S(1)}, bf16[128,256]{1,0:T(8,128)(2,1)S(1)}, u32[]{:S(2)}, u32[]{:S(2)}) %collective-permute-start.19) | collective-permute-done | bytes 65568 | tf_op jit(solution)/shard_map/ppermute | solution.py:306
  38.1 1.1 %collective-permute-start.20 = (bf16[128,256]{1,0:T(8,128)(2,1)S(1)}, bf16[128,256]{1,0:T(8,128)(2,1)S(1)}, u32[]{:S(2)}, u32[]{:S(2)}) collective-permute-start(bf16[128,256]{1,0:T(8,128)(2,1)S(1)} %turn.20.value_ref), channel_id=1, source_target_pairs={{0,4},{1,5},{2,6},{3,7},{4,0},{5,1},{6,2},{7,3},{8,12},{9,13},{10,... | collective-permute-start | bytes 196616 | tf_op jit(solution)/shard_map/ppermute | solution.py:306
  39.2 1.1 %collective-permute-start.25 = (bf16[128,256]{1,0:T(8,128)(2,1)S(1)}, bf16[128,256]{1,0:T(8,128)(2,1)S(1)}, u32[]{:S(2)}, u32[]{:S(2)}) collective-permute-start(bf16[128,256]{1,0:T(8,128)(2,1)S(1)} %turn.25.value_ref), channel_id=1, source_target_pairs={{0,4},{1,5},{2,6},{3,7},{4,0},{5,1},{6,2},{7,3},{8,12},{9,13},{10,... | collective-permute-start | bytes 196616 | tf_op jit(solution)/shard_map/ppermute | solution.py:306
  40.3 1.4 %collective-permute-done.28.other_ref = bf16[128,256]{1,0:T(8,128)(2,1)S(1)} collective-permute-done((bf16[128,256]{1,0:T(8,128)(2,1)S(1)}, bf16[128,256]{1,0:T(8,128)(2,1)S(1)}, u32[]{:S(2)}, u32[]{:S(2)}) %collective-permute-start.28) | collective-permute-done | bytes 65568 | tf_op jit(solution)/shard_map/ppermute | solution.py:306
  41.8 0.3 collective-permute-start.17
  42.1 1.0 %collective-permute-done.20.other_ref = bf16[128,256]{1,0:T(8,128)(2,1)S(1)} collective-permute-done((bf16[128,256]{1,0:T(8,128)(2,1)S(1)}, bf16[128,256]{1,0:T(8,128)(2,1)S(1)}, u32[]{:S(2)}, u32[]{:S(2)}) %collective-permute-start.20) | collective-permute-done | bytes 65568 | tf_op jit(solution)/shard_map/ppermute | solution.py:306
  43.1 0.6 collective-permute-start.21
  43.7 0.3 collective-permute-done.25.other_ref
  44.0 2.2 %collective-permute-start.26 = (bf16[128,256]{1,0:T(8,128)(2,1)S(1)}, bf16[128,256]{1,0:T(8,128)(2,1)S(1)}, u32[]{:S(2)}, u32[]{:S(2)}) collective-permute-start(bf16[128,256]{1,0:T(8,128)(2,1)S(1)} %turn.26.value_ref), channel_id=1, source_target_pairs={{0,8},{1,9},{2,10},{3,11},{4,12},{5,13},{6,14},{7,15},{8,0},{9,1},... | collective-permute-start | bytes 196616 | tf_op jit(solution)/shard_map/ppermute | solution.py:306
  46.2 1.6 %collective-permute-start.30 = (bf16[128,256]{1,0:T(8,128)(2,1)S(1)}, bf16[128,256]{1,0:T(8,128)(2,1)S(1)}, u32[]{:S(2)}, u32[]{:S(2)}) collective-permute-start(bf16[128,256]{1,0:T(8,128)(2,1)S(1)} %turn.30.value_ref), channel_id=1, source_target_pairs={{0,2},{1,3},{2,0},{3,1},{4,6},{5,7},{6,4},{7,5},{8,10},{9,11},{10,... | collective-permute-start | bytes 196616 | tf_op jit(solution)/shard_map/ppermute | solution.py:306
  47.9 0.1 collective-permute-start.18
  48.0 2.7 %collective-permute-done.21.other_ref = bf16[128,256]{1,0:T(8,128)(2,1)S(1)} collective-permute-done((bf16[128,256]{1,0:T(8,128)(2,1)S(1)}, bf16[128,256]{1,0:T(8,128)(2,1)S(1)}, u32[]{:S(2)}, u32[]{:S(2)}) %collective-permute-start.21) | collective-permute-done | bytes 65568 | tf_op jit(solution)/shard_map/ppermute | solution.py:306
  50.8 0.8 %collective-permute-done.26.other_ref = bf16[128,256]{1,0:T(8,128)(2,1)S(1)} collective-permute-done((bf16[128,256]{1,0:T(8,128)(2,1)S(1)}, bf16[128,256]{1,0:T(8,128)(2,1)S(1)}, u32[]{:S(2)}, u32[]{:S(2)}) %collective-permute-start.26) | collective-permute-done | bytes 65568 | tf_op jit(solution)/shard_map/ppermute | solution.py:306
  51.7 0.6 collective-permute-done.18.other_ref
  52.5 0.4 slice-done.3
  52.9 1.4 %down_project.3 = (bf16[48,4096]{1,0:T(8,128)(2,1)S(1)}, bf16[80,4096]{1,0:T(8,128)(2,1)S(1)}) custom-call(f32[1,1024]{1,0:T(1,128)S(1)} %bitcast.4, bf16[1024,8192]{1,0:T(8,128)(2,1)S(1)} %bitcast.3, bf16[128,256]{1,0:T(8,128)(2,1)S(1)} %turn.19.refs_0_, bf16[128,256]{1,0:T(8,128)(2,1)S(1)} %turn.23.refs_1_, bf16[128,256]{1,0:T(8,128)(2,1)S(1)} %turn.27.refs_2_, ...), custom_call_target="tpu_custom_call" | custom-call | flops 1073741824 | tf_op jit(solution)/shard_map/down_project/pallas_call | solution.py:186
  54.5 1.4 %down_project.2 = (bf16[48,4096]{1,0:T(8,128)(2,1)S(1)}, bf16[80,4096]{1,0:T(8,128)(2,1)S(1)}) custom-call(f32[1,1024]{1,0:T(1,128)S(1)} %bitcast.5, bf16[1024,8192]{1,0:T(8,128)(2,1)S(1)} %bitcast.3, bf16[128,256]{1,0:T(8,128)(2,1)S(1)} %turn.19.refs_0_, bf16[128,256]{1,0:T(8,128)(2,1)S(1)} %turn.23.refs_1_, bf16[128,256]{1,0:T(8,128)(2,1)S(1)} %turn.27.refs_2_, ...), custom_call_target="tpu_custom_call" | custom-call | flops 1073741824 | tf_op jit(solution)/shard_map/down_project/pallas_call | solution.py:186
  55.9 0.3 collective-permute-done.31.arrived_ref
  56.2 0.3 collective-permute-start.32
  56.6 2.5 %collective-permute-start.34 = (bf16[16,2048]{1,0:T(8,128)(2,1)S(1)}, bf16[16,2048]{1,0:T(8,128)(2,1)S(1)}, u32[]{:S(2)}, u32[]{:S(2)}) collective-permute-start(bf16[16,2048]{1,0:T(8,128)(2,1)S(1)} %sum.7), channel_id=1, source_target_pairs={{0,8},{1,7},{4,12},{5,3},{8,14},{9,1},{12,10},{13,5},{14,6},{15,9}... | collective-permute-start | bytes 196616 | tf_op jit(solution)/shard_map/ppermute | solution.py:297
  59.2 2.1 %collective-permute-start.40 = (bf16[16,2048]{1,0:T(8,128)(2,1)S(1)}, bf16[16,2048]{1,0:T(8,128)(2,1)S(1)}, u32[]{:S(2)}, u32[]{:S(2)}) collective-permute-start(bf16[16,2048]{1,0:T(8,128)(2,1)S(1)} %sum.9), channel_id=1, source_target_pairs={{0,4},{1,5},{4,8},{5,9},{8,12},{9,13},{12,14},{13,15},{14,10},{15,... | collective-permute-start | bytes 196616 | tf_op jit(solution)/shard_map/ppermute | solution.py:297
  61.3 0.8 %collective-permute-start.41 = (bf16[16,2048]{1,0:T(8,128)(2,1)S(1)}, bf16[16,2048]{1,0:T(8,128)(2,1)S(1)}, u32[]{:S(2)}, u32[]{:S(2)}) collective-permute-start(bf16[16,2048]{1,0:T(8,128)(2,1)S(1)} %sum.10), channel_id=1, source_target_pairs={{0,8},{1,7},{4,12},{5,3},{8,14},{9,1},{12,10},{13,5},{14,6},{15,9}... | collective-permute-start | bytes 196616 | tf_op jit(solution)/shard_map/ppermute | solution.py:297
  62.1 0.4 collective-permute-done.34.refs_1_
  62.5 1.7 %collective-permute-start.44 = (bf16[16,2048]{1,0:T(8,128)(2,1)S(1)}, bf16[16,2048]{1,0:T(8,128)(2,1)S(1)}, u32[]{:S(2)}, u32[]{:S(2)}) collective-permute-start(bf16[16,2048]{1,0:T(8,128)(2,1)S(1)} %sum.11), channel_id=1, source_target_pairs={{0,2},{1,3},{4,0},{5,1},{8,4},{9,5},{12,8},{13,9},{14,12},{15,13},... | collective-permute-start | bytes 196616 | tf_op jit(solution)/shard_map/ppermute | solution.py:297
  64.2 0.4 collective-permute-start.35
  64.6 1.8 %collective-permute-start.38 = (bf16[16,2048]{1,0:T(8,128)(2,1)S(1)}, bf16[16,2048]{1,0:T(8,128)(2,1)S(1)}, u32[]{:S(2)}, u32[]{:S(2)}) collective-permute-start(bf16[16,2048]{1,0:T(8,128)(2,1)S(1)} %relay.10), channel_id=1, source_target_pairs={{0,2},{1,3},{4,0},{5,1},{8,4},{9,5},{12,8},{13,9},{14,12},{15,13},... | collective-permute-start | bytes 196616 | tf_op jit(solution)/shard_map/ppermute | solution.py:297
  66.4 0.9 %collective-permute-done.41.refs_1_ = bf16[16,2048]{1,0:T(8,128)(2,1)S(1)} collective-permute-done((bf16[16,2048]{1,0:T(8,128)(2,1)S(1)}, bf16[16,2048]{1,0:T(8,128)(2,1)S(1)}, u32[]{:S(2)}, u32[]{:S(2)}) %collective-permute-start.41) | collective-permute-done | bytes 65568 | tf_op jit(solution)/shard_map/ppermute | solution.py:297
  67.4 0.6 collective-permute-start.42
  68.0 1.5 %collective-permute-start.45 = (bf16[16,2048]{1,0:T(8,128)(2,1)S(1)}, bf16[16,2048]{1,0:T(8,128)(2,1)S(1)}, u32[]{:S(2)}, u32[]{:S(2)}) collective-permute-start(bf16[16,2048]{1,0:T(8,128)(2,1)S(1)} %relay.14), channel_id=1, source_target_pairs={{0,2},{1,3},{4,0},{5,1},{8,4},{9,5},{12,8},{13,9},{14,12},{15,13},... | collective-permute-start | bytes 196616 | tf_op jit(solution)/shard_map/ppermute | solution.py:297
  69.6 0.6 collective-permute-start.36
  70.2 1.5 %collective-permute-start.39 = (bf16[16,2048]{1,0:T(8,128)(2,1)S(1)}, bf16[16,2048]{1,0:T(8,128)(2,1)S(1)}, u32[]{:S(2)}, u32[]{:S(2)}) collective-permute-start(bf16[16,2048]{1,0:T(8,128)(2,1)S(1)} %relay.11), channel_id=1, source_target_pairs={{0,2},{1,3},{4,0},{5,1},{8,4},{9,5},{12,8},{13,9},{14,12},{15,13},... | collective-permute-start | bytes 196616 | tf_op jit(solution)/shard_map/ppermute | solution.py:297
  71.8 0.6 collective-permute-start.43
  72.4 1.5 %collective-permute-start.46 = (bf16[16,2048]{1,0:T(8,128)(2,1)S(1)}, bf16[16,2048]{1,0:T(8,128)(2,1)S(1)}, u32[]{:S(2)}, u32[]{:S(2)}) collective-permute-start(bf16[16,2048]{1,0:T(8,128)(2,1)S(1)} %relay.15), channel_id=1, source_target_pairs={{0,2},{1,3},{4,0},{5,1},{8,4},{9,5},{12,8},{13,9},{14,12},{15,13},... | collective-permute-start | bytes 196616 | tf_op jit(solution)/shard_map/ppermute | solution.py:297
  73.9 0.6 collective-permute-done.39.refs_1_
  74.5 1.6 %collective-permute-done.43.refs_2_ = bf16[16,2048]{1,0:T(8,128)(2,1)S(1)} collective-permute-done((bf16[16,2048]{1,0:T(8,128)(2,1)S(1)}, bf16[16,2048]{1,0:T(8,128)(2,1)S(1)}, u32[]{:S(2)}, u32[]{:S(2)}) %collective-permute-start.43) | collective-permute-done | bytes 65568 | tf_op jit(solution)/shard_map/ppermute | solution.py:297
  76.1 0.6 collective-permute-done.46.refs_3_
  76.9 1.2 %collective-permute-done.47.take_ref = bf16[8,4096]{1,0:T(8,128)(2,1)S(1)} collective-permute-done((bf16[8,4096]{1,0:T(8,128)(2,1)S(1)}, bf16[8,4096]{1,0:T(8,128)(2,1)S(1)}, u32[]{:S(2)}, u32[]{:S(2)}) %collective-permute-start.47) | collective-permute-done | bytes 65568 | tf_op jit(solution)/shard_map/ppermute | solution.py:306
  78.1 0.7 mix.1
  (87 shorter events, 1.5 us)
Async XLA Ops:
  0.0 23.5 %copy-start = (bf16[8192,1024]{1,0:T(8,128)(2,1)S(1)}, bf16[8192,1024]{1,0:T(8,128)(2,1)}, u32[]{:S(2)}) copy-start(bf16[8192,1024]{1,0:T(8,128)(2,1)} %refs_1_.1) | copy-start | bytes 50331652
  0.0 23.5 %copy-start.1 = (bf16[8192,1024]{1,0:T(8,128)(2,1)S(1)}, bf16[8192,1024]{1,0:T(8,128)(2,1)}, u32[]{:S(2)}) copy-start(bf16[8192,1024]{1,0:T(8,128)(2,1)} %refs_2_.1) | copy-start | bytes 50331652
  1.3 6.6 %collective-permute-start.3 = (bf16[8,8192]{1,0:T(8,128)(2,1)S(1)}, bf16[8,8192]{1,0:T(8,128)(2,1)S(1)}, u32[]{:S(2)}, u32[]{:S(2)}) collective-permute-start(bf16[8,8192]{1,0:T(8,128)(2,1)S(1)} %normalize.1.refs_0_), channel_id=1, source_target_pairs={{0,2},{1,3},{4,0},{5,1},{8,4},{9,5},{12,8},{13,9},{14,12},{15,13},... | collective-permute-start | bytes 393224 | tf_op jit(solution)/shard_map/ppermute | solution.py:297
  4.3 5.2 %collective-permute-start.1 = (bf16[8,8192]{1,0:T(8,128)(2,1)S(1)}, bf16[8,8192]{1,0:T(8,128)(2,1)S(1)}, u32[]{:S(2)}, u32[]{:S(2)}) collective-permute-start(bf16[8,8192]{1,0:T(8,128)(2,1)S(1)} %normalize.1.refs_0_), channel_id=1, source_target_pairs={{0,4},{1,5},{4,8},{5,9},{8,12},{9,13},{12,14},{13,15},{14,10},{15,... | collective-permute-start | bytes 393224 | tf_op jit(solution)/shard_map/ppermute | solution.py:297
  7.8 5.0 %collective-permute-start.7 = (bf16[8,8192]{1,0:T(8,128)(2,1)S(1)}, bf16[8,8192]{1,0:T(8,128)(2,1)S(1)}, u32[]{:S(2)}, u32[]{:S(2)}) collective-permute-start(bf16[8,8192]{1,0:T(8,128)(2,1)S(1)} %collective-permute-done.3.refs_4_), channel_id=1, source_target_pairs={{0,2},{1,3},{4,0},{5,1},{8,4},{9,5},{12,8},{13,9},{14,12},{15,13},... | collective-permute-start | bytes 393224 | tf_op jit(solution)/shard_map/ppermute | solution.py:297
  9.5 5.0 %collective-permute-start.5 = (bf16[8,8192]{1,0:T(8,128)(2,1)S(1)}, bf16[8,8192]{1,0:T(8,128)(2,1)S(1)}, u32[]{:S(2)}, u32[]{:S(2)}) collective-permute-start(bf16[8,8192]{1,0:T(8,128)(2,1)S(1)} %collective-permute-done.1.refs_2_), channel_id=1, source_target_pairs={{0,4},{1,5},{4,8},{5,9},{8,12},{9,13},{12,14},{13,15},{14,10},{15,... | collective-permute-start | bytes 393224 | tf_op jit(solution)/shard_map/ppermute | solution.py:297
  9.9 6.2 %collective-permute-start = (bf16[8,8192]{1,0:T(8,128)(2,1)S(1)}, bf16[8,8192]{1,0:T(8,128)(2,1)S(1)}, u32[]{:S(2)}, u32[]{:S(2)}) collective-permute-start(bf16[8,8192]{1,0:T(8,128)(2,1)S(1)} %normalize.1.refs_0_), channel_id=1, source_target_pairs={{0,1},{1,0},{2,3},{3,2},{4,5},{5,4},{6,7},{7,6},{8,9},{9,8},{10,11... | collective-permute-start | bytes 393224 | tf_op jit(solution)/shard_map/ppermute | solution.py:306
  9.9 7.8 %collective-permute-start.4 = (bf16[8,8192]{1,0:T(8,128)(2,1)S(1)}, bf16[8,8192]{1,0:T(8,128)(2,1)S(1)}, u32[]{:S(2)}, u32[]{:S(2)}) collective-permute-start(bf16[8,8192]{1,0:T(8,128)(2,1)S(1)} %collective-permute-done.3.refs_4_), channel_id=1, source_target_pairs={{0,1},{1,0},{2,3},{3,2},{4,5},{5,4},{6,7},{7,6},{8,9},{9,8},{10,11... | collective-permute-start | bytes 393224 | tf_op jit(solution)/shard_map/ppermute | solution.py:306
  10.4 7.3 %collective-permute-start.2 = (bf16[8,8192]{1,0:T(8,128)(2,1)S(1)}, bf16[8,8192]{1,0:T(8,128)(2,1)S(1)}, u32[]{:S(2)}, u32[]{:S(2)}) collective-permute-start(bf16[8,8192]{1,0:T(8,128)(2,1)S(1)} %collective-permute-done.1.refs_2_), channel_id=1, source_target_pairs={{0,1},{1,0},{2,3},{3,2},{4,5},{5,4},{6,7},{7,6},{8,9},{9,8},{10,11... | collective-permute-start | bytes 393224 | tf_op jit(solution)/shard_map/ppermute | solution.py:306
  12.8 7.4 %collective-permute-start.11 = (bf16[8,8192]{1,0:T(8,128)(2,1)S(1)}, bf16[8,8192]{1,0:T(8,128)(2,1)S(1)}, u32[]{:S(2)}, u32[]{:S(2)}) collective-permute-start(bf16[8,8192]{1,0:T(8,128)(2,1)S(1)} %collective-permute-done.7.odd_ref.refs_8_), channel_id=1, source_target_pairs={{0,2},{1,3},{4,0},{5,1},{8,4},{9,5},{12,8},{13,9},{14,12},{15,13},... | collective-permute-start | bytes 393224 | tf_op jit(solution)/shard_map/ppermute | solution.py:297
  14.5 7.4 %collective-permute-start.13 = (bf16[8,8192]{1,0:T(8,128)(2,1)S(1)}, bf16[8,8192]{1,0:T(8,128)(2,1)S(1)}, u32[]{:S(2)}, u32[]{:S(2)}) collective-permute-start(bf16[8,8192]{1,0:T(8,128)(2,1)S(1)} %pick.1), channel_id=1, source_target_pairs={{0,8},{1,7},{4,12},{5,3},{8,14},{9,1},{12,10},{13,5},{14,6},{15,9}... | collective-permute-start | bytes 393224 | tf_op jit(solution)/shard_map/ppermute | solution.py:297
  16.1 6.0 %collective-permute-start.9 = (bf16[8,8192]{1,0:T(8,128)(2,1)S(1)}, bf16[8,8192]{1,0:T(8,128)(2,1)S(1)}, u32[]{:S(2)}, u32[]{:S(2)}) collective-permute-start(bf16[8,8192]{1,0:T(8,128)(2,1)S(1)} %collective-permute-done.5.even_ref.refs_6_), channel_id=1, source_target_pairs={{0,4},{1,5},{4,8},{5,9},{8,12},{9,13},{12,14},{13,15},{14,10},{15,... | collective-permute-start | bytes 393224 | tf_op jit(solution)/shard_map/ppermute | solution.py:297
  17.7 4.8 %collective-permute-start.8 = (bf16[8,8192]{1,0:T(8,128)(2,1)S(1)}, bf16[8,8192]{1,0:T(8,128)(2,1)S(1)}, u32[]{:S(2)}, u32[]{:S(2)}) collective-permute-start(bf16[8,8192]{1,0:T(8,128)(2,1)S(1)} %collective-permute-done.7.odd_ref.refs_8_), channel_id=1, source_target_pairs={{0,1},{1,0},{2,3},{3,2},{4,5},{5,4},{6,7},{7,6},{8,9},{9,8},{10,11... | collective-permute-start | bytes 393224 | tf_op jit(solution)/shard_map/ppermute | solution.py:306
  17.7 4.8 %collective-permute-start.6 = (bf16[8,8192]{1,0:T(8,128)(2,1)S(1)}, bf16[8,8192]{1,0:T(8,128)(2,1)S(1)}, u32[]{:S(2)}, u32[]{:S(2)}) collective-permute-start(bf16[8,8192]{1,0:T(8,128)(2,1)S(1)} %collective-permute-done.5.even_ref.refs_6_), channel_id=1, source_target_pairs={{0,1},{1,0},{2,3},{3,2},{4,5},{5,4},{6,7},{7,6},{8,9},{9,8},{10,11... | collective-permute-start | bytes 393224 | tf_op jit(solution)/shard_map/ppermute | solution.py:306
  20.2 2.2 %collective-permute-start.12 = (bf16[8,8192]{1,0:T(8,128)(2,1)S(1)}, bf16[8,8192]{1,0:T(8,128)(2,1)S(1)}, u32[]{:S(2)}, u32[]{:S(2)}) collective-permute-start(bf16[8,8192]{1,0:T(8,128)(2,1)S(1)} %collective-permute-done.11.refs_12_), channel_id=1, source_target_pairs={{0,1},{1,0},{2,3},{3,2},{4,5},{5,4},{6,7},{7,6},{8,9},{9,8},{10,11... | collective-permute-start | bytes 393224 | tf_op jit(solution)/shard_map/ppermute | solution.py:306
  21.9 1.3 %collective-permute-start.14 = (bf16[8,8192]{1,0:T(8,128)(2,1)S(1)}, bf16[8,8192]{1,0:T(8,128)(2,1)S(1)}, u32[]{:S(2)}, u32[]{:S(2)}) collective-permute-start(bf16[8,8192]{1,0:T(8,128)(2,1)S(1)} %collective-permute-done.13.refs_14_), channel_id=1, source_target_pairs={{0,1},{1,0},{2,3},{3,2},{4,5},{5,4},{6,7},{7,6},{8,9},{9,8},{10,11... | collective-permute-start | bytes 393224 | tf_op jit(solution)/shard_map/ppermute | solution.py:306
  22.1 1.3 %collective-permute-start.10 = (bf16[8,8192]{1,0:T(8,128)(2,1)S(1)}, bf16[8,8192]{1,0:T(8,128)(2,1)S(1)}, u32[]{:S(2)}, u32[]{:S(2)}) collective-permute-start(bf16[8,8192]{1,0:T(8,128)(2,1)S(1)} %collective-permute-done.9.refs_10_), channel_id=1, source_target_pairs={{0,1},{1,0},{2,3},{3,2},{4,5},{5,4},{6,7},{7,6},{8,9},{9,8},{10,11... | collective-permute-start | bytes 393224 | tf_op jit(solution)/shard_map/ppermute | solution.py:306
  29.0 5.0 %collective-permute-start.23 = (bf16[128,256]{1,0:T(8,128)(2,1)S(1)}, bf16[128,256]{1,0:T(8,128)(2,1)S(1)}, u32[]{:S(2)}, u32[]{:S(2)}) collective-permute-start(bf16[128,256]{1,0:T(8,128)(2,1)S(1)} %get-tuple-element.20.value_ref), channel_id=1, source_target_pairs={{0,1},{1,0},{2,3},{3,2},{4,5},{5,4},{6,7},{7,6},{8,9},{9,8},{10,11... | collective-permute-start | bytes 196616 | tf_op jit(solution)/shard_map/ppermute | solution.py:306
  29.4 6.3 %collective-permute-start.27 = (bf16[128,256]{1,0:T(8,128)(2,1)S(1)}, bf16[128,256]{1,0:T(8,128)(2,1)S(1)}, u32[]{:S(2)}, u32[]{:S(2)}) collective-permute-start(bf16[128,256]{1,0:T(8,128)(2,1)S(1)} %get-tuple-element.21.value_ref), channel_id=1, source_target_pairs={{0,4},{1,5},{2,6},{3,7},{4,0},{5,1},{6,2},{7,3},{8,12},{9,13},{10,... | collective-permute-start | bytes 196616 | tf_op jit(solution)/shard_map/ppermute | solution.py:306
  30.3 6.7 %collective-permute-start.15 = (bf16[128,256]{1,0:T(8,128)(2,1)S(1)}, bf16[128,256]{1,0:T(8,128)(2,1)S(1)}, u32[]{:S(2)}, u32[]{:S(2)}) collective-permute-start(bf16[128,256]{1,0:T(8,128)(2,1)S(1)} %get-tuple-element.17.value_ref), channel_id=1, source_target_pairs={{0,8},{1,9},{2,10},{3,11},{4,12},{5,13},{6,14},{7,15},{8,0},{9,1},... | collective-permute-start | bytes 196616 | tf_op jit(solution)/shard_map/ppermute | solution.py:306
  33.6 4.5 %collective-permute-start.19 = (bf16[128,256]{1,0:T(8,128)(2,1)S(1)}, bf16[128,256]{1,0:T(8,128)(2,1)S(1)}, u32[]{:S(2)}, u32[]{:S(2)}) collective-permute-start(bf16[128,256]{1,0:T(8,128)(2,1)S(1)} %get-tuple-element.18.value_ref), channel_id=1, source_target_pairs={{0,2},{1,3},{2,0},{3,1},{4,6},{5,7},{6,4},{7,5},{8,10},{9,11},{10,... | collective-permute-start | bytes 196616 | tf_op jit(solution)/shard_map/ppermute | solution.py:306
  34.1 5.0 %collective-permute-start.24 = (bf16[128,256]{1,0:T(8,128)(2,1)S(1)}, bf16[128,256]{1,0:T(8,128)(2,1)S(1)}, u32[]{:S(2)}, u32[]{:S(2)}) collective-permute-start(bf16[128,256]{1,0:T(8,128)(2,1)S(1)} %turn.24.value_ref), channel_id=1, source_target_pairs={{0,2},{1,3},{2,0},{3,1},{4,6},{5,7},{6,4},{7,5},{8,10},{9,11},{10,... | collective-permute-start | bytes 196616 | tf_op jit(solution)/shard_map/ppermute | solution.py:306
  35.7 5.9 %collective-permute-start.28 = (bf16[128,256]{1,0:T(8,128)(2,1)S(1)}, bf16[128,256]{1,0:T(8,128)(2,1)S(1)}, u32[]{:S(2)}, u32[]{:S(2)}) collective-permute-start(bf16[128,256]{1,0:T(8,128)(2,1)S(1)} %turn.28.value_ref), channel_id=1, source_target_pairs={{0,8},{1,9},{2,10},{3,11},{4,12},{5,13},{6,14},{7,15},{8,0},{9,1},... | collective-permute-start | bytes 196616 | tf_op jit(solution)/shard_map/ppermute | solution.py:306
  37.0 15.4 %slice-start = ((s8[16777216]{0:T(1024)(128)(4,1)}), s8[4194304]{0:T(1024)(128)(4,1)S(1)}, s32[]{:S(2)}) async-start(s8[16777216]{0:T(1024)(128)(4,1)} %bitcast.2), calls=%async_computation | async-start | bytes 8388608
  37.1 15.4 %copy-start.3 = (f32[1024]{0:T(1024)S(1)}, f32[1024]{0:T(1024)}, u32[]{:S(2)}) copy-start(f32[1024]{0:T(1024)} %param.11) | copy-start | bytes 12292
  37.1 4.7 %collective-permute-start.16 = (bf16[128,256]{1,0:T(8,128)(2,1)S(1)}, bf16[128,256]{1,0:T(8,128)(2,1)S(1)}, u32[]{:S(2)}, u32[]{:S(2)}) collective-permute-start(bf16[128,256]{1,0:T(8,128)(2,1)S(1)} %turn.16.value_ref), channel_id=1, source_target_pairs={{0,1},{1,0},{2,3},{3,2},{4,5},{5,4},{6,7},{7,6},{8,9},{9,8},{10,11... | collective-permute-start | bytes 196616 | tf_op jit(solution)/shard_map/ppermute | solution.py:306
  38.1 5.0 %collective-permute-start.20 = (bf16[128,256]{1,0:T(8,128)(2,1)S(1)}, bf16[128,256]{1,0:T(8,128)(2,1)S(1)}, u32[]{:S(2)}, u32[]{:S(2)}) collective-permute-start(bf16[128,256]{1,0:T(8,128)(2,1)S(1)} %turn.20.value_ref), channel_id=1, source_target_pairs={{0,4},{1,5},{2,6},{3,7},{4,0},{5,1},{6,2},{7,3},{8,12},{9,13},{10,... | collective-permute-start | bytes 196616 | tf_op jit(solution)/shard_map/ppermute | solution.py:306
  39.2 4.8 %collective-permute-start.25 = (bf16[128,256]{1,0:T(8,128)(2,1)S(1)}, bf16[128,256]{1,0:T(8,128)(2,1)S(1)}, u32[]{:S(2)}, u32[]{:S(2)}) collective-permute-start(bf16[128,256]{1,0:T(8,128)(2,1)S(1)} %turn.25.value_ref), channel_id=1, source_target_pairs={{0,4},{1,5},{2,6},{3,7},{4,0},{5,1},{6,2},{7,3},{8,12},{9,13},{10,... | collective-permute-start | bytes 196616 | tf_op jit(solution)/shard_map/ppermute | solution.py:306
  41.7 10.8 %slice-start.1 = ((s8[16777216]{0:T(1024)(128)(4,1)}), s8[4194304]{0:T(1024)(128)(4,1)S(1)}, s32[]{:S(2)}) async-start(s8[16777216]{0:T(1024)(128)(4,1)} %bitcast.2), calls=%async_computation.1 | async-start | bytes 8388608
  41.7 4.5 %collective-permute-start.29 = (bf16[128,256]{1,0:T(8,128)(2,1)S(1)}, bf16[128,256]{1,0:T(8,128)(2,1)S(1)}, u32[]{:S(2)}, u32[]{:S(2)}) collective-permute-start(bf16[128,256]{1,0:T(8,128)(2,1)S(1)} %turn.29.value_ref), channel_id=1, source_target_pairs={{0,1},{1,0},{2,3},{3,2},{4,5},{5,4},{6,7},{7,6},{8,9},{9,8},{10,11... | collective-permute-start | bytes 196616 | tf_op jit(solution)/shard_map/ppermute | solution.py:306
  41.8 6.0 %collective-permute-start.17 = (bf16[128,256]{1,0:T(8,128)(2,1)S(1)}, bf16[128,256]{1,0:T(8,128)(2,1)S(1)}, u32[]{:S(2)}, u32[]{:S(2)}) collective-permute-start(bf16[128,256]{1,0:T(8,128)(2,1)S(1)} %turn.17.value_ref), channel_id=1, source_target_pairs={{0,2},{1,3},{2,0},{3,1},{4,6},{5,7},{6,4},{7,5},{8,10},{9,11},{10,... | collective-permute-start | bytes 196616 | tf_op jit(solution)/shard_map/ppermute | solution.py:306
  43.1 7.6 %collective-permute-start.21 = (bf16[128,256]{1,0:T(8,128)(2,1)S(1)}, bf16[128,256]{1,0:T(8,128)(2,1)S(1)}, u32[]{:S(2)}, u32[]{:S(2)}) collective-permute-start(bf16[128,256]{1,0:T(8,128)(2,1)S(1)} %turn.21.value_ref), channel_id=1, source_target_pairs={{0,8},{1,9},{2,10},{3,11},{4,12},{5,13},{6,14},{7,15},{8,0},{9,1},... | collective-permute-start | bytes 196616 | tf_op jit(solution)/shard_map/ppermute | solution.py:306
  44.0 8.5 %slice-start.2 = ((s8[16777216]{0:T(1024)(128)(4,1)}), s8[4194304]{0:T(1024)(128)(4,1)S(1)}, s32[]{:S(2)}) async-start(s8[16777216]{0:T(1024)(128)(4,1)} %bitcast.2), calls=%async_computation.2 | async-start | bytes 8388608
  44.0 7.7 %collective-permute-start.26 = (bf16[128,256]{1,0:T(8,128)(2,1)S(1)}, bf16[128,256]{1,0:T(8,128)(2,1)S(1)}, u32[]{:S(2)}, u32[]{:S(2)}) collective-permute-start(bf16[128,256]{1,0:T(8,128)(2,1)S(1)} %turn.26.value_ref), channel_id=1, source_target_pairs={{0,8},{1,9},{2,10},{3,11},{4,12},{5,13},{6,14},{7,15},{8,0},{9,1},... | collective-permute-start | bytes 196616 | tf_op jit(solution)/shard_map/ppermute | solution.py:306
  46.2 5.5 %collective-permute-start.30 = (bf16[128,256]{1,0:T(8,128)(2,1)S(1)}, bf16[128,256]{1,0:T(8,128)(2,1)S(1)}, u32[]{:S(2)}, u32[]{:S(2)}) collective-permute-start(bf16[128,256]{1,0:T(8,128)(2,1)S(1)} %turn.30.value_ref), channel_id=1, source_target_pairs={{0,2},{1,3},{2,0},{3,1},{4,6},{5,7},{6,4},{7,5},{8,10},{9,11},{10,... | collective-permute-start | bytes 196616 | tf_op jit(solution)/shard_map/ppermute | solution.py:306
  47.9 4.5 %collective-permute-start.18 = (bf16[128,256]{1,0:T(8,128)(2,1)S(1)}, bf16[128,256]{1,0:T(8,128)(2,1)S(1)}, u32[]{:S(2)}, u32[]{:S(2)}) collective-permute-start(bf16[128,256]{1,0:T(8,128)(2,1)S(1)} %turn.18.value_ref), channel_id=1, source_target_pairs={{0,4},{1,5},{2,6},{3,7},{4,0},{5,1},{6,2},{7,3},{8,12},{9,13},{10,... | collective-permute-start | bytes 196616 | tf_op jit(solution)/shard_map/ppermute | solution.py:306
  50.7 2.2 %slice-start.3 = ((s8[16777216]{0:T(1024)(128)(4,1)}), s8[4194304]{0:T(1024)(128)(4,1)S(1)}, s32[]{:S(2)}) async-start(s8[16777216]{0:T(1024)(128)(4,1)} %bitcast.2), calls=%async_computation.3 | async-start | bytes 8388608
  50.7 1.6 %collective-permute-start.22 = (bf16[128,256]{1,0:T(8,128)(2,1)S(1)}, bf16[128,256]{1,0:T(8,128)(2,1)S(1)}, u32[]{:S(2)}, u32[]{:S(2)}) collective-permute-start(bf16[128,256]{1,0:T(8,128)(2,1)S(1)} %turn.22.value_ref), channel_id=1, source_target_pairs={{0,1},{1,0},{2,3},{3,2},{4,5},{5,4},{6,7},{7,6},{8,9},{9,8},{10,11... | collective-permute-start | bytes 196616 | tf_op jit(solution)/shard_map/ppermute | solution.py:306
  54.4 23.8 %copy-start.2 = (bf16[8,8192]{1,0:T(8,128)(2,1)S(1)}, bf16[8,8192]{1,0:T(8,128)(2,1)}, u32[]{:S(2)}) copy-start(bf16[8,8192]{1,0:T(8,128)(2,1)} %tokens_ref.1) | copy-start | bytes 393220
  54.4 1.8 %collective-permute-start.31 = (bf16[48,4096]{1,0:T(8,128)(2,1)S(1)}, bf16[48,4096]{1,0:T(8,128)(2,1)S(1)}, u32[]{:S(2)}, u32[]{:S(2)}) collective-permute-start(bf16[48,4096]{1,0:T(8,128)(2,1)S(1)} %get-tuple-element.24), channel_id=1, source_target_pairs={{0,1},{1,0},{2,3},{3,2},{4,5},{5,4},{6,7},{7,6},{8,9},{9,8},{10,11... | collective-permute-start | bytes 1179656 | tf_op jit(solution)/shard_map/ppermute | solution.py:306
  56.2 8.0 %collective-permute-start.32 = (bf16[80,4096]{1,0:T(8,128)(2,1)S(1)}, bf16[80,4096]{1,0:T(8,128)(2,1)S(1)}, u32[]{:S(2)}, u32[]{:S(2)}) collective-permute-start(bf16[80,4096]{1,0:T(8,128)(2,1)S(1)} %get-tuple-element.25), channel_id=1, source_target_pairs={{0,1},{1,0},{2,3},{3,2},{4,5},{5,4},{6,7},{7,6},{8,9},{9,8},{10,11... | collective-permute-start | bytes 1966088 | tf_op jit(solution)/shard_map/ppermute | solution.py:306
  56.5 4.7 %collective-permute-start.33 = (bf16[16,2048]{1,0:T(8,128)(2,1)S(1)}, bf16[16,2048]{1,0:T(8,128)(2,1)S(1)}, u32[]{:S(2)}, u32[]{:S(2)}) collective-permute-start(bf16[16,2048]{1,0:T(8,128)(2,1)S(1)} %sum.6), channel_id=1, source_target_pairs={{0,4},{1,5},{4,8},{5,9},{8,12},{9,13},{12,14},{13,15},{14,10},{15,... | collective-permute-start | bytes 196616 | tf_op jit(solution)/shard_map/ppermute | solution.py:297
  56.6 5.9 %collective-permute-start.34 = (bf16[16,2048]{1,0:T(8,128)(2,1)S(1)}, bf16[16,2048]{1,0:T(8,128)(2,1)S(1)}, u32[]{:S(2)}, u32[]{:S(2)}) collective-permute-start(bf16[16,2048]{1,0:T(8,128)(2,1)S(1)} %sum.7), channel_id=1, source_target_pairs={{0,8},{1,7},{4,12},{5,3},{8,14},{9,1},{12,10},{13,5},{14,6},{15,9}... | collective-permute-start | bytes 196616 | tf_op jit(solution)/shard_map/ppermute | solution.py:297
  59.1 5.5 %collective-permute-start.37 = (bf16[16,2048]{1,0:T(8,128)(2,1)S(1)}, bf16[16,2048]{1,0:T(8,128)(2,1)S(1)}, u32[]{:S(2)}, u32[]{:S(2)}) collective-permute-start(bf16[16,2048]{1,0:T(8,128)(2,1)S(1)} %sum.8), channel_id=1, source_target_pairs={{0,2},{1,3},{4,0},{5,1},{8,4},{9,5},{12,8},{13,9},{14,12},{15,13},... | collective-permute-start | bytes 196616 | tf_op jit(solution)/shard_map/ppermute | solution.py:297
  59.2 7.2 %collective-permute-start.40 = (bf16[16,2048]{1,0:T(8,128)(2,1)S(1)}, bf16[16,2048]{1,0:T(8,128)(2,1)S(1)}, u32[]{:S(2)}, u32[]{:S(2)}) collective-permute-start(bf16[16,2048]{1,0:T(8,128)(2,1)S(1)} %sum.9), channel_id=1, source_target_pairs={{0,4},{1,5},{4,8},{5,9},{8,12},{9,13},{12,14},{13,15},{14,10},{15,... | collective-permute-start | bytes 196616 | tf_op jit(solution)/shard_map/ppermute | solution.py:297
  61.3 6.1 %collective-permute-start.41 = (bf16[16,2048]{1,0:T(8,128)(2,1)S(1)}, bf16[16,2048]{1,0:T(8,128)(2,1)S(1)}, u32[]{:S(2)}, u32[]{:S(2)}) collective-permute-start(bf16[16,2048]{1,0:T(8,128)(2,1)S(1)} %sum.10), channel_id=1, source_target_pairs={{0,8},{1,7},{4,12},{5,3},{8,14},{9,1},{12,10},{13,5},{14,6},{15,9}... | collective-permute-start | bytes 196616 | tf_op jit(solution)/shard_map/ppermute | solution.py:297
  62.5 5.5 %collective-permute-start.44 = (bf16[16,2048]{1,0:T(8,128)(2,1)S(1)}, bf16[16,2048]{1,0:T(8,128)(2,1)S(1)}, u32[]{:S(2)}, u32[]{:S(2)}) collective-permute-start(bf16[16,2048]{1,0:T(8,128)(2,1)S(1)} %sum.11), channel_id=1, source_target_pairs={{0,2},{1,3},{4,0},{5,1},{8,4},{9,5},{12,8},{13,9},{14,12},{15,13},... | collective-permute-start | bytes 196616 | tf_op jit(solution)/shard_map/ppermute | solution.py:297
  64.2 5.3 %collective-permute-start.35 = (bf16[16,2048]{1,0:T(8,128)(2,1)S(1)}, bf16[16,2048]{1,0:T(8,128)(2,1)S(1)}, u32[]{:S(2)}, u32[]{:S(2)}) collective-permute-start(bf16[16,2048]{1,0:T(8,128)(2,1)S(1)} %relay.8), channel_id=1, source_target_pairs={{0,4},{1,5},{4,8},{5,9},{8,12},{9,13},{12,14},{13,15},{14,10},{15,... | collective-permute-start | bytes 196616 | tf_op jit(solution)/shard_map/ppermute | solution.py:297
  64.6 5.5 %collective-permute-start.38 = (bf16[16,2048]{1,0:T(8,128)(2,1)S(1)}, bf16[16,2048]{1,0:T(8,128)(2,1)S(1)}, u32[]{:S(2)}, u32[]{:S(2)}) collective-permute-start(bf16[16,2048]{1,0:T(8,128)(2,1)S(1)} %relay.10), channel_id=1, source_target_pairs={{0,2},{1,3},{4,0},{5,1},{8,4},{9,5},{12,8},{13,9},{14,12},{15,13},... | collective-permute-start | bytes 196616 | tf_op jit(solution)/shard_map/ppermute | solution.py:297
  67.4 4.4 %collective-permute-start.42 = (bf16[16,2048]{1,0:T(8,128)(2,1)S(1)}, bf16[16,2048]{1,0:T(8,128)(2,1)S(1)}, u32[]{:S(2)}, u32[]{:S(2)}) collective-permute-start(bf16[16,2048]{1,0:T(8,128)(2,1)S(1)} %relay.12), channel_id=1, source_target_pairs={{0,4},{1,5},{4,8},{5,9},{8,12},{9,13},{12,14},{13,15},{14,10},{15,... | collective-permute-start | bytes 196616 | tf_op jit(solution)/shard_map/ppermute | solution.py:297
  68.0 4.4 %collective-permute-start.45 = (bf16[16,2048]{1,0:T(8,128)(2,1)S(1)}, bf16[16,2048]{1,0:T(8,128)(2,1)S(1)}, u32[]{:S(2)}, u32[]{:S(2)}) collective-permute-start(bf16[16,2048]{1,0:T(8,128)(2,1)S(1)} %relay.14), channel_id=1, source_target_pairs={{0,2},{1,3},{4,0},{5,1},{8,4},{9,5},{12,8},{13,9},{14,12},{15,13},... | collective-permute-start | bytes 196616 | tf_op jit(solution)/shard_map/ppermute | solution.py:297
  69.6 4.4 %collective-permute-start.36 = (bf16[16,2048]{1,0:T(8,128)(2,1)S(1)}, bf16[16,2048]{1,0:T(8,128)(2,1)S(1)}, u32[]{:S(2)}, u32[]{:S(2)}) collective-permute-start(bf16[16,2048]{1,0:T(8,128)(2,1)S(1)} %relay.9), channel_id=1, source_target_pairs={{0,4},{1,5},{4,8},{5,9},{8,12},{9,13},{12,14},{13,15},{14,10},{15,... | collective-permute-start | bytes 196616 | tf_op jit(solution)/shard_map/ppermute | solution.py:297
  70.2 4.3 %collective-permute-start.39 = (bf16[16,2048]{1,0:T(8,128)(2,1)S(1)}, bf16[16,2048]{1,0:T(8,128)(2,1)S(1)}, u32[]{:S(2)}, u32[]{:S(2)}) collective-permute-start(bf16[16,2048]{1,0:T(8,128)(2,1)S(1)} %relay.11), channel_id=1, source_target_pairs={{0,2},{1,3},{4,0},{5,1},{8,4},{9,5},{12,8},{13,9},{14,12},{15,13},... | collective-permute-start | bytes 196616 | tf_op jit(solution)/shard_map/ppermute | solution.py:297
  71.8 4.3 %collective-permute-start.43 = (bf16[16,2048]{1,0:T(8,128)(2,1)S(1)}, bf16[16,2048]{1,0:T(8,128)(2,1)S(1)}, u32[]{:S(2)}, u32[]{:S(2)}) collective-permute-start(bf16[16,2048]{1,0:T(8,128)(2,1)S(1)} %relay.13), channel_id=1, source_target_pairs={{0,4},{1,5},{4,8},{5,9},{8,12},{9,13},{12,14},{13,15},{14,10},{15,... | collective-permute-start | bytes 196616 | tf_op jit(solution)/shard_map/ppermute | solution.py:297
  72.4 4.3 %collective-permute-start.46 = (bf16[16,2048]{1,0:T(8,128)(2,1)S(1)}, bf16[16,2048]{1,0:T(8,128)(2,1)S(1)}, u32[]{:S(2)}, u32[]{:S(2)}) collective-permute-start(bf16[16,2048]{1,0:T(8,128)(2,1)S(1)} %relay.15), channel_id=1, source_target_pairs={{0,2},{1,3},{4,0},{5,1},{8,4},{9,5},{12,8},{13,9},{14,12},{15,13},... | collective-permute-start | bytes 196616 | tf_op jit(solution)/shard_map/ppermute | solution.py:297
  76.8 1.3 %collective-permute-start.47 = (bf16[8,4096]{1,0:T(8,128)(2,1)S(1)}, bf16[8,4096]{1,0:T(8,128)(2,1)S(1)}, u32[]{:S(2)}, u32[]{:S(2)}) collective-permute-start(bf16[8,4096]{1,0:T(8,128)(2,1)S(1)} %get-tuple-element.28), channel_id=1, source_target_pairs={{0,1},{1,0},{2,3},{3,2},{4,5},{5,4},{6,7},{7,6},{8,9},{9,8},{10,11... | collective-permute-start | bytes 196616 | tf_op jit(solution)/shard_map/ppermute | solution.py:306

commit v11 on v9

--- a/solution.py
+++ b/solution.py
@@ -10,7 +10,7 @@
 BLOCK = 256
 MIB = 1 << 20
 OFFSETS = (3, 1, 0, 2)
-TURN = 1_000_000_000
+TURN = 700_000_000
 COST = 20_000_000_000
 
 
@@ -247,19 +247,27 @@
     out_ref[...] = value.astype(jnp.bfloat16)
 
 
-def last_kernel(chips, ahead_in, behind_in, own_ref, arrived_ref, keep_ref, give_ref, sum_ref):
+def deal_kernel(away, chips, own_ref, arrived_ref, *refs):
+    *more, keep_ref, give_ref, sum_ref = refs
     part = keep_ref.shape[0]
     core = lax.axis_index("hid") % 2
-    sum_ref[...] = (
-        chunk(0, chips, own_ref, arrived_ref) + ahead_in[...].astype(jnp.float32) + behind_in[...].astype(jnp.float32)
-    )
-    keep_ref[...] = sum_ref[pl.ds(pl.multiple_of(core * part, part), part), :]
+    value = chunk(away, chips, own_ref, arrived_ref)
+    for arrived_in in more:
+        value = value + arrived_in[...].astype(jnp.float32)
+    sum_ref[...] = value
+    keep_ref[...] = sum_ref[pl.ds(pl.multiple_of(core * part, part), part), :].astype(jnp.bfloat16)
     give_ref[...] = sum_ref[pl.ds(pl.multiple_of((1 - core) * part, part), part), :].astype(jnp.bfloat16)
 
 
-def mix_kernel(tokens_ref, keep_ref, take_ref, out_ref):
-    wide = keep_ref.shape[1]
-    keep, take = keep_ref[...], take_ref[...].astype(jnp.float32)
+def mix_kernel(tokens_ref, *refs):
+    *sums, out_ref = refs
+    wide = out_ref.shape[1] // 2
+    keep, take = [
+        sums[3 * at][...].astype(jnp.float32)
+        + sums[3 * at + 1][...].astype(jnp.float32)
+        + sums[3 * at + 2][...].astype(jnp.float32)
+        for at in range(2)
+    ]
     first = lax.axis_index("hid") % 2 == 0
     low, high = jnp.where(first, keep, take), jnp.where(first, take, keep)
     out_ref[:, :wide] = (tokens_ref[:, :wide].astype(jnp.float32) + low).astype(jnp.bfloat16)
@@ -343,7 +351,22 @@
         for away in (steps - 1, 1 - steps, steps)
     ]
     ahead, behind, far = right(first[0]), left(first[1]), hop(first[2], 2, -2)
-    for away in range(steps - 2, 0, -1):
+    half = jax.ShapeDtypeStruct((rows // 2, wide), jnp.bfloat16)
+
+    def deal(away, *more):
+        body = functools.partial(deal_kernel, away, chips)
+        return small(body, (half, half), (own, arrived, *more), "deal", [pltpu.VMEM((rows, wide), jnp.float32)])
+
+    def skip(value, shift):
+        pairs = []
+        for at, c in enumerate(order):
+            there = order[(at + shift) % chips]
+            pairs += [(2 * c, 2 * there + 1), (2 * c + 1, 2 * there)]
+        return lax.ppermute(value, "hid", pairs)
+
+    keep, give = deal(0)
+    keeps, takes = [keep], [cross(give)]
+    for away in range(steps - 2, 1, -1):
         more = (far,) if away == steps - 2 else ()
         ahead = small(
             functools.partial(relay_kernel, away, chips, 0), part, (own, arrived, ahead, *more), "relay"
@@ -352,17 +375,12 @@
             functools.partial(relay_kernel, -away, chips, 1), part, (own, arrived, behind, *more), "relay"
         )
         ahead, behind = right(ahead), left(behind)
-    half = jax.ShapeDtypeStruct((rows // 2, wide), jnp.bfloat16)
-    kept = jax.ShapeDtypeStruct((rows // 2, wide), jnp.float32)
-    keep, give = small(
-        functools.partial(last_kernel, chips),
-        (kept, half),
-        (ahead, behind, own, arrived),
-        "last",
-        [pltpu.VMEM((rows, wide), jnp.float32)],
-    )
+    for shift, value in ((1, ahead), (-1, behind)):
+        keep, give = deal(shift, value)
+        keeps.append(hop(keep, shift, shift))
+        takes.append(skip(give, shift))
     mixed = jax.ShapeDtypeStruct(tokens.shape, tokens.dtype)
-    return small(mix_kernel, mixed, (tokens, keep, cross(give)), "mix")
+    return small(mix_kernel, mixed, (tokens, *keeps, *takes), "mix")
 
 
 def solution(mesh):

time: 80.2 us -> 78.6 us (0.980)
  waiting for transfers between devices: 32.9 us -> 31.8 us
  local copies, waits for them, and re-layouts: 1.47 us -> 0.5 us
    ppermute x0 -> x2, starting transfers between devices: none -> 1.52 us  [skip(): return lax.ppermute(value, 'hid', pairs)]
    ppermute x27, waiting for transfers between devices: 10.3 us -> 9 us  [cross(): return lax.ppermute(value, 'hid', [(d, d ^ mask) for d in range(count)])]
    ppermute x14, starting transfers between devices: 17.1 us -> 16.1 us  [hop(): return lax.ppermute(value, 'hid', pairs)]
    ppermute x0 -> x2, waiting for transfers between devices: none -> 1.01 us  [skip(): return lax.ppermute(value, 'hid', pairs)]
    unnamed x16, local copies, waits for them, and re-layouts: 1.47 us -> 0.5 us
    ppermute x14, waiting for transfers between devices: 22.6 us -> 21.8 us  [hop(): return lax.ppermute(value, 'hid', pairs)]
  transfers between devices with their start and end apart: 41 -> 43, of which waited for: 22 -> 23; matrix products, arithmetic and copies ran while one was open for 0% -> 0% of each run, Pallas kernels for 3% -> 3%
where the time goes in v11:
time: 78.6 us; the launch traced here: 78.5 us
  starting transfers between devices  34.5 us (44%)
  waiting for transfers between devices  31.8 us (40%)
  Pallas kernels  11.3 us (14%)
    ppermute x14, waiting for transfers between devices, hop(): return lax.ppermute(value, 'hid', pairs)  21.8 us
    ppermute x27, starting transfers between devices, cross(): return lax.ppermute(value, 'hid', [(d, d ^ mask) for d in range(count)])  16.9 us
    ppermute x14, starting transfers between devices, hop(): return lax.ppermute(value, 'hid', pairs)  16.1 us
    ppermute x27, waiting for transfers between devices, cross(): return lax.ppermute(value, 'hid', [(d, d ^ mask) for d in range(count)])  9 us
    pallas_call x2, Pallas kernels, up_project(): pl.pallas_call(functools.partial(up_kernel, shifts, first, slice(at * wid...  5.54 us
    pallas_call x2, Pallas kernels, down_project(): pl.pallas_call(functools.partial(down_kernel, width // BLOCK, chips, tota...  2.89 us
  transfers between devices with their start and end apart: 43, of which 23 were waited for; matrix products, arithmetic and copies ran while one was open for 0% of the time, Pallas kernels for 3%

profile of v11, /device:TPU:0, one launch (start us, length us, event | category | flops | bytes accessed | tf_op | source)
XLA Modules:
  0.0 78.5 jit_solution(9632556644690716887)
XLA Ops:
  0.0 1.3 %normalize.1.refs_0_ = bf16[8,8192]{1,0:T(8,128)(2,1)S(1)} custom-call(bf16[8,8192]{1,0:T(8,128)(2,1)} %tokens_ref.1, f32[1,8192]{1,0:T(1,128)} %bitcast.6), custom_call_target="tpu_custom_call" | custom-call | flops 20000000000 | bytes 262144 | tf_op jit(solution)/shard_map/normalize/pallas_call | solution.py:48
  1.3 3.0 %collective-permute-start.3 = (bf16[8,8192]{1,0:T(8,128)(2,1)S(1)}, bf16[8,8192]{1,0:T(8,128)(2,1)S(1)}, u32[]{:S(2)}, u32[]{:S(2)}) collective-permute-start(bf16[8,8192]{1,0:T(8,128)(2,1)S(1)} %normalize.1.refs_0_), channel_id=1, source_target_pairs={{0,2},{1,3},{4,0},{5,1},{8,4},{9,5},{12,8},{13,9},{14,12},{15,13},... | collective-permute-start | bytes 393224 | tf_op jit(solution)/shard_map/ppermute | solution.py:301
  4.3 0.1 collective-permute-start.1
  4.4 3.4 %collective-permute-done.3.refs_4_ = bf16[8,8192]{1,0:T(8,128)(2,1)S(1)} collective-permute-done((bf16[8,8192]{1,0:T(8,128)(2,1)S(1)}, bf16[8,8192]{1,0:T(8,128)(2,1)S(1)}, u32[]{:S(2)}, u32[]{:S(2)}) %collective-permute-start.3) | collective-permute-done | bytes 131104 | tf_op jit(solution)/shard_map/ppermute | solution.py:301
  7.8 1.7 %collective-permute-start.7 = (bf16[8,8192]{1,0:T(8,128)(2,1)S(1)}, bf16[8,8192]{1,0:T(8,128)(2,1)S(1)}, u32[]{:S(2)}, u32[]{:S(2)}) collective-permute-start(bf16[8,8192]{1,0:T(8,128)(2,1)S(1)} %collective-permute-done.3.refs_4_), channel_id=1, source_target_pairs={{0,2},{1,3},{4,0},{5,1},{8,4},{9,5},{12,8},{13,9},{14,12},{15,13},... | collective-permute-start | bytes 393224 | tf_op jit(solution)/shard_map/ppermute | solution.py:301
  9.5 0.3 collective-permute-start.5
  9.9 0.5 collective-permute-start.4
  10.4 2.4 %collective-permute-done.7.odd_ref.refs_8_ = bf16[8,8192]{1,0:T(8,128)(2,1)S(1)} collective-permute-done((bf16[8,8192]{1,0:T(8,128)(2,1)S(1)}, bf16[8,8192]{1,0:T(8,128)(2,1)S(1)}, u32[]{:S(2)}, u32[]{:S(2)}) %collective-permute-start.7) | collective-permute-done | bytes 131104 | tf_op jit(solution)/shard_map/ppermute | solution.py:301
  12.8 1.7 %collective-permute-start.11 = (bf16[8,8192]{1,0:T(8,128)(2,1)S(1)}, bf16[8,8192]{1,0:T(8,128)(2,1)S(1)}, u32[]{:S(2)}, u32[]{:S(2)}) collective-permute-start(bf16[8,8192]{1,0:T(8,128)(2,1)S(1)} %collective-permute-done.7.odd_ref.refs_8_), channel_id=1, source_target_pairs={{0,2},{1,3},{4,0},{5,1},{8,4},{9,5},{12,8},{13,9},{14,12},{15,13},... | collective-permute-start | bytes 393224 | tf_op jit(solution)/shard_map/ppermute | solution.py:301
  14.5 1.6 %collective-permute-start.13 = (bf16[8,8192]{1,0:T(8,128)(2,1)S(1)}, bf16[8,8192]{1,0:T(8,128)(2,1)S(1)}, u32[]{:S(2)}, u32[]{:S(2)}) collective-permute-start(bf16[8,8192]{1,0:T(8,128)(2,1)S(1)} %pick.1), channel_id=1, source_target_pairs={{0,8},{1,7},{4,12},{5,3},{8,14},{9,1},{12,10},{13,5},{14,6},{15,9}... | collective-permute-start | bytes 393224 | tf_op jit(solution)/shard_map/ppermute | solution.py:301
  16.1 1.6 %collective-permute-start.9 = (bf16[8,8192]{1,0:T(8,128)(2,1)S(1)}, bf16[8,8192]{1,0:T(8,128)(2,1)S(1)}, u32[]{:S(2)}, u32[]{:S(2)}) collective-permute-start(bf16[8,8192]{1,0:T(8,128)(2,1)S(1)} %collective-permute-done.5.even_ref.refs_6_), channel_id=1, source_target_pairs={{0,4},{1,5},{4,8},{5,9},{8,12},{9,13},{12,14},{13,15},{14,10},{15,... | collective-permute-start | bytes 393224 | tf_op jit(solution)/shard_map/ppermute | solution.py:301
  17.7 0.5 collective-permute-start.6
  18.2 2.0 %collective-permute-done.11.refs_12_ = bf16[8,8192]{1,0:T(8,128)(2,1)S(1)} collective-permute-done((bf16[8,8192]{1,0:T(8,128)(2,1)S(1)}, bf16[8,8192]{1,0:T(8,128)(2,1)S(1)}, u32[]{:S(2)}, u32[]{:S(2)}) %collective-permute-start.11) | collective-permute-done | bytes 131104 | tf_op jit(solution)/shard_map/ppermute | solution.py:301
  20.2 1.7 %collective-permute-done.13.refs_14_ = bf16[8,8192]{1,0:T(8,128)(2,1)S(1)} collective-permute-done((bf16[8,8192]{1,0:T(8,128)(2,1)S(1)}, bf16[8,8192]{1,0:T(8,128)(2,1)S(1)}, u32[]{:S(2)}, u32[]{:S(2)}) %collective-permute-start.13) | collective-permute-done | bytes 131104 | tf_op jit(solution)/shard_map/ppermute | solution.py:301
  21.9 0.2 collective-permute-done.9.refs_10_
  22.1 0.3 collective-permute-start.10
  22.4 0.8 %collective-permute-done.14.refs_15_ = bf16[8,8192]{1,0:T(8,128)(2,1)S(1)} collective-permute-done((bf16[8,8192]{1,0:T(8,128)(2,1)S(1)}, bf16[8,8192]{1,0:T(8,128)(2,1)S(1)}, u32[]{:S(2)}, u32[]{:S(2)}) %collective-permute-start.14) | collective-permute-done | bytes 131104 | tf_op jit(solution)/shard_map/ppermute | solution.py:310
  23.3 0.2 collective-permute-done.10.refs_11_
  23.5 2.8 %up_project.2 = (bf16[128,256]{1,0:T(8,128)(2,1)S(1)}, bf16[128,256]{1,0:T(8,128)(2,1)S(1)}, bf16[128,8192]{1,0:T(8,128)(2,1)S(1)}) custom-call(bf16[8,8192]{1,0:T(8,128)(2,1)S(1)} %normalize.1.refs_0_, bf16[8,8192]{1,0:T(8,128)(2,1)S(1)} %collective-permute-done.refs_1_, bf16[8,8192]{1,0:T(8,128)(2,1)S(1)} %collective-permute-done.1.refs_2_, ...), custom_call_target="tpu_custom_call" | custom-call | flops 2147483648 | tf_op jit(solution)/shard_map/up_project/pallas_call | solution.py:126
  26.3 2.8 %up_project.3 = (bf16[128,256]{1,0:T(8,128)(2,1)S(1)}, bf16[128,256]{1,0:T(8,128)(2,1)S(1)}) custom-call(bf16[128,8192]{1,0:T(8,128)(2,1)S(1)} %get-tuple-element.23.refs_0_, bf16[8192,1024]{1,0:T(8,128)(2,1)S(1)} %copy-done, bf16[8192,1024]{1,0:T(8,128)(2,1)S(1)} %copy-done.1), custom_call_target="tpu_custom_call" | custom-call | flops 2147483648 | tf_op jit(solution)/shard_map/up_project/pallas_call | solution.py:126
  29.0 0.4 collective-permute-start.23
  29.4 0.9 %collective-permute-start.27 = (bf16[128,256]{1,0:T(8,128)(2,1)S(1)}, bf16[128,256]{1,0:T(8,128)(2,1)S(1)}, u32[]{:S(2)}, u32[]{:S(2)}) collective-permute-start(bf16[128,256]{1,0:T(8,128)(2,1)S(1)} %get-tuple-element.25.value_ref), channel_id=1, source_target_pairs={{0,4},{1,5},{2,6},{3,7},{4,0},{5,1},{6,2},{7,3},{8,12},{9,13},{10,... | collective-permute-start | bytes 196616 | tf_op jit(solution)/shard_map/ppermute | solution.py:310
  30.3 3.2 %collective-permute-start.15 = (bf16[128,256]{1,0:T(8,128)(2,1)S(1)}, bf16[128,256]{1,0:T(8,128)(2,1)S(1)}, u32[]{:S(2)}, u32[]{:S(2)}) collective-permute-start(bf16[128,256]{1,0:T(8,128)(2,1)S(1)} %get-tuple-element.21.value_ref), channel_id=1, source_target_pairs={{0,8},{1,9},{2,10},{3,11},{4,12},{5,13},{6,14},{7,15},{8,0},{9,1},... | collective-permute-start | bytes 196616 | tf_op jit(solution)/shard_map/ppermute | solution.py:310
  33.6 0.5 collective-permute-start.19
  34.1 1.6 %collective-permute-start.24 = (bf16[128,256]{1,0:T(8,128)(2,1)S(1)}, bf16[128,256]{1,0:T(8,128)(2,1)S(1)}, u32[]{:S(2)}, u32[]{:S(2)}) collective-permute-start(bf16[128,256]{1,0:T(8,128)(2,1)S(1)} %turn.24.value_ref), channel_id=1, source_target_pairs={{0,2},{1,3},{2,0},{3,1},{4,6},{5,7},{6,4},{7,5},{8,10},{9,11},{10,... | collective-permute-start | bytes 196616 | tf_op jit(solution)/shard_map/ppermute | solution.py:310
  35.7 1.3 %collective-permute-start.28 = (bf16[128,256]{1,0:T(8,128)(2,1)S(1)}, bf16[128,256]{1,0:T(8,128)(2,1)S(1)}, u32[]{:S(2)}, u32[]{:S(2)}) collective-permute-start(bf16[128,256]{1,0:T(8,128)(2,1)S(1)} %turn.28.value_ref), channel_id=1, source_target_pairs={{0,8},{1,9},{2,10},{3,11},{4,12},{5,13},{6,14},{7,15},{8,0},{9,1},... | collective-permute-start | bytes 196616 | tf_op jit(solution)/shard_map/ppermute | solution.py:310
  37.1 0.1 collective-permute-start.16
  37.1 0.9 %collective-permute-done.19.other_ref = bf16[128,256]{1,0:T(8,128)(2,1)S(1)} collective-permute-done((bf16[128,256]{1,0:T(8,128)(2,1)S(1)}, bf16[128,256]{1,0:T(8,128)(2,1)S(1)}, u32[]{:S(2)}, u32[]{:S(2)}) %collective-permute-start.19) | collective-permute-done | bytes 65568 | tf_op jit(solution)/shard_map/ppermute | solution.py:310
  38.1 1.1 %collective-permute-start.20 = (bf16[128,256]{1,0:T(8,128)(2,1)S(1)}, bf16[128,256]{1,0:T(8,128)(2,1)S(1)}, u32[]{:S(2)}, u32[]{:S(2)}) collective-permute-start(bf16[128,256]{1,0:T(8,128)(2,1)S(1)} %turn.20.value_ref), channel_id=1, source_target_pairs={{0,4},{1,5},{2,6},{3,7},{4,0},{5,1},{6,2},{7,3},{8,12},{9,13},{10,... | collective-permute-start | bytes 196616 | tf_op jit(solution)/shard_map/ppermute | solution.py:310
  39.2 1.1 %collective-permute-start.25 = (bf16[128,256]{1,0:T(8,128)(2,1)S(1)}, bf16[128,256]{1,0:T(8,128)(2,1)S(1)}, u32[]{:S(2)}, u32[]{:S(2)}) collective-permute-start(bf16[128,256]{1,0:T(8,128)(2,1)S(1)} %turn.25.value_ref), channel_id=1, source_target_pairs={{0,4},{1,5},{2,6},{3,7},{4,0},{5,1},{6,2},{7,3},{8,12},{9,13},{10,... | collective-permute-start | bytes 196616 | tf_op jit(solution)/shard_map/ppermute | solution.py:310
  40.3 1.4 %collective-permute-done.28.other_ref = bf16[128,256]{1,0:T(8,128)(2,1)S(1)} collective-permute-done((bf16[128,256]{1,0:T(8,128)(2,1)S(1)}, bf16[128,256]{1,0:T(8,128)(2,1)S(1)}, u32[]{:S(2)}, u32[]{:S(2)}) %collective-permute-start.28) | collective-permute-done | bytes 65568 | tf_op jit(solution)/shard_map/ppermute | solution.py:310
  41.7 0.1 collective-permute-start.29
  41.8 0.3 collective-permute-start.17
  42.1 1.0 %collective-permute-done.20.other_ref = bf16[128,256]{1,0:T(8,128)(2,1)S(1)} collective-permute-done((bf16[128,256]{1,0:T(8,128)(2,1)S(1)}, bf16[128,256]{1,0:T(8,128)(2,1)S(1)}, u32[]{:S(2)}, u32[]{:S(2)}) %collective-permute-start.20) | collective-permute-done | bytes 65568 | tf_op jit(solution)/shard_map/ppermute | solution.py:310
  43.1 0.6 collective-permute-start.21
  43.7 0.3 collective-permute-done.25.other_ref
  44.0 2.2 %collective-permute-start.26 = (bf16[128,256]{1,0:T(8,128)(2,1)S(1)}, bf16[128,256]{1,0:T(8,128)(2,1)S(1)}, u32[]{:S(2)}, u32[]{:S(2)}) collective-permute-start(bf16[128,256]{1,0:T(8,128)(2,1)S(1)} %turn.26.value_ref), channel_id=1, source_target_pairs={{0,8},{1,9},{2,10},{3,11},{4,12},{5,13},{6,14},{7,15},{8,0},{9,1},... | collective-permute-start | bytes 196616 | tf_op jit(solution)/shard_map/ppermute | solution.py:310
  46.2 1.6 %collective-permute-start.30 = (bf16[128,256]{1,0:T(8,128)(2,1)S(1)}, bf16[128,256]{1,0:T(8,128)(2,1)S(1)}, u32[]{:S(2)}, u32[]{:S(2)}) collective-permute-start(bf16[128,256]{1,0:T(8,128)(2,1)S(1)} %turn.30.value_ref), channel_id=1, source_target_pairs={{0,2},{1,3},{2,0},{3,1},{4,6},{5,7},{6,4},{7,5},{8,10},{9,11},{10,... | collective-permute-start | bytes 196616 | tf_op jit(solution)/shard_map/ppermute | solution.py:310
  47.9 0.1 collective-permute-start.18
  48.0 2.7 %collective-permute-done.21.other_ref = bf16[128,256]{1,0:T(8,128)(2,1)S(1)} collective-permute-done((bf16[128,256]{1,0:T(8,128)(2,1)S(1)}, bf16[128,256]{1,0:T(8,128)(2,1)S(1)}, u32[]{:S(2)}, u32[]{:S(2)}) %collective-permute-start.21) | collective-permute-done | bytes 65568 | tf_op jit(solution)/shard_map/ppermute | solution.py:310
  50.8 0.8 %collective-permute-done.26.other_ref = bf16[128,256]{1,0:T(8,128)(2,1)S(1)} collective-permute-done((bf16[128,256]{1,0:T(8,128)(2,1)S(1)}, bf16[128,256]{1,0:T(8,128)(2,1)S(1)}, u32[]{:S(2)}, u32[]{:S(2)}) %collective-permute-start.26) | collective-permute-done | bytes 65568 | tf_op jit(solution)/shard_map/ppermute | solution.py:310
  51.7 0.6 collective-permute-done.18.other_ref
  52.5 0.4 slice-done.3
  52.9 1.4 %down_project.3 = (bf16[48,4096]{1,0:T(8,128)(2,1)S(1)}, bf16[80,4096]{1,0:T(8,128)(2,1)S(1)}) custom-call(f32[1,1024]{1,0:T(1,128)S(1)} %bitcast.4, bf16[1024,8192]{1,0:T(8,128)(2,1)S(1)} %bitcast.3, bf16[128,256]{1,0:T(8,128)(2,1)S(1)} %turn.19.refs_0_, bf16[128,256]{1,0:T(8,128)(2,1)S(1)} %turn.23.refs_1_, bf16[128,256]{1,0:T(8,128)(2,1)S(1)} %turn.27.refs_2_, ...), custom_call_target="tpu_custom_call" | custom-call | flops 1073741824 | tf_op jit(solution)/shard_map/down_project/pallas_call | solution.py:186
  54.5 1.4 %down_project.2 = (bf16[48,4096]{1,0:T(8,128)(2,1)S(1)}, bf16[80,4096]{1,0:T(8,128)(2,1)S(1)}) custom-call(f32[1,1024]{1,0:T(1,128)S(1)} %bitcast.5, bf16[1024,8192]{1,0:T(8,128)(2,1)S(1)} %bitcast.3, bf16[128,256]{1,0:T(8,128)(2,1)S(1)} %turn.19.refs_0_, bf16[128,256]{1,0:T(8,128)(2,1)S(1)} %turn.23.refs_1_, bf16[128,256]{1,0:T(8,128)(2,1)S(1)} %turn.27.refs_2_, ...), custom_call_target="tpu_custom_call" | custom-call | flops 1073741824 | tf_op jit(solution)/shard_map/down_project/pallas_call | solution.py:186
  55.9 0.3 collective-permute-done.31.arrived_ref
  56.2 0.3 collective-permute-start.32
  56.6 2.5 %collective-permute-start.34 = (bf16[16,4096]{1,0:T(8,128)(2,1)S(1)}, bf16[16,4096]{1,0:T(8,128)(2,1)S(1)}, u32[]{:S(2)}, u32[]{:S(2)}) collective-permute-start(bf16[16,4096]{1,0:T(8,128)(2,1)S(1)} %sum.4), channel_id=1, source_target_pairs={{0,8},{1,7},{4,12},{5,3},{8,14},{9,1},{12,10},{13,5},{14,6},{15,9}... | collective-permute-start | bytes 393224 | tf_op jit(solution)/shard_map/ppermute | solution.py:301
  59.2 3.0 %collective-permute-done.33.refs_0_ = bf16[16,4096]{1,0:T(8,128)(2,1)S(1)} collective-permute-done((bf16[16,4096]{1,0:T(8,128)(2,1)S(1)}, bf16[16,4096]{1,0:T(8,128)(2,1)S(1)}, u32[]{:S(2)}, u32[]{:S(2)}) %collective-permute-start.33) | collective-permute-done | bytes 131104 | tf_op jit(solution)/shard_map/ppermute | solution.py:301
  62.2 3.6 %collective-permute-done.34.refs_1_ = bf16[16,4096]{1,0:T(8,128)(2,1)S(1)} collective-permute-done((bf16[16,4096]{1,0:T(8,128)(2,1)S(1)}, bf16[16,4096]{1,0:T(8,128)(2,1)S(1)}, u32[]{:S(2)}, u32[]{:S(2)}) %collective-permute-start.34) | collective-permute-done | bytes 131104 | tf_op jit(solution)/shard_map/ppermute | solution.py:301
  65.8 0.1 relay.2
  65.9 0.1 collective-permute-done.37.refs_0_
  66.0 0.1 relay.3
  66.1 2.0 %collective-permute-start.38 = (bf16[16,4096]{1,0:T(8,128)(2,1)S(1)}, bf16[16,4096]{1,0:T(8,128)(2,1)S(1)}, u32[]{:S(2)}, u32[]{:S(2)}) collective-permute-start(bf16[16,4096]{1,0:T(8,128)(2,1)S(1)} %relay.3), channel_id=1, source_target_pairs={{0,2},{1,3},{4,0},{5,1},{8,4},{9,5},{12,8},{13,9},{14,12},{15,13},... | collective-permute-start | bytes 393224 | tf_op jit(solution)/shard_map/ppermute | solution.py:301
  68.2 2.7 %collective-permute-done.35.refs_0_ = bf16[16,4096]{1,0:T(8,128)(2,1)S(1)} collective-permute-done((bf16[16,4096]{1,0:T(8,128)(2,1)S(1)}, bf16[16,4096]{1,0:T(8,128)(2,1)S(1)}, u32[]{:S(2)}, u32[]{:S(2)}) %collective-permute-start.35) | collective-permute-done | bytes 131104 | tf_op jit(solution)/shard_map/ppermute | solution.py:301
  70.9 0.1 deal.4
  71.1 0.6 collective-permute-done.38.refs_0_
  71.7 0.1 deal.5
  71.7 1.4 %collective-permute-start.39 = (bf16[8,4096]{1,0:T(8,128)(2,1)S(1)}, bf16[8,4096]{1,0:T(8,128)(2,1)S(1)}, u32[]{:S(2)}, u32[]{:S(2)}) collective-permute-start(bf16[8,4096]{1,0:T(8,128)(2,1)S(1)} %get-tuple-element.33), channel_id=1, source_target_pairs={{0,2},{1,3},{4,0},{5,1},{8,4},{9,5},{12,8},{13,9},{14,12},{15,13},... | collective-permute-start | bytes 196616 | tf_op jit(solution)/shard_map/ppermute | solution.py:301
  73.2 1.5 %collective-permute-start.42 = (bf16[8,4096]{1,0:T(8,128)(2,1)S(1)}, bf16[8,4096]{1,0:T(8,128)(2,1)S(1)}, u32[]{:S(2)}, u32[]{:S(2)}) collective-permute-start(bf16[8,4096]{1,0:T(8,128)(2,1)S(1)} %get-tuple-element.36), channel_id=1, source_target_pairs={{0,3},{1,2},{4,1},{5,0},{8,5},{9,4},{12,9},{13,8},{14,13},{15,12},... | collective-permute-start | bytes 196616 | tf_op jit(solution)/shard_map/ppermute | solution.py:365
  74.7 0.8 %collective-permute-done.36.refs_1_ = bf16[8,4096]{1,0:T(8,128)(2,1)S(1)} collective-permute-done((bf16[8,4096]{1,0:T(8,128)(2,1)S(1)}, bf16[8,4096]{1,0:T(8,128)(2,1)S(1)}, u32[]{:S(2)}, u32[]{:S(2)}) %collective-permute-start.36) | collective-permute-done | bytes 65568 | tf_op jit(solution)/shard_map/ppermute | solution.py:301
  75.5 1.3 %collective-permute-done.39.refs_2_ = bf16[8,4096]{1,0:T(8,128)(2,1)S(1)} collective-permute-done((bf16[8,4096]{1,0:T(8,128)(2,1)S(1)}, bf16[8,4096]{1,0:T(8,128)(2,1)S(1)}, u32[]{:S(2)}, u32[]{:S(2)}) %collective-permute-start.39) | collective-permute-done | bytes 65568 | tf_op jit(solution)/shard_map/ppermute | solution.py:301
  76.8 1.0 %collective-permute-done.42.refs_5_ = bf16[8,4096]{1,0:T(8,128)(2,1)S(1)} collective-permute-done((bf16[8,4096]{1,0:T(8,128)(2,1)S(1)}, bf16[8,4096]{1,0:T(8,128)(2,1)S(1)}, u32[]{:S(2)}, u32[]{:S(2)}) %collective-permute-start.42) | collective-permute-done | bytes 65568 | tf_op jit(solution)/shard_map/ppermute | solution.py:365
  77.8 0.7 mix.1
  (70 shorter events, 1.2 us)
Async XLA Ops:
  0.0 23.5 %copy-start = (bf16[8192,1024]{1,0:T(8,128)(2,1)S(1)}, bf16[8192,1024]{1,0:T(8,128)(2,1)}, u32[]{:S(2)}) copy-start(bf16[8192,1024]{1,0:T(8,128)(2,1)} %refs_1_.1) | copy-start | bytes 50331652
  0.0 23.5 %copy-start.1 = (bf16[8192,1024]{1,0:T(8,128)(2,1)S(1)}, bf16[8192,1024]{1,0:T(8,128)(2,1)}, u32[]{:S(2)}) copy-start(bf16[8192,1024]{1,0:T(8,128)(2,1)} %refs_2_.1) | copy-start | bytes 50331652
  1.3 6.6 %collective-permute-start.3 = (bf16[8,8192]{1,0:T(8,128)(2,1)S(1)}, bf16[8,8192]{1,0:T(8,128)(2,1)S(1)}, u32[]{:S(2)}, u32[]{:S(2)}) collective-permute-start(bf16[8,8192]{1,0:T(8,128)(2,1)S(1)} %normalize.1.refs_0_), channel_id=1, source_target_pairs={{0,2},{1,3},{4,0},{5,1},{8,4},{9,5},{12,8},{13,9},{14,12},{15,13},... | collective-permute-start | bytes 393224 | tf_op jit(solution)/shard_map/ppermute | solution.py:301
  4.3 5.2 %collective-permute-start.1 = (bf16[8,8192]{1,0:T(8,128)(2,1)S(1)}, bf16[8,8192]{1,0:T(8,128)(2,1)S(1)}, u32[]{:S(2)}, u32[]{:S(2)}) collective-permute-start(bf16[8,8192]{1,0:T(8,128)(2,1)S(1)} %normalize.1.refs_0_), channel_id=1, source_target_pairs={{0,4},{1,5},{4,8},{5,9},{8,12},{9,13},{12,14},{13,15},{14,10},{15,... | collective-permute-start | bytes 393224 | tf_op jit(solution)/shard_map/ppermute | solution.py:301
  7.8 5.0 %collective-permute-start.7 = (bf16[8,8192]{1,0:T(8,128)(2,1)S(1)}, bf16[8,8192]{1,0:T(8,128)(2,1)S(1)}, u32[]{:S(2)}, u32[]{:S(2)}) collective-permute-start(bf16[8,8192]{1,0:T(8,128)(2,1)S(1)} %collective-permute-done.3.refs_4_), channel_id=1, source_target_pairs={{0,2},{1,3},{4,0},{5,1},{8,4},{9,5},{12,8},{13,9},{14,12},{15,13},... | collective-permute-start | bytes 393224 | tf_op jit(solution)/shard_map/ppermute | solution.py:301
  9.5 5.0 %collective-permute-start.5 = (bf16[8,8192]{1,0:T(8,128)(2,1)S(1)}, bf16[8,8192]{1,0:T(8,128)(2,1)S(1)}, u32[]{:S(2)}, u32[]{:S(2)}) collective-permute-start(bf16[8,8192]{1,0:T(8,128)(2,1)S(1)} %collective-permute-done.1.refs_2_), channel_id=1, source_target_pairs={{0,4},{1,5},{4,8},{5,9},{8,12},{9,13},{12,14},{13,15},{14,10},{15,... | collective-permute-start | bytes 393224 | tf_op jit(solution)/shard_map/ppermute | solution.py:301
  9.9 6.2 %collective-permute-start = (bf16[8,8192]{1,0:T(8,128)(2,1)S(1)}, bf16[8,8192]{1,0:T(8,128)(2,1)S(1)}, u32[]{:S(2)}, u32[]{:S(2)}) collective-permute-start(bf16[8,8192]{1,0:T(8,128)(2,1)S(1)} %normalize.1.refs_0_), channel_id=1, source_target_pairs={{0,1},{1,0},{2,3},{3,2},{4,5},{5,4},{6,7},{7,6},{8,9},{9,8},{10,11... | collective-permute-start | bytes 393224 | tf_op jit(solution)/shard_map/ppermute | solution.py:310
  9.9 7.8 %collective-permute-start.4 = (bf16[8,8192]{1,0:T(8,128)(2,1)S(1)}, bf16[8,8192]{1,0:T(8,128)(2,1)S(1)}, u32[]{:S(2)}, u32[]{:S(2)}) collective-permute-start(bf16[8,8192]{1,0:T(8,128)(2,1)S(1)} %collective-permute-done.3.refs_4_), channel_id=1, source_target_pairs={{0,1},{1,0},{2,3},{3,2},{4,5},{5,4},{6,7},{7,6},{8,9},{9,8},{10,11... | collective-permute-start | bytes 393224 | tf_op jit(solution)/shard_map/ppermute | solution.py:310
  10.4 7.3 %collective-permute-start.2 = (bf16[8,8192]{1,0:T(8,128)(2,1)S(1)}, bf16[8,8192]{1,0:T(8,128)(2,1)S(1)}, u32[]{:S(2)}, u32[]{:S(2)}) collective-permute-start(bf16[8,8192]{1,0:T(8,128)(2,1)S(1)} %collective-permute-done.1.refs_2_), channel_id=1, source_target_pairs={{0,1},{1,0},{2,3},{3,2},{4,5},{5,4},{6,7},{7,6},{8,9},{9,8},{10,11... | collective-permute-start | bytes 393224 | tf_op jit(solution)/shard_map/ppermute | solution.py:310
  12.8 7.4 %collective-permute-start.11 = (bf16[8,8192]{1,0:T(8,128)(2,1)S(1)}, bf16[8,8192]{1,0:T(8,128)(2,1)S(1)}, u32[]{:S(2)}, u32[]{:S(2)}) collective-permute-start(bf16[8,8192]{1,0:T(8,128)(2,1)S(1)} %collective-permute-done.7.odd_ref.refs_8_), channel_id=1, source_target_pairs={{0,2},{1,3},{4,0},{5,1},{8,4},{9,5},{12,8},{13,9},{14,12},{15,13},... | collective-permute-start | bytes 393224 | tf_op jit(solution)/shard_map/ppermute | solution.py:301
  14.5 7.4 %collective-permute-start.13 = (bf16[8,8192]{1,0:T(8,128)(2,1)S(1)}, bf16[8,8192]{1,0:T(8,128)(2,1)S(1)}, u32[]{:S(2)}, u32[]{:S(2)}) collective-permute-start(bf16[8,8192]{1,0:T(8,128)(2,1)S(1)} %pick.1), channel_id=1, source_target_pairs={{0,8},{1,7},{4,12},{5,3},{8,14},{9,1},{12,10},{13,5},{14,6},{15,9}... | collective-permute-start | bytes 393224 | tf_op jit(solution)/shard_map/ppermute | solution.py:301
  16.1 6.0 %collective-permute-start.9 = (bf16[8,8192]{1,0:T(8,128)(2,1)S(1)}, bf16[8,8192]{1,0:T(8,128)(2,1)S(1)}, u32[]{:S(2)}, u32[]{:S(2)}) collective-permute-start(bf16[8,8192]{1,0:T(8,128)(2,1)S(1)} %collective-permute-done.5.even_ref.refs_6_), channel_id=1, source_target_pairs={{0,4},{1,5},{4,8},{5,9},{8,12},{9,13},{12,14},{13,15},{14,10},{15,... | collective-permute-start | bytes 393224 | tf_op jit(solution)/shard_map/ppermute | solution.py:301
  17.7 4.8 %collective-permute-start.8 = (bf16[8,8192]{1,0:T(8,128)(2,1)S(1)}, bf16[8,8192]{1,0:T(8,128)(2,1)S(1)}, u32[]{:S(2)}, u32[]{:S(2)}) collective-permute-start(bf16[8,8192]{1,0:T(8,128)(2,1)S(1)} %collective-permute-done.7.odd_ref.refs_8_), channel_id=1, source_target_pairs={{0,1},{1,0},{2,3},{3,2},{4,5},{5,4},{6,7},{7,6},{8,9},{9,8},{10,11... | collective-permute-start | bytes 393224 | tf_op jit(solution)/shard_map/ppermute | solution.py:310
  17.7 4.8 %collective-permute-start.6 = (bf16[8,8192]{1,0:T(8,128)(2,1)S(1)}, bf16[8,8192]{1,0:T(8,128)(2,1)S(1)}, u32[]{:S(2)}, u32[]{:S(2)}) collective-permute-start(bf16[8,8192]{1,0:T(8,128)(2,1)S(1)} %collective-permute-done.5.even_ref.refs_6_), channel_id=1, source_target_pairs={{0,1},{1,0},{2,3},{3,2},{4,5},{5,4},{6,7},{7,6},{8,9},{9,8},{10,11... | collective-permute-start | bytes 393224 | tf_op jit(solution)/shard_map/ppermute | solution.py:310
  20.2 2.2 %collective-permute-start.12 = (bf16[8,8192]{1,0:T(8,128)(2,1)S(1)}, bf16[8,8192]{1,0:T(8,128)(2,1)S(1)}, u32[]{:S(2)}, u32[]{:S(2)}) collective-permute-start(bf16[8,8192]{1,0:T(8,128)(2,1)S(1)} %collective-permute-done.11.refs_12_), channel_id=1, source_target_pairs={{0,1},{1,0},{2,3},{3,2},{4,5},{5,4},{6,7},{7,6},{8,9},{9,8},{10,11... | collective-permute-start | bytes 393224 | tf_op jit(solution)/shard_map/ppermute | solution.py:310
  21.9 1.3 %collective-permute-start.14 = (bf16[8,8192]{1,0:T(8,128)(2,1)S(1)}, bf16[8,8192]{1,0:T(8,128)(2,1)S(1)}, u32[]{:S(2)}, u32[]{:S(2)}) collective-permute-start(bf16[8,8192]{1,0:T(8,128)(2,1)S(1)} %collective-permute-done.13.refs_14_), channel_id=1, source_target_pairs={{0,1},{1,0},{2,3},{3,2},{4,5},{5,4},{6,7},{7,6},{8,9},{9,8},{10,11... | collective-permute-start | bytes 393224 | tf_op jit(solution)/shard_map/ppermute | solution.py:310
  22.1 1.3 %collective-permute-start.10 = (bf16[8,8192]{1,0:T(8,128)(2,1)S(1)}, bf16[8,8192]{1,0:T(8,128)(2,1)S(1)}, u32[]{:S(2)}, u32[]{:S(2)}) collective-permute-start(bf16[8,8192]{1,0:T(8,128)(2,1)S(1)} %collective-permute-done.9.refs_10_), channel_id=1, source_target_pairs={{0,1},{1,0},{2,3},{3,2},{4,5},{5,4},{6,7},{7,6},{8,9},{9,8},{10,11... | collective-permute-start | bytes 393224 | tf_op jit(solution)/shard_map/ppermute | solution.py:310
  29.0 5.0 %collective-permute-start.23 = (bf16[128,256]{1,0:T(8,128)(2,1)S(1)}, bf16[128,256]{1,0:T(8,128)(2,1)S(1)}, u32[]{:S(2)}, u32[]{:S(2)}) collective-permute-start(bf16[128,256]{1,0:T(8,128)(2,1)S(1)} %get-tuple-element.24.value_ref), channel_id=1, source_target_pairs={{0,1},{1,0},{2,3},{3,2},{4,5},{5,4},{6,7},{7,6},{8,9},{9,8},{10,11... | collective-permute-start | bytes 196616 | tf_op jit(solution)/shard_map/ppermute | solution.py:310
  29.4 6.3 %collective-permute-start.27 = (bf16[128,256]{1,0:T(8,128)(2,1)S(1)}, bf16[128,256]{1,0:T(8,128)(2,1)S(1)}, u32[]{:S(2)}, u32[]{:S(2)}) collective-permute-start(bf16[128,256]{1,0:T(8,128)(2,1)S(1)} %get-tuple-element.25.value_ref), channel_id=1, source_target_pairs={{0,4},{1,5},{2,6},{3,7},{4,0},{5,1},{6,2},{7,3},{8,12},{9,13},{10,... | collective-permute-start | bytes 196616 | tf_op jit(solution)/shard_map/ppermute | solution.py:310
  30.3 6.7 %collective-permute-start.15 = (bf16[128,256]{1,0:T(8,128)(2,1)S(1)}, bf16[128,256]{1,0:T(8,128)(2,1)S(1)}, u32[]{:S(2)}, u32[]{:S(2)}) collective-permute-start(bf16[128,256]{1,0:T(8,128)(2,1)S(1)} %get-tuple-element.21.value_ref), channel_id=1, source_target_pairs={{0,8},{1,9},{2,10},{3,11},{4,12},{5,13},{6,14},{7,15},{8,0},{9,1},... | collective-permute-start | bytes 196616 | tf_op jit(solution)/shard_map/ppermute | solution.py:310
  33.6 4.5 %collective-permute-start.19 = (bf16[128,256]{1,0:T(8,128)(2,1)S(1)}, bf16[128,256]{1,0:T(8,128)(2,1)S(1)}, u32[]{:S(2)}, u32[]{:S(2)}) collective-permute-start(bf16[128,256]{1,0:T(8,128)(2,1)S(1)} %get-tuple-element.22.value_ref), channel_id=1, source_target_pairs={{0,2},{1,3},{2,0},{3,1},{4,6},{5,7},{6,4},{7,5},{8,10},{9,11},{10,... | collective-permute-start | bytes 196616 | tf_op jit(solution)/shard_map/ppermute | solution.py:310
  34.1 5.0 %collective-permute-start.24 = (bf16[128,256]{1,0:T(8,128)(2,1)S(1)}, bf16[128,256]{1,0:T(8,128)(2,1)S(1)}, u32[]{:S(2)}, u32[]{:S(2)}) collective-permute-start(bf16[128,256]{1,0:T(8,128)(2,1)S(1)} %turn.24.value_ref), channel_id=1, source_target_pairs={{0,2},{1,3},{2,0},{3,1},{4,6},{5,7},{6,4},{7,5},{8,10},{9,11},{10,... | collective-permute-start | bytes 196616 | tf_op jit(solution)/shard_map/ppermute | solution.py:310
  35.7 5.9 %collective-permute-start.28 = (bf16[128,256]{1,0:T(8,128)(2,1)S(1)}, bf16[128,256]{1,0:T(8,128)(2,1)S(1)}, u32[]{:S(2)}, u32[]{:S(2)}) collective-permute-start(bf16[128,256]{1,0:T(8,128)(2,1)S(1)} %turn.28.value_ref), channel_id=1, source_target_pairs={{0,8},{1,9},{2,10},{3,11},{4,12},{5,13},{6,14},{7,15},{8,0},{9,1},... | collective-permute-start | bytes 196616 | tf_op jit(solution)/shard_map/ppermute | solution.py:310
  37.0 15.4 %slice-start = ((s8[16777216]{0:T(1024)(128)(4,1)}), s8[4194304]{0:T(1024)(128)(4,1)S(1)}, s32[]{:S(2)}) async-start(s8[16777216]{0:T(1024)(128)(4,1)} %bitcast.2), calls=%async_computation | async-start | bytes 8388608
  37.1 15.4 %copy-start.3 = (f32[1024]{0:T(1024)S(1)}, f32[1024]{0:T(1024)}, u32[]{:S(2)}) copy-start(f32[1024]{0:T(1024)} %param.11) | copy-start | bytes 12292
  37.1 4.7 %collective-permute-start.16 = (bf16[128,256]{1,0:T(8,128)(2,1)S(1)}, bf16[128,256]{1,0:T(8,128)(2,1)S(1)}, u32[]{:S(2)}, u32[]{:S(2)}) collective-permute-start(bf16[128,256]{1,0:T(8,128)(2,1)S(1)} %turn.16.value_ref), channel_id=1, source_target_pairs={{0,1},{1,0},{2,3},{3,2},{4,5},{5,4},{6,7},{7,6},{8,9},{9,8},{10,11... | collective-permute-start | bytes 196616 | tf_op jit(solution)/shard_map/ppermute | solution.py:310
  38.1 5.0 %collective-permute-start.20 = (bf16[128,256]{1,0:T(8,128)(2,1)S(1)}, bf16[128,256]{1,0:T(8,128)(2,1)S(1)}, u32[]{:S(2)}, u32[]{:S(2)}) collective-permute-start(bf16[128,256]{1,0:T(8,128)(2,1)S(1)} %turn.20.value_ref), channel_id=1, source_target_pairs={{0,4},{1,5},{2,6},{3,7},{4,0},{5,1},{6,2},{7,3},{8,12},{9,13},{10,... | collective-permute-start | bytes 196616 | tf_op jit(solution)/shard_map/ppermute | solution.py:310
  39.2 4.8 %collective-permute-start.25 = (bf16[128,256]{1,0:T(8,128)(2,1)S(1)}, bf16[128,256]{1,0:T(8,128)(2,1)S(1)}, u32[]{:S(2)}, u32[]{:S(2)}) collective-permute-start(bf16[128,256]{1,0:T(8,128)(2,1)S(1)} %turn.25.value_ref), channel_id=1, source_target_pairs={{0,4},{1,5},{2,6},{3,7},{4,0},{5,1},{6,2},{7,3},{8,12},{9,13},{10,... | collective-permute-start | bytes 196616 | tf_op jit(solution)/shard_map/ppermute | solution.py:310
  41.7 10.8 %slice-start.1 = ((s8[16777216]{0:T(1024)(128)(4,1)}), s8[4194304]{0:T(1024)(128)(4,1)S(1)}, s32[]{:S(2)}) async-start(s8[16777216]{0:T(1024)(128)(4,1)} %bitcast.2), calls=%async_computation.1 | async-start | bytes 8388608
  41.7 4.5 %collective-permute-start.29 = (bf16[128,256]{1,0:T(8,128)(2,1)S(1)}, bf16[128,256]{1,0:T(8,128)(2,1)S(1)}, u32[]{:S(2)}, u32[]{:S(2)}) collective-permute-start(bf16[128,256]{1,0:T(8,128)(2,1)S(1)} %turn.29.value_ref), channel_id=1, source_target_pairs={{0,1},{1,0},{2,3},{3,2},{4,5},{5,4},{6,7},{7,6},{8,9},{9,8},{10,11... | collective-permute-start | bytes 196616 | tf_op jit(solution)/shard_map/ppermute | solution.py:310
  41.8 6.0 %collective-permute-start.17 = (bf16[128,256]{1,0:T(8,128)(2,1)S(1)}, bf16[128,256]{1,0:T(8,128)(2,1)S(1)}, u32[]{:S(2)}, u32[]{:S(2)}) collective-permute-start(bf16[128,256]{1,0:T(8,128)(2,1)S(1)} %turn.17.value_ref), channel_id=1, source_target_pairs={{0,2},{1,3},{2,0},{3,1},{4,6},{5,7},{6,4},{7,5},{8,10},{9,11},{10,... | collective-permute-start | bytes 196616 | tf_op jit(solution)/shard_map/ppermute | solution.py:310
  43.1 7.6 %collective-permute-start.21 = (bf16[128,256]{1,0:T(8,128)(2,1)S(1)}, bf16[128,256]{1,0:T(8,128)(2,1)S(1)}, u32[]{:S(2)}, u32[]{:S(2)}) collective-permute-start(bf16[128,256]{1,0:T(8,128)(2,1)S(1)} %turn.21.value_ref), channel_id=1, source_target_pairs={{0,8},{1,9},{2,10},{3,11},{4,12},{5,13},{6,14},{7,15},{8,0},{9,1},... | collective-permute-start | bytes 196616 | tf_op jit(solution)/shard_map/ppermute | solution.py:310
  44.0 8.5 %slice-start.2 = ((s8[16777216]{0:T(1024)(128)(4,1)}), s8[4194304]{0:T(1024)(128)(4,1)S(1)}, s32[]{:S(2)}) async-start(s8[16777216]{0:T(1024)(128)(4,1)} %bitcast.2), calls=%async_computation.2 | async-start | bytes 8388608
  44.0 7.7 %collective-permute-start.26 = (bf16[128,256]{1,0:T(8,128)(2,1)S(1)}, bf16[128,256]{1,0:T(8,128)(2,1)S(1)}, u32[]{:S(2)}, u32[]{:S(2)}) collective-permute-start(bf16[128,256]{1,0:T(8,128)(2,1)S(1)} %turn.26.value_ref), channel_id=1, source_target_pairs={{0,8},{1,9},{2,10},{3,11},{4,12},{5,13},{6,14},{7,15},{8,0},{9,1},... | collective-permute-start | bytes 196616 | tf_op jit(solution)/shard_map/ppermute | solution.py:310
  46.2 5.5 %collective-permute-start.30 = (bf16[128,256]{1,0:T(8,128)(2,1)S(1)}, bf16[128,256]{1,0:T(8,128)(2,1)S(1)}, u32[]{:S(2)}, u32[]{:S(2)}) collective-permute-start(bf16[128,256]{1,0:T(8,128)(2,1)S(1)} %turn.30.value_ref), channel_id=1, source_target_pairs={{0,2},{1,3},{2,0},{3,1},{4,6},{5,7},{6,4},{7,5},{8,10},{9,11},{10,... | collective-permute-start | bytes 196616 | tf_op jit(solution)/shard_map/ppermute | solution.py:310
  47.9 4.5 %collective-permute-start.18 = (bf16[128,256]{1,0:T(8,128)(2,1)S(1)}, bf16[128,256]{1,0:T(8,128)(2,1)S(1)}, u32[]{:S(2)}, u32[]{:S(2)}) collective-permute-start(bf16[128,256]{1,0:T(8,128)(2,1)S(1)} %turn.18.value_ref), channel_id=1, source_target_pairs={{0,4},{1,5},{2,6},{3,7},{4,0},{5,1},{6,2},{7,3},{8,12},{9,13},{10,... | collective-permute-start | bytes 196616 | tf_op jit(solution)/shard_map/ppermute | solution.py:310
  50.7 2.2 %slice-start.3 = ((s8[16777216]{0:T(1024)(128)(4,1)}), s8[4194304]{0:T(1024)(128)(4,1)S(1)}, s32[]{:S(2)}) async-start(s8[16777216]{0:T(1024)(128)(4,1)} %bitcast.2), calls=%async_computation.3 | async-start | bytes 8388608
  50.7 1.6 %collective-permute-start.22 = (bf16[128,256]{1,0:T(8,128)(2,1)S(1)}, bf16[128,256]{1,0:T(8,128)(2,1)S(1)}, u32[]{:S(2)}, u32[]{:S(2)}) collective-permute-start(bf16[128,256]{1,0:T(8,128)(2,1)S(1)} %turn.22.value_ref), channel_id=1, source_target_pairs={{0,1},{1,0},{2,3},{3,2},{4,5},{5,4},{6,7},{7,6},{8,9},{9,8},{10,11... | collective-permute-start | bytes 196616 | tf_op jit(solution)/shard_map/ppermute | solution.py:310
  54.4 23.4 %copy-start.2 = (bf16[8,8192]{1,0:T(8,128)(2,1)S(1)}, bf16[8,8192]{1,0:T(8,128)(2,1)}, u32[]{:S(2)}) copy-start(bf16[8,8192]{1,0:T(8,128)(2,1)} %tokens_ref.1) | copy-start | bytes 393220
  54.4 1.8 %collective-permute-start.31 = (bf16[48,4096]{1,0:T(8,128)(2,1)S(1)}, bf16[48,4096]{1,0:T(8,128)(2,1)S(1)}, u32[]{:S(2)}, u32[]{:S(2)}) collective-permute-start(bf16[48,4096]{1,0:T(8,128)(2,1)S(1)} %get-tuple-element.28), channel_id=1, source_target_pairs={{0,1},{1,0},{2,3},{3,2},{4,5},{5,4},{6,7},{7,6},{8,9},{9,8},{10,11... | collective-permute-start | bytes 1179656 | tf_op jit(solution)/shard_map/ppermute | solution.py:310
  56.2 9.6 %collective-permute-start.32 = (bf16[80,4096]{1,0:T(8,128)(2,1)S(1)}, bf16[80,4096]{1,0:T(8,128)(2,1)S(1)}, u32[]{:S(2)}, u32[]{:S(2)}) collective-permute-start(bf16[80,4096]{1,0:T(8,128)(2,1)S(1)} %get-tuple-element.29), channel_id=1, source_target_pairs={{0,1},{1,0},{2,3},{3,2},{4,5},{5,4},{6,7},{7,6},{8,9},{9,8},{10,11... | collective-permute-start | bytes 1966088 | tf_op jit(solution)/shard_map/ppermute | solution.py:310
  56.5 5.6 %collective-permute-start.33 = (bf16[16,4096]{1,0:T(8,128)(2,1)S(1)}, bf16[16,4096]{1,0:T(8,128)(2,1)S(1)}, u32[]{:S(2)}, u32[]{:S(2)}) collective-permute-start(bf16[16,4096]{1,0:T(8,128)(2,1)S(1)} %sum.3), channel_id=1, source_target_pairs={{0,4},{1,5},{4,8},{5,9},{8,12},{9,13},{12,14},{13,15},{14,10},{15,... | collective-permute-start | bytes 393224 | tf_op jit(solution)/shard_map/ppermute | solution.py:301
  56.6 9.2 %collective-permute-start.34 = (bf16[16,4096]{1,0:T(8,128)(2,1)S(1)}, bf16[16,4096]{1,0:T(8,128)(2,1)S(1)}, u32[]{:S(2)}, u32[]{:S(2)}) collective-permute-start(bf16[16,4096]{1,0:T(8,128)(2,1)S(1)} %sum.4), channel_id=1, source_target_pairs={{0,8},{1,7},{4,12},{5,3},{8,14},{9,1},{12,10},{13,5},{14,6},{15,9}... | collective-permute-start | bytes 393224 | tf_op jit(solution)/shard_map/ppermute | solution.py:301
  59.1 6.9 %collective-permute-start.37 = (bf16[16,4096]{1,0:T(8,128)(2,1)S(1)}, bf16[16,4096]{1,0:T(8,128)(2,1)S(1)}, u32[]{:S(2)}, u32[]{:S(2)}) collective-permute-start(bf16[16,4096]{1,0:T(8,128)(2,1)S(1)} %sum.5), channel_id=1, source_target_pairs={{0,2},{1,3},{4,0},{5,1},{8,4},{9,5},{12,8},{13,9},{14,12},{15,13},... | collective-permute-start | bytes 393224 | tf_op jit(solution)/shard_map/ppermute | solution.py:301
  65.9 5.0 %collective-permute-start.35 = (bf16[16,4096]{1,0:T(8,128)(2,1)S(1)}, bf16[16,4096]{1,0:T(8,128)(2,1)S(1)}, u32[]{:S(2)}, u32[]{:S(2)}) collective-permute-start(bf16[16,4096]{1,0:T(8,128)(2,1)S(1)} %relay.2), channel_id=1, source_target_pairs={{0,4},{1,5},{4,8},{5,9},{8,12},{9,13},{12,14},{13,15},{14,10},{15,... | collective-permute-start | bytes 393224 | tf_op jit(solution)/shard_map/ppermute | solution.py:301
  66.1 5.5 %collective-permute-start.38 = (bf16[16,4096]{1,0:T(8,128)(2,1)S(1)}, bf16[16,4096]{1,0:T(8,128)(2,1)S(1)}, u32[]{:S(2)}, u32[]{:S(2)}) collective-permute-start(bf16[16,4096]{1,0:T(8,128)(2,1)S(1)} %relay.3), channel_id=1, source_target_pairs={{0,2},{1,3},{4,0},{5,1},{8,4},{9,5},{12,8},{13,9},{14,12},{15,13},... | collective-permute-start | bytes 393224 | tf_op jit(solution)/shard_map/ppermute | solution.py:301
  68.1 6.5 %collective-permute-start.40 = (bf16[8,4096]{1,0:T(8,128)(2,1)S(1)}, bf16[8,4096]{1,0:T(8,128)(2,1)S(1)}, u32[]{:S(2)}, u32[]{:S(2)}) collective-permute-start(bf16[8,4096]{1,0:T(8,128)(2,1)S(1)} %get-tuple-element.34), channel_id=1, source_target_pairs={{0,1},{1,0},{2,3},{3,2},{4,5},{5,4},{6,7},{7,6},{8,9},{9,8},{10,11... | collective-permute-start | bytes 196616 | tf_op jit(solution)/shard_map/ppermute | solution.py:310
  71.0 4.5 %collective-permute-start.36 = (bf16[8,4096]{1,0:T(8,128)(2,1)S(1)}, bf16[8,4096]{1,0:T(8,128)(2,1)S(1)}, u32[]{:S(2)}, u32[]{:S(2)}) collective-permute-start(bf16[8,4096]{1,0:T(8,128)(2,1)S(1)} %get-tuple-element.32), channel_id=1, source_target_pairs={{0,4},{1,5},{4,8},{5,9},{8,12},{9,13},{12,14},{13,15},{14,10},{15,... | collective-permute-start | bytes 196616 | tf_op jit(solution)/shard_map/ppermute | solution.py:301
  71.0 4.4 %collective-permute-start.41 = (bf16[8,4096]{1,0:T(8,128)(2,1)S(1)}, bf16[8,4096]{1,0:T(8,128)(2,1)S(1)}, u32[]{:S(2)}, u32[]{:S(2)}) collective-permute-start(bf16[8,4096]{1,0:T(8,128)(2,1)S(1)} %get-tuple-element.35), channel_id=1, source_target_pairs={{0,5},{1,4},{4,9},{5,8},{8,13},{9,12},{12,15},{13,14},{14,11},{15,... | collective-permute-start | bytes 196616 | tf_op jit(solution)/shard_map/ppermute | solution.py:365
  71.7 5.0 %collective-permute-start.39 = (bf16[8,4096]{1,0:T(8,128)(2,1)S(1)}, bf16[8,4096]{1,0:T(8,128)(2,1)S(1)}, u32[]{:S(2)}, u32[]{:S(2)}) collective-permute-start(bf16[8,4096]{1,0:T(8,128)(2,1)S(1)} %get-tuple-element.33), channel_id=1, source_target_pairs={{0,2},{1,3},{4,0},{5,1},{8,4},{9,5},{12,8},{13,9},{14,12},{15,13},... | collective-permute-start | bytes 196616 | tf_op jit(solution)/shard_map/ppermute | solution.py:301
  73.2 4.6 %collective-permute-start.42 = (bf16[8,4096]{1,0:T(8,128)(2,1)S(1)}, bf16[8,4096]{1,0:T(8,128)(2,1)S(1)}, u32[]{:S(2)}, u32[]{:S(2)}) collective-permute-start(bf16[8,4096]{1,0:T(8,128)(2,1)S(1)} %get-tuple-element.36), channel_id=1, source_target_pairs={{0,3},{1,2},{4,1},{5,0},{8,5},{9,4},{12,9},{13,8},{14,13},{15,12},... | collective-permute-start | bytes 196616 | tf_op jit(solution)/shard_map/ppermute | solution.py:365

commit v12 on v11

--- a/solution.py
+++ b/solution.py
@@ -82,54 +82,50 @@
         out_ref[2 * own * pair : 2 * own * (pair + 1), :] = jnp.concatenate(both, axis=0).astype(jnp.bfloat16)
 
 
-def up_kernel(shifts, first, lanes_of, *refs):
+def up_kernel(shifts, pieces, *refs):
     count = 2 * len(shifts)
-    if first:
-        gate_ref, up_ref, *outs, rows_ref, hidden_ref = refs[count:]
-        join_rows(refs[:count], rows_ref)
-    else:
-        rows_ref, gate_ref, up_ref, *outs, hidden_ref = refs
+    gate_ref, up_ref, *outs, rows_ref, hidden_ref = refs[count:]
+    join_rows(refs[:count], rows_ref)
     me = lax.axis_index("hid")
     chip, core = me // 2, me % 2
     own = rows_ref.shape[0] // count
     turn = hadamard(BLOCK)
     values = rows_ref[...]
-    gate = jnp.dot(values, gate_ref[:, lanes_of], preferred_element_type=jnp.float32)
-    up = jnp.dot(values, up_ref[:, lanes_of], preferred_element_type=jnp.float32)
-    hidden = gate / (1.0 + jnp.exp(-gate)) * up
-    high = hidden.astype(jnp.bfloat16)
-    low = (hidden - high.astype(jnp.float32)).astype(jnp.bfloat16)
-    for block in range(gate.shape[1] // BLOCK):
-        lanes = slice(block * BLOCK, (block + 1) * BLOCK)
-        turned = jnp.dot(high[:, lanes], turn, preferred_element_type=jnp.float32) + jnp.dot(
-            low[:, lanes], turn, preferred_element_type=jnp.float32
-        )
-        for part in range(count):
-            there = 2 * ring_place(chip, shifts[part // 2], count // 2)
-            there = there + core if part % 2 == 0 else there + 1 - core
-            spot = pl.multiple_of(there * own, own)
-            hidden_ref[pl.ds(spot, own), lanes] = turned[part * own : (part + 1) * own]
+    wide = gate_ref.shape[1] // pieces
+    for piece in range(pieces):
+        gate = jnp.dot(values, gate_ref[:, piece * wide : (piece + 1) * wide], preferred_element_type=jnp.float32)
+        up = jnp.dot(values, up_ref[:, piece * wide : (piece + 1) * wide], preferred_element_type=jnp.float32)
+        hidden = gate / (1.0 + jnp.exp(-gate)) * up
+        high = hidden.astype(jnp.bfloat16)
+        low = (hidden - high.astype(jnp.float32)).astype(jnp.bfloat16)
+        for block in range(wide // BLOCK):
+            lanes = slice(block * BLOCK, (block + 1) * BLOCK)
+            outer = slice(piece * wide + block * BLOCK, piece * wide + (block + 1) * BLOCK)
+            turned = jnp.dot(high[:, lanes], turn, preferred_element_type=jnp.float32) + jnp.dot(
+                low[:, lanes], turn, preferred_element_type=jnp.float32
+            )
+            for part in range(count):
+                there = 2 * ring_place(chip, shifts[part // 2], count // 2)
+                there = there + core if part % 2 == 0 else there + 1 - core
+                spot = pl.multiple_of(there * own, own)
+                hidden_ref[pl.ds(spot, own), outer] = turned[part * own : (part + 1) * own]
     cols = outs[0].shape[1]
     for at, out_ref in enumerate(outs):
         out_ref[...] = hidden_ref[:, at * cols : (at + 1) * cols].astype(jnp.bfloat16)
 
 
-def up_project(shifts, parts, gate_weight, up_weight, at, pieces):
-    first = len(parts) > 1
+def up_project(shifts, parts, gate_weight, up_weight, pieces):
     depth, width = gate_weight.shape
-    width = width // pieces
     rows = sum(part.shape[0] for part in parts)
     vmem = pl.BlockSpec(memory_space=pltpu.VMEM)
-    outs = [jax.ShapeDtypeStruct((rows, width // 2), jnp.bfloat16)] * 2
-    if first:
-        outs.append(jax.ShapeDtypeStruct((rows, depth), jnp.bfloat16))
-    return pl.pallas_call(
-        functools.partial(up_kernel, shifts, first, slice(at * width, (at + 1) * width)),
+    outs = [jax.ShapeDtypeStruct((rows, width // (2 * pieces)), jnp.bfloat16)] * (2 * pieces)
+    return pl.pallas_call(
+        functools.partial(up_kernel, shifts, pieces),
         out_shape=outs,
         in_specs=[vmem] * (len(parts) + 2),
         out_specs=[vmem] * len(outs),
-        scratch_shapes=[pltpu.VMEM((rows, width), jnp.float32)],
-        compiler_params=pltpu.CompilerParams(vmem_limit_bytes=4 * MIB + 2 * rows * depth),
+        scratch_shapes=[pltpu.VMEM((rows, depth), jnp.bfloat16), pltpu.VMEM((rows, width), jnp.float32)],
+        compiler_params=pltpu.CompilerParams(vmem_limit_bytes=4 * MIB + 4 * rows * depth),
         cost_estimate=pl.CostEstimate(flops=4 * rows * depth * width, bytes_accessed=0, transcendentals=rows * width),
         name="up_project",
     )(*parts, gate_weight, up_weight)
@@ -324,9 +320,7 @@
     shifts.append(steps)
     parts = [block for own in mine for block in (own, cross(own))]
 
-    *slices, joined = up_project(shifts, parts, gate_weight, up_weight, 0, pieces)
-    for at in range(1, pieces):
-        slices += up_project(shifts, [joined], gate_weight, up_weight, at, pieces)
+    slices = [*up_project(shifts, parts, gate_weight, up_weight, pieces)]
 
     def turn(value, mask, *others):
         return both(functools.partial(turn_kernel, mask), value, once(cross(value, mask), *others), "turn")

time: 78.6 us -> 80 us (1.018)
  waiting for transfers between devices: 31.8 us -> 34.2 us
    ppermute x27, waiting for transfers between devices: 9 us -> 11.1 us  [cross(): return lax.ppermute(value, 'hid', [(d, d ^ mask) for d in range(count)])]
    ppermute x14, starting transfers between devices: 16.1 us -> 15.3 us  [hop(): return lax.ppermute(value, 'hid', pairs)]
    pallas_call x2 -> x1, Pallas kernels: 5.54 us -> 5.13 us  [up_project(): pl.pallas_call(functools.partial(up_kernel, shifts, pieces), out_shape=ou...]
where the time goes in v12:
time: 80 us; the launch traced here: 79.8 us
  starting transfers between devices  34.3 us (43%)
  waiting for transfers between devices  34.2 us (43%)
  Pallas kernels  10.9 us (14%)
    ppermute x14, waiting for transfers between devices, hop(): return lax.ppermute(value, 'hid', pairs)  22.6 us
    ppermute x27, starting transfers between devices, cross(): return lax.ppermute(value, 'hid', [(d, d ^ mask) for d in range(count)])  17.5 us
    ppermute x14, starting transfers between devices, hop(): return lax.ppermute(value, 'hid', pairs)  15.3 us
    ppermute x27, waiting for transfers between devices, cross(): return lax.ppermute(value, 'hid', [(d, d ^ mask) for d in range(count)])  11.1 us
    pallas_call x1, Pallas kernels, up_project(): pl.pallas_call(functools.partial(up_kernel, shifts, pieces), out_shape=ou...  5.13 us
    pallas_call x2, Pallas kernels, down_project(): pl.pallas_call(functools.partial(down_kernel, width // BLOCK, chips, tota...  2.9 us
  transfers between devices with their start and end apart: 43, of which 23 were waited for; matrix products, arithmetic and copies ran while one was open for 0% of the time, Pallas kernels for 3%

profile of v12, /device:TPU:0, one launch (start us, length us, event | category | flops | bytes accessed | tf_op | source)
XLA Modules:
  0.0 79.8 jit_solution(6865001280432593654)
XLA Ops:
  0.0 1.3 %normalize.1.refs_0_ = bf16[8,8192]{1,0:T(8,128)(2,1)S(1)} custom-call(bf16[8,8192]{1,0:T(8,128)(2,1)} %tokens_ref.1, f32[1,8192]{1,0:T(1,128)} %bitcast.6), custom_call_target="tpu_custom_call" | custom-call | flops 20000000000 | bytes 262144 | tf_op jit(solution)/shard_map/normalize/pallas_call | solution.py:48
  1.3 3.0 %collective-permute-start.3 = (bf16[8,8192]{1,0:T(8,128)(2,1)S(1)}, bf16[8,8192]{1,0:T(8,128)(2,1)S(1)}, u32[]{:S(2)}, u32[]{:S(2)}) collective-permute-start(bf16[8,8192]{1,0:T(8,128)(2,1)S(1)} %normalize.1.refs_0_), channel_id=1, source_target_pairs={{0,2},{1,3},{4,0},{5,1},{8,4},{9,5},{12,8},{13,9},{14,12},{15,13},... | collective-permute-start | bytes 393224 | tf_op jit(solution)/shard_map/ppermute | solution.py:297
  4.3 0.1 collective-permute-start.1
  4.4 3.4 %collective-permute-done.3.refs_4_ = bf16[8,8192]{1,0:T(8,128)(2,1)S(1)} collective-permute-done((bf16[8,8192]{1,0:T(8,128)(2,1)S(1)}, bf16[8,8192]{1,0:T(8,128)(2,1)S(1)}, u32[]{:S(2)}, u32[]{:S(2)}) %collective-permute-start.3) | collective-permute-done | bytes 131104 | tf_op jit(solution)/shard_map/ppermute | solution.py:297
  7.8 1.7 %collective-permute-start.7 = (bf16[8,8192]{1,0:T(8,128)(2,1)S(1)}, bf16[8,8192]{1,0:T(8,128)(2,1)S(1)}, u32[]{:S(2)}, u32[]{:S(2)}) collective-permute-start(bf16[8,8192]{1,0:T(8,128)(2,1)S(1)} %collective-permute-done.3.refs_4_), channel_id=1, source_target_pairs={{0,2},{1,3},{4,0},{5,1},{8,4},{9,5},{12,8},{13,9},{14,12},{15,13},... | collective-permute-start | bytes 393224 | tf_op jit(solution)/shard_map/ppermute | solution.py:297
  9.5 0.3 collective-permute-start.5
  9.9 0.5 collective-permute-start.4
  10.4 2.4 %collective-permute-done.7.odd_ref.refs_8_ = bf16[8,8192]{1,0:T(8,128)(2,1)S(1)} collective-permute-done((bf16[8,8192]{1,0:T(8,128)(2,1)S(1)}, bf16[8,8192]{1,0:T(8,128)(2,1)S(1)}, u32[]{:S(2)}, u32[]{:S(2)}) %collective-permute-start.7) | collective-permute-done | bytes 131104 | tf_op jit(solution)/shard_map/ppermute | solution.py:297
  12.8 1.7 %collective-permute-start.11 = (bf16[8,8192]{1,0:T(8,128)(2,1)S(1)}, bf16[8,8192]{1,0:T(8,128)(2,1)S(1)}, u32[]{:S(2)}, u32[]{:S(2)}) collective-permute-start(bf16[8,8192]{1,0:T(8,128)(2,1)S(1)} %collective-permute-done.7.odd_ref.refs_8_), channel_id=1, source_target_pairs={{0,2},{1,3},{4,0},{5,1},{8,4},{9,5},{12,8},{13,9},{14,12},{15,13},... | collective-permute-start | bytes 393224 | tf_op jit(solution)/shard_map/ppermute | solution.py:297
  14.5 1.6 %collective-permute-start.13 = (bf16[8,8192]{1,0:T(8,128)(2,1)S(1)}, bf16[8,8192]{1,0:T(8,128)(2,1)S(1)}, u32[]{:S(2)}, u32[]{:S(2)}) collective-permute-start(bf16[8,8192]{1,0:T(8,128)(2,1)S(1)} %pick.1), channel_id=1, source_target_pairs={{0,8},{1,7},{4,12},{5,3},{8,14},{9,1},{12,10},{13,5},{14,6},{15,9}... | collective-permute-start | bytes 393224 | tf_op jit(solution)/shard_map/ppermute | solution.py:297
  16.1 1.6 %collective-permute-start.9 = (bf16[8,8192]{1,0:T(8,128)(2,1)S(1)}, bf16[8,8192]{1,0:T(8,128)(2,1)S(1)}, u32[]{:S(2)}, u32[]{:S(2)}) collective-permute-start(bf16[8,8192]{1,0:T(8,128)(2,1)S(1)} %collective-permute-done.5.even_ref.refs_6_), channel_id=1, source_target_pairs={{0,4},{1,5},{4,8},{5,9},{8,12},{9,13},{12,14},{13,15},{14,10},{15,... | collective-permute-start | bytes 393224 | tf_op jit(solution)/shard_map/ppermute | solution.py:297
  17.7 0.5 collective-permute-start.6
  18.2 2.0 %collective-permute-done.11.refs_12_ = bf16[8,8192]{1,0:T(8,128)(2,1)S(1)} collective-permute-done((bf16[8,8192]{1,0:T(8,128)(2,1)S(1)}, bf16[8,8192]{1,0:T(8,128)(2,1)S(1)}, u32[]{:S(2)}, u32[]{:S(2)}) %collective-permute-start.11) | collective-permute-done | bytes 131104 | tf_op jit(solution)/shard_map/ppermute | solution.py:297
  20.2 1.7 %collective-permute-done.13.refs_14_ = bf16[8,8192]{1,0:T(8,128)(2,1)S(1)} collective-permute-done((bf16[8,8192]{1,0:T(8,128)(2,1)S(1)}, bf16[8,8192]{1,0:T(8,128)(2,1)S(1)}, u32[]{:S(2)}, u32[]{:S(2)}) %collective-permute-start.13) | collective-permute-done | bytes 131104 | tf_op jit(solution)/shard_map/ppermute | solution.py:297
  21.9 0.2 collective-permute-done.9.refs_10_
  22.1 0.3 collective-permute-start.10
  22.4 0.8 %collective-permute-done.14.refs_15_ = bf16[8,8192]{1,0:T(8,128)(2,1)S(1)} collective-permute-done((bf16[8,8192]{1,0:T(8,128)(2,1)S(1)}, bf16[8,8192]{1,0:T(8,128)(2,1)S(1)}, u32[]{:S(2)}, u32[]{:S(2)}) %collective-permute-start.14) | collective-permute-done | bytes 131104 | tf_op jit(solution)/shard_map/ppermute | solution.py:306
  23.3 0.2 collective-permute-done.10.refs_11_
  23.5 5.1 %up_project.1 = (bf16[128,256]{1,0:T(8,128)(2,1)S(1)}, bf16[128,256]{1,0:T(8,128)(2,1)S(1)}, bf16[128,256]{1,0:T(8,128)(2,1)S(1)}, bf16[128,256]{1,0:T(8,128)(2,1)S(1)}) custom-call(bf16[8,8192]{1,0:T(8,128)(2,1)S(1)} %normalize.1.refs_0_, bf16[8,8192]{1,0:T(8,128)(2,1)S(1)} %collective-permute-done.refs_1_, ...), custom_call_target="tpu_custom_call" | custom-call | flops 4294967296 | tf_op jit(solution)/shard_map/up_project/pallas_call | solution.py:122
  28.6 2.8 %collective-permute-start.15 = (bf16[128,256]{1,0:T(8,128)(2,1)S(1)}, bf16[128,256]{1,0:T(8,128)(2,1)S(1)}, u32[]{:S(2)}, u32[]{:S(2)}) collective-permute-start(bf16[128,256]{1,0:T(8,128)(2,1)S(1)} %get-tuple-element.20.value_ref), channel_id=1, source_target_pairs={{0,8},{1,9},{2,10},{3,11},{4,12},{5,13},{6,14},{7,15},{8,0},{9,1},... | collective-permute-start | bytes 196616 | tf_op jit(solution)/shard_map/ppermute | solution.py:306
  31.4 0.7 collective-permute-start.19
  32.1 1.4 %collective-permute-start.27 = (bf16[128,256]{1,0:T(8,128)(2,1)S(1)}, bf16[128,256]{1,0:T(8,128)(2,1)S(1)}, u32[]{:S(2)}, u32[]{:S(2)}) collective-permute-start(bf16[128,256]{1,0:T(8,128)(2,1)S(1)} %get-tuple-element.23.value_ref), channel_id=1, source_target_pairs={{0,4},{1,5},{2,6},{3,7},{4,0},{5,1},{6,2},{7,3},{8,12},{9,13},{10,... | collective-permute-start | bytes 196616 | tf_op jit(solution)/shard_map/ppermute | solution.py:306
  33.5 1.8 %collective-permute-done.15.other_ref = bf16[128,256]{1,0:T(8,128)(2,1)S(1)} collective-permute-done((bf16[128,256]{1,0:T(8,128)(2,1)S(1)}, bf16[128,256]{1,0:T(8,128)(2,1)S(1)}, u32[]{:S(2)}, u32[]{:S(2)}) %collective-permute-start.15) | collective-permute-done | bytes 65568 | tf_op jit(solution)/shard_map/ppermute | solution.py:306
  35.3 0.1 collective-permute-start.16
  35.4 0.3 collective-permute-done.19.other_ref
  35.7 1.6 %collective-permute-start.20 = (bf16[128,256]{1,0:T(8,128)(2,1)S(1)}, bf16[128,256]{1,0:T(8,128)(2,1)S(1)}, u32[]{:S(2)}, u32[]{:S(2)}) collective-permute-start(bf16[128,256]{1,0:T(8,128)(2,1)S(1)} %turn.20.value_ref), channel_id=1, source_target_pairs={{0,4},{1,5},{2,6},{3,7},{4,0},{5,1},{6,2},{7,3},{8,12},{9,13},{10,... | collective-permute-start | bytes 196616 | tf_op jit(solution)/shard_map/ppermute | solution.py:306
  37.4 0.9 %collective-permute-start.24 = (bf16[128,256]{1,0:T(8,128)(2,1)S(1)}, bf16[128,256]{1,0:T(8,128)(2,1)S(1)}, u32[]{:S(2)}, u32[]{:S(2)}) collective-permute-start(bf16[128,256]{1,0:T(8,128)(2,1)S(1)} %turn.24.value_ref), channel_id=1, source_target_pairs={{0,2},{1,3},{2,0},{3,1},{4,6},{5,7},{6,4},{7,5},{8,10},{9,11},{10,... | collective-permute-start | bytes 196616 | tf_op jit(solution)/shard_map/ppermute | solution.py:306
  38.4 2.1 %collective-permute-start.28 = (bf16[128,256]{1,0:T(8,128)(2,1)S(1)}, bf16[128,256]{1,0:T(8,128)(2,1)S(1)}, u32[]{:S(2)}, u32[]{:S(2)}) collective-permute-start(bf16[128,256]{1,0:T(8,128)(2,1)S(1)} %turn.28.value_ref), channel_id=1, source_target_pairs={{0,8},{1,9},{2,10},{3,11},{4,12},{5,13},{6,14},{7,15},{8,0},{9,1},... | collective-permute-start | bytes 196616 | tf_op jit(solution)/shard_map/ppermute | solution.py:306
  40.5 1.5 %collective-permute-start.17 = (bf16[128,256]{1,0:T(8,128)(2,1)S(1)}, bf16[128,256]{1,0:T(8,128)(2,1)S(1)}, u32[]{:S(2)}, u32[]{:S(2)}) collective-permute-start(bf16[128,256]{1,0:T(8,128)(2,1)S(1)} %turn.17.value_ref), channel_id=1, source_target_pairs={{0,2},{1,3},{2,0},{3,1},{4,6},{5,7},{6,4},{7,5},{8,10},{9,11},{10,... | collective-permute-start | bytes 196616 | tf_op jit(solution)/shard_map/ppermute | solution.py:306
  42.0 0.7 collective-permute-start.21
  42.7 1.6 %collective-permute-start.25 = (bf16[128,256]{1,0:T(8,128)(2,1)S(1)}, bf16[128,256]{1,0:T(8,128)(2,1)S(1)}, u32[]{:S(2)}, u32[]{:S(2)}) collective-permute-start(bf16[128,256]{1,0:T(8,128)(2,1)S(1)} %turn.25.value_ref), channel_id=1, source_target_pairs={{0,4},{1,5},{2,6},{3,7},{4,0},{5,1},{6,2},{7,3},{8,12},{9,13},{10,... | collective-permute-start | bytes 196616 | tf_op jit(solution)/shard_map/ppermute | solution.py:306
  44.3 1.6 %collective-permute-done.28.other_ref = bf16[128,256]{1,0:T(8,128)(2,1)S(1)} collective-permute-done((bf16[128,256]{1,0:T(8,128)(2,1)S(1)}, bf16[128,256]{1,0:T(8,128)(2,1)S(1)}, u32[]{:S(2)}, u32[]{:S(2)}) %collective-permute-start.28) | collective-permute-done | bytes 65568 | tf_op jit(solution)/shard_map/ppermute | solution.py:306
  46.0 0.1 collective-permute-start.29
  46.2 1.6 %collective-permute-done.21.other_ref = bf16[128,256]{1,0:T(8,128)(2,1)S(1)} collective-permute-done((bf16[128,256]{1,0:T(8,128)(2,1)S(1)}, bf16[128,256]{1,0:T(8,128)(2,1)S(1)}, u32[]{:S(2)}, u32[]{:S(2)}) %collective-permute-start.21) | collective-permute-done | bytes 65568 | tf_op jit(solution)/shard_map/ppermute | solution.py:306
  48.1 1.4 %collective-permute-start.26 = (bf16[128,256]{1,0:T(8,128)(2,1)S(1)}, bf16[128,256]{1,0:T(8,128)(2,1)S(1)}, u32[]{:S(2)}, u32[]{:S(2)}) collective-permute-start(bf16[128,256]{1,0:T(8,128)(2,1)S(1)} %turn.26.value_ref), channel_id=1, source_target_pairs={{0,8},{1,9},{2,10},{3,11},{4,12},{5,13},{6,14},{7,15},{8,0},{9,1},... | collective-permute-start | bytes 196616 | tf_op jit(solution)/shard_map/ppermute | solution.py:306
  49.5 0.7 collective-permute-start.30
  50.2 0.5 collective-permute-done.18.other_ref
  50.8 3.9 %collective-permute-done.26.other_ref = bf16[128,256]{1,0:T(8,128)(2,1)S(1)} collective-permute-done((bf16[128,256]{1,0:T(8,128)(2,1)S(1)}, bf16[128,256]{1,0:T(8,128)(2,1)S(1)}, u32[]{:S(2)}, u32[]{:S(2)}) %collective-permute-start.26) | collective-permute-done | bytes 65568 | tf_op jit(solution)/shard_map/ppermute | solution.py:306
  54.8 1.4 %down_project.3 = (bf16[48,4096]{1,0:T(8,128)(2,1)S(1)}, bf16[80,4096]{1,0:T(8,128)(2,1)S(1)}) custom-call(f32[1,1024]{1,0:T(1,128)S(1)} %bitcast.4, bf16[1024,8192]{1,0:T(8,128)(2,1)S(1)} %bitcast.3, bf16[128,256]{1,0:T(8,128)(2,1)S(1)} %turn.19.refs_0_, bf16[128,256]{1,0:T(8,128)(2,1)S(1)} %turn.23.refs_1_, bf16[128,256]{1,0:T(8,128)(2,1)S(1)} %turn.27.refs_2_, ...), custom_call_target="tpu_custom_call" | custom-call | flops 1073741824 | tf_op jit(solution)/shard_map/down_project/pallas_call | solution.py:182
  56.3 0.1 collective-permute-start.31
  56.4 1.5 %down_project.2 = (bf16[48,4096]{1,0:T(8,128)(2,1)S(1)}, bf16[80,4096]{1,0:T(8,128)(2,1)S(1)}) custom-call(f32[1,1024]{1,0:T(1,128)S(1)} %bitcast.5, bf16[1024,8192]{1,0:T(8,128)(2,1)S(1)} %bitcast.3, bf16[128,256]{1,0:T(8,128)(2,1)S(1)} %turn.19.refs_0_, bf16[128,256]{1,0:T(8,128)(2,1)S(1)} %turn.23.refs_1_, bf16[128,256]{1,0:T(8,128)(2,1)S(1)} %turn.27.refs_2_, ...), custom_call_target="tpu_custom_call" | custom-call | flops 1073741824 | tf_op jit(solution)/shard_map/down_project/pallas_call | solution.py:182
  57.9 0.2 collective-permute-done.31.arrived_ref
  58.1 0.3 collective-permute-start.32
  58.4 0.2 collective-permute-start.33
  58.6 2.2 %collective-permute-start.34 = (bf16[16,4096]{1,0:T(8,128)(2,1)S(1)}, bf16[16,4096]{1,0:T(8,128)(2,1)S(1)}, u32[]{:S(2)}, u32[]{:S(2)}) collective-permute-start(bf16[16,4096]{1,0:T(8,128)(2,1)S(1)} %sum.4), channel_id=1, source_target_pairs={{0,8},{1,7},{4,12},{5,3},{8,14},{9,1},{12,10},{13,5},{14,6},{15,9}... | collective-permute-start | bytes 393224 | tf_op jit(solution)/shard_map/ppermute | solution.py:297
  60.9 0.5 collective-permute-start.37
  61.4 2.7 %collective-permute-done.33.refs_0_ = bf16[16,4096]{1,0:T(8,128)(2,1)S(1)} collective-permute-done((bf16[16,4096]{1,0:T(8,128)(2,1)S(1)}, bf16[16,4096]{1,0:T(8,128)(2,1)S(1)}, u32[]{:S(2)}, u32[]{:S(2)}) %collective-permute-start.33) | collective-permute-done | bytes 131104 | tf_op jit(solution)/shard_map/ppermute | solution.py:297
  64.1 3.0 %collective-permute-done.34.refs_1_ = bf16[16,4096]{1,0:T(8,128)(2,1)S(1)} collective-permute-done((bf16[16,4096]{1,0:T(8,128)(2,1)S(1)}, bf16[16,4096]{1,0:T(8,128)(2,1)S(1)}, u32[]{:S(2)}, u32[]{:S(2)}) %collective-permute-start.34) | collective-permute-done | bytes 131104 | tf_op jit(solution)/shard_map/ppermute | solution.py:297
  67.1 0.1 relay.2
  67.2 0.1 collective-permute-start.35
  67.3 0.7 collective-permute-done.37.refs_0_
  67.9 0.1 relay.3
  68.0 1.4 %collective-permute-start.38 = (bf16[16,4096]{1,0:T(8,128)(2,1)S(1)}, bf16[16,4096]{1,0:T(8,128)(2,1)S(1)}, u32[]{:S(2)}, u32[]{:S(2)}) collective-permute-start(bf16[16,4096]{1,0:T(8,128)(2,1)S(1)} %relay.3), channel_id=1, source_target_pairs={{0,2},{1,3},{4,0},{5,1},{8,4},{9,5},{12,8},{13,9},{14,12},{15,13},... | collective-permute-start | bytes 393224 | tf_op jit(solution)/shard_map/ppermute | solution.py:297
  69.5 2.7 %collective-permute-done.35.refs_0_ = bf16[16,4096]{1,0:T(8,128)(2,1)S(1)} collective-permute-done((bf16[16,4096]{1,0:T(8,128)(2,1)S(1)}, bf16[16,4096]{1,0:T(8,128)(2,1)S(1)}, u32[]{:S(2)}, u32[]{:S(2)}) %collective-permute-start.35) | collective-permute-done | bytes 131104 | tf_op jit(solution)/shard_map/ppermute | solution.py:297
  72.2 0.1 deal.4
  72.3 0.1 collective-permute-start.36
  72.4 1.1 %collective-permute-done.38.refs_0_ = bf16[16,4096]{1,0:T(8,128)(2,1)S(1)} collective-permute-done((bf16[16,4096]{1,0:T(8,128)(2,1)S(1)}, bf16[16,4096]{1,0:T(8,128)(2,1)S(1)}, u32[]{:S(2)}, u32[]{:S(2)}) %collective-permute-start.38) | collective-permute-done | bytes 131104 | tf_op jit(solution)/shard_map/ppermute | solution.py:297
  73.6 0.1 deal.5
  73.6 0.9 %collective-permute-start.39 = (bf16[8,4096]{1,0:T(8,128)(2,1)S(1)}, bf16[8,4096]{1,0:T(8,128)(2,1)S(1)}, u32[]{:S(2)}, u32[]{:S(2)}) collective-permute-start(bf16[8,4096]{1,0:T(8,128)(2,1)S(1)} %get-tuple-element.31), channel_id=1, source_target_pairs={{0,2},{1,3},{4,0},{5,1},{8,4},{9,5},{12,8},{13,9},{14,12},{15,13},... | collective-permute-start | bytes 196616 | tf_op jit(solution)/shard_map/ppermute | solution.py:297
  74.5 1.5 %collective-permute-start.42 = (bf16[8,4096]{1,0:T(8,128)(2,1)S(1)}, bf16[8,4096]{1,0:T(8,128)(2,1)S(1)}, u32[]{:S(2)}, u32[]{:S(2)}) collective-permute-start(bf16[8,4096]{1,0:T(8,128)(2,1)S(1)} %get-tuple-element.34), channel_id=1, source_target_pairs={{0,3},{1,2},{4,1},{5,0},{8,5},{9,4},{12,9},{13,8},{14,13},{15,12},... | collective-permute-start | bytes 196616 | tf_op jit(solution)/shard_map/ppermute | solution.py:359
  76.0 0.8 %collective-permute-done.36.refs_1_ = bf16[8,4096]{1,0:T(8,128)(2,1)S(1)} collective-permute-done((bf16[8,4096]{1,0:T(8,128)(2,1)S(1)}, bf16[8,4096]{1,0:T(8,128)(2,1)S(1)}, u32[]{:S(2)}, u32[]{:S(2)}) %collective-permute-start.36) | collective-permute-done | bytes 65568 | tf_op jit(solution)/shard_map/ppermute | solution.py:297
  76.8 1.8 %collective-permute-done.39.refs_2_ = bf16[8,4096]{1,0:T(8,128)(2,1)S(1)} collective-permute-done((bf16[8,4096]{1,0:T(8,128)(2,1)S(1)}, bf16[8,4096]{1,0:T(8,128)(2,1)S(1)}, u32[]{:S(2)}, u32[]{:S(2)}) %collective-permute-start.39) | collective-permute-done | bytes 65568 | tf_op jit(solution)/shard_map/ppermute | solution.py:297
  78.6 0.5 collective-permute-done.42.refs_5_
  79.1 0.7 mix.1
  (69 shorter events, 1.0 us)
Async XLA Ops:
  0.0 23.5 %copy-start = (bf16[8192,1024]{1,0:T(8,128)(2,1)S(1)}, bf16[8192,1024]{1,0:T(8,128)(2,1)}, u32[]{:S(2)}) copy-start(bf16[8192,1024]{1,0:T(8,128)(2,1)} %refs_16_.1) | copy-start | bytes 50331652
  0.0 23.5 %copy-start.1 = (bf16[8192,1024]{1,0:T(8,128)(2,1)S(1)}, bf16[8192,1024]{1,0:T(8,128)(2,1)}, u32[]{:S(2)}) copy-start(bf16[8192,1024]{1,0:T(8,128)(2,1)} %refs_17_.1) | copy-start | bytes 50331652
  1.3 6.6 %collective-permute-start.3 = (bf16[8,8192]{1,0:T(8,128)(2,1)S(1)}, bf16[8,8192]{1,0:T(8,128)(2,1)S(1)}, u32[]{:S(2)}, u32[]{:S(2)}) collective-permute-start(bf16[8,8192]{1,0:T(8,128)(2,1)S(1)} %normalize.1.refs_0_), channel_id=1, source_target_pairs={{0,2},{1,3},{4,0},{5,1},{8,4},{9,5},{12,8},{13,9},{14,12},{15,13},... | collective-permute-start | bytes 393224 | tf_op jit(solution)/shard_map/ppermute | solution.py:297
  4.3 5.2 %collective-permute-start.1 = (bf16[8,8192]{1,0:T(8,128)(2,1)S(1)}, bf16[8,8192]{1,0:T(8,128)(2,1)S(1)}, u32[]{:S(2)}, u32[]{:S(2)}) collective-permute-start(bf16[8,8192]{1,0:T(8,128)(2,1)S(1)} %normalize.1.refs_0_), channel_id=1, source_target_pairs={{0,4},{1,5},{4,8},{5,9},{8,12},{9,13},{12,14},{13,15},{14,10},{15,... | collective-permute-start | bytes 393224 | tf_op jit(solution)/shard_map/ppermute | solution.py:297
  7.8 5.0 %collective-permute-start.7 = (bf16[8,8192]{1,0:T(8,128)(2,1)S(1)}, bf16[8,8192]{1,0:T(8,128)(2,1)S(1)}, u32[]{:S(2)}, u32[]{:S(2)}) collective-permute-start(bf16[8,8192]{1,0:T(8,128)(2,1)S(1)} %collective-permute-done.3.refs_4_), channel_id=1, source_target_pairs={{0,2},{1,3},{4,0},{5,1},{8,4},{9,5},{12,8},{13,9},{14,12},{15,13},... | collective-permute-start | bytes 393224 | tf_op jit(solution)/shard_map/ppermute | solution.py:297
  9.5 5.0 %collective-permute-start.5 = (bf16[8,8192]{1,0:T(8,128)(2,1)S(1)}, bf16[8,8192]{1,0:T(8,128)(2,1)S(1)}, u32[]{:S(2)}, u32[]{:S(2)}) collective-permute-start(bf16[8,8192]{1,0:T(8,128)(2,1)S(1)} %collective-permute-done.1.refs_2_), channel_id=1, source_target_pairs={{0,4},{1,5},{4,8},{5,9},{8,12},{9,13},{12,14},{13,15},{14,10},{15,... | collective-permute-start | bytes 393224 | tf_op jit(solution)/shard_map/ppermute | solution.py:297
  9.9 6.2 %collective-permute-start = (bf16[8,8192]{1,0:T(8,128)(2,1)S(1)}, bf16[8,8192]{1,0:T(8,128)(2,1)S(1)}, u32[]{:S(2)}, u32[]{:S(2)}) collective-permute-start(bf16[8,8192]{1,0:T(8,128)(2,1)S(1)} %normalize.1.refs_0_), channel_id=1, source_target_pairs={{0,1},{1,0},{2,3},{3,2},{4,5},{5,4},{6,7},{7,6},{8,9},{9,8},{10,11... | collective-permute-start | bytes 393224 | tf_op jit(solution)/shard_map/ppermute | solution.py:306
  9.9 7.8 %collective-permute-start.4 = (bf16[8,8192]{1,0:T(8,128)(2,1)S(1)}, bf16[8,8192]{1,0:T(8,128)(2,1)S(1)}, u32[]{:S(2)}, u32[]{:S(2)}) collective-permute-start(bf16[8,8192]{1,0:T(8,128)(2,1)S(1)} %collective-permute-done.3.refs_4_), channel_id=1, source_target_pairs={{0,1},{1,0},{2,3},{3,2},{4,5},{5,4},{6,7},{7,6},{8,9},{9,8},{10,11... | collective-permute-start | bytes 393224 | tf_op jit(solution)/shard_map/ppermute | solution.py:306
  10.4 7.3 %collective-permute-start.2 = (bf16[8,8192]{1,0:T(8,128)(2,1)S(1)}, bf16[8,8192]{1,0:T(8,128)(2,1)S(1)}, u32[]{:S(2)}, u32[]{:S(2)}) collective-permute-start(bf16[8,8192]{1,0:T(8,128)(2,1)S(1)} %collective-permute-done.1.refs_2_), channel_id=1, source_target_pairs={{0,1},{1,0},{2,3},{3,2},{4,5},{5,4},{6,7},{7,6},{8,9},{9,8},{10,11... | collective-permute-start | bytes 393224 | tf_op jit(solution)/shard_map/ppermute | solution.py:306
  12.8 7.4 %collective-permute-start.11 = (bf16[8,8192]{1,0:T(8,128)(2,1)S(1)}, bf16[8,8192]{1,0:T(8,128)(2,1)S(1)}, u32[]{:S(2)}, u32[]{:S(2)}) collective-permute-start(bf16[8,8192]{1,0:T(8,128)(2,1)S(1)} %collective-permute-done.7.odd_ref.refs_8_), channel_id=1, source_target_pairs={{0,2},{1,3},{4,0},{5,1},{8,4},{9,5},{12,8},{13,9},{14,12},{15,13},... | collective-permute-start | bytes 393224 | tf_op jit(solution)/shard_map/ppermute | solution.py:297
  14.5 7.4 %collective-permute-start.13 = (bf16[8,8192]{1,0:T(8,128)(2,1)S(1)}, bf16[8,8192]{1,0:T(8,128)(2,1)S(1)}, u32[]{:S(2)}, u32[]{:S(2)}) collective-permute-start(bf16[8,8192]{1,0:T(8,128)(2,1)S(1)} %pick.1), channel_id=1, source_target_pairs={{0,8},{1,7},{4,12},{5,3},{8,14},{9,1},{12,10},{13,5},{14,6},{15,9}... | collective-permute-start | bytes 393224 | tf_op jit(solution)/shard_map/ppermute | solution.py:297
  16.1 6.0 %collective-permute-start.9 = (bf16[8,8192]{1,0:T(8,128)(2,1)S(1)}, bf16[8,8192]{1,0:T(8,128)(2,1)S(1)}, u32[]{:S(2)}, u32[]{:S(2)}) collective-permute-start(bf16[8,8192]{1,0:T(8,128)(2,1)S(1)} %collective-permute-done.5.even_ref.refs_6_), channel_id=1, source_target_pairs={{0,4},{1,5},{4,8},{5,9},{8,12},{9,13},{12,14},{13,15},{14,10},{15,... | collective-permute-start | bytes 393224 | tf_op jit(solution)/shard_map/ppermute | solution.py:297
  17.7 4.8 %collective-permute-start.8 = (bf16[8,8192]{1,0:T(8,128)(2,1)S(1)}, bf16[8,8192]{1,0:T(8,128)(2,1)S(1)}, u32[]{:S(2)}, u32[]{:S(2)}) collective-permute-start(bf16[8,8192]{1,0:T(8,128)(2,1)S(1)} %collective-permute-done.7.odd_ref.refs_8_), channel_id=1, source_target_pairs={{0,1},{1,0},{2,3},{3,2},{4,5},{5,4},{6,7},{7,6},{8,9},{9,8},{10,11... | collective-permute-start | bytes 393224 | tf_op jit(solution)/shard_map/ppermute | solution.py:306
  17.7 4.8 %collective-permute-start.6 = (bf16[8,8192]{1,0:T(8,128)(2,1)S(1)}, bf16[8,8192]{1,0:T(8,128)(2,1)S(1)}, u32[]{:S(2)}, u32[]{:S(2)}) collective-permute-start(bf16[8,8192]{1,0:T(8,128)(2,1)S(1)} %collective-permute-done.5.even_ref.refs_6_), channel_id=1, source_target_pairs={{0,1},{1,0},{2,3},{3,2},{4,5},{5,4},{6,7},{7,6},{8,9},{9,8},{10,11... | collective-permute-start | bytes 393224 | tf_op jit(solution)/shard_map/ppermute | solution.py:306
  20.2 2.2 %collective-permute-start.12 = (bf16[8,8192]{1,0:T(8,128)(2,1)S(1)}, bf16[8,8192]{1,0:T(8,128)(2,1)S(1)}, u32[]{:S(2)}, u32[]{:S(2)}) collective-permute-start(bf16[8,8192]{1,0:T(8,128)(2,1)S(1)} %collective-permute-done.11.refs_12_), channel_id=1, source_target_pairs={{0,1},{1,0},{2,3},{3,2},{4,5},{5,4},{6,7},{7,6},{8,9},{9,8},{10,11... | collective-permute-start | bytes 393224 | tf_op jit(solution)/shard_map/ppermute | solution.py:306
  21.9 1.3 %collective-permute-start.14 = (bf16[8,8192]{1,0:T(8,128)(2,1)S(1)}, bf16[8,8192]{1,0:T(8,128)(2,1)S(1)}, u32[]{:S(2)}, u32[]{:S(2)}) collective-permute-start(bf16[8,8192]{1,0:T(8,128)(2,1)S(1)} %collective-permute-done.13.refs_14_), channel_id=1, source_target_pairs={{0,1},{1,0},{2,3},{3,2},{4,5},{5,4},{6,7},{7,6},{8,9},{9,8},{10,11... | collective-permute-start | bytes 393224 | tf_op jit(solution)/shard_map/ppermute | solution.py:306
  22.1 1.3 %collective-permute-start.10 = (bf16[8,8192]{1,0:T(8,128)(2,1)S(1)}, bf16[8,8192]{1,0:T(8,128)(2,1)S(1)}, u32[]{:S(2)}, u32[]{:S(2)}) collective-permute-start(bf16[8,8192]{1,0:T(8,128)(2,1)S(1)} %collective-permute-done.9.refs_10_), channel_id=1, source_target_pairs={{0,1},{1,0},{2,3},{3,2},{4,5},{5,4},{6,7},{7,6},{8,9},{9,8},{10,11... | collective-permute-start | bytes 393224 | tf_op jit(solution)/shard_map/ppermute | solution.py:306
  28.6 6.7 %collective-permute-start.15 = (bf16[128,256]{1,0:T(8,128)(2,1)S(1)}, bf16[128,256]{1,0:T(8,128)(2,1)S(1)}, u32[]{:S(2)}, u32[]{:S(2)}) collective-permute-start(bf16[128,256]{1,0:T(8,128)(2,1)S(1)} %get-tuple-element.20.value_ref), channel_id=1, source_target_pairs={{0,8},{1,9},{2,10},{3,11},{4,12},{5,13},{6,14},{7,15},{8,0},{9,1},... | collective-permute-start | bytes 196616 | tf_op jit(solution)/shard_map/ppermute | solution.py:306
  31.4 4.3 %collective-permute-start.19 = (bf16[128,256]{1,0:T(8,128)(2,1)S(1)}, bf16[128,256]{1,0:T(8,128)(2,1)S(1)}, u32[]{:S(2)}, u32[]{:S(2)}) collective-permute-start(bf16[128,256]{1,0:T(8,128)(2,1)S(1)} %get-tuple-element.21.value_ref), channel_id=1, source_target_pairs={{0,2},{1,3},{2,0},{3,1},{4,6},{5,7},{6,4},{7,5},{8,10},{9,11},{10,... | collective-permute-start | bytes 196616 | tf_op jit(solution)/shard_map/ppermute | solution.py:306
  32.1 5.2 %collective-permute-start.23 = (bf16[128,256]{1,0:T(8,128)(2,1)S(1)}, bf16[128,256]{1,0:T(8,128)(2,1)S(1)}, u32[]{:S(2)}, u32[]{:S(2)}) collective-permute-start(bf16[128,256]{1,0:T(8,128)(2,1)S(1)} %get-tuple-element.22.value_ref), channel_id=1, source_target_pairs={{0,1},{1,0},{2,3},{3,2},{4,5},{5,4},{6,7},{7,6},{8,9},{9,8},{10,11... | collective-permute-start | bytes 196616 | tf_op jit(solution)/shard_map/ppermute | solution.py:306
  32.1 6.2 %collective-permute-start.27 = (bf16[128,256]{1,0:T(8,128)(2,1)S(1)}, bf16[128,256]{1,0:T(8,128)(2,1)S(1)}, u32[]{:S(2)}, u32[]{:S(2)}) collective-permute-start(bf16[128,256]{1,0:T(8,128)(2,1)S(1)} %get-tuple-element.23.value_ref), channel_id=1, source_target_pairs={{0,4},{1,5},{2,6},{3,7},{4,0},{5,1},{6,2},{7,3},{8,12},{9,13},{10,... | collective-permute-start | bytes 196616 | tf_op jit(solution)/shard_map/ppermute | solution.py:306
  35.3 5.2 %collective-permute-start.16 = (bf16[128,256]{1,0:T(8,128)(2,1)S(1)}, bf16[128,256]{1,0:T(8,128)(2,1)S(1)}, u32[]{:S(2)}, u32[]{:S(2)}) collective-permute-start(bf16[128,256]{1,0:T(8,128)(2,1)S(1)} %turn.16.value_ref), channel_id=1, source_target_pairs={{0,1},{1,0},{2,3},{3,2},{4,5},{5,4},{6,7},{7,6},{8,9},{9,8},{10,11... | collective-permute-start | bytes 196616 | tf_op jit(solution)/shard_map/ppermute | solution.py:306
  35.7 6.3 %collective-permute-start.20 = (bf16[128,256]{1,0:T(8,128)(2,1)S(1)}, bf16[128,256]{1,0:T(8,128)(2,1)S(1)}, u32[]{:S(2)}, u32[]{:S(2)}) collective-permute-start(bf16[128,256]{1,0:T(8,128)(2,1)S(1)} %turn.20.value_ref), channel_id=1, source_target_pairs={{0,4},{1,5},{2,6},{3,7},{4,0},{5,1},{6,2},{7,3},{8,12},{9,13},{10,... | collective-permute-start | bytes 196616 | tf_op jit(solution)/shard_map/ppermute | solution.py:306
  37.4 17.4 %slice-start = ((s8[16777216]{0:T(1024)(128)(4,1)}), s8[4194304]{0:T(1024)(128)(4,1)S(1)}, s32[]{:S(2)}) async-start(s8[16777216]{0:T(1024)(128)(4,1)} %bitcast.2), calls=%async_computation | async-start | bytes 8388608
  37.4 17.4 %copy-start.3 = (f32[1024]{0:T(1024)S(1)}, f32[1024]{0:T(1024)}, u32[]{:S(2)}) copy-start(f32[1024]{0:T(1024)} %param.11) | copy-start | bytes 12292
  37.4 5.3 %collective-permute-start.24 = (bf16[128,256]{1,0:T(8,128)(2,1)S(1)}, bf16[128,256]{1,0:T(8,128)(2,1)S(1)}, u32[]{:S(2)}, u32[]{:S(2)}) collective-permute-start(bf16[128,256]{1,0:T(8,128)(2,1)S(1)} %turn.24.value_ref), channel_id=1, source_target_pairs={{0,2},{1,3},{2,0},{3,1},{4,6},{5,7},{6,4},{7,5},{8,10},{9,11},{10,... | collective-permute-start | bytes 196616 | tf_op jit(solution)/shard_map/ppermute | solution.py:306
  38.4 7.6 %collective-permute-start.28 = (bf16[128,256]{1,0:T(8,128)(2,1)S(1)}, bf16[128,256]{1,0:T(8,128)(2,1)S(1)}, u32[]{:S(2)}, u32[]{:S(2)}) collective-permute-start(bf16[128,256]{1,0:T(8,128)(2,1)S(1)} %turn.28.value_ref), channel_id=1, source_target_pairs={{0,8},{1,9},{2,10},{3,11},{4,12},{5,13},{6,14},{7,15},{8,0},{9,1},... | collective-permute-start | bytes 196616 | tf_op jit(solution)/shard_map/ppermute | solution.py:306
  40.5 5.6 %collective-permute-start.17 = (bf16[128,256]{1,0:T(8,128)(2,1)S(1)}, bf16[128,256]{1,0:T(8,128)(2,1)S(1)}, u32[]{:S(2)}, u32[]{:S(2)}) collective-permute-start(bf16[128,256]{1,0:T(8,128)(2,1)S(1)} %turn.17.value_ref), channel_id=1, source_target_pairs={{0,2},{1,3},{2,0},{3,1},{4,6},{5,7},{6,4},{7,5},{8,10},{9,11},{10,... | collective-permute-start | bytes 196616 | tf_op jit(solution)/shard_map/ppermute | solution.py:306
  42.0 12.7 %slice-start.1 = ((s8[16777216]{0:T(1024)(128)(4,1)}), s8[4194304]{0:T(1024)(128)(4,1)S(1)}, s32[]{:S(2)}) async-start(s8[16777216]{0:T(1024)(128)(4,1)} %bitcast.2), calls=%async_computation.1 | async-start | bytes 8388608
  42.0 5.8 %collective-permute-start.21 = (bf16[128,256]{1,0:T(8,128)(2,1)S(1)}, bf16[128,256]{1,0:T(8,128)(2,1)S(1)}, u32[]{:S(2)}, u32[]{:S(2)}) collective-permute-start(bf16[128,256]{1,0:T(8,128)(2,1)S(1)} %turn.21.value_ref), channel_id=1, source_target_pairs={{0,8},{1,9},{2,10},{3,11},{4,12},{5,13},{6,14},{7,15},{8,0},{9,1},... | collective-permute-start | bytes 196616 | tf_op jit(solution)/shard_map/ppermute | solution.py:306
  42.7 5.3 %collective-permute-start.25 = (bf16[128,256]{1,0:T(8,128)(2,1)S(1)}, bf16[128,256]{1,0:T(8,128)(2,1)S(1)}, u32[]{:S(2)}, u32[]{:S(2)}) collective-permute-start(bf16[128,256]{1,0:T(8,128)(2,1)S(1)} %turn.25.value_ref), channel_id=1, source_target_pairs={{0,4},{1,5},{2,6},{3,7},{4,0},{5,1},{6,2},{7,3},{8,12},{9,13},{10,... | collective-permute-start | bytes 196616 | tf_op jit(solution)/shard_map/ppermute | solution.py:306
  46.0 3.5 %collective-permute-start.29 = (bf16[128,256]{1,0:T(8,128)(2,1)S(1)}, bf16[128,256]{1,0:T(8,128)(2,1)S(1)}, u32[]{:S(2)}, u32[]{:S(2)}) collective-permute-start(bf16[128,256]{1,0:T(8,128)(2,1)S(1)} %turn.29.value_ref), channel_id=1, source_target_pairs={{0,1},{1,0},{2,3},{3,2},{4,5},{5,4},{6,7},{7,6},{8,9},{9,8},{10,11... | collective-permute-start | bytes 196616 | tf_op jit(solution)/shard_map/ppermute | solution.py:306
  46.1 8.7 %slice-start.2 = ((s8[16777216]{0:T(1024)(128)(4,1)}), s8[4194304]{0:T(1024)(128)(4,1)S(1)}, s32[]{:S(2)}) async-start(s8[16777216]{0:T(1024)(128)(4,1)} %bitcast.2), calls=%async_computation.2 | async-start | bytes 8388608
  46.1 4.5 %collective-permute-start.18 = (bf16[128,256]{1,0:T(8,128)(2,1)S(1)}, bf16[128,256]{1,0:T(8,128)(2,1)S(1)}, u32[]{:S(2)}, u32[]{:S(2)}) collective-permute-start(bf16[128,256]{1,0:T(8,128)(2,1)S(1)} %turn.18.value_ref), channel_id=1, source_target_pairs={{0,4},{1,5},{2,6},{3,7},{4,0},{5,1},{6,2},{7,3},{8,12},{9,13},{10,... | collective-permute-start | bytes 196616 | tf_op jit(solution)/shard_map/ppermute | solution.py:306
  47.9 2.8 %collective-permute-start.22 = (bf16[128,256]{1,0:T(8,128)(2,1)S(1)}, bf16[128,256]{1,0:T(8,128)(2,1)S(1)}, u32[]{:S(2)}, u32[]{:S(2)}) collective-permute-start(bf16[128,256]{1,0:T(8,128)(2,1)S(1)} %turn.22.value_ref), channel_id=1, source_target_pairs={{0,1},{1,0},{2,3},{3,2},{4,5},{5,4},{6,7},{7,6},{8,9},{9,8},{10,11... | collective-permute-start | bytes 196616 | tf_op jit(solution)/shard_map/ppermute | solution.py:306
  48.1 6.6 %collective-permute-start.26 = (bf16[128,256]{1,0:T(8,128)(2,1)S(1)}, bf16[128,256]{1,0:T(8,128)(2,1)S(1)}, u32[]{:S(2)}, u32[]{:S(2)}) collective-permute-start(bf16[128,256]{1,0:T(8,128)(2,1)S(1)} %turn.26.value_ref), channel_id=1, source_target_pairs={{0,8},{1,9},{2,10},{3,11},{4,12},{5,13},{6,14},{7,15},{8,0},{9,1},... | collective-permute-start | bytes 196616 | tf_op jit(solution)/shard_map/ppermute | solution.py:306
  49.5 5.3 %slice-start.3 = ((s8[16777216]{0:T(1024)(128)(4,1)}), s8[4194304]{0:T(1024)(128)(4,1)S(1)}, s32[]{:S(2)}) async-start(s8[16777216]{0:T(1024)(128)(4,1)} %bitcast.2), calls=%async_computation.3 | async-start | bytes 8388608
  49.5 5.2 %collective-permute-start.30 = (bf16[128,256]{1,0:T(8,128)(2,1)S(1)}, bf16[128,256]{1,0:T(8,128)(2,1)S(1)}, u32[]{:S(2)}, u32[]{:S(2)}) collective-permute-start(bf16[128,256]{1,0:T(8,128)(2,1)S(1)} %turn.30.value_ref), channel_id=1, source_target_pairs={{0,2},{1,3},{2,0},{3,1},{4,6},{5,7},{6,4},{7,5},{8,10},{9,11},{10,... | collective-permute-start | bytes 196616 | tf_op jit(solution)/shard_map/ppermute | solution.py:306
  56.3 22.8 %copy-start.2 = (bf16[8,8192]{1,0:T(8,128)(2,1)S(1)}, bf16[8,8192]{1,0:T(8,128)(2,1)}, u32[]{:S(2)}) copy-start(bf16[8,8192]{1,0:T(8,128)(2,1)} %tokens_ref.1) | copy-start | bytes 393220
  56.3 1.8 %collective-permute-start.31 = (bf16[48,4096]{1,0:T(8,128)(2,1)S(1)}, bf16[48,4096]{1,0:T(8,128)(2,1)S(1)}, u32[]{:S(2)}, u32[]{:S(2)}) collective-permute-start(bf16[48,4096]{1,0:T(8,128)(2,1)S(1)} %get-tuple-element.26), channel_id=1, source_target_pairs={{0,1},{1,0},{2,3},{3,2},{4,5},{5,4},{6,7},{7,6},{8,9},{9,8},{10,11... | collective-permute-start | bytes 1179656 | tf_op jit(solution)/shard_map/ppermute | solution.py:306
  58.1 9.0 %collective-permute-start.32 = (bf16[80,4096]{1,0:T(8,128)(2,1)S(1)}, bf16[80,4096]{1,0:T(8,128)(2,1)S(1)}, u32[]{:S(2)}, u32[]{:S(2)}) collective-permute-start(bf16[80,4096]{1,0:T(8,128)(2,1)S(1)} %get-tuple-element.27), channel_id=1, source_target_pairs={{0,1},{1,0},{2,3},{3,2},{4,5},{5,4},{6,7},{7,6},{8,9},{9,8},{10,11... | collective-permute-start | bytes 1966088 | tf_op jit(solution)/shard_map/ppermute | solution.py:306
  58.4 5.6 %collective-permute-start.33 = (bf16[16,4096]{1,0:T(8,128)(2,1)S(1)}, bf16[16,4096]{1,0:T(8,128)(2,1)S(1)}, u32[]{:S(2)}, u32[]{:S(2)}) collective-permute-start(bf16[16,4096]{1,0:T(8,128)(2,1)S(1)} %sum.3), channel_id=1, source_target_pairs={{0,4},{1,5},{4,8},{5,9},{8,12},{9,13},{12,14},{13,15},{14,10},{15,... | collective-permute-start | bytes 393224 | tf_op jit(solution)/shard_map/ppermute | solution.py:297
  58.6 8.5 %collective-permute-start.34 = (bf16[16,4096]{1,0:T(8,128)(2,1)S(1)}, bf16[16,4096]{1,0:T(8,128)(2,1)S(1)}, u32[]{:S(2)}, u32[]{:S(2)}) collective-permute-start(bf16[16,4096]{1,0:T(8,128)(2,1)S(1)} %sum.4), channel_id=1, source_target_pairs={{0,8},{1,7},{4,12},{5,3},{8,14},{9,1},{12,10},{13,5},{14,6},{15,9}... | collective-permute-start | bytes 393224 | tf_op jit(solution)/shard_map/ppermute | solution.py:297
  60.9 7.0 %collective-permute-start.37 = (bf16[16,4096]{1,0:T(8,128)(2,1)S(1)}, bf16[16,4096]{1,0:T(8,128)(2,1)S(1)}, u32[]{:S(2)}, u32[]{:S(2)}) collective-permute-start(bf16[16,4096]{1,0:T(8,128)(2,1)S(1)} %sum.5), channel_id=1, source_target_pairs={{0,2},{1,3},{4,0},{5,1},{8,4},{9,5},{12,8},{13,9},{14,12},{15,13},... | collective-permute-start | bytes 393224 | tf_op jit(solution)/shard_map/ppermute | solution.py:297
  67.2 5.0 %collective-permute-start.35 = (bf16[16,4096]{1,0:T(8,128)(2,1)S(1)}, bf16[16,4096]{1,0:T(8,128)(2,1)S(1)}, u32[]{:S(2)}, u32[]{:S(2)}) collective-permute-start(bf16[16,4096]{1,0:T(8,128)(2,1)S(1)} %relay.2), channel_id=1, source_target_pairs={{0,4},{1,5},{4,8},{5,9},{8,12},{9,13},{12,14},{13,15},{14,10},{15,... | collective-permute-start | bytes 393224 | tf_op jit(solution)/shard_map/ppermute | solution.py:297
  68.0 5.5 %collective-permute-start.38 = (bf16[16,4096]{1,0:T(8,128)(2,1)S(1)}, bf16[16,4096]{1,0:T(8,128)(2,1)S(1)}, u32[]{:S(2)}, u32[]{:S(2)}) collective-permute-start(bf16[16,4096]{1,0:T(8,128)(2,1)S(1)} %relay.3), channel_id=1, source_target_pairs={{0,2},{1,3},{4,0},{5,1},{8,4},{9,5},{12,8},{13,9},{14,12},{15,13},... | collective-permute-start | bytes 393224 | tf_op jit(solution)/shard_map/ppermute | solution.py:297
  69.4 6.5 %collective-permute-start.40 = (bf16[8,4096]{1,0:T(8,128)(2,1)S(1)}, bf16[8,4096]{1,0:T(8,128)(2,1)S(1)}, u32[]{:S(2)}, u32[]{:S(2)}) collective-permute-start(bf16[8,4096]{1,0:T(8,128)(2,1)S(1)} %get-tuple-element.32), channel_id=1, source_target_pairs={{0,1},{1,0},{2,3},{3,2},{4,5},{5,4},{6,7},{7,6},{8,9},{9,8},{10,11... | collective-permute-start | bytes 196616 | tf_op jit(solution)/shard_map/ppermute | solution.py:306
  72.3 4.5 %collective-permute-start.36 = (bf16[8,4096]{1,0:T(8,128)(2,1)S(1)}, bf16[8,4096]{1,0:T(8,128)(2,1)S(1)}, u32[]{:S(2)}, u32[]{:S(2)}) collective-permute-start(bf16[8,4096]{1,0:T(8,128)(2,1)S(1)} %get-tuple-element.30), channel_id=1, source_target_pairs={{0,4},{1,5},{4,8},{5,9},{8,12},{9,13},{12,14},{13,15},{14,10},{15,... | collective-permute-start | bytes 196616 | tf_op jit(solution)/shard_map/ppermute | solution.py:297
  72.3 4.4 %collective-permute-start.41 = (bf16[8,4096]{1,0:T(8,128)(2,1)S(1)}, bf16[8,4096]{1,0:T(8,128)(2,1)S(1)}, u32[]{:S(2)}, u32[]{:S(2)}) collective-permute-start(bf16[8,4096]{1,0:T(8,128)(2,1)S(1)} %get-tuple-element.33), channel_id=1, source_target_pairs={{0,5},{1,4},{4,9},{5,8},{8,13},{9,12},{12,15},{13,14},{14,11},{15,... | collective-permute-start | bytes 196616 | tf_op jit(solution)/shard_map/ppermute | solution.py:359
  73.6 4.9 %collective-permute-start.39 = (bf16[8,4096]{1,0:T(8,128)(2,1)S(1)}, bf16[8,4096]{1,0:T(8,128)(2,1)S(1)}, u32[]{:S(2)}, u32[]{:S(2)}) collective-permute-start(bf16[8,4096]{1,0:T(8,128)(2,1)S(1)} %get-tuple-element.31), channel_id=1, source_target_pairs={{0,2},{1,3},{4,0},{5,1},{8,4},{9,5},{12,8},{13,9},{14,12},{15,13},... | collective-permute-start | bytes 196616 | tf_op jit(solution)/shard_map/ppermute | solution.py:297
  74.5 4.6 %collective-permute-start.42 = (bf16[8,4096]{1,0:T(8,128)(2,1)S(1)}, bf16[8,4096]{1,0:T(8,128)(2,1)S(1)}, u32[]{:S(2)}, u32[]{:S(2)}) collective-permute-start(bf16[8,4096]{1,0:T(8,128)(2,1)S(1)} %get-tuple-element.34), channel_id=1, source_target_pairs={{0,3},{1,2},{4,1},{5,0},{8,5},{9,4},{12,9},{13,8},{14,13},{15,12},... | collective-permute-start | bytes 196616 | tf_op jit(solution)/shard_map/ppermute | solution.py:359
